TPU v7x, 512 devices: a whole 4x8x8 slice. The times are simulated.
512 devices in a mesh: amp: 32 (over z_lo, x, core), intg: 16 (over z_hi, y).
Axes of the slice: x: 4, y: 8, z: 8 (z_hi: 2, z_lo: 4; z = z_hi * 4 + z_lo), core: 2. Of those that a mesh axis runs over, the one named last changes fastest.
Arguments:
- amplitudes: float32 [1, 128, 53248], P(None, 'intg', 'amp'), may hold values from -6 to 6
- cycle_block: float32 [8192, 8192], P('intg', 'amp'), may hold values from -0.0625 to 0.0625
- ladder_block: float32 [64, 64, 53248], P('intg', None, 'amp'), may hold values from -0.09375 to 0.09375
- occupied_energy: float32 [128], replicated, may hold values from -2.5 to -0.5
- virtual_energy: float32 [832], replicated, may hold values from 0.5 to 4
- window_tiles: int32 [2], replicated, may hold values from 0 to 12
Outputs:
- updated: float32 [1, 128, 53248], P(None, 'intg', 'amp')
Inputs may be any that keep to these rules, and one draw needn't show every extreme that they name: `window_tiles`: virtual tile indices.
All inputs are finite; a program needn't handle non-finite values.
Results may differ from a plain program's by a relative error of at most 0.00007.
Values sent between devices are 32-bit elements; how exact they have to be, the bound alone decides.
No kernel may reach another device: no remote copies, remote signals or barrier semaphores. Data moves between devices by JAX's collectives and lax.ppermute only.
A program may use at most 128 MiB of HBM per device.

v0:
```python
import jax
import jax.numpy as jnp
from jax import lax
from jax.sharding import PartitionSpec as P


def per_device(
    amplitudes, cycle_block, ladder_block, occupied_energy, virtual_energy, window_tiles
):
    highest = lax.Precision.HIGHEST
    tile_width = ladder_block.shape[1]
    slab_count, local_rows, local_flat = amplitudes.shape
    local_columns = local_flat // tile_width
    gathered = lax.all_gather(amplitudes, "amp", axis=2, tiled=True)
    all_columns = gathered.shape[2] // tile_width
    cycle_cols = cycle_block.shape[1] // tile_width
    left_matrix = gathered.reshape(slab_count, local_rows, all_columns, tile_width)
    left_matrix = jnp.transpose(left_matrix, (0, 2, 1, 3)).reshape(
        slab_count * all_columns, local_rows * tile_width
    )
    cycle_part = jnp.dot(
        left_matrix, cycle_block, precision=highest, preferred_element_type=jnp.float32
    )
    cycle_part = cycle_part.reshape(slab_count, all_columns, cycle_cols, tile_width)
    cycle_part = jnp.transpose(cycle_part, (0, 2, 1, 3)).reshape(
        slab_count, cycle_cols, all_columns * tile_width
    )
    regrouped = lax.all_to_all(cycle_part, "amp", split_axis=2, concat_axis=1, tiled=True)
    ladder_start = window_tiles[1] * tile_width * tile_width
    ladder_slab = lax.dynamic_slice_in_dim(gathered, ladder_start, tile_width * tile_width, 2)
    ladder_slab = ladder_slab.reshape(slab_count, local_rows, tile_width, tile_width)
    ladder_slab = jnp.transpose(ladder_slab, (0, 1, 3, 2)).reshape(
        slab_count, local_rows, tile_width * tile_width
    )
    ladder_rows = lax.all_to_all(ladder_slab, "intg", split_axis=2, concat_axis=1, tiled=True)
    ladder_local = ladder_block.reshape(ladder_block.shape[0] * tile_width, local_flat)
    ladder_part = jnp.einsum("ijx,xy->ijy", ladder_rows, ladder_local, precision=highest)
    summed = lax.psum_scatter(regrouped + ladder_part, "intg", scatter_dimension=1, tiled=True)
    row_start = lax.axis_index("intg") * local_rows
    column_start = lax.axis_index("amp") * local_columns
    row_energy = lax.dynamic_slice_in_dim(occupied_energy, row_start, local_rows)
    column_energy = lax.dynamic_slice_in_dim(virtual_energy, column_start, local_columns)
    spectator = lax.dynamic_slice_in_dim(virtual_energy, window_tiles[0] * tile_width, tile_width)
    slab_energy = occupied_energy[:slab_count]
    column_term = (column_energy[:, None] + spectator[None, :]).reshape(local_flat)
    denominator = (
        column_term[None, None, :] - slab_energy[:, None, None] - row_energy[None, :, None]
    )
    return summed / denominator


def solution(mesh):
    return jax.shard_map(
        per_device,
        mesh=mesh,
        in_specs=(P(None, "intg", "amp"), P("intg", "amp"), P("intg", None, "amp"), P(), P(), P()),
        out_specs=P(None, "intg", "amp"),
        check_vma=False,
    )
```

profile of v0, /device:TPU:2, one launch (start us, length us, event | category | flops | bytes accessed | tf_op | source)
XLA Modules:
  0.0 712.7 jit_solution(1208564235816539433)
XLA Ops:
  6.5 0.0 copy-start
  6.5 0.0 all-gather.2.cloned.1.call-start
  6.5 0.7 all-gather.2.cloned.1.call-update
  7.3 1.3 fusion.3
  9.2 67.6 %all-gather.2.cloned.1.call-done = f32[1,8,53248]{2,1,0:T(8,128)} async-done(((f32[1,8,1664]{2,1,0:T(8,128)}), f32[1,8,53248]{2,1,0:T(8,128)}) %all-gather.2.cloned.1.call-update) | async-done | bytes 1703952 | tf_op jit(solution)/shard_map/all_gather | solution.py:14
  76.8 0.9 constant_dynamic-slice_fusion
  77.7 0.1 reshape.108
  77.8 2.8 copy.49
  80.6 0.5 broadcast.53
  81.1 20.4 %reduce.2 = f32[4096,8]{1,0:T(8,128)} reduce(f32[4096,1,8]{2,1,0:T(1,128)} %bitcast.42, f32[]{:T(128)} %broadcast.53), dimensions={1}, to_apply=%bitcast.32.reduce_sub_computation | reduce | bytes 262148
  101.5 0.0 copy-start.1
  101.5 3.5 reshape.118
  105.0 10.8 %all-to-all-start.1 = ((f32[16,1,2048]{2,1,0:T(1,128)}), f32[16,1,2048]{2,1,0:T(1,128)}, u32[]{:S(2)}, u32[]{:S(2)}) async-start(f32[16,1,2048]{2,1,0:T(1,128)} %reshape.118), calls=%async_computation.1 | async-start | bytes 262144 | tf_op jit(solution)/shard_map/all_to_all | solution.py:35
  115.9 2.0 copy.37
  117.9 0.0 copy-done.1
  117.9 3.1 reshape.105
  121.0 2.5 copy.36
  123.5 3.9 convolution_bitcast_fusion
  127.4 23.7 %copy.48 = f32[1,4,832,64]{1,3,2,0:T(8,128)} copy(f32[1,4,832,64]{2,3,1,0:T(8,128)} %convolution_bitcast_fusion) | data formatting | bytes 1703936 | tf_op jit(solution)/shard_map/reshape | solution.py:25
  151.2 236.7 %reduce = f32[53248,4]{1,0:T(8,128)} reduce(f32[53248,1,4]{2,1,0:T(1,128)} %bitcast.39, f32[]{:T(128)} %broadcast.53), dimensions={1}, to_apply=%bitcast.30.reduce_sub_computation | reduce | bytes 1703940
  387.9 26.5 %reshape.116 = f32[32,1,6656]{2,1,0:T(1,128)} reshape(f32[53248,4]{1,0:T(8,128)} %reduce) | data formatting | bytes 1703936
  414.4 0.0 all-to-all-done.1
  414.4 5.8 all-to-all-start
  420.2 0.0 all-reduce.3.cloned.1.call-start
  420.3 1.9 reduce.3
  422.2 4.9 reshape.119
  427.0 2.2 copy.50
  429.2 12.8 %all-to-all-done = f32[32,1,6656]{2,1,0:T(1,128)S(1)} async-done(((f32[32,1,6656]{2,1,0:T(1,128)}), f32[32,1,6656]{2,1,0:T(1,128)S(1)}, u32[]{:S(2)}, u32[]{:S(2)}) %all-to-all-start) | async-done | bytes 852000 | tf_op jit(solution)/shard_map/all_to_all | solution.py:28
  442.0 2.7 reduce.1
  444.6 42.2 %reshape.117 = f32[53248,1,4]{2,1,0:T(1,128)} reshape(f32[32,6656]{1,0:T(8,128)S(1)} %reduce.1) | data formatting | bytes 1703936
  486.9 15.0 %copy.41 = f32[1,4,32,1664]{3,1,2,0:T(4,128)S(1)} copy(f32[1,4,32,1664]{1,3,2,0:T(8,128)} %bitcast.40) | data formatting | bytes 1703936 | tf_op jit(solution)/shard_map/all_to_all | solution.py:28
  501.9 0.3 all_to_all.27
  502.2 0.0 copy-done
  502.2 0.0 copy-start.2
  502.2 2.0 fusion
  504.2 0.0 all-reduce.3.cloned.1.call-update
  504.9 0.8 dynamic_slice.13
  505.7 0.8 dynamic_slice.14
  506.4 0.0 copy-done.2
  506.4 0.1 add_subtract_fusion
  506.5 0.1 sub.42
  506.6 0.1 dynamic_slice.15
  506.7 1.3 dynamic-slice
  508.6 195.6 %all-reduce.3.cloned.1.call-done = f32[1,128,1664]{2,1,0:T(8,128)} async-done(((f32[1,128,1664]{2,1,0:T(8,128)}), f32[1,128,1664]{2,1,0:T(8,128)}) %all-reduce.3.cloned.1.call-update) | async-done | bytes 851984
  704.2 1.5 dynamic-slice_divide_fusion
Async XLA Ops:
  6.5 495.6 %copy-start = (f32[4,64,1664]{2,1,0:T(8,128)S(1)}, f32[4,64,1664]{2,1,0:T(8,128)}, u32[]{:S(2)}) copy-start(f32[4,64,1664]{2,1,0:T(8,128)} %param.8) | copy-start | bytes 5111812
  6.5 70.3 %all-gather.2.cloned.1.call-start = ((), (), s32[]{:S(2)}) async-start(), calls=%async_computation.2 | async-start | bytes 1757184 | tf_op jit(solution)/shard_map/all_gather | solution.py:14
  101.5 16.4 %copy-start.1 = (f32[1,8,53248]{2,1,0:T(8,128)S(1)}, f32[1,8,53248]{2,1,0:T(8,128)}, u32[]{:S(2)}) copy-start(f32[1,8,53248]{2,1,0:T(8,128)} %all-gather.2.cloned.1.call-done) | copy-start | bytes 5111812
  105.0 309.4 %all-to-all-start.1 = ((f32[16,1,2048]{2,1,0:T(1,128)}), f32[16,1,2048]{2,1,0:T(1,128)}, u32[]{:S(2)}, u32[]{:S(2)}) async-start(f32[16,1,2048]{2,1,0:T(1,128)} %reshape.118), calls=%async_computation.1 | async-start | bytes 262144 | tf_op jit(solution)/shard_map/all_to_all | solution.py:35
  414.4 27.6 %all-to-all-start = ((f32[32,1,6656]{2,1,0:T(1,128)}), f32[32,1,6656]{2,1,0:T(1,128)S(1)}, u32[]{:S(2)}, u32[]{:S(2)}) async-start(f32[32,1,6656]{2,1,0:T(1,128)} %reshape.116), calls=%async_computation | async-start | bytes 1703936 | tf_op jit(solution)/shard_map/all_to_all | solution.py:28
  420.2 283.9 %all-reduce.3.cloned.1.call-start = ((), (), s32[]{:S(2)}) async-start(), calls=%async_computation.3 | async-start | bytes 1703936
  502.2 4.2 copy-start.2
Sparse Core Ops, SparseCore 0:
  9.5 67.2 all-gather.1
  504.4 199.7 all-reduce.2
where the time goes:
time: 719 us; the launch traced here: 713 us
  waiting for transfers between devices  277 us (39%)
  other arithmetic  263 us (37%)
  local copies, waits for them, and re-layouts  134 us (19%)
  starting transfers between devices  16.7 us (2%)
  between operations  15.7 us (2%)
    unnamed x2, other arithmetic  257 us
    unnamed x3, waiting for transfers between devices  196 us
    unnamed x13, local copies, waits for them, and re-layouts  80.9 us
    all_gather x1, waiting for transfers between devices, per_device(): gathered = lax.all_gather(amplitudes, 'amp', axis=2, tiled=True)  67.6 us
    reshape x1, local copies, waits for them, and re-layouts, per_device(): jnp.transpose(cycle_part, (0, 2, 1, 3))  23.7 us
    all_to_all x2, local copies, waits for them, and re-layouts, per_device(): lax.all_to_all(cycle_part, 'amp', split_axis=2, concat_axis=1, tiled=True)  15.3 us
  transfers between devices with their start and end apart: 4, of which 3 were waited for; matrix products, arithmetic and copies ran while one was open for 44% of the time, Pallas kernels for 0%

commit v1 on v0

v1 whole, which is shorter than its diff:
```python
import functools

import jax
import jax.numpy as jnp
from jax import lax
from jax.experimental import pallas as pl
from jax.experimental.pallas import tpu as pltpu
from jax.sharding import Mesh
from jax.sharding import PartitionSpec as P

ZL, X, CORE, ZH, Y = 4, 4, 2, 2, 8
CHIPS = ZL * X
ROWS = 8
TILE = 64
PAIRS = 13
LANES = 2 * TILE
BLOCK = PAIRS * ROWS
EVERY = ("zl", "x", "core", "zh", "y")
VMEM = pl.BlockSpec(memory_space=pltpu.VMEM)
SMEM = pl.BlockSpec(memory_space=pltpu.SMEM)
PARAMS = pltpu.CompilerParams(vmem_limit_bytes=32 * 1024 * 1024)


def split(value):
    high = value.astype(jnp.bfloat16)
    return high, (value - high.astype(jnp.float32)).astype(jnp.bfloat16)


def product(left, right):
    dot = functools.partial(jnp.dot, preferred_element_type=jnp.float32)
    return dot(left[0], right[1]) + dot(left[1], right[0]) + dot(left[0], right[0])


def low_half(shape):
    return lax.broadcasted_iota(jnp.int32, shape, 1) < TILE


def pair_up(first, second):
    low = low_half(first.shape)
    return (
        jnp.where(low, first, pltpu.roll(second, TILE, 1)),
        jnp.where(low, pltpu.roll(first, TILE, 1), second),
    )


def pack_kernel(amplitudes, out):
    for pair in range(PAIRS):
        tile = amplitudes[0, :, pair * LANES : (pair + 1) * LANES]
        for chip in range(CHIPS):
            out[chip, pair * ROWS : (pair + 1) * ROWS, :] = tile


def window_kernel(tiles, gathered, out, window, columns, turned):
    core = lax.axis_index("core")
    for pair in range(TILE // 2):
        place = tiles[1] * (TILE // 2) + pair
        owner = place // PAIRS
        row = ((owner // 2) * PAIRS + (place - owner * PAIRS)) * ROWS
        tile = gathered[pl.ds(pl.multiple_of(row, ROWS), ROWS), :]
        window[pair * ROWS : (pair + 1) * ROWS, :] = jnp.where(owner % 2 == core, tile, 0.0)
    for half in range(ROWS // 2):
        for inner in range(2):
            both = window[pl.ds(half * 2 + inner, TILE // 2, stride=ROWS), :]
            columns[pl.ds(inner * TILE, TILE // 2, stride=2), :] = both
            columns[pl.ds(inner * TILE + 1, TILE // 2, stride=2), :] = pltpu.roll(both, TILE, 1)
        turned[...] = jnp.transpose(columns[...])
        for part in range(2):
            even = turned[pl.ds(2 * part, CHIPS, stride=4), :]
            odd = turned[pl.ds(2 * part + 1, CHIPS, stride=4), :]
            for inner, value in enumerate(pair_up(even, odd)):
                row = part * ROWS + half * 2 + inner
                for target in range(CORE):
                    out[pl.ds(target * CHIPS * 2 * ROWS + row, CHIPS, stride=2 * ROWS), :] = value


def cycle_kernel(gathered, own, other, out):
    core = lax.axis_index("core")
    chunks = ([], [])
    for k in range(0, ROWS, 2):
        first = gathered[pl.ds(k, CHIPS * PAIRS, stride=ROWS), :]
        second = gathered[pl.ds(k + 1, CHIPS * PAIRS, stride=ROWS), :]
        for chunk, value in zip(chunks, pair_up(first, second)):
            chunk.append(value)
    left = split(jnp.concatenate([jnp.concatenate(chunk, 1) for chunk in chunks], 0))
    for side in range(2):
        right = split(jnp.where(core == side, own[...], other[...]))
        result = product(left, right)
        for quarter in range(2):
            both = result[:, quarter * LANES : (quarter + 1) * LANES]
            rows = pair_up(both[: CHIPS * PAIRS], both[CHIPS * PAIRS :])
            for inner, value in enumerate(rows):
                j = side * 4 + quarter * 2 + inner
                out[pl.ds(j, CHIPS * PAIRS, stride=ROWS), :] = value


def ladder_kernel(received, integrals, out):
    lefts = []
    for part in range(2):
        rows = pl.ds(part * ROWS, ROWS)
        both = received[:CHIPS, rows, :] + received[CHIPS:, rows, :]
        lefts.append(both.reshape(CHIPS * ROWS, LANES))
    left = split(jnp.concatenate(lefts, 1))
    width = PAIRS * LANES
    for start in range(0, width, 2 * LANES):
        stop = min(start + 2 * LANES, width)
        result = product(left, split(integrals[:, start:stop]))
        for column in range(start, stop, LANES):
            value = result[:, column - start : column - start + LANES]
            rows = pl.ds(column // LANES * ROWS, ROWS)
            out[:, rows, :] = value.reshape(CHIPS, ROWS, LANES)


def last_kernel(tiles, occupied, virtual, ladder, near, far, out):
    column = lax.axis_index("zl") * (X * CORE) + lax.axis_index("x") * CORE + lax.axis_index("core")
    row = lax.axis_index("zh") * Y + lax.axis_index("y")
    shape = (ROWS, LANES)
    lane = lax.broadcasted_iota(jnp.int32, shape, 1)
    line = lax.broadcasted_iota(jnp.int32, shape, 0)
    spectator = jnp.zeros(shape, jnp.float32)
    for b in range(TILE):
        spectator = jnp.where(lane % TILE == b, virtual[tiles[0] * TILE + b], spectator)
    rows = jnp.zeros(shape, jnp.float32)
    for j in range(ROWS):
        rows = jnp.where(line == j, occupied[row * ROWS + j], rows)
    for pair in range(PAIRS):
        piece = pl.ds(pair * ROWS, ROWS)
        total = near[piece, :] + far[piece, :]
        for chip in range(CHIPS):
            total = total + ladder[chip, piece, :]
        a = column * (2 * PAIRS) + 2 * pair
        energy = jnp.where(lane < TILE, virtual[a], virtual[a + 1]) + spectator
        out[0, :, pair * LANES : (pair + 1) * LANES] = total / (energy - occupied[0] - rows)


def call(kernel, shape, specs, scratch=()):
    return pl.pallas_call(
        kernel,
        out_shape=jax.ShapeDtypeStruct(shape, jnp.float32),
        in_specs=specs,
        out_specs=VMEM,
        scratch_shapes=[pltpu.VMEM(s, jnp.float32) for s in scratch],
        compiler_params=PARAMS,
    )


def places(rule):
    pairs = []
    for chip in range(CHIPS):
        for core in range(CORE):
            for place in range(ZH * Y):
                to = rule(chip, core, place)
                pairs.append(
                    (
                        (chip * CORE + core) * ZH * Y + place,
                        (to[0] * CORE + to[1]) * ZH * Y + to[2],
                    )
                )
    return pairs


def near_rule(chip, core, place):
    zh, y = divmod(place, Y)
    return 2 * y + zh, core, chip


def far_rule(chip, core, place):
    zh, y = divmod(place, Y)
    return 2 * y + 1 - zh, core, chip


def per_device(amplitudes, cycle_block, ladder_block, occupied, virtual, tiles):
    other = lax.ppermute(cycle_block, "core", [(0, 1), (1, 0)])
    copies = call(pack_kernel, (CHIPS, BLOCK, LANES), [VMEM])(amplitudes)
    gathered = lax.all_to_all(copies, ("zl", "x"), 0, 0, tiled=True)
    gathered = gathered.reshape(CHIPS * BLOCK, LANES)
    window = call(
        window_kernel,
        (CORE * CHIPS * 2 * ROWS, LANES),
        [SMEM, VMEM],
        [(TILE // 2 * ROWS, LANES), (LANES, LANES), (LANES, LANES)],
    )(tiles, gathered)
    window = window.reshape(CORE * CHIPS, 2 * ROWS, LANES)
    window = lax.all_to_all(window, ("core", "zh", "y"), 0, 0, tiled=True)
    cycle = call(cycle_kernel, (CHIPS * BLOCK, LANES), [VMEM] * 3)(gathered, cycle_block, other)
    cycle = cycle.reshape(Y, ZH * BLOCK, LANES)
    cycle = lax.psum_scatter(cycle, "y", scatter_dimension=0, tiled=False)
    first, second = cycle[:BLOCK], cycle[BLOCK:]
    low = lax.axis_index("zh") == 0
    near = lax.ppermute(jnp.where(low, first, second), EVERY, places(near_rule))
    far = lax.ppermute(jnp.where(low, second, first), EVERY, places(far_rule))
    integrals = ladder_block.reshape(-1, ladder_block.shape[2])
    ladder = call(ladder_kernel, (CHIPS, BLOCK, LANES), [VMEM] * 2)(window, integrals)
    ladder = lax.all_to_all(ladder, ("zh", "y"), 0, 0, tiled=True)
    return call(last_kernel, amplitudes.shape, [SMEM] * 3 + [VMEM] * 3)(
        tiles, occupied, virtual, ladder, near, far
    )


def solution(mesh):
    parts = Mesh(mesh.devices.reshape(ZL, X, CORE, ZH, Y), EVERY)
    amp, intg = ("zl", "x", "core"), ("zh", "y")
    return jax.shard_map(
        per_device,
        mesh=parts,
        in_specs=(P(None, intg, amp), P(intg, amp), P(intg, None, amp), P(), P(), P()),
        out_specs=P(None, intg, amp),
        check_vma=False,
    )
```

time: 719 us -> 142 us (0.20)
  the two profiles are of different devices: /device:TPU:2 before, /device:TPU:120 now
where the time goes in v1:
time: 142 us; the launch traced here: 141 us
  waiting for transfers between devices  71.2 us (50%)
  starting transfers between devices  46 us (32%)
  between operations  13.5 us (10%)
  Pallas kernels  9 us (6%)
    reduce_scatter x1, waiting for transfers between devices, per_device(): cycle = lax.psum_scatter(cycle, 'y', scatter_dimension=0, tiled=False)  30.4 us
    all_to_all x1, waiting for transfers between devices, per_device(): gathered = lax.all_to_all(copies, ('zl', 'x'), 0, 0, tiled=True)  19.7 us
    all_to_all x1, starting transfers between devices, per_device(): window = lax.all_to_all(window, ('core', 'zh', 'y'), 0, 0, tiled=True)  12.8 us
    ppermute x1, waiting for transfers between devices, per_device(): far = lax.ppermute(jnp.where(low, second, first), EVERY, places(far_rule))  12.2 us
    ppermute x1, starting transfers between devices, per_device(): near = lax.ppermute(jnp.where(low, first, second), EVERY, places(near_rule))  9.43 us
    all_to_all x1, starting transfers between devices, per_device(): gathered = lax.all_to_all(copies, ('zl', 'x'), 0, 0, tiled=True)  9.39 us
    all_to_all x1, waiting for transfers between devices, per_device(): window = lax.all_to_all(window, ('core', 'zh', 'y'), 0, 0, tiled=True)  8.92 us
    all_to_all x1, starting transfers between devices, per_device(): ladder = lax.all_to_all(ladder, ('zh', 'y'), 0, 0, tiled=True)  7.12 us
  transfers between devices with their start and end apart: 7, of which 4 were waited for; matrix products, arithmetic and copies ran while one was open for 1% of the time, Pallas kernels for 5%

profile of v1, /device:TPU:120, one launch (start us, length us, event | category | flops | bytes accessed | tf_op | source)
XLA Modules:
  0.0 141.4 jit_solution(12119874407132162293)
XLA Ops:
  6.5 0.0 copy-start.1
  6.5 0.0 copy-start.2
  6.5 0.9 copy-done.2
  7.4 0.0 copy-start.4
  7.4 1.0 shard_map.64
  8.4 9.4 %all-to-all-start = ((f32[16,104,128]{2,1,0:T(8,128)}), f32[16,104,128]{2,1,0:T(8,128)S(1)}, u32[]{:S(2)}, u32[]{:S(2)}) async-start(f32[16,104,128]{2,1,0:T(8,128)} %shard_map.64), calls=%async_computation | async-start | bytes 1703936 | tf_op jit(solution)/shard_map/all_to_all | solution.py:174
  17.8 0.0 copy-done.1
  17.8 1.9 %collective-permute-start = (f32[512,256]{1,0:T(8,128)S(1)}, f32[512,256]{1,0:T(8,128)}, u32[]{:S(2)}, u32[]{:S(2)}) collective-permute-start(f32[512,256]{1,0:T(8,128)S(1)} %copy-done.1), channel_id=1, source_target_pairs={{0,16},{16,0},{1,17},{17,1},{2,18},{18,2},{3,19},{19,3},{4,20},{20... | collective-permute-start | bytes 1572872 | tf_op jit(solution)/shard_map/ppermute | solution.py:172
  19.7 19.7 %all-to-all-done = f32[16,104,128]{2,1,0:T(8,128)S(1)} async-done(((f32[16,104,128]{2,1,0:T(8,128)}), f32[16,104,128]{2,1,0:T(8,128)S(1)}, u32[]{:S(2)}, u32[]{:S(2)}) %all-to-all-start) | async-done | bytes 852000 | tf_op jit(solution)/shard_map/all_to_all | solution.py:174
  39.4 0.0 copy-done.4
  39.4 2.0 %shard_map.65 = f32[512,128]{1,0:T(8,128)} custom-call(s32[2]{0:T(128)S(1)} %copy-done.4, f32[1664,128]{1,0:T(8,128)S(1)} %bitcast.8), custom_call_target="tpu_custom_call" | custom-call | tf_op jit(solution)/shard_map/pallas_call | solution.py:176
  41.4 12.8 %all-to-all-start.1 = ((f32[32,16,128]{2,1,0:T(8,128)}), f32[32,16,128]{2,1,0:T(8,128)S(1)}, u32[]{:S(2)}, u32[]{:S(2)}) async-start(f32[32,16,128]{2,1,0:T(8,128)} %bitcast.1), calls=%async_computation.1 | async-start | bytes 524288 | tf_op jit(solution)/shard_map/all_to_all | solution.py:183
  54.2 0.0 copy-start
  54.2 0.0 reduce-scatter.2.cloned.1.call-start
  54.2 0.0 collective-permute-done.other
  54.2 3.2 %shard_map.67 = f32[1664,128]{1,0:T(8,128)} custom-call(f32[1664,128]{1,0:T(8,128)S(1)} %bitcast.9, f32[512,256]{1,0:T(8,128)S(1)} %copy-done.1, f32[512,256]{1,0:T(8,128)} %collective-permute-done.other), custom_call_target="tpu_custom_call" | custom-call | tf_op jit(solution)/shard_map/pallas_call | solution.py:184
  57.4 0.0 reduce-scatter.2.cloned.1.call-update
  57.5 8.9 %all-to-all-done.1.received = f32[32,16,128]{2,1,0:T(8,128)S(1)} async-done(((f32[32,16,128]{2,1,0:T(8,128)}), f32[32,16,128]{2,1,0:T(8,128)S(1)}, u32[]{:S(2)}, u32[]{:S(2)}) %all-to-all-start.1) | async-done | bytes 262176 | tf_op jit(solution)/shard_map/all_to_all | solution.py:183
  66.4 0.0 copy-done
  66.4 0.0 copy-start.3
  66.4 0.0 copy-start.5
  66.4 1.5 %shard_map.66 = f32[16,104,128]{2,1,0:T(8,128)} custom-call(f32[32,16,128]{2,1,0:T(8,128)S(1)} %all-to-all-done.1.received, f32[256,1664]{1,0:T(8,128)S(1)} %bitcast.10), custom_call_target="tpu_custom_call" | custom-call | tf_op jit(solution)/shard_map/pallas_call | solution.py:192
  67.9 7.1 %all-to-all-start.2 = ((f32[16,104,128]{2,1,0:T(8,128)}), f32[16,104,128]{2,1,0:T(8,128)S(1)}, u32[]{:S(2)}, u32[]{:S(2)}) async-start(f32[16,104,128]{2,1,0:T(8,128)} %shard_map.66), calls=%async_computation.2 | async-start | bytes 1703936 | tf_op jit(solution)/shard_map/all_to_all | solution.py:193
  75.1 30.4 %reduce-scatter.2.cloned.1.call-done = f32[1,208,128]{2,1,0:T(8,128)} async-done(((f32[8,208,128]{2,1,0:T(8,128)}), f32[1,208,128]{2,1,0:T(8,128)}) %reduce-scatter.2.cloned.1.call-update) | async-done | bytes 106512 | tf_op jit(solution)/shard_map/reduce_scatter | solution.py:186
  105.4 0.8 select_bitcast_fusion
  106.3 9.4 %collective-permute-start.1 = (f32[104,128]{1,0:T(8,128)S(1)}, f32[104,128]{1,0:T(8,128)S(1)}, u32[]{:S(2)}, u32[]{:S(2)}) collective-permute-start(f32[104,128]{1,0:T(8,128)S(1)} %get-tuple-element.6), channel_id=1, source_target_pairs={{0,0},{1,64},{2,128},{3,192},{4,256},{5,320},{6,384},{7,448},{8,32... | collective-permute-start | bytes 159752 | tf_op jit(solution)/shard_map/ppermute | solution.py:189
  115.7 5.3 %collective-permute-start.2 = (f32[104,128]{1,0:T(8,128)S(1)}, f32[104,128]{1,0:T(8,128)S(1)}, u32[]{:S(2)}, u32[]{:S(2)}) collective-permute-start(f32[104,128]{1,0:T(8,128)S(1)} %get-tuple-element.5), channel_id=1, source_target_pairs={{0,32},{1,96},{2,160},{3,224},{4,288},{5,352},{6,416},{7,480},{8,0... | collective-permute-start | bytes 159752 | tf_op jit(solution)/shard_map/ppermute | solution.py:190
  121.0 0.0 collective-permute-done.1.near
  121.0 12.2 %collective-permute-done.2.far = f32[104,128]{1,0:T(8,128)S(1)} collective-permute-done((f32[104,128]{1,0:T(8,128)S(1)}, f32[104,128]{1,0:T(8,128)S(1)}, u32[]{:S(2)}, u32[]{:S(2)}) %collective-permute-start.2) | collective-permute-done | bytes 53280 | tf_op jit(solution)/shard_map/ppermute | solution.py:190
  133.2 0.0 all-to-all-done.2.ladder
  133.2 0.0 copy-done.3
  133.2 0.0 copy-done.5
  133.2 1.3 shard_map.68
Async XLA Ops:
  6.5 11.2 %copy-start.1 = (f32[512,256]{1,0:T(8,128)S(1)}, f32[512,256]{1,0:T(8,128)}, u32[]{:S(2)}) copy-start(f32[512,256]{1,0:T(8,128)} %own.1) | copy-start | bytes 1572868
  6.5 0.9 copy-start.2
  7.4 32.0 %copy-start.4 = (s32[2]{0:T(128)S(1)}, s32[2]{0:T(128)}, u32[]{:S(2)}) copy-start(s32[2]{0:T(128)} %tiles.3) | copy-start | bytes 28
  8.4 31.0 %all-to-all-start = ((f32[16,104,128]{2,1,0:T(8,128)}), f32[16,104,128]{2,1,0:T(8,128)S(1)}, u32[]{:S(2)}, u32[]{:S(2)}) async-start(f32[16,104,128]{2,1,0:T(8,128)} %shard_map.64), calls=%async_computation | async-start | bytes 1703936 | tf_op jit(solution)/shard_map/all_to_all | solution.py:174
  17.8 36.5 %collective-permute-start = (f32[512,256]{1,0:T(8,128)S(1)}, f32[512,256]{1,0:T(8,128)}, u32[]{:S(2)}, u32[]{:S(2)}) collective-permute-start(f32[512,256]{1,0:T(8,128)S(1)} %copy-done.1), channel_id=1, source_target_pairs={{0,16},{16,0},{1,17},{17,1},{2,18},{18,2},{3,19},{19,3},{4,20},{20... | collective-permute-start | bytes 1572872 | tf_op jit(solution)/shard_map/ppermute | solution.py:172
  41.4 25.0 %all-to-all-start.1 = ((f32[32,16,128]{2,1,0:T(8,128)}), f32[32,16,128]{2,1,0:T(8,128)S(1)}, u32[]{:S(2)}, u32[]{:S(2)}) async-start(f32[32,16,128]{2,1,0:T(8,128)} %bitcast.1), calls=%async_computation.1 | async-start | bytes 524288 | tf_op jit(solution)/shard_map/all_to_all | solution.py:183
  54.2 12.2 %copy-start = (f32[4,64,1664]{2,1,0:T(8,128)S(1)}, f32[4,64,1664]{2,1,0:T(8,128)}, u32[]{:S(2)}) copy-start(f32[4,64,1664]{2,1,0:T(8,128)} %param.8) | copy-start | bytes 5111812
  54.2 51.3 %reduce-scatter.2.cloned.1.call-start = ((), (), s32[]{:S(2)}) async-start(), calls=%async_computation.4 | async-start | bytes 958464 | tf_op jit(solution)/shard_map/reduce_scatter | solution.py:186
  66.4 66.9 %copy-start.3 = (f32[832]{0:T(1024)S(1)}, f32[832]{0:T(1024)}, u32[]{:S(2)}) copy-start(f32[832]{0:T(1024)} %virtual.1) | copy-start | bytes 9988
  66.4 66.9 %copy-start.5 = (f32[128]{0:T(128)S(1)}, f32[128]{0:T(128)}, u32[]{:S(2)}) copy-start(f32[128]{0:T(128)} %occupied.1) | copy-start | bytes 1540
  67.9 65.3 %all-to-all-start.2 = ((f32[16,104,128]{2,1,0:T(8,128)}), f32[16,104,128]{2,1,0:T(8,128)S(1)}, u32[]{:S(2)}, u32[]{:S(2)}) async-start(f32[16,104,128]{2,1,0:T(8,128)} %shard_map.66), calls=%async_computation.2 | async-start | bytes 1703936 | tf_op jit(solution)/shard_map/all_to_all | solution.py:193
  106.3 14.7 %collective-permute-start.1 = (f32[104,128]{1,0:T(8,128)S(1)}, f32[104,128]{1,0:T(8,128)S(1)}, u32[]{:S(2)}, u32[]{:S(2)}) collective-permute-start(f32[104,128]{1,0:T(8,128)S(1)} %get-tuple-element.6), channel_id=1, source_target_pairs={{0,0},{1,64},{2,128},{3,192},{4,256},{5,320},{6,384},{7,448},{8,32... | collective-permute-start | bytes 159752 | tf_op jit(solution)/shard_map/ppermute | solution.py:189
  115.7 17.5 %collective-permute-start.2 = (f32[104,128]{1,0:T(8,128)S(1)}, f32[104,128]{1,0:T(8,128)S(1)}, u32[]{:S(2)}, u32[]{:S(2)}) collective-permute-start(f32[104,128]{1,0:T(8,128)S(1)} %get-tuple-element.5), channel_id=1, source_target_pairs={{0,32},{1,96},{2,160},{3,224},{4,288},{5,352},{6,416},{7,480},{8,0... | collective-permute-start | bytes 159752 | tf_op jit(solution)/shard_map/ppermute | solution.py:190
Sparse Core Ops, SparseCore 0:
  57.8 47.5 reduce-scatter.1

commit v2 on v1

--- a/solution.py
+++ b/solution.py
@@ -46,7 +46,7 @@
 def pack_kernel(amplitudes, out):
     for pair in range(PAIRS):
         tile = amplitudes[0, :, pair * LANES : (pair + 1) * LANES]
-        for chip in range(CHIPS):
+        for chip in range(ZL):
             out[chip, pair * ROWS : (pair + 1) * ROWS, :] = tile
 
 
@@ -55,7 +55,9 @@
     for pair in range(TILE // 2):
         place = tiles[1] * (TILE // 2) + pair
         owner = place // PAIRS
-        row = ((owner // 2) * PAIRS + (place - owner * PAIRS)) * ROWS
+        chip = owner // CORE
+        block = (chip % X) * ZL + chip // X
+        row = (block * PAIRS + (place - owner * PAIRS)) * ROWS
         tile = gathered[pl.ds(pl.multiple_of(row, ROWS), ROWS), :]
         window[pair * ROWS : (pair + 1) * ROWS, :] = jnp.where(owner % 2 == core, tile, 0.0)
     for half in range(ROWS // 2):
@@ -158,21 +160,29 @@
     return pairs
 
 
+def chip_of(block):
+    return block % ZL * X + block // ZL
+
+
 def near_rule(chip, core, place):
     zh, y = divmod(place, Y)
-    return 2 * y + zh, core, chip
+    return chip_of(2 * y + zh), core, chip
 
 
 def far_rule(chip, core, place):
     zh, y = divmod(place, Y)
-    return 2 * y + 1 - zh, core, chip
+    return chip_of(2 * y + 1 - zh), core, chip
 
 
 def per_device(amplitudes, cycle_block, ladder_block, occupied, virtual, tiles):
     other = lax.ppermute(cycle_block, "core", [(0, 1), (1, 0)])
-    copies = call(pack_kernel, (CHIPS, BLOCK, LANES), [VMEM])(amplitudes)
-    gathered = lax.all_to_all(copies, ("zl", "x"), 0, 0, tiled=True)
+    copies = call(pack_kernel, (ZL, BLOCK, LANES), [VMEM])(amplitudes)
+    column = lax.all_to_all(copies, "zl", 0, 0, tiled=True)
+    copies = jnp.broadcast_to(column.reshape(1, ZL * BLOCK, LANES), (X, ZL * BLOCK, LANES))
+    gathered = lax.all_to_all(copies, "x", 0, 0, tiled=True)
     gathered = gathered.reshape(CHIPS * BLOCK, LANES)
+    cycle = call(cycle_kernel, (CHIPS * BLOCK, LANES), [VMEM] * 3)(gathered, cycle_block, other)
+    cycle, gathered = lax.optimization_barrier((cycle, gathered))
     window = call(
         window_kernel,
         (CORE * CHIPS * 2 * ROWS, LANES),
@@ -181,7 +191,6 @@
     )(tiles, gathered)
     window = window.reshape(CORE * CHIPS, 2 * ROWS, LANES)
     window = lax.all_to_all(window, ("core", "zh", "y"), 0, 0, tiled=True)
-    cycle = call(cycle_kernel, (CHIPS * BLOCK, LANES), [VMEM] * 3)(gathered, cycle_block, other)
     cycle = cycle.reshape(Y, ZH * BLOCK, LANES)
     cycle = lax.psum_scatter(cycle, "y", scatter_dimension=0, tiled=False)
     first, second = cycle[:BLOCK], cycle[BLOCK:]

time: 142 us -> 142 us (level)
  the two profiles are of different devices: /device:TPU:120 before, /device:TPU:100 now
where the time goes in v2:
time: 142 us; the launch traced here: 141 us
  waiting for transfers between devices  71.5 us (50%)
  starting transfers between devices  33.6 us (24%)
  between operations  13.5 us (10%)
  blocking collectives  12.8 us (9%)
  Pallas kernels  7.07 us (5%)
  local copies, waits for them, and re-layouts  1.84 us (1%)
    reduce_scatter x1, waiting for transfers between devices, per_device(): cycle = lax.psum_scatter(cycle, 'y', scatter_dimension=0, tiled=False)  31.7 us
    ppermute x1, waiting for transfers between devices, per_device(): near = lax.ppermute(jnp.where(low, first, second), EVERY, places(near_rule))  21.2 us
    all_to_all x1, starting transfers between devices, per_device(): window = lax.all_to_all(window, ('core', 'zh', 'y'), 0, 0, tiled=True)  13.1 us
    all_to_all x1, blocking collectives, per_device(): column = lax.all_to_all(copies, 'zl', 0, 0, tiled=True)  12.8 us
    all_to_all x1, waiting for transfers between devices, per_device(): window = lax.all_to_all(window, ('core', 'zh', 'y'), 0, 0, tiled=True)  11.4 us
    all_to_all x1, starting transfers between devices, per_device(): ladder = lax.all_to_all(ladder, ('zh', 'y'), 0, 0, tiled=True)  7.26 us
    all_to_all x1, starting transfers between devices, per_device(): gathered = lax.all_to_all(copies, 'x', 0, 0, tiled=True)  4.8 us
    all_to_all x1, waiting for transfers between devices, per_device(): gathered = lax.all_to_all(copies, 'x', 0, 0, tiled=True)  4.61 us
  transfers between devices with their start and end apart: 7, of which 5 were waited for; matrix products, arithmetic and copies ran while one was open for 1% of the time, Pallas kernels for 1%

profile of v2, /device:TPU:100, one launch (start us, length us, event | category | flops | bytes accessed | tf_op | source)
XLA Modules:
  0.0 141.1 jit_solution(5714312250400314692)
XLA Ops:
  6.5 0.0 copy-start.1
  6.5 0.0 copy-start.2
  6.5 0.9 copy-done.2
  7.4 12.8 %all_to_all.20 = f32[4,104,128]{2,1,0:T(8,128)S(1)} all-to-all(f32[4,104,128]{2,1,0:T(8,128)S(1)} %shard_map.64), channel_id=1, replica_groups=mesh['zl'=4,'x'=4,'core'=2,'zh'=2,'y'=8] {'zl'}, dimensions={0} | all-to-all | bytes 425984 | tf_op jit(solution)/shard_map/all_to_all | solution.py:180
  20.3 1.0 broadcast_in_dim.8
  21.2 4.8 %all-to-all-start.1 = ((f32[4,416,128]{2,1,0:T(8,128)}), f32[4,416,128]{2,1,0:T(8,128)S(1)}, u32[]{:S(2)}, u32[]{:S(2)}) async-start(f32[4,416,128]{2,1,0:T(8,128)} %broadcast_in_dim.8), calls=%async_computation.1 | async-start | bytes 1703936 | tf_op jit(solution)/shard_map/all_to_all | solution.py:182
  26.0 0.0 copy-done.1
  26.0 0.0 copy-start.4
  26.0 2.0 %collective-permute-start = (f32[512,256]{1,0:T(8,128)S(1)}, f32[512,256]{1,0:T(8,128)S(1)}, u32[]{:S(2)}, u32[]{:S(2)}) collective-permute-start(f32[512,256]{1,0:T(8,128)S(1)} %copy-done.1), channel_id=1, source_target_pairs={{0,16},{16,0},{1,17},{17,1},{2,18},{18,2},{3,19},{19,3},{4,20},{20... | collective-permute-start | bytes 1572872 | tf_op jit(solution)/shard_map/ppermute | solution.py:178
  28.1 1.9 %collective-permute-done.other = f32[512,256]{1,0:T(8,128)S(1)} collective-permute-done((f32[512,256]{1,0:T(8,128)S(1)}, f32[512,256]{1,0:T(8,128)S(1)}, u32[]{:S(2)}, u32[]{:S(2)}) %collective-permute-start) | collective-permute-done | bytes 524320 | tf_op jit(solution)/shard_map/ppermute | solution.py:178
  30.0 4.6 %all-to-all-done.1 = f32[4,416,128]{2,1,0:T(8,128)S(1)} async-done(((f32[4,416,128]{2,1,0:T(8,128)}), f32[4,416,128]{2,1,0:T(8,128)S(1)}, u32[]{:S(2)}, u32[]{:S(2)}) %all-to-all-start.1) | async-done | bytes 852000 | tf_op jit(solution)/shard_map/all_to_all | solution.py:182
  34.6 2.0 %shard_map.65 = f32[1664,128]{1,0:T(8,128)} custom-call(f32[1664,128]{1,0:T(8,128)S(1)} %bitcast.9, f32[512,256]{1,0:T(8,128)S(1)} %copy-done.1, f32[512,256]{1,0:T(8,128)S(1)} %collective-permute-done.other), custom_call_target="tpu_custom_call" | custom-call | tf_op jit(solution)/shard_map/pallas_call | solution.py:184
  36.6 0.0 copy-done.4
  36.6 0.0 copy-start
  36.6 2.1 %shard_map.66 = f32[512,128]{1,0:T(8,128)} custom-call(s32[2]{0:T(128)S(1)} %copy-done.4, f32[1664,128]{1,0:T(8,128)S(1)} %bitcast.10), custom_call_target="tpu_custom_call" | custom-call | tf_op jit(solution)/shard_map/pallas_call | solution.py:186
  38.8 13.1 %all-to-all-start.2 = ((f32[32,16,128]{2,1,0:T(8,128)}), f32[32,16,128]{2,1,0:T(8,128)S(1)}, u32[]{:S(2)}, u32[]{:S(2)}) async-start(f32[32,16,128]{2,1,0:T(8,128)} %bitcast.2), calls=%async_computation.2 | async-start | bytes 524288 | tf_op jit(solution)/shard_map/all_to_all | solution.py:193
  51.9 0.0 reduce-scatter.2.cloned.1.call-start
  51.9 0.7 reduce-scatter.2.cloned.1.call-update
  52.6 11.4 %all-to-all-done.2.received = f32[32,16,128]{2,1,0:T(8,128)S(1)} async-done(((f32[32,16,128]{2,1,0:T(8,128)}), f32[32,16,128]{2,1,0:T(8,128)S(1)}, u32[]{:S(2)}, u32[]{:S(2)}) %all-to-all-start.2) | async-done | bytes 262176 | tf_op jit(solution)/shard_map/all_to_all | solution.py:193
  64.0 0.0 copy-done
  64.0 0.0 copy-start.3
  64.0 0.0 copy-start.5
  64.0 1.5 %shard_map.67 = f32[16,104,128]{2,1,0:T(8,128)} custom-call(f32[32,16,128]{2,1,0:T(8,128)S(1)} %all-to-all-done.2.received, f32[256,1664]{1,0:T(8,128)S(1)} %bitcast.11), custom_call_target="tpu_custom_call" | custom-call | tf_op jit(solution)/shard_map/pallas_call | solution.py:201
  65.6 7.3 %all-to-all-start.3 = ((f32[16,104,128]{2,1,0:T(8,128)}), f32[16,104,128]{2,1,0:T(8,128)S(1)}, u32[]{:S(2)}, u32[]{:S(2)}) async-start(f32[16,104,128]{2,1,0:T(8,128)} %shard_map.67), calls=%async_computation.3 | async-start | bytes 1703936 | tf_op jit(solution)/shard_map/all_to_all | solution.py:202
  72.8 31.7 %reduce-scatter.2.cloned.1.call-done = f32[1,208,128]{2,1,0:T(8,128)} async-done(((f32[8,208,128]{2,1,0:T(8,128)}), f32[1,208,128]{2,1,0:T(8,128)}) %reduce-scatter.2.cloned.1.call-update) | async-done | bytes 106512 | tf_op jit(solution)/shard_map/reduce_scatter | solution.py:195
  104.5 0.8 select_bitcast_fusion
  105.4 2.5 %collective-permute-start.1 = (f32[104,128]{1,0:T(8,128)S(1)}, f32[104,128]{1,0:T(8,128)S(1)}, u32[]{:S(2)}, u32[]{:S(2)}) collective-permute-start(f32[104,128]{1,0:T(8,128)S(1)} %get-tuple-element.10), channel_id=1, source_target_pairs={{0,0},{1,256},{2,32},{3,288},{4,64},{5,320},{6,96},{7,352},{8,128}... | collective-permute-start | bytes 159752 | tf_op jit(solution)/shard_map/ppermute | solution.py:198
  107.8 3.9 %collective-permute-start.2 = (f32[104,128]{1,0:T(8,128)S(1)}, f32[104,128]{1,0:T(8,128)S(1)}, u32[]{:S(2)}, u32[]{:S(2)}) collective-permute-start(f32[104,128]{1,0:T(8,128)S(1)} %get-tuple-element.9), channel_id=1, source_target_pairs={{0,128},{1,384},{2,160},{3,416},{4,192},{5,448},{6,224},{7,480},{8... | collective-permute-start | bytes 159752 | tf_op jit(solution)/shard_map/ppermute | solution.py:199
  111.7 21.2 %collective-permute-done.1.near = f32[104,128]{1,0:T(8,128)S(1)} collective-permute-done((f32[104,128]{1,0:T(8,128)S(1)}, f32[104,128]{1,0:T(8,128)S(1)}, u32[]{:S(2)}, u32[]{:S(2)}) %collective-permute-start.1) | collective-permute-done | bytes 53280 | tf_op jit(solution)/shard_map/ppermute | solution.py:198
  132.9 0.0 collective-permute-done.2.far
  132.9 0.0 all-to-all-done.3.ladder
  132.9 0.0 copy-done.3
  132.9 0.0 copy-done.5
  132.9 1.3 shard_map.68
  (1 shorter events, 0.0 us)
Async XLA Ops:
  6.5 19.5 %copy-start.1 = (f32[512,256]{1,0:T(8,128)S(1)}, f32[512,256]{1,0:T(8,128)}, u32[]{:S(2)}) copy-start(f32[512,256]{1,0:T(8,128)} %own.1) | copy-start | bytes 1572868
  6.5 0.9 copy-start.2
  21.2 13.3 %all-to-all-start.1 = ((f32[4,416,128]{2,1,0:T(8,128)}), f32[4,416,128]{2,1,0:T(8,128)S(1)}, u32[]{:S(2)}, u32[]{:S(2)}) async-start(f32[4,416,128]{2,1,0:T(8,128)} %broadcast_in_dim.8), calls=%async_computation.1 | async-start | bytes 1703936 | tf_op jit(solution)/shard_map/all_to_all | solution.py:182
  26.0 10.6 %copy-start.4 = (s32[2]{0:T(128)S(1)}, s32[2]{0:T(128)}, u32[]{:S(2)}) copy-start(s32[2]{0:T(128)} %tiles.3) | copy-start | bytes 28
  26.0 3.9 %collective-permute-start = (f32[512,256]{1,0:T(8,128)S(1)}, f32[512,256]{1,0:T(8,128)S(1)}, u32[]{:S(2)}, u32[]{:S(2)}) collective-permute-start(f32[512,256]{1,0:T(8,128)S(1)} %copy-done.1), channel_id=1, source_target_pairs={{0,16},{16,0},{1,17},{17,1},{2,18},{18,2},{3,19},{19,3},{4,20},{20... | collective-permute-start | bytes 1572872 | tf_op jit(solution)/shard_map/ppermute | solution.py:178
  36.6 27.4 %copy-start = (f32[4,64,1664]{2,1,0:T(8,128)S(1)}, f32[4,64,1664]{2,1,0:T(8,128)}, u32[]{:S(2)}) copy-start(f32[4,64,1664]{2,1,0:T(8,128)} %param.8) | copy-start | bytes 5111812
  38.8 25.3 %all-to-all-start.2 = ((f32[32,16,128]{2,1,0:T(8,128)}), f32[32,16,128]{2,1,0:T(8,128)S(1)}, u32[]{:S(2)}, u32[]{:S(2)}) async-start(f32[32,16,128]{2,1,0:T(8,128)} %bitcast.2), calls=%async_computation.2 | async-start | bytes 524288 | tf_op jit(solution)/shard_map/all_to_all | solution.py:193
  51.9 52.6 %reduce-scatter.2.cloned.1.call-start = ((), (), s32[]{:S(2)}) async-start(), calls=%async_computation.5 | async-start | bytes 958464 | tf_op jit(solution)/shard_map/reduce_scatter | solution.py:195
  64.0 68.9 %copy-start.3 = (f32[832]{0:T(1024)S(1)}, f32[832]{0:T(1024)}, u32[]{:S(2)}) copy-start(f32[832]{0:T(1024)} %virtual.1) | copy-start | bytes 9988
  64.0 68.9 %copy-start.5 = (f32[128]{0:T(128)S(1)}, f32[128]{0:T(128)}, u32[]{:S(2)}) copy-start(f32[128]{0:T(128)} %occupied.1) | copy-start | bytes 1540
  65.6 67.3 %all-to-all-start.3 = ((f32[16,104,128]{2,1,0:T(8,128)}), f32[16,104,128]{2,1,0:T(8,128)S(1)}, u32[]{:S(2)}, u32[]{:S(2)}) async-start(f32[16,104,128]{2,1,0:T(8,128)} %shard_map.67), calls=%async_computation.3 | async-start | bytes 1703936 | tf_op jit(solution)/shard_map/all_to_all | solution.py:202
  105.4 27.6 %collective-permute-start.1 = (f32[104,128]{1,0:T(8,128)S(1)}, f32[104,128]{1,0:T(8,128)S(1)}, u32[]{:S(2)}, u32[]{:S(2)}) collective-permute-start(f32[104,128]{1,0:T(8,128)S(1)} %get-tuple-element.10), channel_id=1, source_target_pairs={{0,0},{1,256},{2,32},{3,288},{4,64},{5,320},{6,96},{7,352},{8,128}... | collective-permute-start | bytes 159752 | tf_op jit(solution)/shard_map/ppermute | solution.py:198
  107.8 25.1 %collective-permute-start.2 = (f32[104,128]{1,0:T(8,128)S(1)}, f32[104,128]{1,0:T(8,128)S(1)}, u32[]{:S(2)}, u32[]{:S(2)}) collective-permute-start(f32[104,128]{1,0:T(8,128)S(1)} %get-tuple-element.9), channel_id=1, source_target_pairs={{0,128},{1,384},{2,160},{3,416},{4,192},{5,448},{6,224},{7,480},{8... | collective-permute-start | bytes 159752 | tf_op jit(solution)/shard_map/ppermute | solution.py:199
Sparse Core Ops, SparseCore 0:
  55.6 48.9 reduce-scatter.1

commit v3 on v2

--- a/solution.py
+++ b/solution.py
@@ -71,8 +71,7 @@
             odd = turned[pl.ds(2 * part + 1, CHIPS, stride=4), :]
             for inner, value in enumerate(pair_up(even, odd)):
                 row = part * ROWS + half * 2 + inner
-                for target in range(CORE):
-                    out[pl.ds(target * CHIPS * 2 * ROWS + row, CHIPS, stride=2 * ROWS), :] = value
+                out[pl.ds(row, CHIPS, stride=2 * ROWS), :] = value
 
 
 def cycle_kernel(gathered, own, other, out):
@@ -95,12 +94,24 @@
                 out[pl.ds(j, CHIPS * PAIRS, stride=ROWS), :] = value
 
 
+def join_kernel(cycle, own, other, out):
+    for place in range(CHIPS):
+        out[place, :BLOCK, :] = cycle[place, :, :]
+        out[place, BLOCK:, :] = own[place, :, :] + other[place, :, :]
+
+
+def sum_kernel(received, out):
+    total = received[0, :BLOCK, :]
+    for place in range(1, CHIPS):
+        total = total + received[place, :BLOCK, :]
+    out[...] = total
+
+
 def ladder_kernel(received, integrals, out):
     lefts = []
     for part in range(2):
-        rows = pl.ds(part * ROWS, ROWS)
-        both = received[:CHIPS, rows, :] + received[CHIPS:, rows, :]
-        lefts.append(both.reshape(CHIPS * ROWS, LANES))
+        rows = received[:, BLOCK + part * ROWS : BLOCK + (part + 1) * ROWS, :]
+        lefts.append(rows.reshape(CHIPS * ROWS, LANES))
     left = split(jnp.concatenate(lefts, 1))
     width = PAIRS * LANES
     for start in range(0, width, 2 * LANES):
@@ -112,7 +123,7 @@
             out[:, rows, :] = value.reshape(CHIPS, ROWS, LANES)
 
 
-def last_kernel(tiles, occupied, virtual, ladder, near, far, out):
+def last_kernel(tiles, occupied, virtual, ladder, cycle, out):
     column = lax.axis_index("zl") * (X * CORE) + lax.axis_index("x") * CORE + lax.axis_index("core")
     row = lax.axis_index("zh") * Y + lax.axis_index("y")
     shape = (ROWS, LANES)
@@ -126,7 +137,7 @@
         rows = jnp.where(line == j, occupied[row * ROWS + j], rows)
     for pair in range(PAIRS):
         piece = pl.ds(pair * ROWS, ROWS)
-        total = near[piece, :] + far[piece, :]
+        total = cycle[piece, :]
         for chip in range(CHIPS):
             total = total + ladder[chip, piece, :]
         a = column * (2 * PAIRS) + 2 * pair
@@ -164,14 +175,8 @@
     return block % ZL * X + block // ZL
 
 
-def near_rule(chip, core, place):
-    zh, y = divmod(place, Y)
-    return chip_of(2 * y + zh), core, chip
-
-
-def far_rule(chip, core, place):
-    zh, y = divmod(place, Y)
-    return chip_of(2 * y + 1 - zh), core, chip
+def owner_rule(chip, core, place):
+    return chip_of(place), core, chip
 
 
 def per_device(amplitudes, cycle_block, ladder_block, occupied, virtual, tiles):
@@ -181,27 +186,27 @@
     copies = jnp.broadcast_to(column.reshape(1, ZL * BLOCK, LANES), (X, ZL * BLOCK, LANES))
     gathered = lax.all_to_all(copies, "x", 0, 0, tiled=True)
     gathered = gathered.reshape(CHIPS * BLOCK, LANES)
-    cycle = call(cycle_kernel, (CHIPS * BLOCK, LANES), [VMEM] * 3)(gathered, cycle_block, other)
-    cycle, gathered = lax.optimization_barrier((cycle, gathered))
     window = call(
         window_kernel,
-        (CORE * CHIPS * 2 * ROWS, LANES),
+        (CHIPS * 2 * ROWS, LANES),
         [SMEM, VMEM],
         [(TILE // 2 * ROWS, LANES), (LANES, LANES), (LANES, LANES)],
     )(tiles, gathered)
-    window = window.reshape(CORE * CHIPS, 2 * ROWS, LANES)
-    window = lax.all_to_all(window, ("core", "zh", "y"), 0, 0, tiled=True)
-    cycle = cycle.reshape(Y, ZH * BLOCK, LANES)
-    cycle = lax.psum_scatter(cycle, "y", scatter_dimension=0, tiled=False)
-    first, second = cycle[:BLOCK], cycle[BLOCK:]
-    low = lax.axis_index("zh") == 0
-    near = lax.ppermute(jnp.where(low, first, second), EVERY, places(near_rule))
-    far = lax.ppermute(jnp.where(low, second, first), EVERY, places(far_rule))
+    window = window.reshape(CHIPS, 2 * ROWS, LANES)
+    other_window = lax.ppermute(window, "core", [(0, 1), (1, 0)])
+    cycle = call(cycle_kernel, (CHIPS * BLOCK, LANES), [VMEM] * 3)(gathered, cycle_block, other)
+    cycle = cycle.reshape(CHIPS, BLOCK, LANES)
+    joined = (CHIPS, BLOCK + 2 * ROWS, LANES)
+    joined = call(join_kernel, joined, [VMEM] * 3)(cycle, window, other_window)
+    received = lax.all_to_all(joined, ("zh", "y"), 0, 0, tiled=True)
     integrals = ladder_block.reshape(-1, ladder_block.shape[2])
-    ladder = call(ladder_kernel, (CHIPS, BLOCK, LANES), [VMEM] * 2)(window, integrals)
+    ladder = call(ladder_kernel, (CHIPS, BLOCK, LANES), [VMEM] * 2)(received, integrals)
+    ladder, received = lax.optimization_barrier((ladder, received))
+    cycle = call(sum_kernel, (BLOCK, LANES), [VMEM])(received)
+    cycle = lax.ppermute(cycle, EVERY, places(owner_rule))
     ladder = lax.all_to_all(ladder, ("zh", "y"), 0, 0, tiled=True)
-    return call(last_kernel, amplitudes.shape, [SMEM] * 3 + [VMEM] * 3)(
-        tiles, occupied, virtual, ladder, near, far
+    return call(last_kernel, amplitudes.shape, [SMEM] * 3 + [VMEM] * 2)(
+        tiles, occupied, virtual, ladder, cycle
     )
 
 

time: 142 us -> 120 us (0.85)
  the two profiles are of different devices: /device:TPU:100 before, /device:TPU:110 now
where the time goes in v3:
time: 120 us
  blocking collectives  53.6 us (45%)
  waiting for transfers between devices  39.4 us (33%)
  starting transfers between devices  19.4 us (16%)
  Pallas kernels  5.51 us (5%)
  local copies, waits for them, and re-layouts  1.86 us (2%)
    all_to_all x1, blocking collectives, per_device(): received = lax.all_to_all(joined, ('zh', 'y'), 0, 0, tiled=True)  40.7 us
    ppermute x1, waiting for transfers between devices, per_device(): cycle = lax.ppermute(cycle, EVERY, places(owner_rule))  31.7 us
    all_to_all x1, blocking collectives, per_device(): column = lax.all_to_all(copies, 'zl', 0, 0, tiled=True)  12.8 us
    all_to_all x1, waiting for transfers between devices, per_device(): gathered = lax.all_to_all(copies, 'x', 0, 0, tiled=True)  7.52 us
    all_to_all x1, starting transfers between devices, per_device(): ladder = lax.all_to_all(ladder, ('zh', 'y'), 0, 0, tiled=True)  6.8 us
    all_to_all x1, starting transfers between devices, per_device(): gathered = lax.all_to_all(copies, 'x', 0, 0, tiled=True)  4.77 us
    ppermute x1, starting transfers between devices, per_device(): cycle = lax.ppermute(cycle, EVERY, places(owner_rule))  3.99 us
  transfers between devices with their start and end apart: 5, of which 3 were waited for; matrix products, arithmetic and copies ran while one was open for 0% of the time, Pallas kernels for 2%

profile of v3, /device:TPU:110, one launch (start us, length us, event | category | flops | bytes accessed | tf_op | source)
XLA Modules:
  0.0 119.8 jit_solution(12518431590333798638)
XLA Ops:
  0.0 0.0 copy-start.1
  0.0 0.0 copy-start.2
  0.0 0.9 copy-done.2
  0.9 0.0 copy-start.4
  0.9 12.8 %all_to_all.20 = f32[4,104,128]{2,1,0:T(8,128)S(1)} all-to-all(f32[4,104,128]{2,1,0:T(8,128)S(1)} %shard_map.64), channel_id=1, replica_groups=mesh['zl'=4,'x'=4,'core'=2,'zh'=2,'y'=8] {'zl'}, dimensions={0} | all-to-all | bytes 425984 | tf_op jit(solution)/shard_map/all_to_all | solution.py:185
  13.7 1.0 broadcast_in_dim.8
  14.7 4.8 %all-to-all-start.1 = ((f32[4,416,128]{2,1,0:T(8,128)}), f32[4,416,128]{2,1,0:T(8,128)S(1)}, u32[]{:S(2)}, u32[]{:S(2)}) async-start(f32[4,416,128]{2,1,0:T(8,128)} %broadcast_in_dim.8), calls=%async_computation.1 | async-start | bytes 1703936 | tf_op jit(solution)/shard_map/all_to_all | solution.py:187
  19.5 0.0 copy-done.1
  19.5 1.9 %collective-permute-start = (f32[512,256]{1,0:T(8,128)S(1)}, f32[512,256]{1,0:T(8,128)S(1)}, u32[]{:S(2)}, u32[]{:S(2)}) collective-permute-start(f32[512,256]{1,0:T(8,128)S(1)} %copy-done.1), channel_id=1, source_target_pairs={{0,16},{16,0},{1,17},{17,1},{2,18},{18,2},{3,19},{19,3},{4,20},{20... | collective-permute-start | bytes 1572872 | tf_op jit(solution)/shard_map/ppermute | solution.py:183
  21.4 7.5 %all-to-all-done.1 = f32[4,416,128]{2,1,0:T(8,128)S(1)} async-done(((f32[4,416,128]{2,1,0:T(8,128)}), f32[4,416,128]{2,1,0:T(8,128)S(1)}, u32[]{:S(2)}, u32[]{:S(2)}) %all-to-all-start.1) | async-done | bytes 852000 | tf_op jit(solution)/shard_map/all_to_all | solution.py:187
  28.9 0.0 copy-done.4
  28.9 1.4 %shard_map.66 = f32[256,128]{1,0:T(8,128)S(1)} custom-call(s32[2]{0:T(128)S(1)} %copy-done.4, f32[1664,128]{1,0:T(8,128)S(1)} %bitcast.5), custom_call_target="tpu_custom_call" | custom-call | tf_op jit(solution)/shard_map/pallas_call | solution.py:189
  30.4 1.9 %collective-permute-start.1 = (f32[16,16,128]{2,1,0:T(8,128)S(1)}, f32[16,16,128]{2,1,0:T(8,128)S(1)}, u32[]{:S(2)}, u32[]{:S(2)}) collective-permute-start(f32[16,16,128]{2,1,0:T(8,128)S(1)} %bitcast.9), channel_id=1, source_target_pairs={{0,16},{16,0},{1,17},{17,1},{2,18},{18,2},{3,19},{19,3},{4,20},{20... | collective-permute-start | bytes 393224 | tf_op jit(solution)/shard_map/ppermute | solution.py:196
  32.3 0.0 collective-permute-done.other
  32.3 1.1 shard_map.65
  33.4 0.2 collective-permute-done.1.other
  33.6 0.0 copy-start
  33.6 0.1 shard_map.67
  33.7 40.7 %all_to_all.21.received = f32[16,120,128]{2,1,0:T(8,128)S(1)} all-to-all(f32[16,120,128]{2,1,0:T(8,128)S(1)} %shard_map.67), channel_id=1, replica_groups=mesh['zl'=4,'x'=4,'core'=2,'zh'=2,'y'=8] {'zh','y'}, dimensions={0} | all-to-all | bytes 1966080 | tf_op jit(solution)/shard_map/all_to_all | solution.py:201
  74.4 0.0 copy-done
  74.4 1.5 %shard_map.68 = f32[16,104,128]{2,1,0:T(8,128)} custom-call(f32[16,120,128]{2,1,0:T(8,128)S(1)} %all_to_all.21.received, f32[256,1664]{1,0:T(8,128)S(1)} %bitcast.8), custom_call_target="tpu_custom_call" | custom-call | tf_op jit(solution)/shard_map/pallas_call | solution.py:203
  75.9 0.0 copy-start.3
  75.9 0.0 copy-start.5
  75.9 6.8 %all-to-all-start.3 = ((f32[16,104,128]{2,1,0:T(8,128)}), f32[16,104,128]{2,1,0:T(8,128)S(1)}, u32[]{:S(2)}, u32[]{:S(2)}) async-start(f32[16,104,128]{2,1,0:T(8,128)} %shard_map.68), calls=%async_computation.3 | async-start | bytes 1703936 | tf_op jit(solution)/shard_map/all_to_all | solution.py:207
  82.8 4.0 %collective-permute-start.2 = (f32[104,128]{1,0:T(8,128)S(1)}, f32[104,128]{1,0:T(8,128)S(1)}, u32[]{:S(2)}, u32[]{:S(2)}) collective-permute-start(f32[104,128]{1,0:T(8,128)S(1)} %shard_map.69), channel_id=1, source_target_pairs={{0,0},{1,128},{2,256},{3,384},{4,32},{5,160},{6,288},{7,416},{8,64... | collective-permute-start | bytes 159752 | tf_op jit(solution)/shard_map/ppermute | solution.py:206
  86.8 31.7 %collective-permute-done.2.cycle = f32[104,128]{1,0:T(8,128)S(1)} collective-permute-done((f32[104,128]{1,0:T(8,128)S(1)}, f32[104,128]{1,0:T(8,128)S(1)}, u32[]{:S(2)}, u32[]{:S(2)}) %collective-permute-start.2) | collective-permute-done | bytes 53280 | tf_op jit(solution)/shard_map/ppermute | solution.py:206
  118.5 0.0 all-to-all-done.3.ladder
  118.5 0.0 copy-done.3
  118.5 0.0 copy-done.5
  118.5 1.3 %shard_map.70 = f32[1,8,1664]{2,1,0:T(8,128)} custom-call(s32[2]{0:T(128)S(1)} %copy-done.4, f32[128]{0:T(128)S(1)} %copy-done.5, f32[832]{0:T(1024)S(1)} %copy-done.3, f32[16,104,128]{2,1,0:T(8,128)S(1)} %all-to-all-done.3.ladder, f32[104,128]{1,0:T(8,128)S(1)} %collective-permute-done.2.cycle), custom_call_target="tpu_custom_call" | custom-call | tf_op jit(solution)/shard_map/pallas_call | solution.py:208
  (2 shorter events, 0.1 us)
Async XLA Ops:
  0.0 19.5 %copy-start.1 = (f32[512,256]{1,0:T(8,128)S(1)}, f32[512,256]{1,0:T(8,128)}, u32[]{:S(2)}) copy-start(f32[512,256]{1,0:T(8,128)} %own.1) | copy-start | bytes 1572868
  0.0 0.9 copy-start.2
  0.9 28.1 %copy-start.4 = (s32[2]{0:T(128)S(1)}, s32[2]{0:T(128)}, u32[]{:S(2)}) copy-start(s32[2]{0:T(128)} %tiles.3) | copy-start | bytes 28
  14.7 14.2 %all-to-all-start.1 = ((f32[4,416,128]{2,1,0:T(8,128)}), f32[4,416,128]{2,1,0:T(8,128)S(1)}, u32[]{:S(2)}, u32[]{:S(2)}) async-start(f32[4,416,128]{2,1,0:T(8,128)} %broadcast_in_dim.8), calls=%async_computation.1 | async-start | bytes 1703936 | tf_op jit(solution)/shard_map/all_to_all | solution.py:187
  19.5 12.8 %collective-permute-start = (f32[512,256]{1,0:T(8,128)S(1)}, f32[512,256]{1,0:T(8,128)S(1)}, u32[]{:S(2)}, u32[]{:S(2)}) collective-permute-start(f32[512,256]{1,0:T(8,128)S(1)} %copy-done.1), channel_id=1, source_target_pairs={{0,16},{16,0},{1,17},{17,1},{2,18},{18,2},{3,19},{19,3},{4,20},{20... | collective-permute-start | bytes 1572872 | tf_op jit(solution)/shard_map/ppermute | solution.py:183
  30.4 3.2 %collective-permute-start.1 = (f32[16,16,128]{2,1,0:T(8,128)S(1)}, f32[16,16,128]{2,1,0:T(8,128)S(1)}, u32[]{:S(2)}, u32[]{:S(2)}) collective-permute-start(f32[16,16,128]{2,1,0:T(8,128)S(1)} %bitcast.9), channel_id=1, source_target_pairs={{0,16},{16,0},{1,17},{17,1},{2,18},{18,2},{3,19},{19,3},{4,20},{20... | collective-permute-start | bytes 393224 | tf_op jit(solution)/shard_map/ppermute | solution.py:196
  33.6 40.8 %copy-start = (f32[4,64,1664]{2,1,0:T(8,128)S(1)}, f32[4,64,1664]{2,1,0:T(8,128)}, u32[]{:S(2)}) copy-start(f32[4,64,1664]{2,1,0:T(8,128)} %param.8) | copy-start | bytes 5111812
  75.9 42.6 %copy-start.3 = (f32[832]{0:T(1024)S(1)}, f32[832]{0:T(1024)}, u32[]{:S(2)}) copy-start(f32[832]{0:T(1024)} %virtual.1) | copy-start | bytes 9988
  75.9 42.6 %copy-start.5 = (f32[128]{0:T(128)S(1)}, f32[128]{0:T(128)}, u32[]{:S(2)}) copy-start(f32[128]{0:T(128)} %occupied.1) | copy-start | bytes 1540
  75.9 42.6 %all-to-all-start.3 = ((f32[16,104,128]{2,1,0:T(8,128)}), f32[16,104,128]{2,1,0:T(8,128)S(1)}, u32[]{:S(2)}, u32[]{:S(2)}) async-start(f32[16,104,128]{2,1,0:T(8,128)} %shard_map.68), calls=%async_computation.3 | async-start | bytes 1703936 | tf_op jit(solution)/shard_map/all_to_all | solution.py:207
  82.8 35.7 %collective-permute-start.2 = (f32[104,128]{1,0:T(8,128)S(1)}, f32[104,128]{1,0:T(8,128)S(1)}, u32[]{:S(2)}, u32[]{:S(2)}) collective-permute-start(f32[104,128]{1,0:T(8,128)S(1)} %shard_map.69), channel_id=1, source_target_pairs={{0,0},{1,128},{2,256},{3,384},{4,32},{5,160},{6,288},{7,416},{8,64... | collective-permute-start | bytes 159752 | tf_op jit(solution)/shard_map/ppermute | solution.py:206

commit v4 on v2

--- a/solution.py
+++ b/solution.py
@@ -72,7 +72,8 @@
             for inner, value in enumerate(pair_up(even, odd)):
                 row = part * ROWS + half * 2 + inner
                 for target in range(CORE):
-                    out[pl.ds(target * CHIPS * 2 * ROWS + row, CHIPS, stride=2 * ROWS), :] = value
+                    start = target * CHIPS * 2 * ROWS + row
+                    out[pl.ds(start, CHIPS, stride=2 * ROWS), :] = value
 
 
 def cycle_kernel(gathered, own, other, out):
@@ -95,12 +96,36 @@
                 out[pl.ds(j, CHIPS * PAIRS, stride=ROWS), :] = value
 
 
+def join_kernel(cycle, window, out):
+    for y in range(Y):
+        out[y, : ZH * BLOCK, :] = cycle[y, :, :]
+        rows = slice(y * 2 * ROWS, (y + 1) * 2 * ROWS)
+        for zh in range(ZH):
+            start = ZH * BLOCK + zh * 2 * ROWS
+            out[y, start : start + 2 * ROWS, :] = window[zh, rows, :] + window[ZH + zh, rows, :]
+
+
+def cycle_sum_kernel(received, near, far):
+    first = lax.axis_index("zh") == 0
+    for row in range(0, BLOCK, ROWS):
+        halves = []
+        for start in (row, BLOCK + row):
+            total = received[0, start : start + ROWS, :]
+            for place in range(1, Y):
+                total = total + received[place, start : start + ROWS, :]
+            halves.append(total)
+        near[row : row + ROWS, :] = jnp.where(first, halves[0], halves[1])
+        far[row : row + ROWS, :] = jnp.where(first, halves[1], halves[0])
+
+
 def ladder_kernel(received, integrals, out):
     lefts = []
     for part in range(2):
-        rows = pl.ds(part * ROWS, ROWS)
-        both = received[:CHIPS, rows, :] + received[CHIPS:, rows, :]
-        lefts.append(both.reshape(CHIPS * ROWS, LANES))
+        halves = []
+        for zh in range(ZH):
+            start = ZH * BLOCK + (zh * 2 + part) * ROWS
+            halves.append(received[:, start : start + ROWS, :].reshape(Y * ROWS, LANES))
+        lefts.append(jnp.concatenate(halves, 0))
     left = split(jnp.concatenate(lefts, 1))
     width = PAIRS * LANES
     for start in range(0, width, 2 * LANES):
@@ -126,21 +151,22 @@
         rows = jnp.where(line == j, occupied[row * ROWS + j], rows)
     for pair in range(PAIRS):
         piece = pl.ds(pair * ROWS, ROWS)
-        total = near[piece, :] + far[piece, :]
-        for chip in range(CHIPS):
-            total = total + ladder[chip, piece, :]
+        total = ladder[0, piece, :]
+        for place in range(1, ZH * Y):
+            total = total + ladder[place, piece, :]
+        total = total + (near[piece, :] + far[piece, :])
         a = column * (2 * PAIRS) + 2 * pair
         energy = jnp.where(lane < TILE, virtual[a], virtual[a + 1]) + spectator
         out[0, :, pair * LANES : (pair + 1) * LANES] = total / (energy - occupied[0] - rows)
 
 
-def call(kernel, shape, specs, scratch=()):
+def call(kernel, shapes, specs, scratch=()):
     return pl.pallas_call(
         kernel,
-        out_shape=jax.ShapeDtypeStruct(shape, jnp.float32),
+        out_shape=[jax.ShapeDtypeStruct(shape, jnp.float32) for shape in shapes],
         in_specs=specs,
-        out_specs=VMEM,
-        scratch_shapes=[pltpu.VMEM(s, jnp.float32) for s in scratch],
+        out_specs=[VMEM] * len(shapes),
+        scratch_shapes=[pltpu.VMEM(shape, jnp.float32) for shape in scratch],
         compiler_params=PARAMS,
     )
 
@@ -175,34 +201,39 @@
 
 
 def per_device(amplitudes, cycle_block, ladder_block, occupied, virtual, tiles):
-    other = lax.ppermute(cycle_block, "core", [(0, 1), (1, 0)])
-    copies = call(pack_kernel, (ZL, BLOCK, LANES), [VMEM])(amplitudes)
+    swap = [(0, 1), (1, 0)]
+    other = lax.ppermute(cycle_block, "core", swap)
+    (copies,) = call(pack_kernel, [(ZL, BLOCK, LANES)], [VMEM])(amplitudes)
     column = lax.all_to_all(copies, "zl", 0, 0, tiled=True)
     copies = jnp.broadcast_to(column.reshape(1, ZL * BLOCK, LANES), (X, ZL * BLOCK, LANES))
     gathered = lax.all_to_all(copies, "x", 0, 0, tiled=True)
     gathered = gathered.reshape(CHIPS * BLOCK, LANES)
-    cycle = call(cycle_kernel, (CHIPS * BLOCK, LANES), [VMEM] * 3)(gathered, cycle_block, other)
-    cycle, gathered = lax.optimization_barrier((cycle, gathered))
-    window = call(
+
+    (window,) = call(
         window_kernel,
-        (CORE * CHIPS * 2 * ROWS, LANES),
+        [(CORE * CHIPS * 2 * ROWS, LANES)],
         [SMEM, VMEM],
         [(TILE // 2 * ROWS, LANES), (LANES, LANES), (LANES, LANES)],
     )(tiles, gathered)
-    window = window.reshape(CORE * CHIPS, 2 * ROWS, LANES)
-    window = lax.all_to_all(window, ("core", "zh", "y"), 0, 0, tiled=True)
+    window = window.reshape(CORE * ZH, Y * 2 * ROWS, LANES)
+    window = lax.all_to_all(window, ("core", "zh"), 0, 0, tiled=True)
+    (cycle,) = call(cycle_kernel, [(CHIPS * BLOCK, LANES)], [VMEM] * 3)(gathered, cycle_block, other)
     cycle = cycle.reshape(Y, ZH * BLOCK, LANES)
-    cycle = lax.psum_scatter(cycle, "y", scatter_dimension=0, tiled=False)
-    first, second = cycle[:BLOCK], cycle[BLOCK:]
-    low = lax.axis_index("zh") == 0
-    near = lax.ppermute(jnp.where(low, first, second), EVERY, places(near_rule))
-    far = lax.ppermute(jnp.where(low, second, first), EVERY, places(far_rule))
+    joined = (Y, ZH * (BLOCK + 2 * ROWS), LANES)
+    (joined,) = call(join_kernel, [joined], [VMEM] * 2)(cycle, window)
+    received = lax.all_to_all(joined, "y", 0, 0, tiled=True)
+
     integrals = ladder_block.reshape(-1, ladder_block.shape[2])
-    ladder = call(ladder_kernel, (CHIPS, BLOCK, LANES), [VMEM] * 2)(window, integrals)
+    (ladder,) = call(ladder_kernel, [(CHIPS, BLOCK, LANES)], [VMEM] * 2)(received, integrals)
+    ladder, received = lax.optimization_barrier((ladder, received))
+    near, far = call(cycle_sum_kernel, [(BLOCK, LANES)] * 2, [VMEM])(received)
+    near = lax.ppermute(near, EVERY, places(near_rule))
+    far = lax.ppermute(far, EVERY, places(far_rule))
     ladder = lax.all_to_all(ladder, ("zh", "y"), 0, 0, tiled=True)
-    return call(last_kernel, amplitudes.shape, [SMEM] * 3 + [VMEM] * 3)(
+    (result,) = call(last_kernel, [amplitudes.shape], [SMEM] * 3 + [VMEM] * 3)(
         tiles, occupied, virtual, ladder, near, far
     )
+    return result
 
 
 def solution(mesh):

time: 142 us -> 135 us (0.951)
  the two profiles are of different devices: /device:TPU:100 before, /device:TPU:46 now
where the time goes in v4:
time: 135 us; the launch traced here: 134 us
  blocking collectives  44.5 us (33%)
  waiting for transfers between devices  41.1 us (30%)
  starting transfers between devices  40.5 us (30%)
  Pallas kernels  6.21 us (5%)
  local copies, waits for them, and re-layouts  1.85 us (1%)
    all_to_all x1, blocking collectives, per_device(): received = lax.all_to_all(joined, 'y', 0, 0, tiled=True)  29.6 us
    all_to_all x1, blocking collectives, per_device(): column = lax.all_to_all(copies, 'zl', 0, 0, tiled=True)  14.9 us
    ppermute x1, waiting for transfers between devices, per_device(): far = lax.ppermute(far, EVERY, places(far_rule))  13.5 us
    ppermute x1, waiting for transfers between devices, per_device(): near = lax.ppermute(near, EVERY, places(near_rule))  12.1 us
    ppermute x1, starting transfers between devices, per_device(): far = lax.ppermute(far, EVERY, places(far_rule))  11 us
    all_to_all x1, waiting for transfers between devices, per_device(): window = lax.all_to_all(window, ('core', 'zh'), 0, 0, tiled=True)  8.92 us
    all_to_all x1, starting transfers between devices, per_device(): ladder = lax.all_to_all(ladder, ('zh', 'y'), 0, 0, tiled=True)  8.04 us
    all_to_all x1, starting transfers between devices, per_device(): window = lax.all_to_all(window, ('core', 'zh'), 0, 0, tiled=True)  7.58 us
  transfers between devices with their start and end apart: 6, of which 4 were waited for; matrix products, arithmetic and copies ran while one was open for 0% of the time, Pallas kernels for 2%

profile of v4, /device:TPU:46, one launch (start us, length us, event | category | flops | bytes accessed | tf_op | source)
XLA Modules:
  0.0 134.2 jit_solution(10645224984135134493)
XLA Ops:
  0.0 0.0 copy-start.1
  0.0 0.0 copy-start.2
  0.0 0.9 copy-done.2
  0.9 0.0 copy-start.4
  0.9 14.9 %all_to_all.25 = f32[4,104,128]{2,1,0:T(8,128)S(1)} all-to-all(f32[4,104,128]{2,1,0:T(8,128)S(1)} %shard_map.64), channel_id=1, replica_groups=mesh['zl'=4,'x'=4,'core'=2,'zh'=2,'y'=8] {'zl'}, dimensions={0} | all-to-all | bytes 425984 | tf_op jit(solution)/shard_map/all_to_all | solution.py:207
  15.8 1.0 broadcast_in_dim.8
  16.7 4.8 %all-to-all-start.1 = ((f32[4,416,128]{2,1,0:T(8,128)}), f32[4,416,128]{2,1,0:T(8,128)S(1)}, u32[]{:S(2)}, u32[]{:S(2)}) async-start(f32[4,416,128]{2,1,0:T(8,128)} %broadcast_in_dim.8), calls=%async_computation.1 | async-start | bytes 1703936 | tf_op jit(solution)/shard_map/all_to_all | solution.py:209
  21.5 0.0 copy-done.1
  21.5 1.9 %collective-permute-start = (f32[512,256]{1,0:T(8,128)S(1)}, f32[512,256]{1,0:T(8,128)S(1)}, u32[]{:S(2)}, u32[]{:S(2)}) collective-permute-start(f32[512,256]{1,0:T(8,128)S(1)} %copy-done.1), channel_id=1, source_target_pairs={{0,16},{16,0},{1,17},{17,1},{2,18},{18,2},{3,19},{19,3},{4,20},{20... | collective-permute-start | bytes 1572872 | tf_op jit(solution)/shard_map/ppermute | solution.py:205
  23.4 6.7 %all-to-all-done.1 = f32[4,416,128]{2,1,0:T(8,128)S(1)} async-done(((f32[4,416,128]{2,1,0:T(8,128)}), f32[4,416,128]{2,1,0:T(8,128)S(1)}, u32[]{:S(2)}, u32[]{:S(2)}) %all-to-all-start.1) | async-done | bytes 852000 | tf_op jit(solution)/shard_map/all_to_all | solution.py:209
  30.1 0.0 copy-done.4
  30.1 2.1 %shard_map.66 = f32[512,128]{1,0:T(8,128)} custom-call(s32[2]{0:T(128)S(1)} %copy-done.4, f32[1664,128]{1,0:T(8,128)S(1)} %bitcast.5), custom_call_target="tpu_custom_call" | custom-call | tf_op jit(solution)/shard_map/pallas_call | solution.py:212
  32.2 7.6 %all-to-all-start.2 = ((f32[4,128,128]{2,1,0:T(8,128)}), f32[4,128,128]{2,1,0:T(8,128)S(1)}, u32[]{:S(2)}, u32[]{:S(2)}) async-start(f32[4,128,128]{2,1,0:T(8,128)} %bitcast.3), calls=%async_computation.2 | async-start | bytes 524288 | tf_op jit(solution)/shard_map/all_to_all | solution.py:219
  39.8 0.0 collective-permute-done.other
  39.8 1.1 shard_map.65
  40.9 8.9 %all-to-all-done.2.window = f32[4,128,128]{2,1,0:T(8,128)S(1)} async-done(((f32[4,128,128]{2,1,0:T(8,128)}), f32[4,128,128]{2,1,0:T(8,128)S(1)}, u32[]{:S(2)}, u32[]{:S(2)}) %all-to-all-start.2) | async-done | bytes 262176 | tf_op jit(solution)/shard_map/all_to_all | solution.py:219
  49.9 0.0 copy-start
  49.9 0.1 shard_map.67
  49.9 29.6 %all_to_all.26.received = f32[8,240,128]{2,1,0:T(8,128)S(1)} all-to-all(f32[8,240,128]{2,1,0:T(8,128)S(1)} %shard_map.67), channel_id=1, replica_groups=mesh['zl'=4,'x'=4,'core'=2,'zh'=2,'y'=8] {'y'}, dimensions={0} | all-to-all | bytes 1966080 | tf_op jit(solution)/shard_map/all_to_all | solution.py:224
  79.5 0.0 copy-done
  79.5 1.5 %shard_map.68 = f32[16,104,128]{2,1,0:T(8,128)} custom-call(f32[8,240,128]{2,1,0:T(8,128)S(1)} %all_to_all.26.received, f32[256,1664]{1,0:T(8,128)S(1)} %bitcast.8), custom_call_target="tpu_custom_call" | custom-call | tf_op jit(solution)/shard_map/pallas_call | solution.py:227
  81.0 0.0 copy-start.3
  81.0 0.0 copy-start.5
  81.0 8.0 %all-to-all-start.4 = ((f32[16,104,128]{2,1,0:T(8,128)}), f32[16,104,128]{2,1,0:T(8,128)S(1)}, u32[]{:S(2)}, u32[]{:S(2)}) async-start(f32[16,104,128]{2,1,0:T(8,128)} %shard_map.68), calls=%async_computation.4 | async-start | bytes 1703936 | tf_op jit(solution)/shard_map/all_to_all | solution.py:232
  89.1 7.3 %collective-permute-start.1 = (f32[104,128]{1,0:T(8,128)S(1)}, f32[104,128]{1,0:T(8,128)S(1)}, u32[]{:S(2)}, u32[]{:S(2)}) collective-permute-start(f32[104,128]{1,0:T(8,128)S(1)} %get-tuple-element.11), channel_id=1, source_target_pairs={{0,0},{1,256},{2,32},{3,288},{4,64},{5,320},{6,96},{7,352},{8,128}... | collective-permute-start | bytes 159752 | tf_op jit(solution)/shard_map/ppermute | solution.py:230
  96.4 11.0 %collective-permute-start.2 = (f32[104,128]{1,0:T(8,128)S(1)}, f32[104,128]{1,0:T(8,128)S(1)}, u32[]{:S(2)}, u32[]{:S(2)}) collective-permute-start(f32[104,128]{1,0:T(8,128)S(1)} %get-tuple-element.12), channel_id=1, source_target_pairs={{0,128},{1,384},{2,160},{3,416},{4,192},{5,448},{6,224},{7,480},{8... | collective-permute-start | bytes 159752 | tf_op jit(solution)/shard_map/ppermute | solution.py:231
  107.4 12.1 %collective-permute-done.1.near = f32[104,128]{1,0:T(8,128)S(1)} collective-permute-done((f32[104,128]{1,0:T(8,128)S(1)}, f32[104,128]{1,0:T(8,128)S(1)}, u32[]{:S(2)}, u32[]{:S(2)}) %collective-permute-start.1) | collective-permute-done | bytes 53280 | tf_op jit(solution)/shard_map/ppermute | solution.py:230
  119.5 13.5 %collective-permute-done.2.far = f32[104,128]{1,0:T(8,128)S(1)} collective-permute-done((f32[104,128]{1,0:T(8,128)S(1)}, f32[104,128]{1,0:T(8,128)S(1)}, u32[]{:S(2)}, u32[]{:S(2)}) %collective-permute-start.2) | collective-permute-done | bytes 53280 | tf_op jit(solution)/shard_map/ppermute | solution.py:231
  132.9 0.0 all-to-all-done.4.ladder
  132.9 0.0 copy-done.3
  132.9 0.0 copy-done.5
  132.9 1.3 shard_map.70
  (2 shorter events, 0.1 us)
Async XLA Ops:
  0.0 21.5 %copy-start.1 = (f32[512,256]{1,0:T(8,128)S(1)}, f32[512,256]{1,0:T(8,128)}, u32[]{:S(2)}) copy-start(f32[512,256]{1,0:T(8,128)} %own.1) | copy-start | bytes 1572868
  0.0 0.9 copy-start.2
  0.9 29.2 %copy-start.4 = (s32[2]{0:T(128)S(1)}, s32[2]{0:T(128)}, u32[]{:S(2)}) copy-start(s32[2]{0:T(128)} %tiles.3) | copy-start | bytes 28
  16.7 13.3 %all-to-all-start.1 = ((f32[4,416,128]{2,1,0:T(8,128)}), f32[4,416,128]{2,1,0:T(8,128)S(1)}, u32[]{:S(2)}, u32[]{:S(2)}) async-start(f32[4,416,128]{2,1,0:T(8,128)} %broadcast_in_dim.8), calls=%async_computation.1 | async-start | bytes 1703936 | tf_op jit(solution)/shard_map/all_to_all | solution.py:209
  21.5 18.3 %collective-permute-start = (f32[512,256]{1,0:T(8,128)S(1)}, f32[512,256]{1,0:T(8,128)S(1)}, u32[]{:S(2)}, u32[]{:S(2)}) collective-permute-start(f32[512,256]{1,0:T(8,128)S(1)} %copy-done.1), channel_id=1, source_target_pairs={{0,16},{16,0},{1,17},{17,1},{2,18},{18,2},{3,19},{19,3},{4,20},{20... | collective-permute-start | bytes 1572872 | tf_op jit(solution)/shard_map/ppermute | solution.py:205
  32.2 17.6 %all-to-all-start.2 = ((f32[4,128,128]{2,1,0:T(8,128)}), f32[4,128,128]{2,1,0:T(8,128)S(1)}, u32[]{:S(2)}, u32[]{:S(2)}) async-start(f32[4,128,128]{2,1,0:T(8,128)} %bitcast.3), calls=%async_computation.2 | async-start | bytes 524288 | tf_op jit(solution)/shard_map/all_to_all | solution.py:219
  49.9 29.7 %copy-start = (f32[4,64,1664]{2,1,0:T(8,128)S(1)}, f32[4,64,1664]{2,1,0:T(8,128)}, u32[]{:S(2)}) copy-start(f32[4,64,1664]{2,1,0:T(8,128)} %param.8) | copy-start | bytes 5111812
  81.0 51.9 %copy-start.3 = (f32[832]{0:T(1024)S(1)}, f32[832]{0:T(1024)}, u32[]{:S(2)}) copy-start(f32[832]{0:T(1024)} %virtual.1) | copy-start | bytes 9988
  81.0 51.9 %copy-start.5 = (f32[128]{0:T(128)S(1)}, f32[128]{0:T(128)}, u32[]{:S(2)}) copy-start(f32[128]{0:T(128)} %occupied.1) | copy-start | bytes 1540
  81.0 51.9 %all-to-all-start.4 = ((f32[16,104,128]{2,1,0:T(8,128)}), f32[16,104,128]{2,1,0:T(8,128)S(1)}, u32[]{:S(2)}, u32[]{:S(2)}) async-start(f32[16,104,128]{2,1,0:T(8,128)} %shard_map.68), calls=%async_computation.4 | async-start | bytes 1703936 | tf_op jit(solution)/shard_map/all_to_all | solution.py:232
  89.1 30.4 %collective-permute-start.1 = (f32[104,128]{1,0:T(8,128)S(1)}, f32[104,128]{1,0:T(8,128)S(1)}, u32[]{:S(2)}, u32[]{:S(2)}) collective-permute-start(f32[104,128]{1,0:T(8,128)S(1)} %get-tuple-element.11), channel_id=1, source_target_pairs={{0,0},{1,256},{2,32},{3,288},{4,64},{5,320},{6,96},{7,352},{8,128}... | collective-permute-start | bytes 159752 | tf_op jit(solution)/shard_map/ppermute | solution.py:230
  96.4 36.5 %collective-permute-start.2 = (f32[104,128]{1,0:T(8,128)S(1)}, f32[104,128]{1,0:T(8,128)S(1)}, u32[]{:S(2)}, u32[]{:S(2)}) collective-permute-start(f32[104,128]{1,0:T(8,128)S(1)} %get-tuple-element.12), channel_id=1, source_target_pairs={{0,128},{1,384},{2,160},{3,416},{4,192},{5,448},{6,224},{7,480},{8... | collective-permute-start | bytes 159752 | tf_op jit(solution)/shard_map/ppermute | solution.py:231

commit v5 on v3

--- a/solution.py
+++ b/solution.py
@@ -15,6 +15,8 @@
 PAIRS = 13
 LANES = 2 * TILE
 BLOCK = PAIRS * ROWS
+SIDE = (PAIRS + 1) // 2
+SKIP = PAIRS - SIDE
 EVERY = ("zl", "x", "core", "zh", "y")
 VMEM = pl.BlockSpec(memory_space=pltpu.VMEM)
 SMEM = pl.BlockSpec(memory_space=pltpu.SMEM)
@@ -97,7 +99,8 @@
 def join_kernel(cycle, own, other, out):
     for place in range(CHIPS):
         out[place, :BLOCK, :] = cycle[place, :, :]
-        out[place, BLOCK:, :] = own[place, :, :] + other[place, :, :]
+        for start, source in ((BLOCK, place), (BLOCK + 2 * ROWS, place ^ 1)):
+            out[place, start : start + 2 * ROWS, :] = own[source, :, :] + other[source, :, :]
 
 
 def sum_kernel(received, out):
@@ -107,16 +110,19 @@
     out[...] = total
 
 
-def ladder_kernel(received, integrals, out):
+def ladder_kernel(received, own, other, out):
     lefts = []
-    for part in range(2):
+    for part in range(4):
         rows = received[:, BLOCK + part * ROWS : BLOCK + (part + 1) * ROWS, :]
         lefts.append(rows.reshape(CHIPS * ROWS, LANES))
     left = split(jnp.concatenate(lefts, 1))
-    width = PAIRS * LANES
+    first = lax.axis_index("y") % 2 * (SKIP * LANES)
+    width = SIDE * LANES
     for start in range(0, width, 2 * LANES):
         stop = min(start + 2 * LANES, width)
-        result = product(left, split(integrals[:, start:stop]))
+        columns = pl.ds(pl.multiple_of(first + start, LANES), stop - start)
+        right = jnp.concatenate([own[:, columns], other[:, start:stop]], 0)
+        result = product(left, split(right))
         for column in range(start, stop, LANES):
             value = result[:, column - start : column - start + LANES]
             rows = pl.ds(column // LANES * ROWS, ROWS)
@@ -138,8 +144,10 @@
     for pair in range(PAIRS):
         piece = pl.ds(pair * ROWS, ROWS)
         total = cycle[piece, :]
-        for chip in range(CHIPS):
-            total = total + ladder[chip, piece, :]
+        side = int(pair >= SIDE)
+        rows_of_side = pl.ds((pair - side * SKIP) * ROWS, ROWS)
+        for place in range(side, ZH * Y, 2):
+            total = total + ladder[place, rows_of_side, :]
         a = column * (2 * PAIRS) + 2 * pair
         energy = jnp.where(lane < TILE, virtual[a], virtual[a + 1]) + spectator
         out[0, :, pair * LANES : (pair + 1) * LANES] = total / (energy - occupied[0] - rows)
@@ -181,6 +189,10 @@
 
 def per_device(amplitudes, cycle_block, ladder_block, occupied, virtual, tiles):
     other = lax.ppermute(cycle_block, "core", [(0, 1), (1, 0)])
+    integrals = ladder_block.reshape(-1, ladder_block.shape[2])
+    start = (1 - lax.axis_index("y") % 2) * (SKIP * LANES)
+    side = lax.dynamic_slice_in_dim(integrals, start, SIDE * LANES, 1)
+    side = lax.ppermute(side, "y", [(y, y ^ 1) for y in range(Y)])
     copies = call(pack_kernel, (ZL, BLOCK, LANES), [VMEM])(amplitudes)
     column = lax.all_to_all(copies, "zl", 0, 0, tiled=True)
     copies = jnp.broadcast_to(column.reshape(1, ZL * BLOCK, LANES), (X, ZL * BLOCK, LANES))
@@ -196,14 +208,13 @@
     other_window = lax.ppermute(window, "core", [(0, 1), (1, 0)])
     cycle = call(cycle_kernel, (CHIPS * BLOCK, LANES), [VMEM] * 3)(gathered, cycle_block, other)
     cycle = cycle.reshape(CHIPS, BLOCK, LANES)
-    joined = (CHIPS, BLOCK + 2 * ROWS, LANES)
+    joined = (CHIPS, BLOCK + 4 * ROWS, LANES)
     joined = call(join_kernel, joined, [VMEM] * 3)(cycle, window, other_window)
     received = lax.all_to_all(joined, ("zh", "y"), 0, 0, tiled=True)
-    integrals = ladder_block.reshape(-1, ladder_block.shape[2])
-    ladder = call(ladder_kernel, (CHIPS, BLOCK, LANES), [VMEM] * 2)(received, integrals)
-    ladder, received = lax.optimization_barrier((ladder, received))
     cycle = call(sum_kernel, (BLOCK, LANES), [VMEM])(received)
+    cycle, received = lax.optimization_barrier((cycle, received))
     cycle = lax.ppermute(cycle, EVERY, places(owner_rule))
+    ladder = call(ladder_kernel, (CHIPS, SIDE * ROWS, LANES), [VMEM] * 3)(received, integrals, side)
     ladder = lax.all_to_all(ladder, ("zh", "y"), 0, 0, tiled=True)
     return call(last_kernel, amplitudes.shape, [SMEM] * 3 + [VMEM] * 2)(
         tiles, occupied, virtual, ladder, cycle

time: 120 us -> 137 us (1.14)
  the two profiles are of different devices: /device:TPU:110 before, /device:TPU:68 now
where the time goes in v5:
time: 137 us; the launch traced here: 136 us
  waiting for transfers between devices  67.6 us (49%)
  starting transfers between devices  45.4 us (33%)
  blocking collectives  12.8 us (9%)
  Pallas kernels  7.57 us (6%)
  local copies, waits for them, and re-layouts  2.87 us (2%)
    all_to_all x1, waiting for transfers between devices, per_device(): received = lax.all_to_all(joined, ('zh', 'y'), 0, 0, tiled=True)  29.6 us
    ppermute x1, waiting for transfers between devices, per_device(): cycle = lax.ppermute(cycle, EVERY, places(owner_rule))  19.3 us
    all_to_all x1, starting transfers between devices, per_device(): received = lax.all_to_all(joined, ('zh', 'y'), 0, 0, tiled=True)  13 us
    all_to_all x1, blocking collectives, per_device(): column = lax.all_to_all(copies, 'zl', 0, 0, tiled=True)  12.8 us
    ppermute x1, waiting for transfers between devices, per_device(): side = lax.ppermute(side, 'y', [(y, y ^ 1) for y in range(Y)])  11.9 us
    all_to_all x1, starting transfers between devices, per_device(): ladder = lax.all_to_all(ladder, ('zh', 'y'), 0, 0, tiled=True)  10.8 us
    ppermute x1, starting transfers between devices, per_device(): cycle = lax.ppermute(cycle, EVERY, places(owner_rule))  9.25 us
    all_to_all x1, waiting for transfers between devices, per_device(): gathered = lax.all_to_all(copies, 'x', 0, 0, tiled=True)  6.62 us
  transfers between devices with their start and end apart: 7, of which 5 were waited for; matrix products, arithmetic and copies ran while one was open for 1% of the time, Pallas kernels for 2%

profile of v5, /device:TPU:68, one launch (start us, length us, event | category | flops | bytes accessed | tf_op | source)
XLA Modules:
  0.0 136.4 jit_solution(13630262514484079990)
XLA Ops:
  0.0 0.0 copy-start.1
  0.0 0.0 copy-start.2
  0.0 0.9 copy-done.2
  0.9 0.0 copy-start.4
  0.9 12.8 %all_to_all.20 = f32[4,104,128]{2,1,0:T(8,128)S(1)} all-to-all(f32[4,104,128]{2,1,0:T(8,128)S(1)} %shard_map.64), channel_id=1, replica_groups=mesh['zl'=4,'x'=4,'core'=2,'zh'=2,'y'=8] {'zl'}, dimensions={0} | all-to-all | bytes 425984 | tf_op jit(solution)/shard_map/all_to_all | solution.py:197
  13.7 1.0 broadcast_in_dim.8
  14.7 4.8 %all-to-all-start.1 = ((f32[4,416,128]{2,1,0:T(8,128)}), f32[4,416,128]{2,1,0:T(8,128)S(1)}, u32[]{:S(2)}, u32[]{:S(2)}) async-start(f32[4,416,128]{2,1,0:T(8,128)} %broadcast_in_dim.8), calls=%async_computation.1 | async-start | bytes 1703936 | tf_op jit(solution)/shard_map/all_to_all | solution.py:199
  19.5 0.0 copy-done.1
  19.5 1.9 %collective-permute-start = (f32[512,256]{1,0:T(8,128)S(1)}, f32[512,256]{1,0:T(8,128)S(1)}, u32[]{:S(2)}, u32[]{:S(2)}) collective-permute-start(f32[512,256]{1,0:T(8,128)S(1)} %copy-done.1), channel_id=1, source_target_pairs={{0,16},{16,0},{1,17},{17,1},{2,18},{18,2},{3,19},{19,3},{4,20},{20... | collective-permute-start | bytes 1572872 | tf_op jit(solution)/shard_map/ppermute | solution.py:191
  21.4 6.6 %all-to-all-done.1 = f32[4,416,128]{2,1,0:T(8,128)S(1)} async-done(((f32[4,416,128]{2,1,0:T(8,128)}), f32[4,416,128]{2,1,0:T(8,128)S(1)}, u32[]{:S(2)}, u32[]{:S(2)}) %all-to-all-start.1) | async-done | bytes 852000 | tf_op jit(solution)/shard_map/all_to_all | solution.py:199
  28.0 0.0 copy-done.4
  28.0 1.4 %shard_map.66 = f32[256,128]{1,0:T(8,128)S(1)} custom-call(s32[2]{0:T(128)S(1)} %copy-done.4, f32[1664,128]{1,0:T(8,128)S(1)} %bitcast.5), custom_call_target="tpu_custom_call" | custom-call | tf_op jit(solution)/shard_map/pallas_call | solution.py:201
  29.5 1.9 %collective-permute-start.1 = (f32[16,16,128]{2,1,0:T(8,128)S(1)}, f32[16,16,128]{2,1,0:T(8,128)S(1)}, u32[]{:S(2)}, u32[]{:S(2)}) collective-permute-start(f32[16,16,128]{2,1,0:T(8,128)S(1)} %bitcast.10), channel_id=1, source_target_pairs={{0,16},{16,0},{1,17},{17,1},{2,18},{18,2},{3,19},{19,3},{4,20},{20... | collective-permute-start | bytes 393224 | tf_op jit(solution)/shard_map/ppermute | solution.py:208
  31.4 0.0 collective-permute-done.other
  31.4 1.1 shard_map.65
  32.5 0.2 collective-permute-done.1.other
  32.7 0.0 copy-start
  32.7 1.1 shard_map.67
  33.8 13.0 %all-to-all-start.2 = ((f32[16,136,128]{2,1,0:T(8,128)}), f32[16,136,128]{2,1,0:T(8,128)S(1)}, u32[]{:S(2)}, u32[]{:S(2)}) async-start(f32[16,136,128]{2,1,0:T(8,128)} %shard_map.67), calls=%async_computation.2 | async-start | bytes 2228224 | tf_op jit(solution)/shard_map/all_to_all | solution.py:213
  46.8 0.0 copy-done
  46.8 1.0 constant_dynamic-slice_fusion
  47.8 3.8 %collective-permute-start.2 = (f32[256,896]{1,0:T(8,128)}, f32[256,896]{1,0:T(8,128)}, u32[]{:S(2)}, u32[]{:S(2)}) collective-permute-start(f32[256,896]{1,0:T(8,128)} %constant_dynamic-slice_fusion), channel_id=1, source_target_pairs={{0,1},{1,0},{2,3},{3,2},{4,5},{5,4},{6,7},{7,6},{8,9},{9,8},{10,11... | collective-permute-start | bytes 2752520 | tf_op jit(solution)/shard_map/ppermute | solution.py:195
  51.6 29.6 %all-to-all-done.2.received = f32[16,136,128]{2,1,0:T(8,128)S(1)} async-done(((f32[16,136,128]{2,1,0:T(8,128)}), f32[16,136,128]{2,1,0:T(8,128)S(1)}, u32[]{:S(2)}, u32[]{:S(2)}) %all-to-all-start.2) | async-done | bytes 1114144 | tf_op jit(solution)/shard_map/all_to_all | solution.py:213
  81.2 0.0 copy-start.3
  81.3 0.0 copy-start.5
  81.3 11.9 %collective-permute-done.2.other = f32[256,896]{1,0:T(8,128)} collective-permute-done((f32[256,896]{1,0:T(8,128)}, f32[256,896]{1,0:T(8,128)}, u32[]{:S(2)}, u32[]{:S(2)}) %collective-permute-start.2) | collective-permute-done | bytes 917536 | tf_op jit(solution)/shard_map/ppermute | solution.py:195
  93.2 2.6 %shard_map.69 = f32[16,56,128]{2,1,0:T(8,128)} custom-call(f32[16,136,128]{2,1,0:T(8,128)S(1)} %all-to-all-done.2.received, f32[256,1664]{1,0:T(8,128)S(1)} %bitcast.8, f32[256,896]{1,0:T(8,128)} %collective-permute-done.2.other), custom_call_target="tpu_custom_call" | custom-call | tf_op jit(solution)/shard_map/pallas_call | solution.py:217
  95.7 10.8 %all-to-all-start.3 = ((f32[16,56,128]{2,1,0:T(8,128)}), f32[16,56,128]{2,1,0:T(8,128)S(1)}, u32[]{:S(2)}, u32[]{:S(2)}) async-start(f32[16,56,128]{2,1,0:T(8,128)} %shard_map.69), calls=%async_computation.3 | async-start | bytes 917504 | tf_op jit(solution)/shard_map/all_to_all | solution.py:218
  106.5 9.3 %collective-permute-start.3 = (f32[104,128]{1,0:T(8,128)S(1)}, f32[104,128]{1,0:T(8,128)S(1)}, u32[]{:S(2)}, u32[]{:S(2)}) collective-permute-start(f32[104,128]{1,0:T(8,128)S(1)} %shard_map.68), channel_id=1, source_target_pairs={{0,0},{1,128},{2,256},{3,384},{4,32},{5,160},{6,288},{7,416},{8,64... | collective-permute-start | bytes 159752 | tf_op jit(solution)/shard_map/ppermute | solution.py:216
  115.8 19.3 %collective-permute-done.3.cycle = f32[104,128]{1,0:T(8,128)S(1)} collective-permute-done((f32[104,128]{1,0:T(8,128)S(1)}, f32[104,128]{1,0:T(8,128)S(1)}, u32[]{:S(2)}, u32[]{:S(2)}) %collective-permute-start.3) | collective-permute-done | bytes 53280 | tf_op jit(solution)/shard_map/ppermute | solution.py:216
  135.1 0.0 all-to-all-done.3.ladder
  135.1 0.0 copy-done.3
  135.1 0.0 copy-done.5
  135.1 1.3 shard_map.70
  (2 shorter events, 0.1 us)
Async XLA Ops:
  0.0 19.5 %copy-start.1 = (f32[512,256]{1,0:T(8,128)S(1)}, f32[512,256]{1,0:T(8,128)}, u32[]{:S(2)}) copy-start(f32[512,256]{1,0:T(8,128)} %own.1) | copy-start | bytes 1572868
  0.0 0.9 copy-start.2
  0.9 27.2 %copy-start.4 = (s32[2]{0:T(128)S(1)}, s32[2]{0:T(128)}, u32[]{:S(2)}) copy-start(s32[2]{0:T(128)} %tiles.3) | copy-start | bytes 28
  14.7 13.3 %all-to-all-start.1 = ((f32[4,416,128]{2,1,0:T(8,128)}), f32[4,416,128]{2,1,0:T(8,128)S(1)}, u32[]{:S(2)}, u32[]{:S(2)}) async-start(f32[4,416,128]{2,1,0:T(8,128)} %broadcast_in_dim.8), calls=%async_computation.1 | async-start | bytes 1703936 | tf_op jit(solution)/shard_map/all_to_all | solution.py:199
  19.5 11.9 %collective-permute-start = (f32[512,256]{1,0:T(8,128)S(1)}, f32[512,256]{1,0:T(8,128)S(1)}, u32[]{:S(2)}, u32[]{:S(2)}) collective-permute-start(f32[512,256]{1,0:T(8,128)S(1)} %copy-done.1), channel_id=1, source_target_pairs={{0,16},{16,0},{1,17},{17,1},{2,18},{18,2},{3,19},{19,3},{4,20},{20... | collective-permute-start | bytes 1572872 | tf_op jit(solution)/shard_map/ppermute | solution.py:191
  29.5 3.2 %collective-permute-start.1 = (f32[16,16,128]{2,1,0:T(8,128)S(1)}, f32[16,16,128]{2,1,0:T(8,128)S(1)}, u32[]{:S(2)}, u32[]{:S(2)}) collective-permute-start(f32[16,16,128]{2,1,0:T(8,128)S(1)} %bitcast.10), channel_id=1, source_target_pairs={{0,16},{16,0},{1,17},{17,1},{2,18},{18,2},{3,19},{19,3},{4,20},{20... | collective-permute-start | bytes 393224 | tf_op jit(solution)/shard_map/ppermute | solution.py:208
  32.7 14.1 %copy-start = (f32[4,64,1664]{2,1,0:T(8,128)S(1)}, f32[4,64,1664]{2,1,0:T(8,128)}, u32[]{:S(2)}) copy-start(f32[4,64,1664]{2,1,0:T(8,128)} %param.8) | copy-start | bytes 5111812
  33.8 47.4 %all-to-all-start.2 = ((f32[16,136,128]{2,1,0:T(8,128)}), f32[16,136,128]{2,1,0:T(8,128)S(1)}, u32[]{:S(2)}, u32[]{:S(2)}) async-start(f32[16,136,128]{2,1,0:T(8,128)} %shard_map.67), calls=%async_computation.2 | async-start | bytes 2228224 | tf_op jit(solution)/shard_map/all_to_all | solution.py:213
  47.8 45.4 %collective-permute-start.2 = (f32[256,896]{1,0:T(8,128)}, f32[256,896]{1,0:T(8,128)}, u32[]{:S(2)}, u32[]{:S(2)}) collective-permute-start(f32[256,896]{1,0:T(8,128)} %constant_dynamic-slice_fusion), channel_id=1, source_target_pairs={{0,1},{1,0},{2,3},{3,2},{4,5},{5,4},{6,7},{7,6},{8,9},{9,8},{10,11... | collective-permute-start | bytes 2752520 | tf_op jit(solution)/shard_map/ppermute | solution.py:195
  81.2 53.8 %copy-start.3 = (f32[832]{0:T(1024)S(1)}, f32[832]{0:T(1024)}, u32[]{:S(2)}) copy-start(f32[832]{0:T(1024)} %virtual.1) | copy-start | bytes 9988
  81.3 53.8 %copy-start.5 = (f32[128]{0:T(128)S(1)}, f32[128]{0:T(128)}, u32[]{:S(2)}) copy-start(f32[128]{0:T(128)} %occupied.1) | copy-start | bytes 1540
  95.7 39.3 %all-to-all-start.3 = ((f32[16,56,128]{2,1,0:T(8,128)}), f32[16,56,128]{2,1,0:T(8,128)S(1)}, u32[]{:S(2)}, u32[]{:S(2)}) async-start(f32[16,56,128]{2,1,0:T(8,128)} %shard_map.69), calls=%async_computation.3 | async-start | bytes 917504 | tf_op jit(solution)/shard_map/all_to_all | solution.py:218
  106.5 28.6 %collective-permute-start.3 = (f32[104,128]{1,0:T(8,128)S(1)}, f32[104,128]{1,0:T(8,128)S(1)}, u32[]{:S(2)}, u32[]{:S(2)}) collective-permute-start(f32[104,128]{1,0:T(8,128)S(1)} %shard_map.68), channel_id=1, source_target_pairs={{0,0},{1,128},{2,256},{3,384},{4,32},{5,160},{6,288},{7,416},{8,64... | collective-permute-start | bytes 159752 | tf_op jit(solution)/shard_map/ppermute | solution.py:216

commit v6 on v4

--- a/solution.py
+++ b/solution.py
@@ -71,9 +71,7 @@
             odd = turned[pl.ds(2 * part + 1, CHIPS, stride=4), :]
             for inner, value in enumerate(pair_up(even, odd)):
                 row = part * ROWS + half * 2 + inner
-                for target in range(CORE):
-                    start = target * CHIPS * 2 * ROWS + row
-                    out[pl.ds(start, CHIPS, stride=2 * ROWS), :] = value
+                out[pl.ds(row, CHIPS, stride=2 * ROWS), :] = value
 
 
 def cycle_kernel(gathered, own, other, out):
@@ -96,36 +94,28 @@
                 out[pl.ds(j, CHIPS * PAIRS, stride=ROWS), :] = value
 
 
-def join_kernel(cycle, window, out):
-    for y in range(Y):
-        out[y, : ZH * BLOCK, :] = cycle[y, :, :]
-        rows = slice(y * 2 * ROWS, (y + 1) * 2 * ROWS)
-        for zh in range(ZH):
-            start = ZH * BLOCK + zh * 2 * ROWS
-            out[y, start : start + 2 * ROWS, :] = window[zh, rows, :] + window[ZH + zh, rows, :]
-
-
-def cycle_sum_kernel(received, near, far):
+def sum_kernel(received, near_cycle, far_cycle, near, far):
     first = lax.axis_index("zh") == 0
     for row in range(0, BLOCK, ROWS):
-        halves = []
-        for start in (row, BLOCK + row):
+        sums = []
+        for start in range(row, 4 * BLOCK, BLOCK):
             total = received[0, start : start + ROWS, :]
             for place in range(1, Y):
                 total = total + received[place, start : start + ROWS, :]
-            halves.append(total)
-        near[row : row + ROWS, :] = jnp.where(first, halves[0], halves[1])
-        far[row : row + ROWS, :] = jnp.where(first, halves[1], halves[0])
-
-
-def ladder_kernel(received, integrals, out):
+            sums.append(total)
+        rows = slice(row, row + ROWS)
+        near_cycle[rows, :] = jnp.where(first, sums[0], sums[1])
+        far_cycle[rows, :] = jnp.where(first, sums[1], sums[0])
+        near[rows, :] = jnp.where(first, sums[2], sums[3])
+        far[rows, :] = jnp.where(first, sums[3], sums[2])
+
+
+def ladder_kernel(window, integrals, cycle, out):
+    out[:, : ZH * BLOCK, :] = cycle[...]
     lefts = []
     for part in range(2):
-        halves = []
-        for zh in range(ZH):
-            start = ZH * BLOCK + (zh * 2 + part) * ROWS
-            halves.append(received[:, start : start + ROWS, :].reshape(Y * ROWS, LANES))
-        lefts.append(jnp.concatenate(halves, 0))
+        rows = window[:, part * ROWS : (part + 1) * ROWS, :]
+        lefts.append(rows.reshape(CHIPS * ROWS, LANES))
     left = split(jnp.concatenate(lefts, 1))
     width = PAIRS * LANES
     for start in range(0, width, 2 * LANES):
@@ -133,11 +123,13 @@
         result = product(left, split(integrals[:, start:stop]))
         for column in range(start, stop, LANES):
             value = result[:, column - start : column - start + LANES]
-            rows = pl.ds(column // LANES * ROWS, ROWS)
-            out[:, rows, :] = value.reshape(CHIPS, ROWS, LANES)
-
-
-def last_kernel(tiles, occupied, virtual, ladder, near, far, out):
+            for zh in range(ZH):
+                rows = pl.ds((ZH + zh) * BLOCK + column // LANES * ROWS, ROWS)
+                part = value[zh * Y * ROWS : (zh + 1) * Y * ROWS]
+                out[:, rows, :] = part.reshape(Y, ROWS, LANES)
+
+
+def last_kernel(tiles, occupied, virtual, near, far, near_cycle, far_cycle, out):
     column = lax.axis_index("zl") * (X * CORE) + lax.axis_index("x") * CORE + lax.axis_index("core")
     row = lax.axis_index("zh") * Y + lax.axis_index("y")
     shape = (ROWS, LANES)
@@ -151,10 +143,7 @@
         rows = jnp.where(line == j, occupied[row * ROWS + j], rows)
     for pair in range(PAIRS):
         piece = pl.ds(pair * ROWS, ROWS)
-        total = ladder[0, piece, :]
-        for place in range(1, ZH * Y):
-            total = total + ladder[place, piece, :]
-        total = total + (near[piece, :] + far[piece, :])
+        total = (near[piece, :] + far[piece, :]) + (near_cycle[piece, :] + far_cycle[piece, :])
         a = column * (2 * PAIRS) + 2 * pair
         energy = jnp.where(lane < TILE, virtual[a], virtual[a + 1]) + spectator
         out[0, :, pair * LANES : (pair + 1) * LANES] = total / (energy - occupied[0] - rows)
@@ -211,27 +200,25 @@
 
     (window,) = call(
         window_kernel,
-        [(CORE * CHIPS * 2 * ROWS, LANES)],
+        [(CHIPS * 2 * ROWS, LANES)],
         [SMEM, VMEM],
         [(TILE // 2 * ROWS, LANES), (LANES, LANES), (LANES, LANES)],
     )(tiles, gathered)
-    window = window.reshape(CORE * ZH, Y * 2 * ROWS, LANES)
-    window = lax.all_to_all(window, ("core", "zh"), 0, 0, tiled=True)
+    window = window + lax.ppermute(window, "core", swap)
+    window = lax.all_to_all(window.reshape(CHIPS, 2 * ROWS, LANES), ("zh", "y"), 0, 0, tiled=True)
+
     (cycle,) = call(cycle_kernel, [(CHIPS * BLOCK, LANES)], [VMEM] * 3)(gathered, cycle_block, other)
-    cycle = cycle.reshape(Y, ZH * BLOCK, LANES)
-    joined = (Y, ZH * (BLOCK + 2 * ROWS), LANES)
-    (joined,) = call(join_kernel, [joined], [VMEM] * 2)(cycle, window)
-    received = lax.all_to_all(joined, "y", 0, 0, tiled=True)
-
     integrals = ladder_block.reshape(-1, ladder_block.shape[2])
-    (ladder,) = call(ladder_kernel, [(CHIPS, BLOCK, LANES)], [VMEM] * 2)(received, integrals)
-    ladder, received = lax.optimization_barrier((ladder, received))
-    near, far = call(cycle_sum_kernel, [(BLOCK, LANES)] * 2, [VMEM])(received)
-    near = lax.ppermute(near, EVERY, places(near_rule))
-    far = lax.ppermute(far, EVERY, places(far_rule))
-    ladder = lax.all_to_all(ladder, ("zh", "y"), 0, 0, tiled=True)
-    (result,) = call(last_kernel, [amplitudes.shape], [SMEM] * 3 + [VMEM] * 3)(
-        tiles, occupied, virtual, ladder, near, far
+    (parts,) = call(ladder_kernel, [(Y, 4 * BLOCK, LANES)], [VMEM] * 3)(
+        window, integrals, cycle.reshape(Y, ZH * BLOCK, LANES)
+    )
+    parts = lax.all_to_all(parts, "y", 0, 0, tiled=True)
+    near_cycle, far_cycle, near, far = call(sum_kernel, [(BLOCK, LANES)] * 4, [VMEM])(parts)
+    near_cycle = lax.ppermute(near_cycle, EVERY, places(near_rule))
+    far_cycle = lax.ppermute(far_cycle, EVERY, places(far_rule))
+    far = lax.ppermute(far, "zh", swap)
+    (result,) = call(last_kernel, [amplitudes.shape], [SMEM] * 3 + [VMEM] * 4)(
+        tiles, occupied, virtual, near, far, near_cycle, far_cycle
     )
     return result
 

time: 135 us -> 135 us (level)
  the two profiles are of different devices: /device:TPU:46 before, /device:TPU:129 now
where the time goes in v6:
time: 135 us; the launch traced here: 134 us
  blocking collectives  54 us (40%)
  starting transfers between devices  37.4 us (28%)
  waiting for transfers between devices  33.3 us (25%)
  Pallas kernels  5.74 us (4%)
  local copies, waits for them, and re-layouts  2.88 us (2%)
    all_to_all x1, blocking collectives, per_device(): parts = lax.all_to_all(parts, 'y', 0, 0, tiled=True)  44.2 us
    ppermute x1, waiting for transfers between devices, per_device(): far_cycle = lax.ppermute(far_cycle, EVERY, places(far_rule))  16.2 us
    all_to_all x1, starting transfers between devices, per_device(): lax.all_to_all(window.reshape(CHIPS, 2 * ROWS, LANES), ('zh', 'y'), 0, 0,...  12.7 us
    all_to_all x1, blocking collectives, per_device(): column = lax.all_to_all(copies, 'zl', 0, 0, tiled=True)  9.81 us
    all_to_all x1, waiting for transfers between devices, per_device(): lax.all_to_all(window.reshape(CHIPS, 2 * ROWS, LANES), ('zh', 'y'), 0, 0,...  8.1 us
    all_to_all x1, waiting for transfers between devices, per_device(): gathered = lax.all_to_all(copies, 'x', 0, 0, tiled=True)  8.09 us
    ppermute x1, starting transfers between devices, per_device(): near_cycle = lax.ppermute(near_cycle, EVERY, places(near_rule))  4.71 us
    all_to_all x1, starting transfers between devices, per_device(): gathered = lax.all_to_all(copies, 'x', 0, 0, tiled=True)  4.69 us
  transfers between devices with their start and end apart: 7, of which 4 were waited for; matrix products, arithmetic and copies ran while one was open for 1% of the time, Pallas kernels for 3%

profile of v6, /device:TPU:129, one launch (start us, length us, event | category | flops | bytes accessed | tf_op | source)
XLA Modules:
  0.0 134.1 jit_solution(15354039619228331435)
XLA Ops:
  0.0 0.0 copy-start.1
  0.0 0.0 copy-start.3
  0.0 0.9 copy-done.3
  0.9 0.0 copy-start.5
  0.9 9.8 %all_to_all.20 = f32[4,104,128]{2,1,0:T(8,128)S(1)} all-to-all(f32[4,104,128]{2,1,0:T(8,128)S(1)} %shard_map.64), channel_id=1, replica_groups=mesh['zl'=4,'x'=4,'core'=2,'zh'=2,'y'=8] {'zl'}, dimensions={0} | all-to-all | bytes 425984 | tf_op jit(solution)/shard_map/all_to_all | solution.py:196
  10.7 1.0 broadcast_in_dim.8
  11.7 4.7 %all-to-all-start.1 = ((f32[4,416,128]{2,1,0:T(8,128)}), f32[4,416,128]{2,1,0:T(8,128)S(1)}, u32[]{:S(2)}, u32[]{:S(2)}) async-start(f32[4,416,128]{2,1,0:T(8,128)} %broadcast_in_dim.8), calls=%async_computation.1 | async-start | bytes 1703936 | tf_op jit(solution)/shard_map/all_to_all | solution.py:198
  16.3 0.0 copy-done.1
  16.3 3.4 %collective-permute-start.1 = (f32[512,256]{1,0:T(8,128)S(1)}, f32[512,256]{1,0:T(8,128)}, u32[]{:S(2)}, u32[]{:S(2)}) collective-permute-start(f32[512,256]{1,0:T(8,128)S(1)} %copy-done.1), channel_id=1, source_target_pairs={{0,16},{16,0},{1,17},{17,1},{2,18},{18,2},{3,19},{19,3},{4,20},{20... | collective-permute-start | bytes 1572872 | tf_op jit(solution)/shard_map/ppermute | solution.py:194
  19.8 8.1 %all-to-all-done.1 = f32[4,416,128]{2,1,0:T(8,128)S(1)} async-done(((f32[4,416,128]{2,1,0:T(8,128)}), f32[4,416,128]{2,1,0:T(8,128)S(1)}, u32[]{:S(2)}, u32[]{:S(2)}) %all-to-all-start.1) | async-done | bytes 852000 | tf_op jit(solution)/shard_map/all_to_all | solution.py:198
  27.9 0.0 copy-done.5
  27.9 1.4 %shard_map.65 = f32[256,128]{1,0:T(8,128)S(1)} custom-call(s32[2]{0:T(128)S(1)} %copy-done.5, f32[1664,128]{1,0:T(8,128)S(1)} %bitcast.5), custom_call_target="tpu_custom_call" | custom-call | tf_op jit(solution)/shard_map/pallas_call | solution.py:201
  29.3 0.0 copy-start
  29.3 4.5 %collective-permute-start = (f32[256,128]{1,0:T(8,128)S(1)}, f32[256,128]{1,0:T(8,128)S(1)}, u32[]{:S(2)}, u32[]{:S(2)}) collective-permute-start(f32[256,128]{1,0:T(8,128)S(1)} %shard_map.65), channel_id=1, source_target_pairs={{0,16},{16,0},{1,17},{17,1},{2,18},{18,2},{3,19},{19,3},{4,20},{20... | collective-permute-start | bytes 393224 | tf_op jit(solution)/shard_map/ppermute | solution.py:207
  33.8 1.0 collective-permute-done
  34.7 0.7 add.3
  35.4 12.7 %all-to-all-start.2 = ((f32[16,16,128]{2,1,0:T(8,128)}), f32[16,16,128]{2,1,0:T(8,128)S(1)}, u32[]{:S(2)}, u32[]{:S(2)}) async-start(f32[16,16,128]{2,1,0:T(8,128)} %bitcast.2), calls=%async_computation.2 | async-start | bytes 262144 | tf_op jit(solution)/shard_map/all_to_all | solution.py:208
  48.1 0.0 collective-permute-done.1.other
  48.1 0.0 copy-start.2
  48.1 1.0 copy-done.2
  49.2 2.2 %shard_map.66 = f32[1664,128]{1,0:T(8,128)S(1)} custom-call(f32[1664,128]{1,0:T(8,128)S(1)} %bitcast.6, f32[512,256]{1,0:T(8,128)S(1)} %copy-done.2, f32[512,256]{1,0:T(8,128)} %collective-permute-done.1.other), custom_call_target="tpu_custom_call" | custom-call | tf_op jit(solution)/shard_map/pallas_call | solution.py:210
  51.3 8.1 %all-to-all-done.2.window = f32[16,16,128]{2,1,0:T(8,128)S(1)} async-done(((f32[16,16,128]{2,1,0:T(8,128)}), f32[16,16,128]{2,1,0:T(8,128)S(1)}, u32[]{:S(2)}, u32[]{:S(2)}) %all-to-all-start.2) | async-done | bytes 131104 | tf_op jit(solution)/shard_map/all_to_all | solution.py:208
  59.4 0.0 copy-done
  59.4 0.7 shard_map.67
  60.2 44.2 %all_to_all.21.received = f32[8,416,128]{2,1,0:T(8,128)S(1)} all-to-all(f32[8,416,128]{2,1,0:T(8,128)S(1)} %shard_map.67), channel_id=1, replica_groups=mesh['zl'=4,'x'=4,'core'=2,'zh'=2,'y'=8] {'y'}, dimensions={0} | all-to-all | bytes 3407872 | tf_op jit(solution)/shard_map/all_to_all | solution.py:215
  104.4 0.0 copy-start.4
  104.4 0.0 copy-start.6
  104.4 0.1 shard_map.68
  104.4 3.5 %collective-permute-start.2 = (f32[104,128]{1,0:T(8,128)S(1)}, f32[104,128]{1,0:T(8,128)S(1)}, u32[]{:S(2)}, u32[]{:S(2)}) collective-permute-start(f32[104,128]{1,0:T(8,128)S(1)} %get-tuple-element.10), channel_id=1, source_target_pairs={{0,8},{8,0},{1,9},{9,1},{2,10},{10,2},{3,11},{11,3},{4,12},{12,4},... | collective-permute-start | bytes 159752 | tf_op jit(solution)/shard_map/ppermute | solution.py:219
  107.9 4.7 %collective-permute-start.3 = (f32[104,128]{1,0:T(8,128)S(1)}, f32[104,128]{1,0:T(8,128)S(1)}, u32[]{:S(2)}, u32[]{:S(2)}) collective-permute-start(f32[104,128]{1,0:T(8,128)S(1)} %get-tuple-element.11), channel_id=1, source_target_pairs={{0,0},{1,256},{2,32},{3,288},{4,64},{5,320},{6,96},{7,352},{8,128}... | collective-permute-start | bytes 159752 | tf_op jit(solution)/shard_map/ppermute | solution.py:217
  112.6 4.0 %collective-permute-start.4 = (f32[104,128]{1,0:T(8,128)S(1)}, f32[104,128]{1,0:T(8,128)S(1)}, u32[]{:S(2)}, u32[]{:S(2)}) collective-permute-start(f32[104,128]{1,0:T(8,128)S(1)} %get-tuple-element.12), channel_id=1, source_target_pairs={{0,128},{1,384},{2,160},{3,416},{4,192},{5,448},{6,224},{7,480},{8... | collective-permute-start | bytes 159752 | tf_op jit(solution)/shard_map/ppermute | solution.py:218
  116.6 0.0 collective-permute-done.2.far
  116.7 0.0 collective-permute-done.3.near_cycle
  116.7 16.2 %collective-permute-done.4.far_cycle = f32[104,128]{1,0:T(8,128)S(1)} collective-permute-done((f32[104,128]{1,0:T(8,128)S(1)}, f32[104,128]{1,0:T(8,128)S(1)}, u32[]{:S(2)}, u32[]{:S(2)}) %collective-permute-start.4) | collective-permute-done | bytes 53280 | tf_op jit(solution)/shard_map/ppermute | solution.py:218
  132.8 0.0 copy-done.4
  132.8 0.0 copy-done.6
  132.8 1.3 shard_map.69
  (1 shorter events, 0.0 us)
Async XLA Ops:
  0.0 16.3 %copy-start.1 = (f32[512,256]{1,0:T(8,128)S(1)}, f32[512,256]{1,0:T(8,128)}, u32[]{:S(2)}) copy-start(f32[512,256]{1,0:T(8,128)} %own.1) | copy-start | bytes 1572868
  0.0 0.9 copy-start.3
  0.9 27.0 %copy-start.5 = (s32[2]{0:T(128)S(1)}, s32[2]{0:T(128)}, u32[]{:S(2)}) copy-start(s32[2]{0:T(128)} %tiles.3) | copy-start | bytes 28
  11.7 16.2 %all-to-all-start.1 = ((f32[4,416,128]{2,1,0:T(8,128)}), f32[4,416,128]{2,1,0:T(8,128)S(1)}, u32[]{:S(2)}, u32[]{:S(2)}) async-start(f32[4,416,128]{2,1,0:T(8,128)} %broadcast_in_dim.8), calls=%async_computation.1 | async-start | bytes 1703936 | tf_op jit(solution)/shard_map/all_to_all | solution.py:198
  16.3 31.8 %collective-permute-start.1 = (f32[512,256]{1,0:T(8,128)S(1)}, f32[512,256]{1,0:T(8,128)}, u32[]{:S(2)}, u32[]{:S(2)}) collective-permute-start(f32[512,256]{1,0:T(8,128)S(1)} %copy-done.1), channel_id=1, source_target_pairs={{0,16},{16,0},{1,17},{17,1},{2,18},{18,2},{3,19},{19,3},{4,20},{20... | collective-permute-start | bytes 1572872 | tf_op jit(solution)/shard_map/ppermute | solution.py:194
  29.3 30.2 %copy-start = (f32[4,64,1664]{2,1,0:T(8,128)S(1)}, f32[4,64,1664]{2,1,0:T(8,128)}, u32[]{:S(2)}) copy-start(f32[4,64,1664]{2,1,0:T(8,128)} %param.8) | copy-start | bytes 5111812
  29.3 5.4 %collective-permute-start = (f32[256,128]{1,0:T(8,128)S(1)}, f32[256,128]{1,0:T(8,128)S(1)}, u32[]{:S(2)}, u32[]{:S(2)}) collective-permute-start(f32[256,128]{1,0:T(8,128)S(1)} %shard_map.65), channel_id=1, source_target_pairs={{0,16},{16,0},{1,17},{17,1},{2,18},{18,2},{3,19},{19,3},{4,20},{20... | collective-permute-start | bytes 393224 | tf_op jit(solution)/shard_map/ppermute | solution.py:207
  35.4 24.0 %all-to-all-start.2 = ((f32[16,16,128]{2,1,0:T(8,128)}), f32[16,16,128]{2,1,0:T(8,128)S(1)}, u32[]{:S(2)}, u32[]{:S(2)}) async-start(f32[16,16,128]{2,1,0:T(8,128)} %bitcast.2), calls=%async_computation.2 | async-start | bytes 262144 | tf_op jit(solution)/shard_map/all_to_all | solution.py:208
  48.1 1.0 copy-start.2
  104.4 28.5 %copy-start.4 = (f32[832]{0:T(1024)S(1)}, f32[832]{0:T(1024)}, u32[]{:S(2)}) copy-start(f32[832]{0:T(1024)} %virtual.1) | copy-start | bytes 9988
  104.4 28.5 %copy-start.6 = (f32[128]{0:T(128)S(1)}, f32[128]{0:T(128)}, u32[]{:S(2)}) copy-start(f32[128]{0:T(128)} %occupied.1) | copy-start | bytes 1540
  104.4 12.2 %collective-permute-start.2 = (f32[104,128]{1,0:T(8,128)S(1)}, f32[104,128]{1,0:T(8,128)S(1)}, u32[]{:S(2)}, u32[]{:S(2)}) collective-permute-start(f32[104,128]{1,0:T(8,128)S(1)} %get-tuple-element.10), channel_id=1, source_target_pairs={{0,8},{8,0},{1,9},{9,1},{2,10},{10,2},{3,11},{11,3},{4,12},{12,4},... | collective-permute-start | bytes 159752 | tf_op jit(solution)/shard_map/ppermute | solution.py:219
  107.9 8.7 %collective-permute-start.3 = (f32[104,128]{1,0:T(8,128)S(1)}, f32[104,128]{1,0:T(8,128)S(1)}, u32[]{:S(2)}, u32[]{:S(2)}) collective-permute-start(f32[104,128]{1,0:T(8,128)S(1)} %get-tuple-element.11), channel_id=1, source_target_pairs={{0,0},{1,256},{2,32},{3,288},{4,64},{5,320},{6,96},{7,352},{8,128}... | collective-permute-start | bytes 159752 | tf_op jit(solution)/shard_map/ppermute | solution.py:217
  112.6 20.2 %collective-permute-start.4 = (f32[104,128]{1,0:T(8,128)S(1)}, f32[104,128]{1,0:T(8,128)S(1)}, u32[]{:S(2)}, u32[]{:S(2)}) collective-permute-start(f32[104,128]{1,0:T(8,128)S(1)} %get-tuple-element.12), channel_id=1, source_target_pairs={{0,128},{1,384},{2,160},{3,416},{4,192},{5,448},{6,224},{7,480},{8... | collective-permute-start | bytes 159752 | tf_op jit(solution)/shard_map/ppermute | solution.py:218

commit v7 on v5

v7 whole, which is shorter than its diff:
```python
import functools

import jax
import jax.numpy as jnp
from jax import lax
from jax.experimental import pallas as pl
from jax.experimental.pallas import tpu as pltpu
from jax.sharding import Mesh
from jax.sharding import PartitionSpec as P

ZL, X, CORE, ZH, Y = 4, 4, 2, 2, 8
CHIPS = ZL * X
ROWS = 8
TILE = 64
PAIRS = 13
LANES = 2 * TILE
BLOCK = PAIRS * ROWS
SIDE = (PAIRS + 1) // 2
SKIP = PAIRS - SIDE
HALF = ROWS // ZH
PIECE = PAIRS * HALF
EVERY = ("zl", "x", "core", "zh", "y")
VMEM = pl.BlockSpec(memory_space=pltpu.VMEM)
SMEM = pl.BlockSpec(memory_space=pltpu.SMEM)
PARAMS = pltpu.CompilerParams(vmem_limit_bytes=32 * 1024 * 1024)


def split(value):
    high = value.astype(jnp.bfloat16)
    return high, (value - high.astype(jnp.float32)).astype(jnp.bfloat16)


def product(left, right):
    dot = functools.partial(jnp.dot, preferred_element_type=jnp.float32)
    return dot(left[0], right[1]) + dot(left[1], right[0]) + dot(left[0], right[0])


def low_half(shape):
    return lax.broadcasted_iota(jnp.int32, shape, 1) < TILE


def pair_up(first, second):
    low = low_half(first.shape)
    return (
        jnp.where(low, first, pltpu.roll(second, TILE, 1)),
        jnp.where(low, pltpu.roll(first, TILE, 1), second),
    )


def pack_kernel(amplitudes, out):
    for pair in range(PAIRS):
        tile = amplitudes[0, :, pair * LANES : (pair + 1) * LANES]
        for chip in range(ZH * ZL):
            out[chip, pair * ROWS : (pair + 1) * ROWS, :] = tile


def window_kernel(tiles, gathered, out, window, columns, turned):
    core, first = lax.axis_index("core"), lax.axis_index("zh") == 0
    for pair in range(TILE // 2):
        place = tiles[1] * (TILE // 2) + pair
        owner = place // PAIRS
        chip = owner // CORE
        for zh in range(ZH):
            block = (chip % X * ZH + zh) * ZL + chip // X
            row = (block * PAIRS + (place - owner * PAIRS)) * ROWS
            tile = gathered[pl.ds(pl.multiple_of(row, ROWS), ROWS), :]
            start = (zh * (TILE // 2) + pair) * ROWS
            window[start : start + ROWS, :] = jnp.where(owner % CORE == core, tile, 0.0)
    for zh in range(ZH):
        for half in range(ROWS // 2):
            for inner in range(2):
                start = zh * (TILE // 2) * ROWS + half * 2 + inner
                both = window[pl.ds(start, TILE // 2, stride=ROWS), :]
                columns[pl.ds(inner * TILE, TILE // 2, stride=2), :] = both
                columns[pl.ds(inner * TILE + 1, TILE // 2, stride=2), :] = pltpu.roll(both, TILE, 1)
            turned[...] = jnp.transpose(columns[...])
            for part in range(2):
                even = turned[pl.ds(2 * part, CHIPS, stride=4), :]
                odd = turned[pl.ds(2 * part + 1, CHIPS, stride=4), :]
                for inner, value in enumerate(pair_up(even, odd)):
                    row = (zh * 2 + part) * ROWS + half * 2 + inner
                    mine = jnp.where(first, value[:Y], value[Y:])
                    out[pl.ds(row, Y, stride=4 * ROWS), :] = mine


def cycle_kernel(gathered, own, first, second, out, ordered):
    core, zh = lax.axis_index("core"), lax.axis_index("zh")
    span = ZL * BLOCK
    for x in range(X):
        for half in range(ZH):
            ordered[half, x * span : (x + 1) * span, :] = gathered[pl.ds((x * ZH + half) * span, span), :]
    chunks = ([], [])
    for half in range(ZH):
        for k in range(0, ROWS, 2):
            even = ordered[half, pl.ds(k, CHIPS * PAIRS, stride=ROWS), :]
            odd = ordered[half, pl.ds(k + 1, CHIPS * PAIRS, stride=ROWS), :]
            for chunk, value in zip(chunks, pair_up(even, odd)):
                chunk.append(value)
    left = split(jnp.concatenate([jnp.concatenate(chunk, 1) for chunk in chunks], 0))
    same = core == zh
    near = jnp.where(same, own[...], first[...])
    far = jnp.where(same, first[...], second[...])
    right = jnp.concatenate([jnp.where(zh == 0, near, far), jnp.where(zh == 0, far, near)], 0)
    result = product(left, split(right))
    for quarter in range(2):
        both = result[:, quarter * LANES : (quarter + 1) * LANES]
        rows = pair_up(both[: CHIPS * PAIRS], both[CHIPS * PAIRS :])
        for inner, value in enumerate(rows):
            out[pl.ds(quarter * 2 + inner, CHIPS * PAIRS, stride=HALF), :] = value


def join_kernel(cycle, own, other, out):
    for y in range(Y):
        out[y, :BLOCK, :] = cycle[y, :, :]
        for slot in range(2):
            start = BLOCK + slot * 4 * ROWS
            out[y, start : start + 4 * ROWS, :] = own[y ^ slot, :, :] + other[y ^ slot, :, :]


def sum_kernel(received, near, far):
    total = received[0, :BLOCK, :]
    for place in range(1, Y):
        total = total + received[place, :BLOCK, :]
    first = lax.axis_index("zh") == 0
    near[...] = jnp.where(first, total[:PIECE], total[PIECE:])
    far[...] = jnp.where(first, total[PIECE:], total[:PIECE])


def ladder_kernel(received, own, other, out):
    lefts = []
    for slot in range(2):
        for part in range(2):
            halves = []
            for zh in range(ZH):
                start = BLOCK + ((slot * ZH + zh) * 2 + part) * ROWS
                halves.append(received[:, start : start + ROWS, :].reshape(Y * ROWS, LANES))
            lefts.append(jnp.concatenate(halves, 0))
    left = split(jnp.concatenate(lefts, 1))
    first = lax.axis_index("y") % 2 * (SKIP * LANES)
    width = SIDE * LANES
    for start in range(0, width, 2 * LANES):
        stop = min(start + 2 * LANES, width)
        columns = pl.ds(pl.multiple_of(first + start, LANES), stop - start)
        right = jnp.concatenate([own[:, columns], other[:, start:stop]], 0)
        result = product(left, split(right))
        for column in range(start, stop, LANES):
            value = result[:, column - start : column - start + LANES]
            rows = pl.ds(column // LANES * ROWS, ROWS)
            out[:, rows, :] = value.reshape(CHIPS, ROWS, LANES)


def last_kernel(tiles, occupied, virtual, ladder, near, far, out):
    column = lax.axis_index("zl") * (X * CORE) + lax.axis_index("x") * CORE + lax.axis_index("core")
    row = lax.axis_index("zh") * Y + lax.axis_index("y")
    shape = (ROWS, LANES)
    lane = lax.broadcasted_iota(jnp.int32, shape, 1)
    line = lax.broadcasted_iota(jnp.int32, shape, 0)
    spectator = jnp.zeros(shape, jnp.float32)
    for b in range(TILE):
        spectator = jnp.where(lane % TILE == b, virtual[tiles[0] * TILE + b], spectator)
    rows = jnp.zeros(shape, jnp.float32)
    for j in range(ROWS):
        rows = jnp.where(line == j, occupied[row * ROWS + j], rows)
    straight = lax.axis_index("zl") % 2 == 0
    for pair in range(PAIRS):
        piece = pl.ds(pair * HALF, HALF)
        one, two = near[piece, :], far[piece, :]
        low, high = jnp.where(straight, one, two), jnp.where(straight, two, one)
        total = jnp.concatenate([low, high], 0)
        side = int(pair >= SIDE)
        rows_of_side = pl.ds((pair - side * SKIP) * ROWS, ROWS)
        for place in range(side, ZH * Y, 2):
            total = total + ladder[place, rows_of_side, :]
        a = column * (2 * PAIRS) + 2 * pair
        energy = jnp.where(lane < TILE, virtual[a], virtual[a + 1]) + spectator
        out[0, :, pair * LANES : (pair + 1) * LANES] = total / (energy - occupied[0] - rows)


def call(kernel, shapes, specs, scratch=()):
    return pl.pallas_call(
        kernel,
        out_shape=[jax.ShapeDtypeStruct(shape, jnp.float32) for shape in shapes],
        in_specs=specs,
        out_specs=[VMEM] * len(shapes),
        scratch_shapes=[pltpu.VMEM(shape, jnp.float32) for shape in scratch],
        compiler_params=PARAMS,
    )


def places(rule):
    pairs = []
    for chip in range(CHIPS):
        for core in range(CORE):
            for place in range(ZH * Y):
                to = rule(chip, core, place)
                pairs.append(
                    (
                        (chip * CORE + core) * ZH * Y + place,
                        (to[0] * CORE + to[1]) * ZH * Y + to[2],
                    )
                )
    return pairs


def chip_of(block):
    return block % ZL * X + block // ZL


def near_rule(chip, core, place):
    zh, y = divmod(place, Y)
    return chip_of(2 * y + zh), core, chip


def far_rule(chip, core, place):
    zh, y = divmod(place, Y)
    return chip_of(2 * y + 1 - zh), core, chip


def per_device(amplitudes, cycle_block, ladder_block, occupied, virtual, tiles):
    first = lax.ppermute(cycle_block, ("core", "zh"), [(0, 2), (3, 1), (2, 3), (1, 0)])
    second = lax.ppermute(first, ("core", "zh"), [(0, 2), (3, 1)])
    integrals = ladder_block.reshape(-1, ladder_block.shape[2])
    start = (1 - lax.axis_index("y") % 2) * (SKIP * LANES)
    side = lax.dynamic_slice_in_dim(integrals, start, SIDE * LANES, 1)
    side = lax.ppermute(side, "y", [(y, y ^ 1) for y in range(Y)])

    (copies,) = call(pack_kernel, [(ZH * ZL, BLOCK, LANES)], [VMEM])(amplitudes)
    column = lax.all_to_all(copies, ("zh", "zl"), 0, 0, tiled=True)
    span = ZH * ZL * BLOCK
    copies = jnp.broadcast_to(column.reshape(1, span, LANES), (X, span, LANES))
    gathered = lax.all_to_all(copies, "x", 0, 0, tiled=True)
    gathered = gathered.reshape(X * span, LANES)
    gathered, side = lax.optimization_barrier((gathered, side))

    (window,) = call(
        window_kernel,
        [(Y * 4 * ROWS, LANES)],
        [SMEM, VMEM],
        [(ZH * TILE // 2 * ROWS, LANES), (LANES, LANES), (LANES, LANES)],
    )(tiles, gathered)
    window = window.reshape(Y, 4 * ROWS, LANES)
    other_window = lax.ppermute(window, "core", [(0, 1), (1, 0)])
    (cycle,) = call(
        cycle_kernel, [(CHIPS * PIECE, LANES)], [VMEM] * 4, [(ZH, CHIPS * BLOCK, LANES)]
    )(gathered, cycle_block, first, second)
    (joined,) = call(join_kernel, [(Y, BLOCK + 8 * ROWS, LANES)], [VMEM] * 3)(
        cycle.reshape(Y, BLOCK, LANES), window, other_window
    )
    received = lax.all_to_all(joined, "y", 0, 0, tiled=True)
    (ladder,) = call(ladder_kernel, [(CHIPS, SIDE * ROWS, LANES)], [VMEM] * 3)(
        received, integrals, side
    )
    ladder, received = lax.optimization_barrier((ladder, received))
    near, far = call(sum_kernel, [(PIECE, LANES)] * 2, [VMEM])(received)
    near = lax.ppermute(near, EVERY, places(near_rule))
    far = lax.ppermute(far, EVERY, places(far_rule))
    ladder = lax.all_to_all(ladder, ("zh", "y"), 0, 0, tiled=True)
    (result,) = call(last_kernel, [amplitudes.shape], [SMEM] * 3 + [VMEM] * 3)(
        tiles, occupied, virtual, ladder, near, far
    )
    return result


def solution(mesh):
    parts = Mesh(mesh.devices.reshape(ZL, X, CORE, ZH, Y), EVERY)
    amp, intg = ("zl", "x", "core"), ("zh", "y")
    return jax.shard_map(
        per_device,
        mesh=parts,
        in_specs=(P(None, intg, amp), P(intg, amp), P(intg, None, amp), P(), P(), P()),
        out_specs=P(None, intg, amp),
        check_vma=False,
    )
```

time: 137 us -> 125 us (0.912)
  the two profiles are of different devices: /device:TPU:68 before, /device:TPU:28 now
where the time goes in v7:
time: 125 us; the launch traced here: 124 us
  blocking collectives  51.2 us (41%)
  starting transfers between devices  33 us (26%)
  waiting for transfers between devices  29.4 us (24%)
  Pallas kernels  7.32 us (6%)
  local copies, waits for them, and re-layouts  3.17 us (3%)
    all_to_all x1, blocking collectives, per_device(): received = lax.all_to_all(joined, 'y', 0, 0, tiled=True)  25.7 us
    all_to_all x1, blocking collectives, per_device(): column = lax.all_to_all(copies, ('zh', 'zl'), 0, 0, tiled=True)  25.5 us
    ppermute x1, waiting for transfers between devices, per_device(): lax.ppermute(cycle_block, ('core', 'zh'), [(0, 2), (3, 1), (2, 3), (1, 0)])  18.4 us
    ppermute x1, starting transfers between devices, per_device(): far = lax.ppermute(far, EVERY, places(far_rule))  10.9 us
    all_to_all x1, starting transfers between devices, per_device(): ladder = lax.all_to_all(ladder, ('zh', 'y'), 0, 0, tiled=True)  6.84 us
    ppermute x1, waiting for transfers between devices, per_device(): far = lax.ppermute(far, EVERY, places(far_rule))  5.6 us
    ppermute x1, waiting for transfers between devices, per_device(): near = lax.ppermute(near, EVERY, places(near_rule))  5.36 us
    all_to_all x1, starting transfers between devices, per_device(): gathered = lax.all_to_all(copies, 'x', 0, 0, tiled=True)  4.93 us
  transfers between devices with their start and end apart: 8, of which 3 were waited for; matrix products, arithmetic and copies ran while one was open for 0% of the time, Pallas kernels for 4%

profile of v7, /device:TPU:28, one launch (start us, length us, event | category | flops | bytes accessed | tf_op | source)
XLA Modules:
  0.0 124.2 jit_solution(130746422703544050)
XLA Ops:
  0.0 0.0 copy-start.5
  0.0 0.8 copy-done.5
  0.8 25.5 %all_to_all.20 = f32[8,104,128]{2,1,0:T(8,128)S(1)} all-to-all(f32[8,104,128]{2,1,0:T(8,128)S(1)} %shard_map.64), channel_id=1, replica_groups=mesh['zl'=4,'x'=4,'core'=2,'zh'=2,'y'=8] {'zh','zl'}, dimensions={0} | all-to-all | bytes 851968 | tf_op jit(solution)/shard_map/all_to_all | solution.py:228
  26.3 1.3 %broadcast_in_dim.8 = f32[4,832,128]{2,1,0:T(8,128)} broadcast(f32[832,128]{1,0:T(8,128)S(1)} %bitcast.12), dimensions={1,2} | broadcast | bytes 2129920 | tf_op jit(solution)/shard_map/broadcast_in_dim | solution.py:230
  27.7 0.0 copy-start
  27.7 4.9 %all-to-all-start.1 = ((f32[4,832,128]{2,1,0:T(8,128)}), f32[4,832,128]{2,1,0:T(8,128)S(1)}, u32[]{:S(2)}, u32[]{:S(2)}) async-start(f32[4,832,128]{2,1,0:T(8,128)} %broadcast_in_dim.8), calls=%async_computation.1 | async-start | bytes 3407872 | tf_op jit(solution)/shard_map/all_to_all | solution.py:231
  32.6 0.0 copy-start.7
  32.6 0.0 copy-start.3
  32.6 0.0 copy-done
  32.6 0.1 constant_dynamic-slice_fusion
  32.7 2.5 %collective-permute-start = (f32[256,896]{1,0:T(8,128)S(1)}, f32[256,896]{1,0:T(8,128)S(1)}, u32[]{:S(2)}, u32[]{:S(2)}) collective-permute-start(f32[256,896]{1,0:T(8,128)S(1)} %constant_dynamic-slice_fusion), channel_id=1, source_target_pairs={{0,1},{1,0},{2,3},{3,2},{4,5},{5,4},{6,7},{7,6},{8,9},{9,8},{10,11... | collective-permute-start | bytes 2752520 | tf_op jit(solution)/shard_map/ppermute | solution.py:225
  35.2 0.0 copy-done.3
  35.2 1.9 %collective-permute-start.1 = (f32[512,256]{1,0:T(8,128)S(1)}, f32[512,256]{1,0:T(8,128)}, u32[]{:S(2)}, u32[]{:S(2)}) collective-permute-start(f32[512,256]{1,0:T(8,128)S(1)} %copy-done.3), channel_id=1, source_target_pairs={{0,16},{24,8},{16,24},{8,0},{1,17},{25,9},{17,25},{9,1},{2,18},{26... | collective-permute-start | bytes 1572872 | tf_op jit(solution)/shard_map/ppermute | solution.py:220
  37.1 18.4 %collective-permute-done.1.first = f32[512,256]{1,0:T(8,128)} collective-permute-done((f32[512,256]{1,0:T(8,128)S(1)}, f32[512,256]{1,0:T(8,128)}, u32[]{:S(2)}, u32[]{:S(2)}) %collective-permute-start.1) | collective-permute-done | bytes 524320 | tf_op jit(solution)/shard_map/ppermute | solution.py:220
  55.5 2.1 %collective-permute-start.2 = (f32[512,256]{1,0:T(8,128)}, f32[512,256]{1,0:T(8,128)}, u32[]{:S(2)}, u32[]{:S(2)}) collective-permute-start(f32[512,256]{1,0:T(8,128)} %collective-permute-done.1.first), channel_id=1, source_target_pairs={{0,16},{24,8},{1,17},{25,9},{2,18},{26,10},{3,19},{27,11},{4,20},{... | collective-permute-start | bytes 1572872 | tf_op jit(solution)/shard_map/ppermute | solution.py:221
  57.6 0.0 collective-permute-done.other
  57.6 0.0 copy-start.1
  57.6 0.9 copy-done.1
  58.6 0.0 all-to-all-done.1
  58.6 0.0 copy-start.4
  58.6 0.0 copy-done.7
  58.6 1.8 %shard_map.66 = f32[256,128]{1,0:T(8,128)S(1)} custom-call(s32[2]{0:T(128)S(1)} %copy-done.7, f32[3328,128]{1,0:T(8,128)S(1)} %bitcast.5), custom_call_target="tpu_custom_call" | custom-call | tf_op jit(solution)/shard_map/pallas_call | solution.py:235
  60.4 1.9 %collective-permute-start.3 = (f32[8,32,128]{2,1,0:T(8,128)S(1)}, f32[8,32,128]{2,1,0:T(8,128)S(1)}, u32[]{:S(2)}, u32[]{:S(2)}) collective-permute-start(f32[8,32,128]{2,1,0:T(8,128)S(1)} %bitcast.10), channel_id=1, source_target_pairs={{0,16},{16,0},{1,17},{17,1},{2,18},{18,2},{3,19},{19,3},{4,20},{20... | collective-permute-start | bytes 393224 | tf_op jit(solution)/shard_map/ppermute | solution.py:242
  62.3 0.0 collective-permute-done.2.second
  62.3 0.0 copy-done.4
  62.4 2.6 %shard_map.65 = f32[832,128]{1,0:T(8,128)S(1)} custom-call(f32[3328,128]{1,0:T(8,128)S(1)} %bitcast.6, f32[512,256]{1,0:T(8,128)S(1)} %copy-done.4, f32[512,256]{1,0:T(8,128)} %collective-permute-done.1.first, f32[512,256]{1,0:T(8,128)} %collective-permute-done.2.second), custom_call_target="tpu_custom_call" | custom-call | tf_op jit(solution)/shard_map/pallas_call | solution.py:243
  65.0 0.0 copy-start.2
  65.0 0.0 collective-permute-done.3.other
  65.1 25.7 %all_to_all.21.received = f32[8,168,128]{2,1,0:T(8,128)S(1)} all-to-all(f32[8,168,128]{2,1,0:T(8,128)S(1)} %shard_map.67), channel_id=1, replica_groups=mesh['zl'=4,'x'=4,'core'=2,'zh'=2,'y'=8] {'y'}, dimensions={0} | all-to-all | bytes 1376256 | tf_op jit(solution)/shard_map/all_to_all | solution.py:249
  90.7 0.0 copy-done.2
  90.7 0.0 copy-start.6
  90.7 0.0 copy-start.8
  90.7 1.5 %shard_map.68 = f32[16,56,128]{2,1,0:T(8,128)} custom-call(f32[8,168,128]{2,1,0:T(8,128)S(1)} %all_to_all.21.received, f32[256,1664]{1,0:T(8,128)S(1)} %bitcast.8, f32[256,896]{1,0:T(8,128)S(1)} %copy-done.2), custom_call_target="tpu_custom_call" | custom-call | tf_op jit(solution)/shard_map/pallas_call | solution.py:250
  92.2 6.8 %all-to-all-start.3 = ((f32[16,56,128]{2,1,0:T(8,128)}), f32[16,56,128]{2,1,0:T(8,128)S(1)}, u32[]{:S(2)}, u32[]{:S(2)}) async-start(f32[16,56,128]{2,1,0:T(8,128)} %shard_map.68), calls=%async_computation.3 | async-start | bytes 917504 | tf_op jit(solution)/shard_map/all_to_all | solution.py:257
  99.1 1.9 %collective-permute-start.4 = (f32[52,128]{1,0:T(8,128)S(1)}, f32[52,128]{1,0:T(8,128)S(1)}, u32[]{:S(2)}, u32[]{:S(2)}) collective-permute-start(f32[52,128]{1,0:T(8,128)S(1)} %get-tuple-element.15), channel_id=1, source_target_pairs={{0,0},{1,256},{2,32},{3,288},{4,64},{5,320},{6,96},{7,352},{8,128}... | collective-permute-start | bytes 79880 | tf_op jit(solution)/shard_map/ppermute | solution.py:255
  101.0 10.9 %collective-permute-start.5 = (f32[52,128]{1,0:T(8,128)S(1)}, f32[52,128]{1,0:T(8,128)S(1)}, u32[]{:S(2)}, u32[]{:S(2)}) collective-permute-start(f32[52,128]{1,0:T(8,128)S(1)} %get-tuple-element.16), channel_id=1, source_target_pairs={{0,128},{1,384},{2,160},{3,416},{4,192},{5,448},{6,224},{7,480},{8... | collective-permute-start | bytes 79880 | tf_op jit(solution)/shard_map/ppermute | solution.py:256
  111.9 5.4 %collective-permute-done.4.near = f32[52,128]{1,0:T(8,128)S(1)} collective-permute-done((f32[52,128]{1,0:T(8,128)S(1)}, f32[52,128]{1,0:T(8,128)S(1)}, u32[]{:S(2)}, u32[]{:S(2)}) %collective-permute-start.4) | collective-permute-done | bytes 26656 | tf_op jit(solution)/shard_map/ppermute | solution.py:255
  117.3 5.6 %collective-permute-done.5.far = f32[52,128]{1,0:T(8,128)S(1)} collective-permute-done((f32[52,128]{1,0:T(8,128)S(1)}, f32[52,128]{1,0:T(8,128)S(1)}, u32[]{:S(2)}, u32[]{:S(2)}) %collective-permute-start.5) | collective-permute-done | bytes 26656 | tf_op jit(solution)/shard_map/ppermute | solution.py:256
  122.9 0.0 all-to-all-done.3.ladder
  122.9 0.0 copy-done.6
  122.9 0.0 copy-done.8
  122.9 1.3 %shard_map.70 = f32[1,8,1664]{2,1,0:T(8,128)} custom-call(s32[2]{0:T(128)S(1)} %copy-done.7, f32[128]{0:T(128)S(1)} %copy-done.8, f32[832]{0:T(1024)S(1)} %copy-done.6, f32[16,56,128]{2,1,0:T(8,128)S(1)} %all-to-all-done.3.ladder, f32[52,128]{1,0:T(8,128)S(1)} %collective-permute-done.4.near, f32[52,128]{1,0:T(8,128)S(1)} %collective-permute-done.5.far), custom_call_target="tpu_custom_call" | custom-call | tf_op jit(solution)/shard_map/pallas_call | solution.py:258
  (3 shorter events, 0.1 us)
Async XLA Ops:
  0.0 0.8 copy-start.5
  27.7 4.9 %copy-start = (f32[4,64,1664]{2,1,0:T(8,128)S(1)}, f32[4,64,1664]{2,1,0:T(8,128)}, u32[]{:S(2)}) copy-start(f32[4,64,1664]{2,1,0:T(8,128)} %param.8) | copy-start | bytes 5111812
  27.7 30.9 %all-to-all-start.1 = ((f32[4,832,128]{2,1,0:T(8,128)}), f32[4,832,128]{2,1,0:T(8,128)S(1)}, u32[]{:S(2)}, u32[]{:S(2)}) async-start(f32[4,832,128]{2,1,0:T(8,128)} %broadcast_in_dim.8), calls=%async_computation.1 | async-start | bytes 3407872 | tf_op jit(solution)/shard_map/all_to_all | solution.py:231
  32.6 26.0 %copy-start.7 = (s32[2]{0:T(128)S(1)}, s32[2]{0:T(128)}, u32[]{:S(2)}) copy-start(s32[2]{0:T(128)} %tiles.3) | copy-start | bytes 28
  32.6 2.6 %copy-start.3 = (f32[512,256]{1,0:T(8,128)S(1)}, f32[512,256]{1,0:T(8,128)}, u32[]{:S(2)}) copy-start(f32[512,256]{1,0:T(8,128)} %own.1) | copy-start | bytes 1572868
  32.7 24.9 %collective-permute-start = (f32[256,896]{1,0:T(8,128)S(1)}, f32[256,896]{1,0:T(8,128)S(1)}, u32[]{:S(2)}, u32[]{:S(2)}) collective-permute-start(f32[256,896]{1,0:T(8,128)S(1)} %constant_dynamic-slice_fusion), channel_id=1, source_target_pairs={{0,1},{1,0},{2,3},{3,2},{4,5},{5,4},{6,7},{7,6},{8,9},{9,8},{10,11... | collective-permute-start | bytes 2752520 | tf_op jit(solution)/shard_map/ppermute | solution.py:225
  35.2 20.4 %collective-permute-start.1 = (f32[512,256]{1,0:T(8,128)S(1)}, f32[512,256]{1,0:T(8,128)}, u32[]{:S(2)}, u32[]{:S(2)}) collective-permute-start(f32[512,256]{1,0:T(8,128)S(1)} %copy-done.3), channel_id=1, source_target_pairs={{0,16},{24,8},{16,24},{8,0},{1,17},{25,9},{17,25},{9,1},{2,18},{26... | collective-permute-start | bytes 1572872 | tf_op jit(solution)/shard_map/ppermute | solution.py:220
  55.5 6.8 %collective-permute-start.2 = (f32[512,256]{1,0:T(8,128)}, f32[512,256]{1,0:T(8,128)}, u32[]{:S(2)}, u32[]{:S(2)}) collective-permute-start(f32[512,256]{1,0:T(8,128)} %collective-permute-done.1.first), channel_id=1, source_target_pairs={{0,16},{24,8},{1,17},{25,9},{2,18},{26,10},{3,19},{27,11},{4,20},{... | collective-permute-start | bytes 1572872 | tf_op jit(solution)/shard_map/ppermute | solution.py:221
  57.6 0.9 copy-start.1
  58.6 3.8 %copy-start.4 = (f32[512,256]{1,0:T(8,128)S(1)}, f32[512,256]{1,0:T(8,128)}, u32[]{:S(2)}) copy-start(f32[512,256]{1,0:T(8,128)} %own.1) | copy-start | bytes 1572868
  60.4 4.6 %collective-permute-start.3 = (f32[8,32,128]{2,1,0:T(8,128)S(1)}, f32[8,32,128]{2,1,0:T(8,128)S(1)}, u32[]{:S(2)}, u32[]{:S(2)}) collective-permute-start(f32[8,32,128]{2,1,0:T(8,128)S(1)} %bitcast.10), channel_id=1, source_target_pairs={{0,16},{16,0},{1,17},{17,1},{2,18},{18,2},{3,19},{19,3},{4,20},{20... | collective-permute-start | bytes 393224 | tf_op jit(solution)/shard_map/ppermute | solution.py:242
  65.0 25.8 %copy-start.2 = (f32[256,896]{1,0:T(8,128)S(1)}, f32[256,896]{1,0:T(8,128)}, u32[]{:S(2)}) copy-start(f32[256,896]{1,0:T(8,128)} %copy-done.1) | copy-start | bytes 2752516
  90.7 32.1 %copy-start.6 = (f32[832]{0:T(1024)S(1)}, f32[832]{0:T(1024)}, u32[]{:S(2)}) copy-start(f32[832]{0:T(1024)} %virtual.1) | copy-start | bytes 9988
  90.7 32.1 %copy-start.8 = (f32[128]{0:T(128)S(1)}, f32[128]{0:T(128)}, u32[]{:S(2)}) copy-start(f32[128]{0:T(128)} %occupied.1) | copy-start | bytes 1540
  92.2 30.7 %all-to-all-start.3 = ((f32[16,56,128]{2,1,0:T(8,128)}), f32[16,56,128]{2,1,0:T(8,128)S(1)}, u32[]{:S(2)}, u32[]{:S(2)}) async-start(f32[16,56,128]{2,1,0:T(8,128)} %shard_map.68), calls=%async_computation.3 | async-start | bytes 917504 | tf_op jit(solution)/shard_map/all_to_all | solution.py:257
  99.1 18.2 %collective-permute-start.4 = (f32[52,128]{1,0:T(8,128)S(1)}, f32[52,128]{1,0:T(8,128)S(1)}, u32[]{:S(2)}, u32[]{:S(2)}) collective-permute-start(f32[52,128]{1,0:T(8,128)S(1)} %get-tuple-element.15), channel_id=1, source_target_pairs={{0,0},{1,256},{2,32},{3,288},{4,64},{5,320},{6,96},{7,352},{8,128}... | collective-permute-start | bytes 79880 | tf_op jit(solution)/shard_map/ppermute | solution.py:255
  101.0 21.9 %collective-permute-start.5 = (f32[52,128]{1,0:T(8,128)S(1)}, f32[52,128]{1,0:T(8,128)S(1)}, u32[]{:S(2)}, u32[]{:S(2)}) collective-permute-start(f32[52,128]{1,0:T(8,128)S(1)} %get-tuple-element.16), channel_id=1, source_target_pairs={{0,128},{1,384},{2,160},{3,416},{4,192},{5,448},{6,224},{7,480},{8... | collective-permute-start | bytes 79880 | tf_op jit(solution)/shard_map/ppermute | solution.py:256

commit v8 on v5

--- a/solution.py
+++ b/solution.py
@@ -198,6 +198,7 @@
     copies = jnp.broadcast_to(column.reshape(1, ZL * BLOCK, LANES), (X, ZL * BLOCK, LANES))
     gathered = lax.all_to_all(copies, "x", 0, 0, tiled=True)
     gathered = gathered.reshape(CHIPS * BLOCK, LANES)
+    gathered, side = lax.optimization_barrier((gathered, side))
     window = call(
         window_kernel,
         (CHIPS * 2 * ROWS, LANES),
@@ -211,10 +212,10 @@
     joined = (CHIPS, BLOCK + 4 * ROWS, LANES)
     joined = call(join_kernel, joined, [VMEM] * 3)(cycle, window, other_window)
     received = lax.all_to_all(joined, ("zh", "y"), 0, 0, tiled=True)
+    ladder = call(ladder_kernel, (CHIPS, SIDE * ROWS, LANES), [VMEM] * 3)(received, integrals, side)
+    ladder, received = lax.optimization_barrier((ladder, received))
     cycle = call(sum_kernel, (BLOCK, LANES), [VMEM])(received)
-    cycle, received = lax.optimization_barrier((cycle, received))
     cycle = lax.ppermute(cycle, EVERY, places(owner_rule))
-    ladder = call(ladder_kernel, (CHIPS, SIDE * ROWS, LANES), [VMEM] * 3)(received, integrals, side)
     ladder = lax.all_to_all(ladder, ("zh", "y"), 0, 0, tiled=True)
     return call(last_kernel, amplitudes.shape, [SMEM] * 3 + [VMEM] * 2)(
         tiles, occupied, virtual, ladder, cycle

time: 137 us -> 120 us (0.88)
  the two profiles are of different devices: /device:TPU:68 before, /device:TPU:111 now
where the time goes in v8:
time: 120 us; the launch traced here: 119 us
  blocking collectives  43.1 us (36%)
  waiting for transfers between devices  34.4 us (29%)
  starting transfers between devices  31.7 us (26%)
  Pallas kernels  6.13 us (5%)
  local copies, waits for them, and re-layouts  4.01 us (3%)
    all_to_all x1, blocking collectives, per_device(): received = lax.all_to_all(joined, ('zh', 'y'), 0, 0, tiled=True)  43.1 us
    ppermute x1, waiting for transfers between devices, per_device(): cycle = lax.ppermute(cycle, EVERY, places(owner_rule))  24.5 us
    ppermute x1, waiting for transfers between devices, per_device(): side = lax.ppermute(side, 'y', [(y, y ^ 1) for y in range(Y)])  9.85 us
    all_to_all x1, starting transfers between devices, per_device(): column = lax.all_to_all(copies, 'zl', 0, 0, tiled=True)  6.35 us
    all_to_all x1, starting transfers between devices, per_device(): ladder = lax.all_to_all(ladder, ('zh', 'y'), 0, 0, tiled=True)  6.27 us
    ppermute x1, starting transfers between devices, per_device(): other = lax.ppermute(cycle_block, 'core', [(0, 1), (1, 0)])  4.63 us
    all_to_all x1, starting transfers between devices, per_device(): gathered = lax.all_to_all(copies, 'x', 0, 0, tiled=True)  4.21 us
    ppermute x1, starting transfers between devices, per_device(): other_window = lax.ppermute(window, 'core', [(0, 1), (1, 0)])  4.07 us
  transfers between devices with their start and end apart: 7, of which 2 were waited for; matrix products, arithmetic and copies ran while one was open for 3% of the time, Pallas kernels for 2%

profile of v8, /device:TPU:111, one launch (start us, length us, event | category | flops | bytes accessed | tf_op | source)
XLA Modules:
  0.0 119.3 jit_solution(12007256095732941847)
XLA Ops:
  0.0 0.0 copy-start.2
  0.0 0.8 copy-done.2
  0.8 0.7 shard_map.64
  1.5 6.3 %all-to-all-start = ((f32[4,104,128]{2,1,0:T(8,128)}), f32[4,104,128]{2,1,0:T(8,128)S(1)}, u32[]{:S(2)}, u32[]{:S(2)}) async-start(f32[4,104,128]{2,1,0:T(8,128)} %shard_map.64), calls=%async_computation | async-start | bytes 425984 | tf_op jit(solution)/shard_map/all_to_all | solution.py:197
  7.9 2.2 %constant_dynamic-slice_fusion = f32[256,896]{1,0:T(8,128)} fusion(f32[256,1664]{1,0:T(8,128)} %bitcast.7, s32[]{:T(128)S(6)} %select_n.11), kind=kLoop, calls=%fused_computation | loop fusion | bytes 1835012 | tf_op jit(solution)/shard_map/dynamic_slice | solution.py:194
  10.0 0.0 copy-start.1
  10.0 0.0 copy-start.4
  10.0 3.1 %collective-permute-start = (f32[256,896]{1,0:T(8,128)}, f32[256,896]{1,0:T(8,128)S(1)}, u32[]{:S(2)}, u32[]{:S(2)}) collective-permute-start(f32[256,896]{1,0:T(8,128)} %constant_dynamic-slice_fusion), channel_id=1, source_target_pairs={{0,1},{1,0},{2,3},{3,2},{4,5},{5,4},{6,7},{7,6},{8,9},{9,8},{10,11... | collective-permute-start | bytes 2752520 | tf_op jit(solution)/shard_map/ppermute | solution.py:195
  13.1 0.0 all-to-all-done
  13.1 1.0 broadcast_in_dim.8
  14.2 4.2 %all-to-all-start.1 = ((f32[4,416,128]{2,1,0:T(8,128)}), f32[4,416,128]{2,1,0:T(8,128)S(1)}, u32[]{:S(2)}, u32[]{:S(2)}) async-start(f32[4,416,128]{2,1,0:T(8,128)} %broadcast_in_dim.8), calls=%async_computation.1 | async-start | bytes 1703936 | tf_op jit(solution)/shard_map/all_to_all | solution.py:199
  18.4 0.0 copy-done.1
  18.4 4.6 %collective-permute-start.1 = (f32[512,256]{1,0:T(8,128)S(1)}, f32[512,256]{1,0:T(8,128)S(1)}, u32[]{:S(2)}, u32[]{:S(2)}) collective-permute-start(f32[512,256]{1,0:T(8,128)S(1)} %copy-done.1), channel_id=1, source_target_pairs={{0,16},{16,0},{1,17},{17,1},{2,18},{18,2},{3,19},{19,3},{4,20},{20... | collective-permute-start | bytes 1572872 | tf_op jit(solution)/shard_map/ppermute | solution.py:191
  23.0 9.9 %collective-permute-done.other = f32[256,896]{1,0:T(8,128)S(1)} collective-permute-done((f32[256,896]{1,0:T(8,128)}, f32[256,896]{1,0:T(8,128)S(1)}, u32[]{:S(2)}, u32[]{:S(2)}) %collective-permute-start) | collective-permute-done | bytes 917536 | tf_op jit(solution)/shard_map/ppermute | solution.py:195
  32.9 0.0 all-to-all-done.1
  32.9 0.0 copy-done.4
  32.9 1.4 %shard_map.66 = f32[256,128]{1,0:T(8,128)S(1)} custom-call(s32[2]{0:T(128)S(1)} %copy-done.4, f32[1664,128]{1,0:T(8,128)S(1)} %bitcast.5), custom_call_target="tpu_custom_call" | custom-call | tf_op jit(solution)/shard_map/pallas_call | solution.py:202
  34.3 4.1 %collective-permute-start.2 = (f32[16,16,128]{2,1,0:T(8,128)S(1)}, f32[16,16,128]{2,1,0:T(8,128)S(1)}, u32[]{:S(2)}, u32[]{:S(2)}) collective-permute-start(f32[16,16,128]{2,1,0:T(8,128)S(1)} %bitcast.10), channel_id=1, source_target_pairs={{0,16},{16,0},{1,17},{17,1},{2,18},{18,2},{3,19},{19,3},{4,20},{20... | collective-permute-start | bytes 393224 | tf_op jit(solution)/shard_map/ppermute | solution.py:209
  38.4 0.0 collective-permute-done.1.other
  38.4 1.1 shard_map.65
  39.5 0.0 collective-permute-done.2.other
  39.5 0.0 copy-start
  39.5 0.1 shard_map.67
  39.6 43.1 %all_to_all.20.received = f32[16,136,128]{2,1,0:T(8,128)S(1)} all-to-all(f32[16,136,128]{2,1,0:T(8,128)S(1)} %shard_map.67), channel_id=1, replica_groups=mesh['zl'=4,'x'=4,'core'=2,'zh'=2,'y'=8] {'zh','y'}, dimensions={0} | all-to-all | bytes 2228224 | tf_op jit(solution)/shard_map/all_to_all | solution.py:214
  82.7 0.0 copy-done
  82.7 1.4 %shard_map.68 = f32[16,56,128]{2,1,0:T(8,128)} custom-call(f32[16,136,128]{2,1,0:T(8,128)S(1)} %all_to_all.20.received, f32[256,1664]{1,0:T(8,128)S(1)} %bitcast.8, f32[256,896]{1,0:T(8,128)S(1)} %collective-permute-done.other), custom_call_target="tpu_custom_call" | custom-call | tf_op jit(solution)/shard_map/pallas_call | solution.py:215
  84.1 0.0 copy-start.3
  84.1 0.0 copy-start.5
  84.1 6.3 %all-to-all-start.3 = ((f32[16,56,128]{2,1,0:T(8,128)}), f32[16,56,128]{2,1,0:T(8,128)S(1)}, u32[]{:S(2)}, u32[]{:S(2)}) async-start(f32[16,56,128]{2,1,0:T(8,128)} %shard_map.68), calls=%async_computation.3 | async-start | bytes 917504 | tf_op jit(solution)/shard_map/all_to_all | solution.py:219
  90.4 3.0 %collective-permute-start.3 = (f32[104,128]{1,0:T(8,128)S(1)}, f32[104,128]{1,0:T(8,128)S(1)}, u32[]{:S(2)}, u32[]{:S(2)}) collective-permute-start(f32[104,128]{1,0:T(8,128)S(1)} %shard_map.69), channel_id=1, source_target_pairs={{0,0},{1,128},{2,256},{3,384},{4,32},{5,160},{6,288},{7,416},{8,64... | collective-permute-start | bytes 159752 | tf_op jit(solution)/shard_map/ppermute | solution.py:218
  93.5 24.5 %collective-permute-done.3.cycle = f32[104,128]{1,0:T(8,128)S(1)} collective-permute-done((f32[104,128]{1,0:T(8,128)S(1)}, f32[104,128]{1,0:T(8,128)S(1)}, u32[]{:S(2)}, u32[]{:S(2)}) %collective-permute-start.3) | collective-permute-done | bytes 53280 | tf_op jit(solution)/shard_map/ppermute | solution.py:218
  118.0 0.0 all-to-all-done.3.ladder
  118.0 0.0 copy-done.3
  118.0 0.0 copy-done.5
  118.0 1.3 %shard_map.70 = f32[1,8,1664]{2,1,0:T(8,128)} custom-call(s32[2]{0:T(128)S(1)} %copy-done.4, f32[128]{0:T(128)S(1)} %copy-done.5, f32[832]{0:T(1024)S(1)} %copy-done.3, f32[16,56,128]{2,1,0:T(8,128)S(1)} %all-to-all-done.3.ladder, f32[104,128]{1,0:T(8,128)S(1)} %collective-permute-done.3.cycle), custom_call_target="tpu_custom_call" | custom-call | tf_op jit(solution)/shard_map/pallas_call | solution.py:220
  (1 shorter events, 0.0 us)
Async XLA Ops:
  0.0 0.8 copy-start.2
  1.5 11.6 %all-to-all-start = ((f32[4,104,128]{2,1,0:T(8,128)}), f32[4,104,128]{2,1,0:T(8,128)S(1)}, u32[]{:S(2)}, u32[]{:S(2)}) async-start(f32[4,104,128]{2,1,0:T(8,128)} %shard_map.64), calls=%async_computation | async-start | bytes 425984 | tf_op jit(solution)/shard_map/all_to_all | solution.py:197
  10.0 8.3 %copy-start.1 = (f32[512,256]{1,0:T(8,128)S(1)}, f32[512,256]{1,0:T(8,128)}, u32[]{:S(2)}) copy-start(f32[512,256]{1,0:T(8,128)} %own.1) | copy-start | bytes 1572868
  10.0 22.8 %copy-start.4 = (s32[2]{0:T(128)S(1)}, s32[2]{0:T(128)}, u32[]{:S(2)}) copy-start(s32[2]{0:T(128)} %tiles.3) | copy-start | bytes 28
  10.0 22.8 %collective-permute-start = (f32[256,896]{1,0:T(8,128)}, f32[256,896]{1,0:T(8,128)S(1)}, u32[]{:S(2)}, u32[]{:S(2)}) collective-permute-start(f32[256,896]{1,0:T(8,128)} %constant_dynamic-slice_fusion), channel_id=1, source_target_pairs={{0,1},{1,0},{2,3},{3,2},{4,5},{5,4},{6,7},{7,6},{8,9},{9,8},{10,11... | collective-permute-start | bytes 2752520 | tf_op jit(solution)/shard_map/ppermute | solution.py:195
  14.2 18.7 %all-to-all-start.1 = ((f32[4,416,128]{2,1,0:T(8,128)}), f32[4,416,128]{2,1,0:T(8,128)S(1)}, u32[]{:S(2)}, u32[]{:S(2)}) async-start(f32[4,416,128]{2,1,0:T(8,128)} %broadcast_in_dim.8), calls=%async_computation.1 | async-start | bytes 1703936 | tf_op jit(solution)/shard_map/all_to_all | solution.py:199
  18.4 20.0 %collective-permute-start.1 = (f32[512,256]{1,0:T(8,128)S(1)}, f32[512,256]{1,0:T(8,128)S(1)}, u32[]{:S(2)}, u32[]{:S(2)}) collective-permute-start(f32[512,256]{1,0:T(8,128)S(1)} %copy-done.1), channel_id=1, source_target_pairs={{0,16},{16,0},{1,17},{17,1},{2,18},{18,2},{3,19},{19,3},{4,20},{20... | collective-permute-start | bytes 1572872 | tf_op jit(solution)/shard_map/ppermute | solution.py:191
  34.3 5.2 %collective-permute-start.2 = (f32[16,16,128]{2,1,0:T(8,128)S(1)}, f32[16,16,128]{2,1,0:T(8,128)S(1)}, u32[]{:S(2)}, u32[]{:S(2)}) collective-permute-start(f32[16,16,128]{2,1,0:T(8,128)S(1)} %bitcast.10), channel_id=1, source_target_pairs={{0,16},{16,0},{1,17},{17,1},{2,18},{18,2},{3,19},{19,3},{4,20},{20... | collective-permute-start | bytes 393224 | tf_op jit(solution)/shard_map/ppermute | solution.py:209
  39.5 43.2 %copy-start = (f32[4,64,1664]{2,1,0:T(8,128)S(1)}, f32[4,64,1664]{2,1,0:T(8,128)}, u32[]{:S(2)}) copy-start(f32[4,64,1664]{2,1,0:T(8,128)} %param.8) | copy-start | bytes 5111812
  84.1 33.9 %copy-start.3 = (f32[832]{0:T(1024)S(1)}, f32[832]{0:T(1024)}, u32[]{:S(2)}) copy-start(f32[832]{0:T(1024)} %virtual.1) | copy-start | bytes 9988
  84.1 33.9 %copy-start.5 = (f32[128]{0:T(128)S(1)}, f32[128]{0:T(128)}, u32[]{:S(2)}) copy-start(f32[128]{0:T(128)} %occupied.1) | copy-start | bytes 1540
  84.1 33.9 %all-to-all-start.3 = ((f32[16,56,128]{2,1,0:T(8,128)}), f32[16,56,128]{2,1,0:T(8,128)S(1)}, u32[]{:S(2)}, u32[]{:S(2)}) async-start(f32[16,56,128]{2,1,0:T(8,128)} %shard_map.68), calls=%async_computation.3 | async-start | bytes 917504 | tf_op jit(solution)/shard_map/all_to_all | solution.py:219
  90.4 27.6 %collective-permute-start.3 = (f32[104,128]{1,0:T(8,128)S(1)}, f32[104,128]{1,0:T(8,128)S(1)}, u32[]{:S(2)}, u32[]{:S(2)}) collective-permute-start(f32[104,128]{1,0:T(8,128)S(1)} %shard_map.69), channel_id=1, source_target_pairs={{0,0},{1,128},{2,256},{3,384},{4,32},{5,160},{6,288},{7,416},{8,64... | collective-permute-start | bytes 159752 | tf_op jit(solution)/shard_map/ppermute | solution.py:218

commit v9 on v7

v9 whole, which is shorter than its diff:
```python
import functools

import jax
import jax.numpy as jnp
from jax import lax
from jax.experimental import pallas as pl
from jax.experimental.pallas import tpu as pltpu
from jax.sharding import Mesh
from jax.sharding import PartitionSpec as P

ZL, X, CORE, ZH, YH, YL = 4, 4, 2, 2, 4, 2
GROUPS = ZH * YH
PLACES = GROUPS * YL
CHIPS = ZL * X
ROWS = 8
TILE = 64
PAIRS = 13
LANES = 2 * TILE
BLOCK = PAIRS * ROWS
SIDE = (PAIRS + 1) // 2
SKIP = PAIRS - SIDE
HALF = ROWS // YL
PIECE = PAIRS * HALF
EVERY = ("zl", "x", "core", "zh", "yh", "yl")
VMEM = pl.BlockSpec(memory_space=pltpu.VMEM)
SMEM = pl.BlockSpec(memory_space=pltpu.SMEM)
PARAMS = pltpu.CompilerParams(vmem_limit_bytes=32 * 1024 * 1024)


def split(value):
    high = value.astype(jnp.bfloat16)
    return high, (value - high.astype(jnp.float32)).astype(jnp.bfloat16)


def product(left, right):
    dot = functools.partial(jnp.dot, preferred_element_type=jnp.float32)
    return dot(left[0], right[1]) + dot(left[1], right[0]) + dot(left[0], right[0])


def low_half(shape):
    return lax.broadcasted_iota(jnp.int32, shape, 1) < TILE


def pair_up(first, second):
    low = low_half(first.shape)
    return (
        jnp.where(low, first, pltpu.roll(second, TILE, 1)),
        jnp.where(low, pltpu.roll(first, TILE, 1), second),
    )


def pack_kernel(amplitudes, out):
    for pair in range(PAIRS):
        tile = amplitudes[0, :, pair * LANES : (pair + 1) * LANES]
        for chip in range(YL * ZL):
            out[chip, pair * ROWS : (pair + 1) * ROWS, :] = tile


def window_kernel(tiles, gathered, out, window, columns, turned):
    core = lax.axis_index("core")
    for pair in range(TILE // 2):
        place = tiles[1] * (TILE // 2) + pair
        owner = place // PAIRS
        chip = owner // CORE
        for yl in range(YL):
            block = (chip % X * YL + yl) * ZL + chip // X
            row = (block * PAIRS + (place - owner * PAIRS)) * ROWS
            tile = gathered[pl.ds(pl.multiple_of(row, ROWS), ROWS), :]
            start = (yl * (TILE // 2) + pair) * ROWS
            window[start : start + ROWS, :] = jnp.where(owner % CORE == core, tile, 0.0)
    for yl in range(YL):
        for half in range(ROWS // 2):
            for inner in range(2):
                start = yl * (TILE // 2) * ROWS + half * 2 + inner
                both = window[pl.ds(start, TILE // 2, stride=ROWS), :]
                columns[pl.ds(inner * TILE, TILE // 2, stride=2), :] = both
                columns[pl.ds(inner * TILE + 1, TILE // 2, stride=2), :] = pltpu.roll(both, TILE, 1)
            turned[...] = jnp.transpose(columns[...])
            for part in range(2):
                even = turned[pl.ds(2 * part, PLACES, stride=4), :]
                odd = turned[pl.ds(2 * part + 1, PLACES, stride=4), :]
                for inner, value in enumerate(pair_up(even, odd)):
                    row = (yl * 2 + part) * ROWS + half * 2 + inner
                    out[pl.ds(row, PLACES, stride=4 * ROWS), :] = value


def cycle_kernel(gathered, own, first, second, out, ordered):
    core, yl = lax.axis_index("core"), lax.axis_index("yl")
    span = ZL * BLOCK
    for x in range(X):
        for half in range(YL):
            ordered[half, x * span : (x + 1) * span, :] = gathered[pl.ds((x * YL + half) * span, span), :]
    chunks = ([], [])
    for half in range(YL):
        for k in range(0, ROWS, 2):
            even = ordered[half, pl.ds(k, CHIPS * PAIRS, stride=ROWS), :]
            odd = ordered[half, pl.ds(k + 1, CHIPS * PAIRS, stride=ROWS), :]
            for chunk, value in zip(chunks, pair_up(even, odd)):
                chunk.append(value)
    left = split(jnp.concatenate([jnp.concatenate(chunk, 1) for chunk in chunks], 0))
    same = core == yl
    near = jnp.where(same, own[...], first[...])
    far = jnp.where(same, first[...], second[...])
    right = jnp.concatenate([jnp.where(yl == 0, near, far), jnp.where(yl == 0, far, near)], 0)
    result = product(left, split(right))
    for quarter in range(2):
        both = result[:, quarter * LANES : (quarter + 1) * LANES]
        rows = pair_up(both[: CHIPS * PAIRS], both[CHIPS * PAIRS :])
        for inner, value in enumerate(rows):
            out[pl.ds(quarter * 2 + inner, CHIPS * PAIRS, stride=HALF), :] = value


def join_kernel(cycle, own, other, out):
    for group in range(GROUPS):
        out[group, :BLOCK, :] = cycle[group, :, :]
        out[group, BLOCK:, :] = own[group, :, :] + other[group, :, :]


def sum_kernel(received, near, far):
    total = received[0, :BLOCK, :]
    for group in range(1, GROUPS):
        total = total + received[group, :BLOCK, :]
    first = lax.axis_index("yl") == 0
    near[...] = jnp.where(first, total[:PIECE], total[PIECE:])
    far[...] = jnp.where(first, total[PIECE:], total[:PIECE])


def ladder_kernel(received, own, other, out):
    slots = []
    for slot in range(YL):
        lefts = []
        for part in range(2):
            halves = []
            for yl in range(YL):
                start = BLOCK + ((slot * YL + yl) * 2 + part) * ROWS
                rows = received[:, start : start + ROWS, :]
                halves.append(rows.reshape(GROUPS * ROWS, LANES))
            lefts.append(jnp.concatenate(halves, 0))
        slots.append(jnp.concatenate(lefts, 1))
    yl = lax.axis_index("yl")
    mine = jnp.where(yl == 0, slots[0], slots[1])
    theirs = jnp.where(yl == 0, slots[1], slots[0])
    left = split(jnp.concatenate([mine, theirs], 1))
    first = yl * (SKIP * LANES)
    width = SIDE * LANES
    for start in range(0, width, 2 * LANES):
        stop = min(start + 2 * LANES, width)
        columns = pl.ds(pl.multiple_of(first + start, LANES), stop - start)
        right = jnp.concatenate([own[:, columns], other[:, start:stop]], 0)
        result = product(left, split(right))
        for column in range(start, stop, LANES):
            value = result[:, column - start : column - start + LANES]
            rows = pl.ds(column // LANES * ROWS, ROWS)
            for place in range(YL):
                part = value[place * GROUPS * ROWS : (place + 1) * GROUPS * ROWS]
                out[:, place, rows, :] = part.reshape(GROUPS, ROWS, LANES)


def last_kernel(tiles, occupied, virtual, ladder, near, far, out):
    column = lax.axis_index("zl") * (X * CORE) + lax.axis_index("x") * CORE + lax.axis_index("core")
    row = (lax.axis_index("zh") * YH + lax.axis_index("yh")) * YL + lax.axis_index("yl")
    shape = (ROWS, LANES)
    lane = lax.broadcasted_iota(jnp.int32, shape, 1)
    line = lax.broadcasted_iota(jnp.int32, shape, 0)
    spectator = jnp.zeros(shape, jnp.float32)
    for b in range(TILE):
        spectator = jnp.where(lane % TILE == b, virtual[tiles[0] * TILE + b], spectator)
    rows = jnp.zeros(shape, jnp.float32)
    for j in range(ROWS):
        rows = jnp.where(line == j, occupied[row * ROWS + j], rows)
    straight = lax.axis_index("zl") % 2 == 0
    for pair in range(PAIRS):
        piece = pl.ds(pair * HALF, HALF)
        one, two = near[piece, :], far[piece, :]
        low, high = jnp.where(straight, one, two), jnp.where(straight, two, one)
        total = jnp.concatenate([low, high], 0)
        side = int(pair >= SIDE)
        rows_of_side = pl.ds((pair - side * SKIP) * ROWS, ROWS)
        for place in range(side, PLACES, YL):
            total = total + ladder[place, rows_of_side, :]
        a = column * (2 * PAIRS) + 2 * pair
        energy = jnp.where(lane < TILE, virtual[a], virtual[a + 1]) + spectator
        out[0, :, pair * LANES : (pair + 1) * LANES] = total / (energy - occupied[0] - rows)


def call(kernel, shapes, specs, scratch=()):
    return pl.pallas_call(
        kernel,
        out_shape=[jax.ShapeDtypeStruct(shape, jnp.float32) for shape in shapes],
        in_specs=specs,
        out_specs=[VMEM] * len(shapes),
        scratch_shapes=[pltpu.VMEM(shape, jnp.float32) for shape in scratch],
        compiler_params=PARAMS,
    )


def places(rule):
    pairs = []
    for chip in range(CHIPS):
        for core in range(CORE):
            for place in range(PLACES):
                to = rule(chip, core, place)
                source = (chip * CORE + core) * PLACES + place
                pairs.append((source, (to[0] * CORE + to[1]) * PLACES + to[2]))
    return pairs


def chip_of(block):
    return block % ZL * X + block // ZL


def near_rule(chip, core, place):
    return chip_of(place), core, chip


def far_rule(chip, core, place):
    return chip_of(place ^ 1), core, chip


def per_device(amplitudes, cycle_block, ladder_block, occupied, virtual, tiles):
    first = lax.ppermute(cycle_block, ("core", "yl"), [(0, 2), (3, 1), (2, 3), (1, 0)])
    second = lax.ppermute(first, ("core", "yl"), [(0, 2), (3, 1)])
    integrals = ladder_block.reshape(-1, ladder_block.shape[2])
    start = (1 - lax.axis_index("yl")) * (SKIP * LANES)
    side = lax.dynamic_slice_in_dim(integrals, start, SIDE * LANES, 1)
    side = lax.ppermute(side, "yl", [(0, 1), (1, 0)])

    (copies,) = call(pack_kernel, [(YL * ZL, BLOCK, LANES)], [VMEM])(amplitudes)
    column = lax.all_to_all(copies, ("yl", "zl"), 0, 0, tiled=True)
    span = YL * ZL * BLOCK
    copies = jnp.broadcast_to(column.reshape(1, span, LANES), (X, span, LANES))
    gathered = lax.all_to_all(copies, "x", 0, 0, tiled=True)
    gathered = gathered.reshape(X * span, LANES)
    gathered, side = lax.optimization_barrier((gathered, side))

    (window,) = call(
        window_kernel,
        [(PLACES * 4 * ROWS, LANES)],
        [SMEM, VMEM],
        [(YL * TILE // 2 * ROWS, LANES), (LANES, LANES), (LANES, LANES)],
    )(tiles, gathered)
    window = window.reshape(GROUPS, 8 * ROWS, LANES)
    other_window = lax.ppermute(window, "core", [(0, 1), (1, 0)])
    (cycle,) = call(
        cycle_kernel, [(CHIPS * PIECE, LANES)], [VMEM] * 4, [(YL, CHIPS * BLOCK, LANES)]
    )(gathered, cycle_block, first, second)
    (joined,) = call(join_kernel, [(GROUPS, BLOCK + 8 * ROWS, LANES)], [VMEM] * 3)(
        cycle.reshape(GROUPS, BLOCK, LANES), window, other_window
    )
    received = lax.all_to_all(joined, ("zh", "yh"), 0, 0, tiled=True)
    (ladder,) = call(ladder_kernel, [(GROUPS, YL, SIDE * ROWS, LANES)], [VMEM] * 3)(
        received, integrals, side
    )
    ladder, received = lax.optimization_barrier((ladder, received))
    near, far = call(sum_kernel, [(PIECE, LANES)] * 2, [VMEM])(received)
    near = lax.ppermute(near, EVERY, places(near_rule))
    far = lax.ppermute(far, EVERY, places(far_rule))
    ladder = ladder.reshape(PLACES, SIDE * ROWS, LANES)
    ladder = lax.all_to_all(ladder, ("zh", "yh", "yl"), 0, 0, tiled=True)
    (result,) = call(last_kernel, [amplitudes.shape], [SMEM] * 3 + [VMEM] * 3)(
        tiles, occupied, virtual, ladder, near, far
    )
    return result


def solution(mesh):
    parts = Mesh(mesh.devices.reshape(ZL, X, CORE, ZH, YH, YL), EVERY)
    amp, intg = ("zl", "x", "core"), ("zh", "yh", "yl")
    return jax.shard_map(
        per_device,
        mesh=parts,
        in_specs=(P(None, intg, amp), P(intg, amp), P(intg, None, amp), P(), P(), P()),
        out_specs=P(None, intg, amp),
        check_vma=False,
    )
```

time: 125 us -> 134 us (1.072)
  the two profiles are of different devices: /device:TPU:28 before, /device:TPU:111 now
where the time goes in v9:
time: 134 us; the launch traced here: 133 us
  blocking collectives  49.1 us (37%)
  waiting for transfers between devices  42.2 us (31%)
  starting transfers between devices  31.4 us (23%)
  Pallas kernels  7.41 us (6%)
  local copies, waits for them, and re-layouts  3.17 us (2%)
    all_to_all x1, blocking collectives, per_device(): received = lax.all_to_all(joined, ('zh', 'yh'), 0, 0, tiled=True)  32 us
    ppermute x1, waiting for transfers between devices, per_device(): lax.ppermute(cycle_block, ('core', 'yl'), [(0, 2), (3, 1), (2, 3), (1, 0)])  22.9 us
    ppermute x1, waiting for transfers between devices, per_device(): near = lax.ppermute(near, EVERY, places(near_rule))  19.3 us
    all_to_all x1, blocking collectives, per_device(): column = lax.all_to_all(copies, ('yl', 'zl'), 0, 0, tiled=True)  17.1 us
    all_to_all x1, starting transfers between devices, per_device(): ladder = lax.all_to_all(ladder, ('zh', 'yh', 'yl'), 0, 0, tiled=True)  7.29 us
    ppermute x1, starting transfers between devices, per_device(): far = lax.ppermute(far, EVERY, places(far_rule))  5.76 us
    ppermute x1, starting transfers between devices, per_device(): lax.ppermute(cycle_block, ('core', 'yl'), [(0, 2), (3, 1), (2, 3), (1, 0)])  4.89 us
    all_to_all x1, starting transfers between devices, per_device(): gathered = lax.all_to_all(copies, 'x', 0, 0, tiled=True)  4.34 us
  transfers between devices with their start and end apart: 8, of which 2 were waited for; matrix products, arithmetic and copies ran while one was open for 0% of the time, Pallas kernels for 3%

profile of v9, /device:TPU:111, one launch (start us, length us, event | category | flops | bytes accessed | tf_op | source)
XLA Modules:
  0.0 133.5 jit_solution(18109815045528588660)
XLA Ops:
  0.0 0.0 copy-start.5
  0.0 0.8 copy-done.5
  0.8 17.1 %all_to_all.20 = f32[8,104,128]{2,1,0:T(8,128)S(1)} all-to-all(f32[8,104,128]{2,1,0:T(8,128)S(1)} %shard_map.64), channel_id=1, replica_groups=mesh['zl'=4,'x'=4,'core'=2,'zh'=2,'yh'=4,'yl'=2] {'yl','zl'}, dimensions={0} | all-to-all | bytes 851968 | tf_op jit(solution)/shard_map/all_to_all | solution.py:229
  18.0 1.3 broadcast_in_dim.8
  19.3 0.0 copy-start
  19.3 4.3 %all-to-all-start.1 = ((f32[4,832,128]{2,1,0:T(8,128)}), f32[4,832,128]{2,1,0:T(8,128)S(1)}, u32[]{:S(2)}, u32[]{:S(2)}) async-start(f32[4,832,128]{2,1,0:T(8,128)} %broadcast_in_dim.8), calls=%async_computation.1 | async-start | bytes 3407872 | tf_op jit(solution)/shard_map/all_to_all | solution.py:232
  23.6 0.0 copy-start.7
  23.6 0.0 copy-start.3
  23.6 0.0 copy-done
  23.6 0.1 constant_dynamic-slice_fusion
  23.7 2.1 %collective-permute-start = (f32[256,896]{1,0:T(8,128)S(1)}, f32[256,896]{1,0:T(8,128)S(1)}, u32[]{:S(2)}, u32[]{:S(2)}) collective-permute-start(f32[256,896]{1,0:T(8,128)S(1)} %constant_dynamic-slice_fusion), channel_id=1, source_target_pairs={{0,1},{1,0},{2,3},{3,2},{4,5},{5,4},{6,7},{7,6},{8,9},{9,8},{10,11... | collective-permute-start | bytes 2752520 | tf_op jit(solution)/shard_map/ppermute | solution.py:226
  25.8 0.0 copy-done.3
  25.8 4.9 %collective-permute-start.1 = (f32[512,256]{1,0:T(8,128)S(1)}, f32[512,256]{1,0:T(8,128)}, u32[]{:S(2)}, u32[]{:S(2)}) collective-permute-start(f32[512,256]{1,0:T(8,128)S(1)} %copy-done.3), channel_id=1, source_target_pairs={{0,16},{17,1},{16,17},{1,0},{2,18},{19,3},{18,19},{3,2},{4,20},{21... | collective-permute-start | bytes 1572872 | tf_op jit(solution)/shard_map/ppermute | solution.py:221
  30.7 22.9 %collective-permute-done.1.first = f32[512,256]{1,0:T(8,128)} collective-permute-done((f32[512,256]{1,0:T(8,128)S(1)}, f32[512,256]{1,0:T(8,128)}, u32[]{:S(2)}, u32[]{:S(2)}) %collective-permute-start.1) | collective-permute-done | bytes 524320 | tf_op jit(solution)/shard_map/ppermute | solution.py:221
  53.5 2.1 %collective-permute-start.2 = (f32[512,256]{1,0:T(8,128)}, f32[512,256]{1,0:T(8,128)}, u32[]{:S(2)}, u32[]{:S(2)}) collective-permute-start(f32[512,256]{1,0:T(8,128)} %collective-permute-done.1.first), channel_id=1, source_target_pairs={{0,16},{17,1},{2,18},{19,3},{4,20},{21,5},{6,22},{23,7},{8,24},{25... | collective-permute-start | bytes 1572872 | tf_op jit(solution)/shard_map/ppermute | solution.py:222
  55.6 0.0 collective-permute-done.other
  55.6 0.0 copy-start.1
  55.6 0.9 copy-done.1
  56.6 0.0 all-to-all-done.1
  56.6 0.0 copy-start.4
  56.6 0.0 copy-done.7
  56.6 1.9 %shard_map.66 = f32[512,128]{1,0:T(8,128)S(1)} custom-call(s32[2]{0:T(128)S(1)} %copy-done.7, f32[3328,128]{1,0:T(8,128)S(1)} %bitcast.6), custom_call_target="tpu_custom_call" | custom-call | tf_op jit(solution)/shard_map/pallas_call | solution.py:236
  58.4 1.9 %collective-permute-start.3 = (f32[8,64,128]{2,1,0:T(8,128)S(1)}, f32[8,64,128]{2,1,0:T(8,128)S(1)}, u32[]{:S(2)}, u32[]{:S(2)}) collective-permute-start(f32[8,64,128]{2,1,0:T(8,128)S(1)} %bitcast.11), channel_id=1, source_target_pairs={{0,16},{16,0},{1,17},{17,1},{2,18},{18,2},{3,19},{19,3},{4,20},{20... | collective-permute-start | bytes 786440 | tf_op jit(solution)/shard_map/ppermute | solution.py:243
  60.4 0.0 collective-permute-done.2.second
  60.4 0.0 copy-done.4
  60.4 2.6 %shard_map.65 = f32[832,128]{1,0:T(8,128)S(1)} custom-call(f32[3328,128]{1,0:T(8,128)S(1)} %bitcast.7, f32[512,256]{1,0:T(8,128)S(1)} %copy-done.4, f32[512,256]{1,0:T(8,128)} %collective-permute-done.1.first, f32[512,256]{1,0:T(8,128)} %collective-permute-done.2.second), custom_call_target="tpu_custom_call" | custom-call | tf_op jit(solution)/shard_map/pallas_call | solution.py:244
  63.0 0.0 copy-start.2
  63.0 0.0 collective-permute-done.3.other
  63.0 0.1 shard_map.67
  63.1 32.0 %all_to_all.21.received = f32[8,168,128]{2,1,0:T(8,128)S(1)} all-to-all(f32[8,168,128]{2,1,0:T(8,128)S(1)} %shard_map.67), channel_id=1, replica_groups=mesh['zl'=4,'x'=4,'core'=2,'zh'=2,'yh'=4,'yl'=2] {'zh','yh'}, dimensions={0} | all-to-all | bytes 1376256 | tf_op jit(solution)/shard_map/all_to_all | solution.py:250
  95.1 0.0 copy-done.2
  95.1 0.0 copy-start.6
  95.1 0.0 copy-start.8
  95.1 1.5 %shard_map.68 = f32[8,2,56,128]{3,2,1,0:T(8,128)} custom-call(f32[8,168,128]{2,1,0:T(8,128)S(1)} %all_to_all.21.received, f32[256,1664]{1,0:T(8,128)S(1)} %bitcast.9, f32[256,896]{1,0:T(8,128)S(1)} %copy-done.2), custom_call_target="tpu_custom_call" | custom-call | tf_op jit(solution)/shard_map/pallas_call | solution.py:251
  96.6 7.3 %all-to-all-start.3 = ((f32[16,56,128]{2,1,0:T(8,128)}), f32[16,56,128]{2,1,0:T(8,128)S(1)}, u32[]{:S(2)}, u32[]{:S(2)}) async-start(f32[16,56,128]{2,1,0:T(8,128)} %bitcast.5), calls=%async_computation.3 | async-start | bytes 917504 | tf_op jit(solution)/shard_map/all_to_all | solution.py:259
  103.9 3.1 %collective-permute-start.4 = (f32[52,128]{1,0:T(8,128)S(1)}, f32[52,128]{1,0:T(8,128)S(1)}, u32[]{:S(2)}, u32[]{:S(2)}) collective-permute-start(f32[52,128]{1,0:T(8,128)S(1)} %get-tuple-element.15), channel_id=1, source_target_pairs={{0,0},{1,128},{2,256},{3,384},{4,32},{5,160},{6,288},{7,416},{8,64... | collective-permute-start | bytes 79880 | tf_op jit(solution)/shard_map/ppermute | solution.py:256
  107.0 5.8 %collective-permute-start.5 = (f32[52,128]{1,0:T(8,128)S(1)}, f32[52,128]{1,0:T(8,128)S(1)}, u32[]{:S(2)}, u32[]{:S(2)}) collective-permute-start(f32[52,128]{1,0:T(8,128)S(1)} %get-tuple-element.16), channel_id=1, source_target_pairs={{0,128},{1,0},{2,384},{3,256},{4,160},{5,32},{6,416},{7,288},{8,19... | collective-permute-start | bytes 79880 | tf_op jit(solution)/shard_map/ppermute | solution.py:257
  112.8 19.3 %collective-permute-done.4.near = f32[52,128]{1,0:T(8,128)S(1)} collective-permute-done((f32[52,128]{1,0:T(8,128)S(1)}, f32[52,128]{1,0:T(8,128)S(1)}, u32[]{:S(2)}, u32[]{:S(2)}) %collective-permute-start.4) | collective-permute-done | bytes 26656 | tf_op jit(solution)/shard_map/ppermute | solution.py:256
  132.1 0.0 collective-permute-done.5.far
  132.1 0.0 all-to-all-done.3.ladder
  132.1 0.0 copy-done.6
  132.1 0.0 copy-done.8
  132.1 1.3 shard_map.70
  (2 shorter events, 0.1 us)
Async XLA Ops:
  0.0 0.8 copy-start.5
  19.3 4.3 %copy-start = (f32[4,64,1664]{2,1,0:T(8,128)S(1)}, f32[4,64,1664]{2,1,0:T(8,128)}, u32[]{:S(2)}) copy-start(f32[4,64,1664]{2,1,0:T(8,128)} %param.8) | copy-start | bytes 5111812
  19.3 37.3 %all-to-all-start.1 = ((f32[4,832,128]{2,1,0:T(8,128)}), f32[4,832,128]{2,1,0:T(8,128)S(1)}, u32[]{:S(2)}, u32[]{:S(2)}) async-start(f32[4,832,128]{2,1,0:T(8,128)} %broadcast_in_dim.8), calls=%async_computation.1 | async-start | bytes 3407872 | tf_op jit(solution)/shard_map/all_to_all | solution.py:232
  23.6 32.9 %copy-start.7 = (s32[2]{0:T(128)S(1)}, s32[2]{0:T(128)}, u32[]{:S(2)}) copy-start(s32[2]{0:T(128)} %tiles.3) | copy-start | bytes 28
  23.6 2.1 %copy-start.3 = (f32[512,256]{1,0:T(8,128)S(1)}, f32[512,256]{1,0:T(8,128)}, u32[]{:S(2)}) copy-start(f32[512,256]{1,0:T(8,128)} %own.1) | copy-start | bytes 1572868
  23.7 31.9 %collective-permute-start = (f32[256,896]{1,0:T(8,128)S(1)}, f32[256,896]{1,0:T(8,128)S(1)}, u32[]{:S(2)}, u32[]{:S(2)}) collective-permute-start(f32[256,896]{1,0:T(8,128)S(1)} %constant_dynamic-slice_fusion), channel_id=1, source_target_pairs={{0,1},{1,0},{2,3},{3,2},{4,5},{5,4},{6,7},{7,6},{8,9},{9,8},{10,11... | collective-permute-start | bytes 2752520 | tf_op jit(solution)/shard_map/ppermute | solution.py:226
  25.8 27.8 %collective-permute-start.1 = (f32[512,256]{1,0:T(8,128)S(1)}, f32[512,256]{1,0:T(8,128)}, u32[]{:S(2)}, u32[]{:S(2)}) collective-permute-start(f32[512,256]{1,0:T(8,128)S(1)} %copy-done.3), channel_id=1, source_target_pairs={{0,16},{17,1},{16,17},{1,0},{2,18},{19,3},{18,19},{3,2},{4,20},{21... | collective-permute-start | bytes 1572872 | tf_op jit(solution)/shard_map/ppermute | solution.py:221
  53.5 6.8 %collective-permute-start.2 = (f32[512,256]{1,0:T(8,128)}, f32[512,256]{1,0:T(8,128)}, u32[]{:S(2)}, u32[]{:S(2)}) collective-permute-start(f32[512,256]{1,0:T(8,128)} %collective-permute-done.1.first), channel_id=1, source_target_pairs={{0,16},{17,1},{2,18},{19,3},{4,20},{21,5},{6,22},{23,7},{8,24},{25... | collective-permute-start | bytes 1572872 | tf_op jit(solution)/shard_map/ppermute | solution.py:222
  55.6 0.9 copy-start.1
  56.6 3.8 %copy-start.4 = (f32[512,256]{1,0:T(8,128)S(1)}, f32[512,256]{1,0:T(8,128)}, u32[]{:S(2)}) copy-start(f32[512,256]{1,0:T(8,128)} %own.1) | copy-start | bytes 1572868
  58.4 4.6 %collective-permute-start.3 = (f32[8,64,128]{2,1,0:T(8,128)S(1)}, f32[8,64,128]{2,1,0:T(8,128)S(1)}, u32[]{:S(2)}, u32[]{:S(2)}) collective-permute-start(f32[8,64,128]{2,1,0:T(8,128)S(1)} %bitcast.11), channel_id=1, source_target_pairs={{0,16},{16,0},{1,17},{17,1},{2,18},{18,2},{3,19},{19,3},{4,20},{20... | collective-permute-start | bytes 786440 | tf_op jit(solution)/shard_map/ppermute | solution.py:243
  63.0 32.1 %copy-start.2 = (f32[256,896]{1,0:T(8,128)S(1)}, f32[256,896]{1,0:T(8,128)}, u32[]{:S(2)}) copy-start(f32[256,896]{1,0:T(8,128)} %copy-done.1) | copy-start | bytes 2752516
  95.1 37.0 %copy-start.6 = (f32[832]{0:T(1024)S(1)}, f32[832]{0:T(1024)}, u32[]{:S(2)}) copy-start(f32[832]{0:T(1024)} %virtual.1) | copy-start | bytes 9988
  95.1 37.0 %copy-start.8 = (f32[128]{0:T(128)S(1)}, f32[128]{0:T(128)}, u32[]{:S(2)}) copy-start(f32[128]{0:T(128)} %occupied.1) | copy-start | bytes 1540
  96.6 35.5 %all-to-all-start.3 = ((f32[16,56,128]{2,1,0:T(8,128)}), f32[16,56,128]{2,1,0:T(8,128)S(1)}, u32[]{:S(2)}, u32[]{:S(2)}) async-start(f32[16,56,128]{2,1,0:T(8,128)} %bitcast.5), calls=%async_computation.3 | async-start | bytes 917504 | tf_op jit(solution)/shard_map/all_to_all | solution.py:259
  103.9 28.2 %collective-permute-start.4 = (f32[52,128]{1,0:T(8,128)S(1)}, f32[52,128]{1,0:T(8,128)S(1)}, u32[]{:S(2)}, u32[]{:S(2)}) collective-permute-start(f32[52,128]{1,0:T(8,128)S(1)} %get-tuple-element.15), channel_id=1, source_target_pairs={{0,0},{1,128},{2,256},{3,384},{4,32},{5,160},{6,288},{7,416},{8,64... | collective-permute-start | bytes 79880 | tf_op jit(solution)/shard_map/ppermute | solution.py:256
  107.0 25.1 %collective-permute-start.5 = (f32[52,128]{1,0:T(8,128)S(1)}, f32[52,128]{1,0:T(8,128)S(1)}, u32[]{:S(2)}, u32[]{:S(2)}) collective-permute-start(f32[52,128]{1,0:T(8,128)S(1)} %get-tuple-element.16), channel_id=1, source_target_pairs={{0,128},{1,0},{2,384},{3,256},{4,160},{5,32},{6,416},{7,288},{8,19... | collective-permute-start | bytes 79880 | tf_op jit(solution)/shard_map/ppermute | solution.py:257

commit v10 on v3

--- a/solution.py
+++ b/solution.py
@@ -94,23 +94,17 @@
                 out[pl.ds(j, CHIPS * PAIRS, stride=ROWS), :] = value
 
 
-def join_kernel(cycle, own, other, out):
-    for place in range(CHIPS):
-        out[place, :BLOCK, :] = cycle[place, :, :]
-        out[place, BLOCK:, :] = own[place, :, :] + other[place, :, :]
-
-
 def sum_kernel(received, out):
-    total = received[0, :BLOCK, :]
+    total = received[0, :, :]
     for place in range(1, CHIPS):
-        total = total + received[place, :BLOCK, :]
+        total = total + received[place, :, :]
     out[...] = total
 
 
-def ladder_kernel(received, integrals, out):
+def ladder_kernel(window, integrals, out):
     lefts = []
     for part in range(2):
-        rows = received[:, BLOCK + part * ROWS : BLOCK + (part + 1) * ROWS, :]
+        rows = window[:, part * ROWS : (part + 1) * ROWS, :]
         lefts.append(rows.reshape(CHIPS * ROWS, LANES))
     left = split(jnp.concatenate(lefts, 1))
     width = PAIRS * LANES
@@ -186,24 +180,25 @@
     copies = jnp.broadcast_to(column.reshape(1, ZL * BLOCK, LANES), (X, ZL * BLOCK, LANES))
     gathered = lax.all_to_all(copies, "x", 0, 0, tiled=True)
     gathered = gathered.reshape(CHIPS * BLOCK, LANES)
+    cycle = call(cycle_kernel, (CHIPS * BLOCK, LANES), [VMEM] * 3)(gathered, cycle_block, other)
+    cycle, gathered = lax.optimization_barrier((cycle, gathered))
+    cycle = lax.all_to_all(cycle.reshape(CHIPS, BLOCK, LANES), ("zh", "y"), 0, 0, tiled=True)
+
     window = call(
         window_kernel,
         (CHIPS * 2 * ROWS, LANES),
         [SMEM, VMEM],
         [(TILE // 2 * ROWS, LANES), (LANES, LANES), (LANES, LANES)],
     )(tiles, gathered)
-    window = window.reshape(CHIPS, 2 * ROWS, LANES)
-    other_window = lax.ppermute(window, "core", [(0, 1), (1, 0)])
-    cycle = call(cycle_kernel, (CHIPS * BLOCK, LANES), [VMEM] * 3)(gathered, cycle_block, other)
-    cycle = cycle.reshape(CHIPS, BLOCK, LANES)
-    joined = (CHIPS, BLOCK + 2 * ROWS, LANES)
-    joined = call(join_kernel, joined, [VMEM] * 3)(cycle, window, other_window)
-    received = lax.all_to_all(joined, ("zh", "y"), 0, 0, tiled=True)
+    window = window + lax.ppermute(window, "core", [(0, 1), (1, 0)])
+    window, cycle = lax.optimization_barrier((window, cycle))
+    window = lax.all_to_all(window.reshape(CHIPS, 2 * ROWS, LANES), ("zh", "y"), 0, 0, tiled=True)
+    cycle = call(sum_kernel, (BLOCK, LANES), [VMEM])(cycle)
+    cycle = lax.ppermute(cycle, EVERY, places(owner_rule))
+    window, cycle = lax.optimization_barrier((window, cycle))
+
     integrals = ladder_block.reshape(-1, ladder_block.shape[2])
-    ladder = call(ladder_kernel, (CHIPS, BLOCK, LANES), [VMEM] * 2)(received, integrals)
-    ladder, received = lax.optimization_barrier((ladder, received))
-    cycle = call(sum_kernel, (BLOCK, LANES), [VMEM])(received)
-    cycle = lax.ppermute(cycle, EVERY, places(owner_rule))
+    ladder = call(ladder_kernel, (CHIPS, BLOCK, LANES), [VMEM] * 2)(window, integrals)
     ladder = lax.all_to_all(ladder, ("zh", "y"), 0, 0, tiled=True)
     return call(last_kernel, amplitudes.shape, [SMEM] * 3 + [VMEM] * 2)(
         tiles, occupied, virtual, ladder, cycle

time: 120 us -> 127 us (1.058)
  the two profiles are of different devices: /device:TPU:110 before, /device:TPU:138 now
where the time goes in v10:
time: 127 us
  blocking collectives  48.1 us (38%)
  waiting for transfers between devices  37.3 us (29%)
  starting transfers between devices  33.2 us (26%)
  Pallas kernels  5.43 us (4%)
  local copies, waits for them, and re-layouts  1.85 us (1%)
    all_to_all x1, blocking collectives, per_device(): ladder = lax.all_to_all(ladder, ('zh', 'y'), 0, 0, tiled=True)  37 us
    all_to_all x1, waiting for transfers between devices, per_device(): lax.all_to_all(cycle.reshape(CHIPS, BLOCK, LANES), ('zh', 'y'), 0, 0, til...  19 us
    all_to_all x1, starting transfers between devices, per_device(): lax.all_to_all(cycle.reshape(CHIPS, BLOCK, LANES), ('zh', 'y'), 0, 0, til...  13.4 us
    all_to_all x1, blocking collectives, per_device(): column = lax.all_to_all(copies, 'zl', 0, 0, tiled=True)  11 us
    ppermute x1, waiting for transfers between devices, per_device(): cycle = lax.ppermute(cycle, EVERY, places(owner_rule))  7.97 us
    all_to_all x1, waiting for transfers between devices, per_device(): gathered = lax.all_to_all(copies, 'x', 0, 0, tiled=True)  7.17 us
    ppermute x1, starting transfers between devices, per_device(): cycle = lax.ppermute(cycle, EVERY, places(owner_rule))  6.04 us
    all_to_all x1, starting transfers between devices, per_device(): lax.all_to_all(window.reshape(CHIPS, 2 * ROWS, LANES), ('zh', 'y'), 0, 0,...  5.11 us
  transfers between devices with their start and end apart: 6, of which 5 were waited for; matrix products, arithmetic and copies ran while one was open for 1% of the time, Pallas kernels for 1%

profile of v10, /device:TPU:138, one launch (start us, length us, event | category | flops | bytes accessed | tf_op | source)
XLA Modules:
  0.0 126.6 jit_solution(16315735466752725938)
XLA Ops:
  0.0 0.0 copy-start.1
  0.0 0.0 copy-start.2
  0.0 0.9 copy-done.2
  0.9 11.0 %all_to_all.25 = f32[4,104,128]{2,1,0:T(8,128)S(1)} all-to-all(f32[4,104,128]{2,1,0:T(8,128)S(1)} %shard_map.64), channel_id=1, replica_groups=mesh['zl'=4,'x'=4,'core'=2,'zh'=2,'y'=8] {'zl'}, dimensions={0} | all-to-all | bytes 425984 | tf_op jit(solution)/shard_map/all_to_all | solution.py:179
  11.9 1.0 broadcast_in_dim.8
  12.9 4.8 %all-to-all-start.1 = ((f32[4,416,128]{2,1,0:T(8,128)}), f32[4,416,128]{2,1,0:T(8,128)S(1)}, u32[]{:S(2)}, u32[]{:S(2)}) async-start(f32[4,416,128]{2,1,0:T(8,128)} %broadcast_in_dim.8), calls=%async_computation.1 | async-start | bytes 1703936 | tf_op jit(solution)/shard_map/all_to_all | solution.py:181
  17.7 0.0 copy-done.1
  17.7 1.9 %collective-permute-start = (f32[512,256]{1,0:T(8,128)S(1)}, f32[512,256]{1,0:T(8,128)S(1)}, u32[]{:S(2)}, u32[]{:S(2)}) collective-permute-start(f32[512,256]{1,0:T(8,128)S(1)} %copy-done.1), channel_id=1, source_target_pairs={{0,16},{16,0},{1,17},{17,1},{2,18},{18,2},{3,19},{19,3},{4,20},{20... | collective-permute-start | bytes 1572872 | tf_op jit(solution)/shard_map/ppermute | solution.py:177
  19.6 1.9 %collective-permute-done.other = f32[512,256]{1,0:T(8,128)S(1)} collective-permute-done((f32[512,256]{1,0:T(8,128)S(1)}, f32[512,256]{1,0:T(8,128)S(1)}, u32[]{:S(2)}, u32[]{:S(2)}) %collective-permute-start) | collective-permute-done | bytes 524320 | tf_op jit(solution)/shard_map/ppermute | solution.py:177
  21.5 7.2 %all-to-all-done.1 = f32[4,416,128]{2,1,0:T(8,128)S(1)} async-done(((f32[4,416,128]{2,1,0:T(8,128)}), f32[4,416,128]{2,1,0:T(8,128)S(1)}, u32[]{:S(2)}, u32[]{:S(2)}) %all-to-all-start.1) | async-done | bytes 852000 | tf_op jit(solution)/shard_map/all_to_all | solution.py:181
  28.7 0.0 copy-start.4
  28.7 2.0 %shard_map.65 = f32[1664,128]{1,0:T(8,128)} custom-call(f32[1664,128]{1,0:T(8,128)S(1)} %bitcast.5, f32[512,256]{1,0:T(8,128)S(1)} %copy-done.1, f32[512,256]{1,0:T(8,128)S(1)} %collective-permute-done.other), custom_call_target="tpu_custom_call" | custom-call | tf_op jit(solution)/shard_map/pallas_call | solution.py:183
  30.7 0.0 copy-start
  30.7 13.4 %all-to-all-start.2 = ((f32[16,104,128]{2,1,0:T(8,128)}), f32[16,104,128]{2,1,0:T(8,128)S(1)}, u32[]{:S(2)}, u32[]{:S(2)}) async-start(f32[16,104,128]{2,1,0:T(8,128)} %bitcast.2), calls=%async_computation.2 | async-start | bytes 1703936 | tf_op jit(solution)/shard_map/all_to_all | solution.py:185
  44.2 0.0 copy-done.4
  44.2 1.4 %shard_map.66 = f32[256,128]{1,0:T(8,128)S(1)} custom-call(s32[2]{0:T(128)S(1)} %copy-done.4, f32[1664,128]{1,0:T(8,128)S(1)} %bitcast.6), custom_call_target="tpu_custom_call" | custom-call | tf_op jit(solution)/shard_map/pallas_call | solution.py:187
  45.6 1.9 %collective-permute-start.1 = (f32[256,128]{1,0:T(8,128)S(1)}, f32[256,128]{1,0:T(8,128)S(1)}, u32[]{:S(2)}, u32[]{:S(2)}) collective-permute-start(f32[256,128]{1,0:T(8,128)S(1)} %shard_map.66), channel_id=1, source_target_pairs={{0,16},{16,0},{1,17},{17,1},{2,18},{18,2},{3,19},{19,3},{4,20},{20... | collective-permute-start | bytes 393224 | tf_op jit(solution)/shard_map/ppermute | solution.py:193
  47.5 1.3 %collective-permute-done.1 = f32[256,128]{1,0:T(8,128)S(1)} collective-permute-done((f32[256,128]{1,0:T(8,128)S(1)}, f32[256,128]{1,0:T(8,128)S(1)}, u32[]{:S(2)}, u32[]{:S(2)}) %collective-permute-start.1) | collective-permute-done | bytes 131104 | tf_op jit(solution)/shard_map/ppermute | solution.py:193
  48.9 0.7 add.3
  49.5 19.0 %all-to-all-done.2.received = f32[16,104,128]{2,1,0:T(8,128)S(1)} async-done(((f32[16,104,128]{2,1,0:T(8,128)}), f32[16,104,128]{2,1,0:T(8,128)S(1)}, u32[]{:S(2)}, u32[]{:S(2)}) %all-to-all-start.2) | async-done | bytes 852000 | tf_op jit(solution)/shard_map/all_to_all | solution.py:185
  68.5 5.1 %all-to-all-start.3 = ((f32[16,16,128]{2,1,0:T(8,128)}), f32[16,16,128]{2,1,0:T(8,128)S(1)}, u32[]{:S(2)}, u32[]{:S(2)}) async-start(f32[16,16,128]{2,1,0:T(8,128)} %bitcast.3), calls=%async_computation.3 | async-start | bytes 262144 | tf_op jit(solution)/shard_map/all_to_all | solution.py:195
  73.6 6.0 %collective-permute-start.2 = (f32[104,128]{1,0:T(8,128)S(1)}, f32[104,128]{1,0:T(8,128)S(1)}, u32[]{:S(2)}, u32[]{:S(2)}) collective-permute-start(f32[104,128]{1,0:T(8,128)S(1)} %shard_map.67), channel_id=1, source_target_pairs={{0,0},{1,128},{2,256},{3,384},{4,32},{5,160},{6,288},{7,416},{8,64... | collective-permute-start | bytes 159752 | tf_op jit(solution)/shard_map/ppermute | solution.py:197
  79.7 8.0 %collective-permute-done.2.cycle = f32[104,128]{1,0:T(8,128)S(1)} collective-permute-done((f32[104,128]{1,0:T(8,128)S(1)}, f32[104,128]{1,0:T(8,128)S(1)}, u32[]{:S(2)}, u32[]{:S(2)}) %collective-permute-start.2) | collective-permute-done | bytes 53280 | tf_op jit(solution)/shard_map/ppermute | solution.py:197
  87.7 0.0 all-to-all-done.3.window
  87.7 0.0 copy-done
  87.7 0.0 copy-start.3
  87.7 0.0 copy-start.5
  87.7 0.6 shard_map.68
  88.3 37.0 %all_to_all.26.ladder = f32[16,104,128]{2,1,0:T(8,128)S(1)} all-to-all(f32[16,104,128]{2,1,0:T(8,128)S(1)} %shard_map.68), channel_id=1, replica_groups=mesh['zl'=4,'x'=4,'core'=2,'zh'=2,'y'=8] {'zh','y'}, dimensions={0} | all-to-all | bytes 1703936 | tf_op jit(solution)/shard_map/all_to_all | solution.py:202
  125.3 0.0 copy-done.3
  125.3 0.0 copy-done.5
  125.3 1.3 %shard_map.69 = f32[1,8,1664]{2,1,0:T(8,128)} custom-call(s32[2]{0:T(128)S(1)} %copy-done.4, f32[128]{0:T(128)S(1)} %copy-done.5, f32[832]{0:T(1024)S(1)} %copy-done.3, f32[16,104,128]{2,1,0:T(8,128)S(1)} %all_to_all.26.ladder, f32[104,128]{1,0:T(8,128)S(1)} %collective-permute-done.2.cycle), custom_call_target="tpu_custom_call" | custom-call | tf_op jit(solution)/shard_map/pallas_call | solution.py:203
  (2 shorter events, 0.1 us)
Async XLA Ops:
  0.0 17.7 %copy-start.1 = (f32[512,256]{1,0:T(8,128)S(1)}, f32[512,256]{1,0:T(8,128)}, u32[]{:S(2)}) copy-start(f32[512,256]{1,0:T(8,128)} %own.1) | copy-start | bytes 1572868
  0.0 0.9 copy-start.2
  12.9 15.8 %all-to-all-start.1 = ((f32[4,416,128]{2,1,0:T(8,128)}), f32[4,416,128]{2,1,0:T(8,128)S(1)}, u32[]{:S(2)}, u32[]{:S(2)}) async-start(f32[4,416,128]{2,1,0:T(8,128)} %broadcast_in_dim.8), calls=%async_computation.1 | async-start | bytes 1703936 | tf_op jit(solution)/shard_map/all_to_all | solution.py:181
  17.7 3.8 %collective-permute-start = (f32[512,256]{1,0:T(8,128)S(1)}, f32[512,256]{1,0:T(8,128)S(1)}, u32[]{:S(2)}, u32[]{:S(2)}) collective-permute-start(f32[512,256]{1,0:T(8,128)S(1)} %copy-done.1), channel_id=1, source_target_pairs={{0,16},{16,0},{1,17},{17,1},{2,18},{18,2},{3,19},{19,3},{4,20},{20... | collective-permute-start | bytes 1572872 | tf_op jit(solution)/shard_map/ppermute | solution.py:177
  28.7 15.5 %copy-start.4 = (s32[2]{0:T(128)S(1)}, s32[2]{0:T(128)}, u32[]{:S(2)}) copy-start(s32[2]{0:T(128)} %tiles.3) | copy-start | bytes 28
  30.7 56.9 %copy-start = (f32[4,64,1664]{2,1,0:T(8,128)S(1)}, f32[4,64,1664]{2,1,0:T(8,128)}, u32[]{:S(2)}) copy-start(f32[4,64,1664]{2,1,0:T(8,128)} %param.8) | copy-start | bytes 5111812
  30.7 37.7 %all-to-all-start.2 = ((f32[16,104,128]{2,1,0:T(8,128)}), f32[16,104,128]{2,1,0:T(8,128)S(1)}, u32[]{:S(2)}, u32[]{:S(2)}) async-start(f32[16,104,128]{2,1,0:T(8,128)} %bitcast.2), calls=%async_computation.2 | async-start | bytes 1703936 | tf_op jit(solution)/shard_map/all_to_all | solution.py:185
  45.6 3.2 %collective-permute-start.1 = (f32[256,128]{1,0:T(8,128)S(1)}, f32[256,128]{1,0:T(8,128)S(1)}, u32[]{:S(2)}, u32[]{:S(2)}) collective-permute-start(f32[256,128]{1,0:T(8,128)S(1)} %shard_map.66), channel_id=1, source_target_pairs={{0,16},{16,0},{1,17},{17,1},{2,18},{18,2},{3,19},{19,3},{4,20},{20... | collective-permute-start | bytes 393224 | tf_op jit(solution)/shard_map/ppermute | solution.py:193
  68.5 19.2 %all-to-all-start.3 = ((f32[16,16,128]{2,1,0:T(8,128)}), f32[16,16,128]{2,1,0:T(8,128)S(1)}, u32[]{:S(2)}, u32[]{:S(2)}) async-start(f32[16,16,128]{2,1,0:T(8,128)} %bitcast.3), calls=%async_computation.3 | async-start | bytes 262144 | tf_op jit(solution)/shard_map/all_to_all | solution.py:195
  73.6 14.0 %collective-permute-start.2 = (f32[104,128]{1,0:T(8,128)S(1)}, f32[104,128]{1,0:T(8,128)S(1)}, u32[]{:S(2)}, u32[]{:S(2)}) collective-permute-start(f32[104,128]{1,0:T(8,128)S(1)} %shard_map.67), channel_id=1, source_target_pairs={{0,0},{1,128},{2,256},{3,384},{4,32},{5,160},{6,288},{7,416},{8,64... | collective-permute-start | bytes 159752 | tf_op jit(solution)/shard_map/ppermute | solution.py:197
  87.7 37.7 %copy-start.3 = (f32[832]{0:T(1024)S(1)}, f32[832]{0:T(1024)}, u32[]{:S(2)}) copy-start(f32[832]{0:T(1024)} %virtual.1) | copy-start | bytes 9988
  87.7 37.7 %copy-start.5 = (f32[128]{0:T(128)S(1)}, f32[128]{0:T(128)}, u32[]{:S(2)}) copy-start(f32[128]{0:T(128)} %occupied.1) | copy-start | bytes 1540

commit v11 on v7

--- a/solution.py
+++ b/solution.py
@@ -218,7 +218,6 @@
 
 def per_device(amplitudes, cycle_block, ladder_block, occupied, virtual, tiles):
     first = lax.ppermute(cycle_block, ("core", "zh"), [(0, 2), (3, 1), (2, 3), (1, 0)])
-    second = lax.ppermute(first, ("core", "zh"), [(0, 2), (3, 1)])
     integrals = ladder_block.reshape(-1, ladder_block.shape[2])
     start = (1 - lax.axis_index("y") % 2) * (SKIP * LANES)
     side = lax.dynamic_slice_in_dim(integrals, start, SIDE * LANES, 1)
@@ -226,11 +225,14 @@
 
     (copies,) = call(pack_kernel, [(ZH * ZL, BLOCK, LANES)], [VMEM])(amplitudes)
     column = lax.all_to_all(copies, ("zh", "zl"), 0, 0, tiled=True)
+    column, first = lax.optimization_barrier((column, first))
     span = ZH * ZL * BLOCK
     copies = jnp.broadcast_to(column.reshape(1, span, LANES), (X, span, LANES))
     gathered = lax.all_to_all(copies, "x", 0, 0, tiled=True)
     gathered = gathered.reshape(X * span, LANES)
     gathered, side = lax.optimization_barrier((gathered, side))
+
+    second = lax.ppermute(first, ("core", "zh"), [(0, 2), (3, 1)])
 
     (window,) = call(
         window_kernel,

time: 125 us -> 134 us (1.072)
  the two profiles are of different devices: /device:TPU:28 before, /device:TPU:118 now
where the time goes in v11:
time: 134 us; the launch traced here: 133 us
  waiting for transfers between devices  58.2 us (43%)
  starting transfers between devices  38.6 us (29%)
  blocking collectives  24.7 us (18%)
  Pallas kernels  8.08 us (6%)
  local copies, waits for them, and re-layouts  3.16 us (2%)
    all_to_all x1, blocking collectives, per_device(): received = lax.all_to_all(joined, 'y', 0, 0, tiled=True)  24.7 us
    ppermute x1, waiting for transfers between devices, per_device(): lax.ppermute(cycle_block, ('core', 'zh'), [(0, 2), (3, 1), (2, 3), (1, 0)])  23.4 us
    ppermute x1, waiting for transfers between devices, per_device(): near = lax.ppermute(near, EVERY, places(near_rule))  20.8 us
    ppermute x1, waiting for transfers between devices, per_device(): side = lax.ppermute(side, 'y', [(y, y ^ 1) for y in range(Y)])  14.1 us
    all_to_all x1, starting transfers between devices, per_device(): ladder = lax.all_to_all(ladder, ('zh', 'y'), 0, 0, tiled=True)  10.9 us
    all_to_all x1, starting transfers between devices, per_device(): column = lax.all_to_all(copies, ('zh', 'zl'), 0, 0, tiled=True)  9.96 us
    all_to_all x1, starting transfers between devices, per_device(): gathered = lax.all_to_all(copies, 'x', 0, 0, tiled=True)  4.9 us
  transfers between devices with their start and end apart: 9, of which 3 were waited for; matrix products, arithmetic and copies ran while one was open for 0% of the time, Pallas kernels for 3%

profile of v11, /device:TPU:118, one launch (start us, length us, event | category | flops | bytes accessed | tf_op | source)
XLA Modules:
  0.0 132.9 jit_solution(7074740948610806281)
XLA Ops:
  0.0 0.0 copy-start.4
  0.0 0.8 copy-done.4
  0.8 0.8 shard_map.64
  1.6 10.0 %all-to-all-start = ((f32[8,104,128]{2,1,0:T(8,128)}), f32[8,104,128]{2,1,0:T(8,128)S(1)}, u32[]{:S(2)}, u32[]{:S(2)}) async-start(f32[8,104,128]{2,1,0:T(8,128)} %shard_map.64), calls=%async_computation | async-start | bytes 851968 | tf_op jit(solution)/shard_map/all_to_all | solution.py:227
  11.6 1.9 %collective-permute-start = (f32[512,256]{1,0:T(8,128)}, f32[512,256]{1,0:T(8,128)}, u32[]{:S(2)}, u32[]{:S(2)}) collective-permute-start(f32[512,256]{1,0:T(8,128)} %own.1), channel_id=1, source_target_pairs={{0,16},{24,8},{16,24},{8,0},{1,17},{25,9},{17,25},{9,1},{2,18},{26... | collective-permute-start | bytes 1572872 | tf_op jit(solution)/shard_map/ppermute | solution.py:220
  13.5 23.4 %collective-permute-done.first = f32[512,256]{1,0:T(8,128)} collective-permute-done((f32[512,256]{1,0:T(8,128)}, f32[512,256]{1,0:T(8,128)}, u32[]{:S(2)}, u32[]{:S(2)}) %collective-permute-start) | collective-permute-done | bytes 524320 | tf_op jit(solution)/shard_map/ppermute | solution.py:220
  36.8 0.0 all-to-all-done
  36.8 1.3 broadcast_in_dim.8
  38.2 0.0 copy-start
  38.2 4.9 %all-to-all-start.1 = ((f32[4,832,128]{2,1,0:T(8,128)}), f32[4,832,128]{2,1,0:T(8,128)S(1)}, u32[]{:S(2)}, u32[]{:S(2)}) async-start(f32[4,832,128]{2,1,0:T(8,128)} %broadcast_in_dim.8), calls=%async_computation.1 | async-start | bytes 3407872 | tf_op jit(solution)/shard_map/all_to_all | solution.py:231
  43.1 0.0 copy-start.6
  43.1 0.0 copy-done
  43.1 0.1 constant_dynamic-slice_fusion
  43.1 2.6 %collective-permute-start.1 = (f32[256,896]{1,0:T(8,128)S(1)}, f32[256,896]{1,0:T(8,128)S(1)}, u32[]{:S(2)}, u32[]{:S(2)}) collective-permute-start(f32[256,896]{1,0:T(8,128)S(1)} %constant_dynamic-slice_fusion), channel_id=1, source_target_pairs={{0,1},{1,0},{2,3},{3,2},{4,5},{5,4},{6,7},{7,6},{8,9},{9,8},{10,11... | collective-permute-start | bytes 2752520 | tf_op jit(solution)/shard_map/ppermute | solution.py:224
  45.7 2.1 %collective-permute-start.2 = (f32[512,256]{1,0:T(8,128)}, f32[512,256]{1,0:T(8,128)}, u32[]{:S(2)}, u32[]{:S(2)}) collective-permute-start(f32[512,256]{1,0:T(8,128)} %collective-permute-done.first), channel_id=1, source_target_pairs={{0,16},{24,8},{1,17},{25,9},{2,18},{26,10},{3,19},{27,11},{4,20},{... | collective-permute-start | bytes 1572872 | tf_op jit(solution)/shard_map/ppermute | solution.py:235
  47.8 14.1 %collective-permute-done.1.other = f32[256,896]{1,0:T(8,128)S(1)} collective-permute-done((f32[256,896]{1,0:T(8,128)S(1)}, f32[256,896]{1,0:T(8,128)S(1)}, u32[]{:S(2)}, u32[]{:S(2)}) %collective-permute-start.1) | collective-permute-done | bytes 917536 | tf_op jit(solution)/shard_map/ppermute | solution.py:224
  61.9 0.0 copy-start.1
  61.9 0.9 copy-done.1
  62.9 0.0 all-to-all-done.1
  62.9 0.0 copy-start.3
  62.9 0.0 copy-done.6
  62.9 1.8 %shard_map.66 = f32[256,128]{1,0:T(8,128)S(1)} custom-call(s32[2]{0:T(128)S(1)} %copy-done.6, f32[3328,128]{1,0:T(8,128)S(1)} %bitcast.5), custom_call_target="tpu_custom_call" | custom-call | tf_op jit(solution)/shard_map/pallas_call | solution.py:237
  64.7 1.9 %collective-permute-start.3 = (f32[8,32,128]{2,1,0:T(8,128)S(1)}, f32[8,32,128]{2,1,0:T(8,128)S(1)}, u32[]{:S(2)}, u32[]{:S(2)}) collective-permute-start(f32[8,32,128]{2,1,0:T(8,128)S(1)} %bitcast.10), channel_id=1, source_target_pairs={{0,16},{16,0},{1,17},{17,1},{2,18},{18,2},{3,19},{19,3},{4,20},{20... | collective-permute-start | bytes 393224 | tf_op jit(solution)/shard_map/ppermute | solution.py:244
  66.6 0.0 collective-permute-done.2.second
  66.6 0.0 copy-done.3
  66.6 2.6 %shard_map.65 = f32[832,128]{1,0:T(8,128)S(1)} custom-call(f32[3328,128]{1,0:T(8,128)S(1)} %bitcast.6, f32[512,256]{1,0:T(8,128)S(1)} %copy-done.3, f32[512,256]{1,0:T(8,128)} %collective-permute-done.first, f32[512,256]{1,0:T(8,128)} %collective-permute-done.2.second), custom_call_target="tpu_custom_call" | custom-call | tf_op jit(solution)/shard_map/pallas_call | solution.py:245
  69.3 0.0 copy-start.2
  69.3 0.0 collective-permute-done.3.other
  69.3 24.7 %all_to_all.20.received = f32[8,168,128]{2,1,0:T(8,128)S(1)} all-to-all(f32[8,168,128]{2,1,0:T(8,128)S(1)} %shard_map.67), channel_id=1, replica_groups=mesh['zl'=4,'x'=4,'core'=2,'zh'=2,'y'=8] {'y'}, dimensions={0} | all-to-all | bytes 1376256 | tf_op jit(solution)/shard_map/all_to_all | solution.py:251
  94.1 0.0 copy-done.2
  94.1 0.0 copy-start.5
  94.1 0.0 copy-start.7
  94.1 1.5 %shard_map.68 = f32[16,56,128]{2,1,0:T(8,128)} custom-call(f32[8,168,128]{2,1,0:T(8,128)S(1)} %all_to_all.20.received, f32[256,1664]{1,0:T(8,128)S(1)} %bitcast.8, f32[256,896]{1,0:T(8,128)S(1)} %copy-done.2), custom_call_target="tpu_custom_call" | custom-call | tf_op jit(solution)/shard_map/pallas_call | solution.py:252
  95.5 10.9 %all-to-all-start.3 = ((f32[16,56,128]{2,1,0:T(8,128)}), f32[16,56,128]{2,1,0:T(8,128)S(1)}, u32[]{:S(2)}, u32[]{:S(2)}) async-start(f32[16,56,128]{2,1,0:T(8,128)} %shard_map.68), calls=%async_computation.3 | async-start | bytes 917504 | tf_op jit(solution)/shard_map/all_to_all | solution.py:259
  106.4 1.9 %collective-permute-start.4 = (f32[52,128]{1,0:T(8,128)S(1)}, f32[52,128]{1,0:T(8,128)S(1)}, u32[]{:S(2)}, u32[]{:S(2)}) collective-permute-start(f32[52,128]{1,0:T(8,128)S(1)} %get-tuple-element.19), channel_id=1, source_target_pairs={{0,0},{1,256},{2,32},{3,288},{4,64},{5,320},{6,96},{7,352},{8,128}... | collective-permute-start | bytes 79880 | tf_op jit(solution)/shard_map/ppermute | solution.py:257
  108.3 2.5 %collective-permute-start.5 = (f32[52,128]{1,0:T(8,128)S(1)}, f32[52,128]{1,0:T(8,128)S(1)}, u32[]{:S(2)}, u32[]{:S(2)}) collective-permute-start(f32[52,128]{1,0:T(8,128)S(1)} %get-tuple-element.20), channel_id=1, source_target_pairs={{0,128},{1,384},{2,160},{3,416},{4,192},{5,448},{6,224},{7,480},{8... | collective-permute-start | bytes 79880 | tf_op jit(solution)/shard_map/ppermute | solution.py:258
  110.8 20.8 %collective-permute-done.4.near = f32[52,128]{1,0:T(8,128)S(1)} collective-permute-done((f32[52,128]{1,0:T(8,128)S(1)}, f32[52,128]{1,0:T(8,128)S(1)}, u32[]{:S(2)}, u32[]{:S(2)}) %collective-permute-start.4) | collective-permute-done | bytes 26656 | tf_op jit(solution)/shard_map/ppermute | solution.py:257
  131.6 0.0 collective-permute-done.5.far
  131.6 0.0 all-to-all-done.3.ladder
  131.6 0.0 copy-done.5
  131.6 0.0 copy-done.7
  131.6 1.3 shard_map.70
  (2 shorter events, 0.1 us)
Async XLA Ops:
  0.0 0.8 copy-start.4
  1.6 35.2 %all-to-all-start = ((f32[8,104,128]{2,1,0:T(8,128)}), f32[8,104,128]{2,1,0:T(8,128)S(1)}, u32[]{:S(2)}, u32[]{:S(2)}) async-start(f32[8,104,128]{2,1,0:T(8,128)} %shard_map.64), calls=%async_computation | async-start | bytes 851968 | tf_op jit(solution)/shard_map/all_to_all | solution.py:227
  11.6 25.3 %collective-permute-start = (f32[512,256]{1,0:T(8,128)}, f32[512,256]{1,0:T(8,128)}, u32[]{:S(2)}, u32[]{:S(2)}) collective-permute-start(f32[512,256]{1,0:T(8,128)} %own.1), channel_id=1, source_target_pairs={{0,16},{24,8},{16,24},{8,0},{1,17},{25,9},{17,25},{9,1},{2,18},{26... | collective-permute-start | bytes 1572872 | tf_op jit(solution)/shard_map/ppermute | solution.py:220
  38.2 4.9 %copy-start = (f32[4,64,1664]{2,1,0:T(8,128)S(1)}, f32[4,64,1664]{2,1,0:T(8,128)}, u32[]{:S(2)}) copy-start(f32[4,64,1664]{2,1,0:T(8,128)} %param.8) | copy-start | bytes 5111812
  38.2 24.7 %all-to-all-start.1 = ((f32[4,832,128]{2,1,0:T(8,128)}), f32[4,832,128]{2,1,0:T(8,128)S(1)}, u32[]{:S(2)}, u32[]{:S(2)}) async-start(f32[4,832,128]{2,1,0:T(8,128)} %broadcast_in_dim.8), calls=%async_computation.1 | async-start | bytes 3407872 | tf_op jit(solution)/shard_map/all_to_all | solution.py:231
  43.1 19.8 %copy-start.6 = (s32[2]{0:T(128)S(1)}, s32[2]{0:T(128)}, u32[]{:S(2)}) copy-start(s32[2]{0:T(128)} %tiles.3) | copy-start | bytes 28
  43.1 18.8 %collective-permute-start.1 = (f32[256,896]{1,0:T(8,128)S(1)}, f32[256,896]{1,0:T(8,128)S(1)}, u32[]{:S(2)}, u32[]{:S(2)}) collective-permute-start(f32[256,896]{1,0:T(8,128)S(1)} %constant_dynamic-slice_fusion), channel_id=1, source_target_pairs={{0,1},{1,0},{2,3},{3,2},{4,5},{5,4},{6,7},{7,6},{8,9},{9,8},{10,11... | collective-permute-start | bytes 2752520 | tf_op jit(solution)/shard_map/ppermute | solution.py:224
  45.7 20.9 %collective-permute-start.2 = (f32[512,256]{1,0:T(8,128)}, f32[512,256]{1,0:T(8,128)}, u32[]{:S(2)}, u32[]{:S(2)}) collective-permute-start(f32[512,256]{1,0:T(8,128)} %collective-permute-done.first), channel_id=1, source_target_pairs={{0,16},{24,8},{1,17},{25,9},{2,18},{26,10},{3,19},{27,11},{4,20},{... | collective-permute-start | bytes 1572872 | tf_op jit(solution)/shard_map/ppermute | solution.py:235
  61.9 0.9 copy-start.1
  62.9 3.8 %copy-start.3 = (f32[512,256]{1,0:T(8,128)S(1)}, f32[512,256]{1,0:T(8,128)}, u32[]{:S(2)}) copy-start(f32[512,256]{1,0:T(8,128)} %own.1) | copy-start | bytes 1572868
  64.7 4.6 %collective-permute-start.3 = (f32[8,32,128]{2,1,0:T(8,128)S(1)}, f32[8,32,128]{2,1,0:T(8,128)S(1)}, u32[]{:S(2)}, u32[]{:S(2)}) collective-permute-start(f32[8,32,128]{2,1,0:T(8,128)S(1)} %bitcast.10), channel_id=1, source_target_pairs={{0,16},{16,0},{1,17},{17,1},{2,18},{18,2},{3,19},{19,3},{4,20},{20... | collective-permute-start | bytes 393224 | tf_op jit(solution)/shard_map/ppermute | solution.py:244
  69.3 24.8 %copy-start.2 = (f32[256,896]{1,0:T(8,128)S(1)}, f32[256,896]{1,0:T(8,128)}, u32[]{:S(2)}) copy-start(f32[256,896]{1,0:T(8,128)} %copy-done.1) | copy-start | bytes 2752516
  94.1 37.5 %copy-start.5 = (f32[832]{0:T(1024)S(1)}, f32[832]{0:T(1024)}, u32[]{:S(2)}) copy-start(f32[832]{0:T(1024)} %virtual.1) | copy-start | bytes 9988
  94.1 37.5 %copy-start.7 = (f32[128]{0:T(128)S(1)}, f32[128]{0:T(128)}, u32[]{:S(2)}) copy-start(f32[128]{0:T(128)} %occupied.1) | copy-start | bytes 1540
  95.5 36.1 %all-to-all-start.3 = ((f32[16,56,128]{2,1,0:T(8,128)}), f32[16,56,128]{2,1,0:T(8,128)S(1)}, u32[]{:S(2)}, u32[]{:S(2)}) async-start(f32[16,56,128]{2,1,0:T(8,128)} %shard_map.68), calls=%async_computation.3 | async-start | bytes 917504 | tf_op jit(solution)/shard_map/all_to_all | solution.py:259
  106.4 25.2 %collective-permute-start.4 = (f32[52,128]{1,0:T(8,128)S(1)}, f32[52,128]{1,0:T(8,128)S(1)}, u32[]{:S(2)}, u32[]{:S(2)}) collective-permute-start(f32[52,128]{1,0:T(8,128)S(1)} %get-tuple-element.19), channel_id=1, source_target_pairs={{0,0},{1,256},{2,32},{3,288},{4,64},{5,320},{6,96},{7,352},{8,128}... | collective-permute-start | bytes 79880 | tf_op jit(solution)/shard_map/ppermute | solution.py:257
  108.3 23.2 %collective-permute-start.5 = (f32[52,128]{1,0:T(8,128)S(1)}, f32[52,128]{1,0:T(8,128)S(1)}, u32[]{:S(2)}, u32[]{:S(2)}) collective-permute-start(f32[52,128]{1,0:T(8,128)S(1)} %get-tuple-element.20), channel_id=1, source_target_pairs={{0,128},{1,384},{2,160},{3,416},{4,192},{5,448},{6,224},{7,480},{8... | collective-permute-start | bytes 79880 | tf_op jit(solution)/shard_map/ppermute | solution.py:258

commit v12 on v3

--- a/solution.py
+++ b/solution.py
@@ -119,11 +119,26 @@
         result = product(left, split(integrals[:, start:stop]))
         for column in range(start, stop, LANES):
             value = result[:, column - start : column - start + LANES]
-            rows = pl.ds(column // LANES * ROWS, ROWS)
-            out[:, rows, :] = value.reshape(CHIPS, ROWS, LANES)
-
-
-def last_kernel(tiles, occupied, virtual, ladder, cycle, out):
+            for zh in range(ZH):
+                rows = pl.ds(zh * BLOCK + column // LANES * ROWS, ROWS)
+                part = value[zh * Y * ROWS : (zh + 1) * Y * ROWS]
+                out[:, rows, :] = part.reshape(Y, ROWS, LANES)
+
+
+def halves_kernel(received, near, far):
+    first = lax.axis_index("zh") == 0
+    for row in range(0, BLOCK, ROWS):
+        sums = []
+        for start in (row, BLOCK + row):
+            total = received[0, start : start + ROWS, :]
+            for place in range(1, Y):
+                total = total + received[place, start : start + ROWS, :]
+            sums.append(total)
+        near[row : row + ROWS, :] = jnp.where(first, sums[0], sums[1])
+        far[row : row + ROWS, :] = jnp.where(first, sums[1], sums[0])
+
+
+def last_kernel(tiles, occupied, virtual, near, far, cycle, out):
     column = lax.axis_index("zl") * (X * CORE) + lax.axis_index("x") * CORE + lax.axis_index("core")
     row = lax.axis_index("zh") * Y + lax.axis_index("y")
     shape = (ROWS, LANES)
@@ -137,21 +152,19 @@
         rows = jnp.where(line == j, occupied[row * ROWS + j], rows)
     for pair in range(PAIRS):
         piece = pl.ds(pair * ROWS, ROWS)
-        total = cycle[piece, :]
-        for chip in range(CHIPS):
-            total = total + ladder[chip, piece, :]
+        total = cycle[piece, :] + (near[piece, :] + far[piece, :])
         a = column * (2 * PAIRS) + 2 * pair
         energy = jnp.where(lane < TILE, virtual[a], virtual[a + 1]) + spectator
         out[0, :, pair * LANES : (pair + 1) * LANES] = total / (energy - occupied[0] - rows)
 
 
-def call(kernel, shape, specs, scratch=()):
+def call(kernel, shapes, specs, scratch=()):
     return pl.pallas_call(
         kernel,
-        out_shape=jax.ShapeDtypeStruct(shape, jnp.float32),
+        out_shape=[jax.ShapeDtypeStruct(shape, jnp.float32) for shape in shapes],
         in_specs=specs,
-        out_specs=VMEM,
-        scratch_shapes=[pltpu.VMEM(s, jnp.float32) for s in scratch],
+        out_specs=[VMEM] * len(shapes),
+        scratch_shapes=[pltpu.VMEM(shape, jnp.float32) for shape in scratch],
         compiler_params=PARAMS,
     )
 
@@ -180,34 +193,40 @@
 
 
 def per_device(amplitudes, cycle_block, ladder_block, occupied, virtual, tiles):
-    other = lax.ppermute(cycle_block, "core", [(0, 1), (1, 0)])
-    copies = call(pack_kernel, (ZL, BLOCK, LANES), [VMEM])(amplitudes)
+    swap = [(0, 1), (1, 0)]
+    other = lax.ppermute(cycle_block, "core", swap)
+    (copies,) = call(pack_kernel, [(ZL, BLOCK, LANES)], [VMEM])(amplitudes)
     column = lax.all_to_all(copies, "zl", 0, 0, tiled=True)
     copies = jnp.broadcast_to(column.reshape(1, ZL * BLOCK, LANES), (X, ZL * BLOCK, LANES))
     gathered = lax.all_to_all(copies, "x", 0, 0, tiled=True)
     gathered = gathered.reshape(CHIPS * BLOCK, LANES)
-    window = call(
+
+    (window,) = call(
         window_kernel,
-        (CHIPS * 2 * ROWS, LANES),
+        [(CHIPS * 2 * ROWS, LANES)],
         [SMEM, VMEM],
         [(TILE // 2 * ROWS, LANES), (LANES, LANES), (LANES, LANES)],
     )(tiles, gathered)
     window = window.reshape(CHIPS, 2 * ROWS, LANES)
-    other_window = lax.ppermute(window, "core", [(0, 1), (1, 0)])
-    cycle = call(cycle_kernel, (CHIPS * BLOCK, LANES), [VMEM] * 3)(gathered, cycle_block, other)
-    cycle = cycle.reshape(CHIPS, BLOCK, LANES)
-    joined = (CHIPS, BLOCK + 2 * ROWS, LANES)
-    joined = call(join_kernel, joined, [VMEM] * 3)(cycle, window, other_window)
+    other_window = lax.ppermute(window, "core", swap)
+    (cycle,) = call(cycle_kernel, [(CHIPS * BLOCK, LANES)], [VMEM] * 3)(gathered, cycle_block, other)
+    (joined,) = call(join_kernel, [(CHIPS, BLOCK + 2 * ROWS, LANES)], [VMEM] * 3)(
+        cycle.reshape(CHIPS, BLOCK, LANES), window, other_window
+    )
     received = lax.all_to_all(joined, ("zh", "y"), 0, 0, tiled=True)
+
     integrals = ladder_block.reshape(-1, ladder_block.shape[2])
-    ladder = call(ladder_kernel, (CHIPS, BLOCK, LANES), [VMEM] * 2)(received, integrals)
+    (ladder,) = call(ladder_kernel, [(Y, ZH * BLOCK, LANES)], [VMEM] * 2)(received, integrals)
     ladder, received = lax.optimization_barrier((ladder, received))
-    cycle = call(sum_kernel, (BLOCK, LANES), [VMEM])(received)
+    (cycle,) = call(sum_kernel, [(BLOCK, LANES)], [VMEM])(received)
     cycle = lax.ppermute(cycle, EVERY, places(owner_rule))
-    ladder = lax.all_to_all(ladder, ("zh", "y"), 0, 0, tiled=True)
-    return call(last_kernel, amplitudes.shape, [SMEM] * 3 + [VMEM] * 2)(
-        tiles, occupied, virtual, ladder, cycle
-    )
+    ladder = lax.all_to_all(ladder, "y", 0, 0, tiled=True)
+    near, far = call(halves_kernel, [(BLOCK, LANES)] * 2, [VMEM])(ladder)
+    far = lax.ppermute(far, "zh", swap)
+    (result,) = call(last_kernel, [amplitudes.shape], [SMEM] * 3 + [VMEM] * 3)(
+        tiles, occupied, virtual, near, far, cycle
+    )
+    return result
 
 
 def solution(mesh):

time: 120 us -> 123 us (1.025)
  the two profiles are of different devices: /device:TPU:110 before, /device:TPU:14 now
where the time goes in v12:
time: 123 us
  blocking collectives  57.2 us (47%)
  waiting for transfers between devices  35.3 us (29%)
  starting transfers between devices  22.8 us (19%)
  Pallas kernels  5.54 us (5%)
  local copies, waits for them, and re-layouts  1.85 us (2%)
    all_to_all x1, blocking collectives, per_device(): received = lax.all_to_all(joined, ('zh', 'y'), 0, 0, tiled=True)  42.3 us
    all_to_all x1, waiting for transfers between devices, per_device(): ladder = lax.all_to_all(ladder, 'y', 0, 0, tiled=True)  21 us
    all_to_all x1, blocking collectives, per_device(): column = lax.all_to_all(copies, 'zl', 0, 0, tiled=True)  14.9 us
    ppermute x1, waiting for transfers between devices, per_device(): far = lax.ppermute(far, 'zh', swap)  7.55 us
    all_to_all x1, waiting for transfers between devices, per_device(): gathered = lax.all_to_all(copies, 'x', 0, 0, tiled=True)  6.66 us
    ppermute x1, starting transfers between devices, per_device(): cycle = lax.ppermute(cycle, EVERY, places(owner_rule))  5.93 us
    all_to_all x1, starting transfers between devices, per_device(): ladder = lax.all_to_all(ladder, 'y', 0, 0, tiled=True)  5.75 us
    all_to_all x1, starting transfers between devices, per_device(): gathered = lax.all_to_all(copies, 'x', 0, 0, tiled=True)  4.77 us
  transfers between devices with their start and end apart: 6, of which 4 were waited for; matrix products, arithmetic and copies ran while one was open for 0% of the time, Pallas kernels for 2%

profile of v12, /device:TPU:14, one launch (start us, length us, event | category | flops | bytes accessed | tf_op | source)
XLA Modules:
  0.0 122.8 jit_solution(14658471432326767785)
XLA Ops:
  0.0 0.0 copy-start.1
  0.0 0.0 copy-start.2
  0.0 0.9 copy-done.2
  0.9 0.0 copy-start.4
  0.9 14.9 %all_to_all.20 = f32[4,104,128]{2,1,0:T(8,128)S(1)} all-to-all(f32[4,104,128]{2,1,0:T(8,128)S(1)} %shard_map.64), channel_id=1, replica_groups=mesh['zl'=4,'x'=4,'core'=2,'zh'=2,'y'=8] {'zl'}, dimensions={0} | all-to-all | bytes 425984 | tf_op jit(solution)/shard_map/all_to_all | solution.py:199
  15.8 1.0 broadcast_in_dim.8
  16.7 4.8 %all-to-all-start.1 = ((f32[4,416,128]{2,1,0:T(8,128)}), f32[4,416,128]{2,1,0:T(8,128)S(1)}, u32[]{:S(2)}, u32[]{:S(2)}) async-start(f32[4,416,128]{2,1,0:T(8,128)} %broadcast_in_dim.8), calls=%async_computation.1 | async-start | bytes 1703936 | tf_op jit(solution)/shard_map/all_to_all | solution.py:201
  21.5 0.0 copy-done.1
  21.5 1.9 %collective-permute-start = (f32[512,256]{1,0:T(8,128)S(1)}, f32[512,256]{1,0:T(8,128)S(1)}, u32[]{:S(2)}, u32[]{:S(2)}) collective-permute-start(f32[512,256]{1,0:T(8,128)S(1)} %copy-done.1), channel_id=1, source_target_pairs={{0,16},{16,0},{1,17},{17,1},{2,18},{18,2},{3,19},{19,3},{4,20},{20... | collective-permute-start | bytes 1572872 | tf_op jit(solution)/shard_map/ppermute | solution.py:197
  23.4 6.7 %all-to-all-done.1 = f32[4,416,128]{2,1,0:T(8,128)S(1)} async-done(((f32[4,416,128]{2,1,0:T(8,128)}), f32[4,416,128]{2,1,0:T(8,128)S(1)}, u32[]{:S(2)}, u32[]{:S(2)}) %all-to-all-start.1) | async-done | bytes 852000 | tf_op jit(solution)/shard_map/all_to_all | solution.py:201
  30.1 0.0 copy-done.4
  30.1 1.4 %shard_map.66 = f32[256,128]{1,0:T(8,128)S(1)} custom-call(s32[2]{0:T(128)S(1)} %copy-done.4, f32[1664,128]{1,0:T(8,128)S(1)} %bitcast.5), custom_call_target="tpu_custom_call" | custom-call | tf_op jit(solution)/shard_map/pallas_call | solution.py:204
  31.5 1.9 %collective-permute-start.1 = (f32[16,16,128]{2,1,0:T(8,128)S(1)}, f32[16,16,128]{2,1,0:T(8,128)S(1)}, u32[]{:S(2)}, u32[]{:S(2)}) collective-permute-start(f32[16,16,128]{2,1,0:T(8,128)S(1)} %bitcast.9), channel_id=1, source_target_pairs={{0,16},{16,0},{1,17},{17,1},{2,18},{18,2},{3,19},{19,3},{4,20},{20... | collective-permute-start | bytes 393224 | tf_op jit(solution)/shard_map/ppermute | solution.py:211
  33.4 0.0 collective-permute-done.other
  33.5 1.1 shard_map.65
  34.6 0.2 collective-permute-done.1.other
  34.8 0.0 copy-start
  34.8 0.1 shard_map.67
  34.8 42.3 %all_to_all.21.received = f32[16,120,128]{2,1,0:T(8,128)S(1)} all-to-all(f32[16,120,128]{2,1,0:T(8,128)S(1)} %shard_map.67), channel_id=1, replica_groups=mesh['zl'=4,'x'=4,'core'=2,'zh'=2,'y'=8] {'zh','y'}, dimensions={0} | all-to-all | bytes 1966080 | tf_op jit(solution)/shard_map/all_to_all | solution.py:216
  77.2 0.0 copy-done
  77.2 1.5 %shard_map.68 = f32[8,208,128]{2,1,0:T(8,128)} custom-call(f32[16,120,128]{2,1,0:T(8,128)S(1)} %all_to_all.21.received, f32[256,1664]{1,0:T(8,128)S(1)} %bitcast.8), custom_call_target="tpu_custom_call" | custom-call | tf_op jit(solution)/shard_map/pallas_call | solution.py:219
  78.7 0.0 copy-start.3
  78.7 0.0 copy-start.5
  78.7 5.8 %all-to-all-start.3 = ((f32[8,208,128]{2,1,0:T(8,128)}), f32[8,208,128]{2,1,0:T(8,128)S(1)}, u32[]{:S(2)}, u32[]{:S(2)}) async-start(f32[8,208,128]{2,1,0:T(8,128)} %shard_map.68), calls=%async_computation.3 | async-start | bytes 1703936 | tf_op jit(solution)/shard_map/all_to_all | solution.py:223
  84.5 5.9 %collective-permute-start.3 = (f32[104,128]{1,0:T(8,128)S(1)}, f32[104,128]{1,0:T(8,128)S(1)}, u32[]{:S(2)}, u32[]{:S(2)}) collective-permute-start(f32[104,128]{1,0:T(8,128)S(1)} %shard_map.70), channel_id=1, source_target_pairs={{0,0},{1,128},{2,256},{3,384},{4,32},{5,160},{6,288},{7,416},{8,64... | collective-permute-start | bytes 159752 | tf_op jit(solution)/shard_map/ppermute | solution.py:222
  90.4 21.0 %all-to-all-done.3.received = f32[8,208,128]{2,1,0:T(8,128)S(1)} async-done(((f32[8,208,128]{2,1,0:T(8,128)}), f32[8,208,128]{2,1,0:T(8,128)S(1)}, u32[]{:S(2)}, u32[]{:S(2)}) %all-to-all-start.3) | async-done | bytes 852000 | tf_op jit(solution)/shard_map/all_to_all | solution.py:223
  111.4 2.5 %collective-permute-start.2 = (f32[104,128]{1,0:T(8,128)S(1)}, f32[104,128]{1,0:T(8,128)S(1)}, u32[]{:S(2)}, u32[]{:S(2)}) collective-permute-start(f32[104,128]{1,0:T(8,128)S(1)} %get-tuple-element.11), channel_id=1, source_target_pairs={{0,8},{8,0},{1,9},{9,1},{2,10},{10,2},{3,11},{11,3},{4,12},{12,4},... | collective-permute-start | bytes 159752 | tf_op jit(solution)/shard_map/ppermute | solution.py:225
  114.0 0.0 collective-permute-done.3.cycle
  114.0 7.5 %collective-permute-done.2.far = f32[104,128]{1,0:T(8,128)S(1)} collective-permute-done((f32[104,128]{1,0:T(8,128)S(1)}, f32[104,128]{1,0:T(8,128)S(1)}, u32[]{:S(2)}, u32[]{:S(2)}) %collective-permute-start.2) | collective-permute-done | bytes 53280 | tf_op jit(solution)/shard_map/ppermute | solution.py:225
  121.5 0.0 copy-done.3
  121.5 0.0 copy-done.5
  121.5 1.3 %shard_map.71 = f32[1,8,1664]{2,1,0:T(8,128)} custom-call(s32[2]{0:T(128)S(1)} %copy-done.4, f32[128]{0:T(128)S(1)} %copy-done.5, f32[832]{0:T(1024)S(1)} %copy-done.3, f32[104,128]{1,0:T(8,128)S(1)} %get-tuple-element.10.near, f32[104,128]{1,0:T(8,128)S(1)} %collective-permute-done.2.far, f32[104,128]{1,0:T(8,128)S(1)} %collective-permute-done.3.cycle), custom_call_target="tpu_custom_call" | custom-call | tf_op jit(solution)/shard_map/pallas_call | solution.py:226
  (3 shorter events, 0.1 us)
Async XLA Ops:
  0.0 21.5 %copy-start.1 = (f32[512,256]{1,0:T(8,128)S(1)}, f32[512,256]{1,0:T(8,128)}, u32[]{:S(2)}) copy-start(f32[512,256]{1,0:T(8,128)} %own.1) | copy-start | bytes 1572868
  0.0 0.9 copy-start.2
  0.9 29.2 %copy-start.4 = (s32[2]{0:T(128)S(1)}, s32[2]{0:T(128)}, u32[]{:S(2)}) copy-start(s32[2]{0:T(128)} %tiles.3) | copy-start | bytes 28
  16.7 13.3 %all-to-all-start.1 = ((f32[4,416,128]{2,1,0:T(8,128)}), f32[4,416,128]{2,1,0:T(8,128)S(1)}, u32[]{:S(2)}, u32[]{:S(2)}) async-start(f32[4,416,128]{2,1,0:T(8,128)} %broadcast_in_dim.8), calls=%async_computation.1 | async-start | bytes 1703936 | tf_op jit(solution)/shard_map/all_to_all | solution.py:201
  21.5 11.9 %collective-permute-start = (f32[512,256]{1,0:T(8,128)S(1)}, f32[512,256]{1,0:T(8,128)S(1)}, u32[]{:S(2)}, u32[]{:S(2)}) collective-permute-start(f32[512,256]{1,0:T(8,128)S(1)} %copy-done.1), channel_id=1, source_target_pairs={{0,16},{16,0},{1,17},{17,1},{2,18},{18,2},{3,19},{19,3},{4,20},{20... | collective-permute-start | bytes 1572872 | tf_op jit(solution)/shard_map/ppermute | solution.py:197
  31.5 3.2 %collective-permute-start.1 = (f32[16,16,128]{2,1,0:T(8,128)S(1)}, f32[16,16,128]{2,1,0:T(8,128)S(1)}, u32[]{:S(2)}, u32[]{:S(2)}) collective-permute-start(f32[16,16,128]{2,1,0:T(8,128)S(1)} %bitcast.9), channel_id=1, source_target_pairs={{0,16},{16,0},{1,17},{17,1},{2,18},{18,2},{3,19},{19,3},{4,20},{20... | collective-permute-start | bytes 393224 | tf_op jit(solution)/shard_map/ppermute | solution.py:211
  34.8 42.4 %copy-start = (f32[4,64,1664]{2,1,0:T(8,128)S(1)}, f32[4,64,1664]{2,1,0:T(8,128)}, u32[]{:S(2)}) copy-start(f32[4,64,1664]{2,1,0:T(8,128)} %param.8) | copy-start | bytes 5111812
  78.7 42.8 %copy-start.3 = (f32[832]{0:T(1024)S(1)}, f32[832]{0:T(1024)}, u32[]{:S(2)}) copy-start(f32[832]{0:T(1024)} %virtual.1) | copy-start | bytes 9988
  78.7 42.8 %copy-start.5 = (f32[128]{0:T(128)S(1)}, f32[128]{0:T(128)}, u32[]{:S(2)}) copy-start(f32[128]{0:T(128)} %occupied.1) | copy-start | bytes 1540
  78.7 32.7 %all-to-all-start.3 = ((f32[8,208,128]{2,1,0:T(8,128)}), f32[8,208,128]{2,1,0:T(8,128)S(1)}, u32[]{:S(2)}, u32[]{:S(2)}) async-start(f32[8,208,128]{2,1,0:T(8,128)} %shard_map.68), calls=%async_computation.3 | async-start | bytes 1703936 | tf_op jit(solution)/shard_map/all_to_all | solution.py:223
  84.5 29.5 %collective-permute-start.3 = (f32[104,128]{1,0:T(8,128)S(1)}, f32[104,128]{1,0:T(8,128)S(1)}, u32[]{:S(2)}, u32[]{:S(2)}) collective-permute-start(f32[104,128]{1,0:T(8,128)S(1)} %shard_map.70), channel_id=1, source_target_pairs={{0,0},{1,128},{2,256},{3,384},{4,32},{5,160},{6,288},{7,416},{8,64... | collective-permute-start | bytes 159752 | tf_op jit(solution)/shard_map/ppermute | solution.py:222
  111.4 10.1 %collective-permute-start.2 = (f32[104,128]{1,0:T(8,128)S(1)}, f32[104,128]{1,0:T(8,128)S(1)}, u32[]{:S(2)}, u32[]{:S(2)}) collective-permute-start(f32[104,128]{1,0:T(8,128)S(1)} %get-tuple-element.11), channel_id=1, source_target_pairs={{0,8},{8,0},{1,9},{9,1},{2,10},{10,2},{3,11},{11,3},{4,12},{12,4},... | collective-permute-start | bytes 159752 | tf_op jit(solution)/shard_map/ppermute | solution.py:225

commit v13 on v10

--- a/solution.py
+++ b/solution.py
@@ -43,6 +43,10 @@
     )
 
 
+def block_of(chip):
+    return chip % X * ZL + chip // X
+
+
 def pack_kernel(amplitudes, out):
     for pair in range(PAIRS):
         tile = amplitudes[0, :, pair * LANES : (pair + 1) * LANES]
@@ -55,9 +59,7 @@
     for pair in range(TILE // 2):
         place = tiles[1] * (TILE // 2) + pair
         owner = place // PAIRS
-        chip = owner // CORE
-        block = (chip % X) * ZL + chip // X
-        row = (block * PAIRS + (place - owner * PAIRS)) * ROWS
+        row = (block_of(owner // CORE) * PAIRS + (place - owner * PAIRS)) * ROWS
         tile = gathered[pl.ds(pl.multiple_of(row, ROWS), ROWS), :]
         window[pair * ROWS : (pair + 1) * ROWS, :] = jnp.where(owner % 2 == core, tile, 0.0)
     for half in range(ROWS // 2):
@@ -94,14 +96,7 @@
                 out[pl.ds(j, CHIPS * PAIRS, stride=ROWS), :] = value
 
 
-def sum_kernel(received, out):
-    total = received[0, :, :]
-    for place in range(1, CHIPS):
-        total = total + received[place, :, :]
-    out[...] = total
-
-
-def ladder_kernel(window, integrals, out):
+def ladder_kernel(window, integrals, cycle, out):
     lefts = []
     for part in range(2):
         rows = window[:, part * ROWS : (part + 1) * ROWS, :]
@@ -114,10 +109,12 @@
         for column in range(start, stop, LANES):
             value = result[:, column - start : column - start + LANES]
             rows = pl.ds(column // LANES * ROWS, ROWS)
-            out[:, rows, :] = value.reshape(CHIPS, ROWS, LANES)
+            for chip in range(CHIPS):
+                part = value[chip * ROWS : (chip + 1) * ROWS]
+                out[chip, rows, :] = part + cycle[block_of(chip), rows, :]
 
 
-def last_kernel(tiles, occupied, virtual, ladder, cycle, out):
+def last_kernel(tiles, occupied, virtual, parts, out):
     column = lax.axis_index("zl") * (X * CORE) + lax.axis_index("x") * CORE + lax.axis_index("core")
     row = lax.axis_index("zh") * Y + lax.axis_index("y")
     shape = (ROWS, LANES)
@@ -131,9 +128,9 @@
         rows = jnp.where(line == j, occupied[row * ROWS + j], rows)
     for pair in range(PAIRS):
         piece = pl.ds(pair * ROWS, ROWS)
-        total = cycle[piece, :]
-        for chip in range(CHIPS):
-            total = total + ladder[chip, piece, :]
+        total = parts[0, piece, :]
+        for place in range(1, ZH * Y):
+            total = total + parts[place, piece, :]
         a = column * (2 * PAIRS) + 2 * pair
         energy = jnp.where(lane < TILE, virtual[a], virtual[a + 1]) + spectator
         out[0, :, pair * LANES : (pair + 1) * LANES] = total / (energy - occupied[0] - rows)
@@ -150,29 +147,6 @@
     )
 
 
-def places(rule):
-    pairs = []
-    for chip in range(CHIPS):
-        for core in range(CORE):
-            for place in range(ZH * Y):
-                to = rule(chip, core, place)
-                pairs.append(
-                    (
-                        (chip * CORE + core) * ZH * Y + place,
-                        (to[0] * CORE + to[1]) * ZH * Y + to[2],
-                    )
-                )
-    return pairs
-
-
-def chip_of(block):
-    return block % ZL * X + block // ZL
-
-
-def owner_rule(chip, core, place):
-    return chip_of(place), core, chip
-
-
 def per_device(amplitudes, cycle_block, ladder_block, occupied, virtual, tiles):
     other = lax.ppermute(cycle_block, "core", [(0, 1), (1, 0)])
     copies = call(pack_kernel, (ZL, BLOCK, LANES), [VMEM])(amplitudes)
@@ -182,7 +156,7 @@
     gathered = gathered.reshape(CHIPS * BLOCK, LANES)
     cycle = call(cycle_kernel, (CHIPS * BLOCK, LANES), [VMEM] * 3)(gathered, cycle_block, other)
     cycle, gathered = lax.optimization_barrier((cycle, gathered))
-    cycle = lax.all_to_all(cycle.reshape(CHIPS, BLOCK, LANES), ("zh", "y"), 0, 0, tiled=True)
+    cycle = lax.all_to_all(cycle.reshape(CHIPS, BLOCK, LANES), ("x", "zl"), 0, 0, tiled=True)
 
     window = call(
         window_kernel,
@@ -193,15 +167,12 @@
     window = window + lax.ppermute(window, "core", [(0, 1), (1, 0)])
     window, cycle = lax.optimization_barrier((window, cycle))
     window = lax.all_to_all(window.reshape(CHIPS, 2 * ROWS, LANES), ("zh", "y"), 0, 0, tiled=True)
-    cycle = call(sum_kernel, (BLOCK, LANES), [VMEM])(cycle)
-    cycle = lax.ppermute(cycle, EVERY, places(owner_rule))
-    window, cycle = lax.optimization_barrier((window, cycle))
 
     integrals = ladder_block.reshape(-1, ladder_block.shape[2])
-    ladder = call(ladder_kernel, (CHIPS, BLOCK, LANES), [VMEM] * 2)(window, integrals)
-    ladder = lax.all_to_all(ladder, ("zh", "y"), 0, 0, tiled=True)
-    return call(last_kernel, amplitudes.shape, [SMEM] * 3 + [VMEM] * 2)(
-        tiles, occupied, virtual, ladder, cycle
+    parts = call(ladder_kernel, (CHIPS, BLOCK, LANES), [VMEM] * 3)(window, integrals, cycle)
+    parts = lax.all_to_all(parts, ("zh", "y"), 0, 0, tiled=True)
+    return call(last_kernel, amplitudes.shape, [SMEM] * 3 + [VMEM])(
+        tiles, occupied, virtual, parts
     )
 
 

time: 127 us -> 117 us (0.921)
  the two profiles are of different devices: /device:TPU:138 before, /device:TPU:8 now
where the time goes in v13:
time: 117 us; the launch traced here: 116 us
  blocking collectives  67.9 us (58%)
  waiting for transfers between devices  27.4 us (23%)
  starting transfers between devices  13.7 us (12%)
  Pallas kernels  5.4 us (5%)
  local copies, waits for them, and re-layouts  1.87 us (2%)
    all_to_all x1, blocking collectives, per_device(): parts = lax.all_to_all(parts, ('zh', 'y'), 0, 0, tiled=True)  28 us
    all_to_all x1, blocking collectives, per_device(): lax.all_to_all(window.reshape(CHIPS, 2 * ROWS, LANES), ('zh', 'y'), 0, 0,...  25 us
    all_to_all x1, waiting for transfers between devices, per_device(): lax.all_to_all(cycle.reshape(CHIPS, BLOCK, LANES), ('x', 'zl'), 0, 0, til...  17.3 us
    all_to_all x1, blocking collectives, per_device(): column = lax.all_to_all(copies, 'zl', 0, 0, tiled=True)  14.9 us
    all_to_all x1, waiting for transfers between devices, per_device(): gathered = lax.all_to_all(copies, 'x', 0, 0, tiled=True)  6.84 us
    all_to_all x1, starting transfers between devices, per_device(): lax.all_to_all(cycle.reshape(CHIPS, BLOCK, LANES), ('x', 'zl'), 0, 0, til...  5.59 us
    all_to_all x1, starting transfers between devices, per_device(): gathered = lax.all_to_all(copies, 'x', 0, 0, tiled=True)  4.29 us
  transfers between devices with their start and end apart: 4, of which 4 were waited for; matrix products, arithmetic and copies ran while one was open for 0% of the time, Pallas kernels for 1%

profile of v13, /device:TPU:8, one launch (start us, length us, event | category | flops | bytes accessed | tf_op | source)
XLA Modules:
  0.0 116.3 jit_solution(2255772358076751807)
XLA Ops:
  0.0 0.0 copy-start.1
  0.0 0.0 copy-start.2
  0.0 0.9 copy-done.2
  0.9 14.9 %all_to_all.25 = f32[4,104,128]{2,1,0:T(8,128)S(1)} all-to-all(f32[4,104,128]{2,1,0:T(8,128)S(1)} %shard_map.64), channel_id=1, replica_groups=mesh['zl'=4,'x'=4,'core'=2,'zh'=2,'y'=8] {'zl'}, dimensions={0} | all-to-all | bytes 425984 | tf_op jit(solution)/shard_map/all_to_all | solution.py:153
  15.8 1.0 broadcast_in_dim.8
  16.7 4.3 %all-to-all-start.1 = ((f32[4,416,128]{2,1,0:T(8,128)}), f32[4,416,128]{2,1,0:T(8,128)S(1)}, u32[]{:S(2)}, u32[]{:S(2)}) async-start(f32[4,416,128]{2,1,0:T(8,128)} %broadcast_in_dim.8), calls=%async_computation.1 | async-start | bytes 1703936 | tf_op jit(solution)/shard_map/all_to_all | solution.py:155
  21.0 0.0 copy-done.1
  21.0 1.9 %collective-permute-start = (f32[512,256]{1,0:T(8,128)S(1)}, f32[512,256]{1,0:T(8,128)S(1)}, u32[]{:S(2)}, u32[]{:S(2)}) collective-permute-start(f32[512,256]{1,0:T(8,128)S(1)} %copy-done.1), channel_id=1, source_target_pairs={{0,16},{16,0},{1,17},{17,1},{2,18},{18,2},{3,19},{19,3},{4,20},{20... | collective-permute-start | bytes 1572872 | tf_op jit(solution)/shard_map/ppermute | solution.py:151
  23.0 1.9 %collective-permute-done.other = f32[512,256]{1,0:T(8,128)S(1)} collective-permute-done((f32[512,256]{1,0:T(8,128)S(1)}, f32[512,256]{1,0:T(8,128)S(1)}, u32[]{:S(2)}, u32[]{:S(2)}) %collective-permute-start) | collective-permute-done | bytes 524320 | tf_op jit(solution)/shard_map/ppermute | solution.py:151
  24.8 6.8 %all-to-all-done.1 = f32[4,416,128]{2,1,0:T(8,128)S(1)} async-done(((f32[4,416,128]{2,1,0:T(8,128)}), f32[4,416,128]{2,1,0:T(8,128)S(1)}, u32[]{:S(2)}, u32[]{:S(2)}) %all-to-all-start.1) | async-done | bytes 852000 | tf_op jit(solution)/shard_map/all_to_all | solution.py:155
  31.7 0.0 copy-start.4
  31.7 2.1 %shard_map.65 = f32[1664,128]{1,0:T(8,128)} custom-call(f32[1664,128]{1,0:T(8,128)S(1)} %bitcast.5, f32[512,256]{1,0:T(8,128)S(1)} %copy-done.1, f32[512,256]{1,0:T(8,128)S(1)} %collective-permute-done.other), custom_call_target="tpu_custom_call" | custom-call | tf_op jit(solution)/shard_map/pallas_call | solution.py:157
  33.7 0.0 copy-start
  33.7 5.6 %all-to-all-start.2 = ((f32[16,104,128]{2,1,0:T(8,128)}), f32[16,104,128]{2,1,0:T(8,128)S(1)}, u32[]{:S(2)}, u32[]{:S(2)}) async-start(f32[16,104,128]{2,1,0:T(8,128)} %bitcast.2), calls=%async_computation.2 | async-start | bytes 1703936 | tf_op jit(solution)/shard_map/all_to_all | solution.py:159
  39.3 0.0 copy-done.4
  39.3 1.4 %shard_map.66 = f32[256,128]{1,0:T(8,128)S(1)} custom-call(s32[2]{0:T(128)S(1)} %copy-done.4, f32[1664,128]{1,0:T(8,128)S(1)} %bitcast.6), custom_call_target="tpu_custom_call" | custom-call | tf_op jit(solution)/shard_map/pallas_call | solution.py:161
  40.8 1.9 %collective-permute-start.1 = (f32[256,128]{1,0:T(8,128)S(1)}, f32[256,128]{1,0:T(8,128)S(1)}, u32[]{:S(2)}, u32[]{:S(2)}) collective-permute-start(f32[256,128]{1,0:T(8,128)S(1)} %shard_map.66), channel_id=1, source_target_pairs={{0,16},{16,0},{1,17},{17,1},{2,18},{18,2},{3,19},{19,3},{4,20},{20... | collective-permute-start | bytes 393224 | tf_op jit(solution)/shard_map/ppermute | solution.py:167
  42.7 1.3 %collective-permute-done.1 = f32[256,128]{1,0:T(8,128)S(1)} collective-permute-done((f32[256,128]{1,0:T(8,128)S(1)}, f32[256,128]{1,0:T(8,128)S(1)}, u32[]{:S(2)}, u32[]{:S(2)}) %collective-permute-start.1) | collective-permute-done | bytes 131104 | tf_op jit(solution)/shard_map/ppermute | solution.py:167
  44.0 17.3 %all-to-all-done.2.cycle = f32[16,104,128]{2,1,0:T(8,128)S(1)} async-done(((f32[16,104,128]{2,1,0:T(8,128)}), f32[16,104,128]{2,1,0:T(8,128)S(1)}, u32[]{:S(2)}, u32[]{:S(2)}) %all-to-all-start.2) | async-done | bytes 852000 | tf_op jit(solution)/shard_map/all_to_all | solution.py:159
  61.4 25.0 %all_to_all.26.window = f32[16,16,128]{2,1,0:T(8,128)S(1)} all-to-all(f32[16,16,128]{2,1,0:T(8,128)S(1)} %bitcast.9), channel_id=1, replica_groups=mesh['zl'=4,'x'=4,'core'=2,'zh'=2,'y'=8] {'zh','y'}, dimensions={0} | all-to-all | bytes 262144 | tf_op jit(solution)/shard_map/all_to_all | solution.py:169
  86.4 0.0 copy-done
  86.4 0.6 shard_map.67
  87.0 0.0 copy-start.3
  87.0 0.0 copy-start.5
  87.0 28.0 %all_to_all.27.parts = f32[16,104,128]{2,1,0:T(8,128)S(1)} all-to-all(f32[16,104,128]{2,1,0:T(8,128)S(1)} %shard_map.67), channel_id=1, replica_groups=mesh['zl'=4,'x'=4,'core'=2,'zh'=2,'y'=8] {'zh','y'}, dimensions={0} | all-to-all | bytes 1703936 | tf_op jit(solution)/shard_map/all_to_all | solution.py:173
  115.0 0.0 copy-done.3
  115.0 0.0 copy-done.5
  115.0 1.3 %shard_map.68 = f32[1,8,1664]{2,1,0:T(8,128)} custom-call(s32[2]{0:T(128)S(1)} %copy-done.4, f32[128]{0:T(128)S(1)} %copy-done.5, f32[832]{0:T(1024)S(1)} %copy-done.3, f32[16,104,128]{2,1,0:T(8,128)S(1)} %all_to_all.27.parts), custom_call_target="tpu_custom_call" | custom-call | tf_op jit(solution)/shard_map/pallas_call | solution.py:174
  (2 shorter events, 0.0 us)
Async XLA Ops:
  0.0 21.0 %copy-start.1 = (f32[512,256]{1,0:T(8,128)S(1)}, f32[512,256]{1,0:T(8,128)}, u32[]{:S(2)}) copy-start(f32[512,256]{1,0:T(8,128)} %own.1) | copy-start | bytes 1572868
  0.0 0.9 copy-start.2
  16.7 14.9 %all-to-all-start.1 = ((f32[4,416,128]{2,1,0:T(8,128)}), f32[4,416,128]{2,1,0:T(8,128)S(1)}, u32[]{:S(2)}, u32[]{:S(2)}) async-start(f32[4,416,128]{2,1,0:T(8,128)} %broadcast_in_dim.8), calls=%async_computation.1 | async-start | bytes 1703936 | tf_op jit(solution)/shard_map/all_to_all | solution.py:155
  21.0 3.8 %collective-permute-start = (f32[512,256]{1,0:T(8,128)S(1)}, f32[512,256]{1,0:T(8,128)S(1)}, u32[]{:S(2)}, u32[]{:S(2)}) collective-permute-start(f32[512,256]{1,0:T(8,128)S(1)} %copy-done.1), channel_id=1, source_target_pairs={{0,16},{16,0},{1,17},{17,1},{2,18},{18,2},{3,19},{19,3},{4,20},{20... | collective-permute-start | bytes 1572872 | tf_op jit(solution)/shard_map/ppermute | solution.py:151
  31.7 7.7 %copy-start.4 = (s32[2]{0:T(128)S(1)}, s32[2]{0:T(128)}, u32[]{:S(2)}) copy-start(s32[2]{0:T(128)} %tiles.3) | copy-start | bytes 28
  33.7 52.6 %copy-start = (f32[4,64,1664]{2,1,0:T(8,128)S(1)}, f32[4,64,1664]{2,1,0:T(8,128)}, u32[]{:S(2)}) copy-start(f32[4,64,1664]{2,1,0:T(8,128)} %param.8) | copy-start | bytes 5111812
  33.7 27.6 %all-to-all-start.2 = ((f32[16,104,128]{2,1,0:T(8,128)}), f32[16,104,128]{2,1,0:T(8,128)S(1)}, u32[]{:S(2)}, u32[]{:S(2)}) async-start(f32[16,104,128]{2,1,0:T(8,128)} %bitcast.2), calls=%async_computation.2 | async-start | bytes 1703936 | tf_op jit(solution)/shard_map/all_to_all | solution.py:159
  40.8 3.2 %collective-permute-start.1 = (f32[256,128]{1,0:T(8,128)S(1)}, f32[256,128]{1,0:T(8,128)S(1)}, u32[]{:S(2)}, u32[]{:S(2)}) collective-permute-start(f32[256,128]{1,0:T(8,128)S(1)} %shard_map.66), channel_id=1, source_target_pairs={{0,16},{16,0},{1,17},{17,1},{2,18},{18,2},{3,19},{19,3},{4,20},{20... | collective-permute-start | bytes 393224 | tf_op jit(solution)/shard_map/ppermute | solution.py:167
  87.0 28.0 %copy-start.3 = (f32[832]{0:T(1024)S(1)}, f32[832]{0:T(1024)}, u32[]{:S(2)}) copy-start(f32[832]{0:T(1024)} %virtual.1) | copy-start | bytes 9988
  87.0 28.0 %copy-start.5 = (f32[128]{0:T(128)S(1)}, f32[128]{0:T(128)}, u32[]{:S(2)}) copy-start(f32[128]{0:T(128)} %occupied.1) | copy-start | bytes 1540

commit v14 on v13

--- a/solution.py
+++ b/solution.py
@@ -54,8 +54,8 @@
             out[chip, pair * ROWS : (pair + 1) * ROWS, :] = tile
 
 
-def window_kernel(tiles, gathered, out, window, columns, turned):
-    core = lax.axis_index("core")
+def window_kernel(tiles, gathered, near, far, window, columns, turned):
+    core, first = lax.axis_index("core"), lax.axis_index("zh") == 0
     for pair in range(TILE // 2):
         place = tiles[1] * (TILE // 2) + pair
         owner = place // PAIRS
@@ -73,7 +73,14 @@
             odd = turned[pl.ds(2 * part + 1, CHIPS, stride=4), :]
             for inner, value in enumerate(pair_up(even, odd)):
                 row = part * ROWS + half * 2 + inner
-                out[pl.ds(row, CHIPS, stride=2 * ROWS), :] = value
+                rows = pl.ds(row, Y, stride=2 * ROWS)
+                near[rows, :] = jnp.where(first, value[:Y], value[Y:])
+                far[rows, :] = jnp.where(first, value[Y:], value[:Y])
+
+
+def join_kernel(near_own, near_other, far_one, far_two, out):
+    out[:, : 2 * ROWS, :] = near_own[...] + near_other[...]
+    out[:, 2 * ROWS :, :] = far_one[...] + far_two[...]
 
 
 def cycle_kernel(gathered, own, other, out):
@@ -97,10 +104,15 @@
 
 
 def ladder_kernel(window, integrals, cycle, out):
+    first = lax.axis_index("zh") == 0
     lefts = []
     for part in range(2):
-        rows = window[:, part * ROWS : (part + 1) * ROWS, :]
-        lefts.append(rows.reshape(CHIPS * ROWS, LANES))
+        near, far = [
+            window[:, start : start + ROWS, :].reshape(Y * ROWS, LANES)
+            for start in (part * ROWS, (2 + part) * ROWS)
+        ]
+        halves = [jnp.where(first, near, far), jnp.where(first, far, near)]
+        lefts.append(jnp.concatenate(halves, 0))
     left = split(jnp.concatenate(lefts, 1))
     width = PAIRS * LANES
     for start in range(0, width, 2 * LANES):
@@ -114,7 +126,7 @@
                 out[chip, rows, :] = part + cycle[block_of(chip), rows, :]
 
 
-def last_kernel(tiles, occupied, virtual, parts, out):
+def denominator_kernel(tiles, occupied, virtual, out):
     column = lax.axis_index("zl") * (X * CORE) + lax.axis_index("x") * CORE + lax.axis_index("core")
     row = lax.axis_index("zh") * Y + lax.axis_index("y")
     shape = (ROWS, LANES)
@@ -127,53 +139,67 @@
     for j in range(ROWS):
         rows = jnp.where(line == j, occupied[row * ROWS + j], rows)
     for pair in range(PAIRS):
+        a = column * (2 * PAIRS) + 2 * pair
+        energy = jnp.where(lane < TILE, virtual[a], virtual[a + 1]) + spectator
+        out[pair * ROWS : (pair + 1) * ROWS, :] = energy - occupied[0] - rows
+
+
+def last_kernel(denominator, parts, out):
+    for pair in range(PAIRS):
         piece = pl.ds(pair * ROWS, ROWS)
         total = parts[0, piece, :]
         for place in range(1, ZH * Y):
             total = total + parts[place, piece, :]
-        a = column * (2 * PAIRS) + 2 * pair
-        energy = jnp.where(lane < TILE, virtual[a], virtual[a + 1]) + spectator
-        out[0, :, pair * LANES : (pair + 1) * LANES] = total / (energy - occupied[0] - rows)
-
-
-def call(kernel, shape, specs, scratch=()):
+        out[0, :, pair * LANES : (pair + 1) * LANES] = total / denominator[piece, :]
+
+
+def call(kernel, shapes, specs, scratch=()):
     return pl.pallas_call(
         kernel,
-        out_shape=jax.ShapeDtypeStruct(shape, jnp.float32),
+        out_shape=[jax.ShapeDtypeStruct(shape, jnp.float32) for shape in shapes],
         in_specs=specs,
-        out_specs=VMEM,
-        scratch_shapes=[pltpu.VMEM(s, jnp.float32) for s in scratch],
+        out_specs=[VMEM] * len(shapes),
+        scratch_shapes=[pltpu.VMEM(shape, jnp.float32) for shape in scratch],
         compiler_params=PARAMS,
     )
 
 
 def per_device(amplitudes, cycle_block, ladder_block, occupied, virtual, tiles):
-    other = lax.ppermute(cycle_block, "core", [(0, 1), (1, 0)])
-    copies = call(pack_kernel, (ZL, BLOCK, LANES), [VMEM])(amplitudes)
+    swap = [(0, 1), (1, 0)]
+    other = lax.ppermute(cycle_block, "core", swap)
+    (copies,) = call(pack_kernel, [(ZL, BLOCK, LANES)], [VMEM])(amplitudes)
     column = lax.all_to_all(copies, "zl", 0, 0, tiled=True)
     copies = jnp.broadcast_to(column.reshape(1, ZL * BLOCK, LANES), (X, ZL * BLOCK, LANES))
     gathered = lax.all_to_all(copies, "x", 0, 0, tiled=True)
     gathered = gathered.reshape(CHIPS * BLOCK, LANES)
-    cycle = call(cycle_kernel, (CHIPS * BLOCK, LANES), [VMEM] * 3)(gathered, cycle_block, other)
+    (cycle,) = call(cycle_kernel, [(CHIPS * BLOCK, LANES)], [VMEM] * 3)(gathered, cycle_block, other)
     cycle, gathered = lax.optimization_barrier((cycle, gathered))
     cycle = lax.all_to_all(cycle.reshape(CHIPS, BLOCK, LANES), ("x", "zl"), 0, 0, tiled=True)
 
-    window = call(
+    near, far = call(
         window_kernel,
-        (CHIPS * 2 * ROWS, LANES),
+        [(Y * 2 * ROWS, LANES)] * 2,
         [SMEM, VMEM],
         [(TILE // 2 * ROWS, LANES), (LANES, LANES), (LANES, LANES)],
     )(tiles, gathered)
-    window = window + lax.ppermute(window, "core", [(0, 1), (1, 0)])
-    window, cycle = lax.optimization_barrier((window, cycle))
-    window = lax.all_to_all(window.reshape(CHIPS, 2 * ROWS, LANES), ("zh", "y"), 0, 0, tiled=True)
+    near, far = near.reshape(Y, 2 * ROWS, LANES), far.reshape(Y, 2 * ROWS, LANES)
+    near_other = lax.ppermute(near, "core", swap)
+    far_one = lax.ppermute(far, "zh", swap)
+    far_two = lax.ppermute(far, ("core", "zh"), [(0, 3), (1, 2), (2, 1), (3, 0)])
+    (window,) = call(join_kernel, [(Y, 4 * ROWS, LANES)], [VMEM] * 4)(
+        near, near_other, far_one, far_two
+    )
+    (denominator,) = call(denominator_kernel, [(BLOCK, LANES)], [SMEM] * 3)(
+        tiles, occupied, virtual
+    )
+    window, denominator, cycle = lax.optimization_barrier((window, denominator, cycle))
+    window = lax.all_to_all(window, "y", 0, 0, tiled=True)
 
     integrals = ladder_block.reshape(-1, ladder_block.shape[2])
-    parts = call(ladder_kernel, (CHIPS, BLOCK, LANES), [VMEM] * 3)(window, integrals, cycle)
+    (parts,) = call(ladder_kernel, [(CHIPS, BLOCK, LANES)], [VMEM] * 3)(window, integrals, cycle)
     parts = lax.all_to_all(parts, ("zh", "y"), 0, 0, tiled=True)
-    return call(last_kernel, amplitudes.shape, [SMEM] * 3 + [VMEM])(
-        tiles, occupied, virtual, parts
-    )
+    (result,) = call(last_kernel, [amplitudes.shape], [VMEM] * 2)(denominator, parts)
+    return result
 
 
 def solution(mesh):

time: 117 us -> 117 us (level)
  starting transfers between devices: 13.7 us -> 24 us
  waiting for transfers between devices: 27.4 us -> 22 us
  blocking collectives: 67.9 us -> 62.9 us
    all_to_all x1, waiting for transfers between devices: 17.3 us -> 3.37 us  [per_device(): lax.all_to_all(cycle.reshape(CHIPS, BLOCK, LANES), ('x', 'zl'), 0, 0, til...]
    ppermute x2 -> x4, starting transfers between devices: 3.83 us -> 14.1 us  [the longest x1 8.22 us: per_device(): far_one = lax.ppermute(far, 'zh', swap)]
    all_to_all x1, blocking collectives: 25 us -> 15 us  [per_device(): window = lax.all_to_all(window, 'y', 0, 0, tiled=True)]
    ppermute x2 -> x4, waiting for transfers between devices: 3.19 us -> 11.8 us  [the longest x1 7.34 us: per_device(): far_one = lax.ppermute(far, 'zh', swap)]
    all_to_all x1, blocking collectives: 28 us -> 33.1 us  [per_device(): parts = lax.all_to_all(parts, ('zh', 'y'), 0, 0, tiled=True)]
    pallas_call x5 -> x7, Pallas kernels: 5.4 us -> 5.47 us  [the longest x1 2.04 us: per_device(): call(cycle_kernel, [(CHIPS * BLOCK, LANES)], [VMEM] * 3)]
  transfers between devices with their start and end apart: 4 -> 6, of which waited for: 4 -> 5; matrix products, arithmetic and copies ran while one was open for 0% -> 0% of each run, Pallas kernels for 1% -> 2%
where the time goes in v14:
time: 117 us; the launch traced here: 116 us
  blocking collectives  62.9 us (54%)
  starting transfers between devices  24 us (21%)
  waiting for transfers between devices  22 us (19%)
  Pallas kernels  5.47 us (5%)
  local copies, waits for them, and re-layouts  1.85 us (2%)
    all_to_all x1, blocking collectives, per_device(): parts = lax.all_to_all(parts, ('zh', 'y'), 0, 0, tiled=True)  33.1 us
    all_to_all x1, blocking collectives, per_device(): window = lax.all_to_all(window, 'y', 0, 0, tiled=True)  15 us
    all_to_all x1, blocking collectives, per_device(): column = lax.all_to_all(copies, 'zl', 0, 0, tiled=True)  14.9 us
    ppermute x1, starting transfers between devices, per_device(): far_one = lax.ppermute(far, 'zh', swap)  8.22 us
    ppermute x1, waiting for transfers between devices, per_device(): far_one = lax.ppermute(far, 'zh', swap)  7.34 us
    all_to_all x1, waiting for transfers between devices, per_device(): gathered = lax.all_to_all(copies, 'x', 0, 0, tiled=True)  6.84 us
    all_to_all x1, starting transfers between devices, per_device(): lax.all_to_all(cycle.reshape(CHIPS, BLOCK, LANES), ('x', 'zl'), 0, 0, til...  5.59 us
    all_to_all x1, starting transfers between devices, per_device(): gathered = lax.all_to_all(copies, 'x', 0, 0, tiled=True)  4.29 us
  transfers between devices with their start and end apart: 6, of which 5 were waited for; matrix products, arithmetic and copies ran while one was open for 0% of the time, Pallas kernels for 2%

profile of v14, /device:TPU:8, one launch (start us, length us, event | category | flops | bytes accessed | tf_op | source)
XLA Modules:
  0.0 116.3 jit_solution(1536482006332398997)
XLA Ops:
  0.0 0.0 copy-start.1
  0.0 0.0 copy-start.2
  0.0 0.9 copy-done.2
  0.9 14.9 %all_to_all.25 = f32[4,104,128]{2,1,0:T(8,128)S(1)} all-to-all(f32[4,104,128]{2,1,0:T(8,128)S(1)} %shard_map.64), channel_id=1, replica_groups=mesh['zl'=4,'x'=4,'core'=2,'zh'=2,'y'=8] {'zl'}, dimensions={0} | all-to-all | bytes 425984 | tf_op jit(solution)/shard_map/all_to_all | solution.py:171
  15.8 1.0 broadcast_in_dim.8
  16.7 4.3 %all-to-all-start.1 = ((f32[4,416,128]{2,1,0:T(8,128)}), f32[4,416,128]{2,1,0:T(8,128)S(1)}, u32[]{:S(2)}, u32[]{:S(2)}) async-start(f32[4,416,128]{2,1,0:T(8,128)} %broadcast_in_dim.8), calls=%async_computation.1 | async-start | bytes 1703936 | tf_op jit(solution)/shard_map/all_to_all | solution.py:173
  21.0 0.0 copy-done.1
  21.0 1.9 %collective-permute-start = (f32[512,256]{1,0:T(8,128)S(1)}, f32[512,256]{1,0:T(8,128)S(1)}, u32[]{:S(2)}, u32[]{:S(2)}) collective-permute-start(f32[512,256]{1,0:T(8,128)S(1)} %copy-done.1), channel_id=1, source_target_pairs={{0,16},{16,0},{1,17},{17,1},{2,18},{18,2},{3,19},{19,3},{4,20},{20... | collective-permute-start | bytes 1572872 | tf_op jit(solution)/shard_map/ppermute | solution.py:169
  22.9 1.9 %collective-permute-done.other = f32[512,256]{1,0:T(8,128)S(1)} collective-permute-done((f32[512,256]{1,0:T(8,128)S(1)}, f32[512,256]{1,0:T(8,128)S(1)}, u32[]{:S(2)}, u32[]{:S(2)}) %collective-permute-start) | collective-permute-done | bytes 524320 | tf_op jit(solution)/shard_map/ppermute | solution.py:169
  24.8 6.8 %all-to-all-done.1 = f32[4,416,128]{2,1,0:T(8,128)S(1)} async-done(((f32[4,416,128]{2,1,0:T(8,128)}), f32[4,416,128]{2,1,0:T(8,128)S(1)}, u32[]{:S(2)}, u32[]{:S(2)}) %all-to-all-start.1) | async-done | bytes 852000 | tf_op jit(solution)/shard_map/all_to_all | solution.py:173
  31.7 0.0 copy-start.4
  31.7 2.0 %shard_map.65 = f32[1664,128]{1,0:T(8,128)} custom-call(f32[1664,128]{1,0:T(8,128)S(1)} %bitcast.6, f32[512,256]{1,0:T(8,128)S(1)} %copy-done.1, f32[512,256]{1,0:T(8,128)S(1)} %collective-permute-done.other), custom_call_target="tpu_custom_call" | custom-call | tf_op jit(solution)/shard_map/pallas_call | solution.py:175
  33.7 0.0 copy-start.3
  33.7 0.0 copy-start.5
  33.7 0.0 copy-start
  33.7 5.6 %all-to-all-start.2 = ((f32[16,104,128]{2,1,0:T(8,128)}), f32[16,104,128]{2,1,0:T(8,128)S(1)}, u32[]{:S(2)}, u32[]{:S(2)}) async-start(f32[16,104,128]{2,1,0:T(8,128)} %bitcast.4), calls=%async_computation.2 | async-start | bytes 1703936 | tf_op jit(solution)/shard_map/all_to_all | solution.py:177
  39.3 0.0 copy-done.4
  39.3 1.4 %shard_map.66 = (f32[128,128]{1,0:T(8,128)S(1)}, f32[128,128]{1,0:T(8,128)S(1)}) custom-call(s32[2]{0:T(128)S(1)} %copy-done.4, f32[1664,128]{1,0:T(8,128)S(1)} %bitcast.7), custom_call_target="tpu_custom_call" | custom-call | tf_op jit(solution)/shard_map/pallas_call | solution.py:179
  40.8 1.9 %collective-permute-start.1 = (f32[8,16,128]{2,1,0:T(8,128)S(1)}, f32[8,16,128]{2,1,0:T(8,128)S(1)}, u32[]{:S(2)}, u32[]{:S(2)}) collective-permute-start(f32[8,16,128]{2,1,0:T(8,128)S(1)} %bitcast.9), channel_id=1, source_target_pairs={{0,16},{16,0},{1,17},{17,1},{2,18},{18,2},{3,19},{19,3},{4,20},{20... | collective-permute-start | bytes 196616 | tf_op jit(solution)/shard_map/ppermute | solution.py:186
  42.7 8.2 %collective-permute-start.2 = (f32[8,16,128]{2,1,0:T(8,128)S(1)}, f32[8,16,128]{2,1,0:T(8,128)S(1)}, u32[]{:S(2)}, u32[]{:S(2)}) collective-permute-start(f32[8,16,128]{2,1,0:T(8,128)S(1)} %bitcast.11), channel_id=1, source_target_pairs={{0,8},{8,0},{1,9},{9,1},{2,10},{10,2},{3,11},{11,3},{4,12},{12,4},... | collective-permute-start | bytes 196616 | tf_op jit(solution)/shard_map/ppermute | solution.py:187
  50.9 2.0 %collective-permute-start.3 = (f32[8,16,128]{2,1,0:T(8,128)S(1)}, f32[8,16,128]{2,1,0:T(8,128)S(1)}, u32[]{:S(2)}, u32[]{:S(2)}) collective-permute-start(f32[8,16,128]{2,1,0:T(8,128)S(1)} %bitcast.12), channel_id=1, source_target_pairs={{0,24},{8,16},{16,8},{24,0},{1,25},{9,17},{17,9},{25,1},{2,26},{10... | collective-permute-start | bytes 196616 | tf_op jit(solution)/shard_map/ppermute | solution.py:188
  52.9 0.0 copy-done.3
  53.0 0.0 copy-done.5
  53.0 0.7 shard_map.68.denominator
  53.6 0.0 collective-permute-done.1.near_other
  53.7 7.3 %collective-permute-done.2.far_one = f32[8,16,128]{2,1,0:T(8,128)S(1)} collective-permute-done((f32[8,16,128]{2,1,0:T(8,128)S(1)}, f32[8,16,128]{2,1,0:T(8,128)S(1)}, u32[]{:S(2)}, u32[]{:S(2)}) %collective-permute-start.2) | collective-permute-done | bytes 65568 | tf_op jit(solution)/shard_map/ppermute | solution.py:187
  61.0 2.6 %collective-permute-done.3.far_two = f32[8,16,128]{2,1,0:T(8,128)S(1)} collective-permute-done((f32[8,16,128]{2,1,0:T(8,128)S(1)}, f32[8,16,128]{2,1,0:T(8,128)S(1)}, u32[]{:S(2)}, u32[]{:S(2)}) %collective-permute-start.3) | collective-permute-done | bytes 65568 | tf_op jit(solution)/shard_map/ppermute | solution.py:188
  63.6 3.4 %all-to-all-done.2.cycle = f32[16,104,128]{2,1,0:T(8,128)S(1)} async-done(((f32[16,104,128]{2,1,0:T(8,128)}), f32[16,104,128]{2,1,0:T(8,128)S(1)}, u32[]{:S(2)}, u32[]{:S(2)}) %all-to-all-start.2) | async-done | bytes 852000 | tf_op jit(solution)/shard_map/all_to_all | solution.py:177
  67.0 15.0 %all_to_all.26.window = f32[8,32,128]{2,1,0:T(8,128)S(1)} all-to-all(f32[8,32,128]{2,1,0:T(8,128)S(1)} %shard_map.67), channel_id=1, replica_groups=mesh['zl'=4,'x'=4,'core'=2,'zh'=2,'y'=8] {'y'}, dimensions={0} | all-to-all | bytes 262144 | tf_op jit(solution)/shard_map/all_to_all | solution.py:196
  81.9 0.0 copy-done
  81.9 0.6 shard_map.69
  82.5 33.1 %all_to_all.27.parts = f32[16,104,128]{2,1,0:T(8,128)S(1)} all-to-all(f32[16,104,128]{2,1,0:T(8,128)S(1)} %shard_map.69), channel_id=1, replica_groups=mesh['zl'=4,'x'=4,'core'=2,'zh'=2,'y'=8] {'zh','y'}, dimensions={0} | all-to-all | bytes 1703936 | tf_op jit(solution)/shard_map/all_to_all | solution.py:200
  115.6 0.7 shard_map.70
  (2 shorter events, 0.0 us)
Async XLA Ops:
  0.0 21.0 %copy-start.1 = (f32[512,256]{1,0:T(8,128)S(1)}, f32[512,256]{1,0:T(8,128)}, u32[]{:S(2)}) copy-start(f32[512,256]{1,0:T(8,128)} %own.1) | copy-start | bytes 1572868
  0.0 0.9 copy-start.2
  16.7 14.9 %all-to-all-start.1 = ((f32[4,416,128]{2,1,0:T(8,128)}), f32[4,416,128]{2,1,0:T(8,128)S(1)}, u32[]{:S(2)}, u32[]{:S(2)}) async-start(f32[4,416,128]{2,1,0:T(8,128)} %broadcast_in_dim.8), calls=%async_computation.1 | async-start | bytes 1703936 | tf_op jit(solution)/shard_map/all_to_all | solution.py:173
  21.0 3.8 %collective-permute-start = (f32[512,256]{1,0:T(8,128)S(1)}, f32[512,256]{1,0:T(8,128)S(1)}, u32[]{:S(2)}, u32[]{:S(2)}) collective-permute-start(f32[512,256]{1,0:T(8,128)S(1)} %copy-done.1), channel_id=1, source_target_pairs={{0,16},{16,0},{1,17},{17,1},{2,18},{18,2},{3,19},{19,3},{4,20},{20... | collective-permute-start | bytes 1572872 | tf_op jit(solution)/shard_map/ppermute | solution.py:169
  31.7 7.6 %copy-start.4 = (s32[2]{0:T(128)S(1)}, s32[2]{0:T(128)}, u32[]{:S(2)}) copy-start(s32[2]{0:T(128)} %tiles.3) | copy-start | bytes 28
  33.7 19.2 %copy-start.3 = (f32[832]{0:T(1024)S(1)}, f32[832]{0:T(1024)}, u32[]{:S(2)}) copy-start(f32[832]{0:T(1024)} %virtual.1) | copy-start | bytes 9988
  33.7 19.2 %copy-start.5 = (f32[128]{0:T(128)S(1)}, f32[128]{0:T(128)}, u32[]{:S(2)}) copy-start(f32[128]{0:T(128)} %occupied.1) | copy-start | bytes 1540
  33.7 48.2 %copy-start = (f32[4,64,1664]{2,1,0:T(8,128)S(1)}, f32[4,64,1664]{2,1,0:T(8,128)}, u32[]{:S(2)}) copy-start(f32[4,64,1664]{2,1,0:T(8,128)} %param.8) | copy-start | bytes 5111812
  33.7 33.2 %all-to-all-start.2 = ((f32[16,104,128]{2,1,0:T(8,128)}), f32[16,104,128]{2,1,0:T(8,128)S(1)}, u32[]{:S(2)}, u32[]{:S(2)}) async-start(f32[16,104,128]{2,1,0:T(8,128)} %bitcast.4), calls=%async_computation.2 | async-start | bytes 1703936 | tf_op jit(solution)/shard_map/all_to_all | solution.py:177
  40.8 12.9 %collective-permute-start.1 = (f32[8,16,128]{2,1,0:T(8,128)S(1)}, f32[8,16,128]{2,1,0:T(8,128)S(1)}, u32[]{:S(2)}, u32[]{:S(2)}) collective-permute-start(f32[8,16,128]{2,1,0:T(8,128)S(1)} %bitcast.9), channel_id=1, source_target_pairs={{0,16},{16,0},{1,17},{17,1},{2,18},{18,2},{3,19},{19,3},{4,20},{20... | collective-permute-start | bytes 196616 | tf_op jit(solution)/shard_map/ppermute | solution.py:186
  42.7 18.3 %collective-permute-start.2 = (f32[8,16,128]{2,1,0:T(8,128)S(1)}, f32[8,16,128]{2,1,0:T(8,128)S(1)}, u32[]{:S(2)}, u32[]{:S(2)}) collective-permute-start(f32[8,16,128]{2,1,0:T(8,128)S(1)} %bitcast.11), channel_id=1, source_target_pairs={{0,8},{8,0},{1,9},{9,1},{2,10},{10,2},{3,11},{11,3},{4,12},{12,4},... | collective-permute-start | bytes 196616 | tf_op jit(solution)/shard_map/ppermute | solution.py:187
  50.9 12.7 %collective-permute-start.3 = (f32[8,16,128]{2,1,0:T(8,128)S(1)}, f32[8,16,128]{2,1,0:T(8,128)S(1)}, u32[]{:S(2)}, u32[]{:S(2)}) collective-permute-start(f32[8,16,128]{2,1,0:T(8,128)S(1)} %bitcast.12), channel_id=1, source_target_pairs={{0,24},{8,16},{16,8},{24,0},{1,25},{9,17},{17,9},{25,1},{2,26},{10... | collective-permute-start | bytes 196616 | tf_op jit(solution)/shard_map/ppermute | solution.py:188

commit v15 on v14

--- a/solution.py
+++ b/solution.py
@@ -54,7 +54,7 @@
             out[chip, pair * ROWS : (pair + 1) * ROWS, :] = tile
 
 
-def window_kernel(tiles, gathered, near, far, window, columns, turned):
+def window_kernel(tiles, gathered, out, window, columns, turned):
     core, first = lax.axis_index("core"), lax.axis_index("zh") == 0
     for pair in range(TILE // 2):
         place = tiles[1] * (TILE // 2) + pair
@@ -74,13 +74,18 @@
             for inner, value in enumerate(pair_up(even, odd)):
                 row = part * ROWS + half * 2 + inner
                 rows = pl.ds(row, Y, stride=2 * ROWS)
-                near[rows, :] = jnp.where(first, value[:Y], value[Y:])
-                far[rows, :] = jnp.where(first, value[Y:], value[:Y])
-
-
-def join_kernel(near_own, near_other, far_one, far_two, out):
-    out[:, : 2 * ROWS, :] = near_own[...] + near_other[...]
-    out[:, 2 * ROWS :, :] = far_one[...] + far_two[...]
+                out[0, rows, :] = jnp.where(first, value[:Y], value[Y:])
+                out[1, rows, :] = jnp.where(first, value[Y:], value[:Y])
+
+
+def add_kernel(own, other, near, far):
+    near[...] = own[0] + other[0]
+    far[...] = own[1] + other[1]
+
+
+def join_kernel(near, far, out):
+    out[:, : 2 * ROWS, :] = near[...]
+    out[:, 2 * ROWS :, :] = far[...]
 
 
 def cycle_kernel(gathered, own, other, out):
@@ -176,19 +181,17 @@
     cycle, gathered = lax.optimization_barrier((cycle, gathered))
     cycle = lax.all_to_all(cycle.reshape(CHIPS, BLOCK, LANES), ("x", "zl"), 0, 0, tiled=True)
 
-    near, far = call(
+    (window,) = call(
         window_kernel,
-        [(Y * 2 * ROWS, LANES)] * 2,
+        [(2, Y * 2 * ROWS, LANES)],
         [SMEM, VMEM],
         [(TILE // 2 * ROWS, LANES), (LANES, LANES), (LANES, LANES)],
     )(tiles, gathered)
-    near, far = near.reshape(Y, 2 * ROWS, LANES), far.reshape(Y, 2 * ROWS, LANES)
-    near_other = lax.ppermute(near, "core", swap)
-    far_one = lax.ppermute(far, "zh", swap)
-    far_two = lax.ppermute(far, ("core", "zh"), [(0, 3), (1, 2), (2, 1), (3, 0)])
-    (window,) = call(join_kernel, [(Y, 4 * ROWS, LANES)], [VMEM] * 4)(
-        near, near_other, far_one, far_two
-    )
+    window = window.reshape(2, Y, 2 * ROWS, LANES)
+    other_window = lax.ppermute(window, "core", swap)
+    near, far = call(add_kernel, [(Y, 2 * ROWS, LANES)] * 2, [VMEM] * 2)(window, other_window)
+    far = lax.ppermute(far, "zh", swap)
+    (window,) = call(join_kernel, [(Y, 4 * ROWS, LANES)], [VMEM] * 2)(near, far)
     (denominator,) = call(denominator_kernel, [(BLOCK, LANES)], [SMEM] * 3)(
         tiles, occupied, virtual
     )

time: 117 us -> 114 us (0.974)
  starting transfers between devices: 24 us -> 21.9 us
    ppermute x3 -> x2, starting transfers between devices: 12.2 us -> 10.1 us  [the longest x1 8.22 us: per_device(): far = lax.ppermute(far, 'zh', swap)]
    ppermute x3 -> x2, waiting for transfers between devices: 9.91 us -> 8.37 us  [the longest x1 7.05 us: per_device(): far = lax.ppermute(far, 'zh', swap)]
  transfers between devices with their start and end apart: 6 -> 5, of which waited for: 5 -> 5; matrix products, arithmetic and copies ran while one was open for 0% -> 0% of each run, Pallas kernels for 2% -> 2%
where the time goes in v15:
time: 114 us; the launch traced here: 113 us
  blocking collectives  62.9 us (55%)
  starting transfers between devices  21.9 us (19%)
  waiting for transfers between devices  21.2 us (19%)
  Pallas kernels  5.48 us (5%)
  local copies, waits for them, and re-layouts  1.86 us (2%)
    all_to_all x1, blocking collectives, per_device(): parts = lax.all_to_all(parts, ('zh', 'y'), 0, 0, tiled=True)  33.1 us
    all_to_all x1, blocking collectives, per_device(): window = lax.all_to_all(window, 'y', 0, 0, tiled=True)  15 us
    all_to_all x1, blocking collectives, per_device(): column = lax.all_to_all(copies, 'zl', 0, 0, tiled=True)  14.9 us
    ppermute x1, starting transfers between devices, per_device(): far = lax.ppermute(far, 'zh', swap)  8.22 us
    ppermute x1, waiting for transfers between devices, per_device(): far = lax.ppermute(far, 'zh', swap)  7.05 us
    all_to_all x1, waiting for transfers between devices, per_device(): gathered = lax.all_to_all(copies, 'x', 0, 0, tiled=True)  6.84 us
    all_to_all x1, starting transfers between devices, per_device(): lax.all_to_all(cycle.reshape(CHIPS, BLOCK, LANES), ('x', 'zl'), 0, 0, til...  5.59 us
    all_to_all x1, starting transfers between devices, per_device(): gathered = lax.all_to_all(copies, 'x', 0, 0, tiled=True)  4.29 us
  transfers between devices with their start and end apart: 5, of which 5 were waited for; matrix products, arithmetic and copies ran while one was open for 0% of the time, Pallas kernels for 2%

profile of v15, /device:TPU:8, one launch (start us, length us, event | category | flops | bytes accessed | tf_op | source)
XLA Modules:
  0.0 113.5 jit_solution(3367598851901088112)
XLA Ops:
  0.0 0.0 copy-start.1
  0.0 0.0 copy-start.2
  0.0 0.9 copy-done.2
  0.9 14.9 %all_to_all.25 = f32[4,104,128]{2,1,0:T(8,128)S(1)} all-to-all(f32[4,104,128]{2,1,0:T(8,128)S(1)} %shard_map.64), channel_id=1, replica_groups=mesh['zl'=4,'x'=4,'core'=2,'zh'=2,'y'=8] {'zl'}, dimensions={0} | all-to-all | bytes 425984 | tf_op jit(solution)/shard_map/all_to_all | solution.py:176
  15.8 1.0 broadcast_in_dim.8
  16.7 4.3 %all-to-all-start.1 = ((f32[4,416,128]{2,1,0:T(8,128)}), f32[4,416,128]{2,1,0:T(8,128)S(1)}, u32[]{:S(2)}, u32[]{:S(2)}) async-start(f32[4,416,128]{2,1,0:T(8,128)} %broadcast_in_dim.8), calls=%async_computation.1 | async-start | bytes 1703936 | tf_op jit(solution)/shard_map/all_to_all | solution.py:178
  21.0 0.0 copy-done.1
  21.0 1.9 %collective-permute-start = (f32[512,256]{1,0:T(8,128)S(1)}, f32[512,256]{1,0:T(8,128)S(1)}, u32[]{:S(2)}, u32[]{:S(2)}) collective-permute-start(f32[512,256]{1,0:T(8,128)S(1)} %copy-done.1), channel_id=1, source_target_pairs={{0,16},{16,0},{1,17},{17,1},{2,18},{18,2},{3,19},{19,3},{4,20},{20... | collective-permute-start | bytes 1572872 | tf_op jit(solution)/shard_map/ppermute | solution.py:174
  23.0 1.9 %collective-permute-done.other = f32[512,256]{1,0:T(8,128)S(1)} collective-permute-done((f32[512,256]{1,0:T(8,128)S(1)}, f32[512,256]{1,0:T(8,128)S(1)}, u32[]{:S(2)}, u32[]{:S(2)}) %collective-permute-start) | collective-permute-done | bytes 524320 | tf_op jit(solution)/shard_map/ppermute | solution.py:174
  24.8 6.8 %all-to-all-done.1 = f32[4,416,128]{2,1,0:T(8,128)S(1)} async-done(((f32[4,416,128]{2,1,0:T(8,128)}), f32[4,416,128]{2,1,0:T(8,128)S(1)}, u32[]{:S(2)}, u32[]{:S(2)}) %all-to-all-start.1) | async-done | bytes 852000 | tf_op jit(solution)/shard_map/all_to_all | solution.py:178
  31.7 0.0 copy-start.4
  31.7 2.0 %shard_map.65 = f32[1664,128]{1,0:T(8,128)} custom-call(f32[1664,128]{1,0:T(8,128)S(1)} %bitcast.5, f32[512,256]{1,0:T(8,128)S(1)} %copy-done.1, f32[512,256]{1,0:T(8,128)S(1)} %collective-permute-done.other), custom_call_target="tpu_custom_call" | custom-call | tf_op jit(solution)/shard_map/pallas_call | solution.py:180
  33.7 0.0 copy-start.3
  33.7 0.0 copy-start.5
  33.7 0.0 copy-start
  33.7 5.6 %all-to-all-start.2 = ((f32[16,104,128]{2,1,0:T(8,128)}), f32[16,104,128]{2,1,0:T(8,128)S(1)}, u32[]{:S(2)}, u32[]{:S(2)}) async-start(f32[16,104,128]{2,1,0:T(8,128)} %bitcast.3), calls=%async_computation.2 | async-start | bytes 1703936 | tf_op jit(solution)/shard_map/all_to_all | solution.py:182
  39.3 0.0 copy-done.4
  39.3 1.4 %shard_map.66 = f32[2,128,128]{2,1,0:T(8,128)S(1)} custom-call(s32[2]{0:T(128)S(1)} %copy-done.4, f32[1664,128]{1,0:T(8,128)S(1)} %bitcast.6), custom_call_target="tpu_custom_call" | custom-call | tf_op jit(solution)/shard_map/pallas_call | solution.py:184
  40.8 1.9 %collective-permute-start.1 = (f32[2,8,16,128]{3,2,1,0:T(8,128)S(1)}, f32[2,8,16,128]{3,2,1,0:T(8,128)S(1)}, u32[]{:S(2)}, u32[]{:S(2)}) collective-permute-start(f32[2,8,16,128]{3,2,1,0:T(8,128)S(1)} %bitcast.8), channel_id=1, source_target_pairs={{0,16},{16,0},{1,17},{17,1},{2,18},{18,2},{3,19},{19,3},{4,20},{20... | collective-permute-start | bytes 393224 | tf_op jit(solution)/shard_map/ppermute | solution.py:191
  42.7 1.3 %collective-permute-done.1.other = f32[2,8,16,128]{3,2,1,0:T(8,128)S(1)} collective-permute-done((f32[2,8,16,128]{3,2,1,0:T(8,128)S(1)}, f32[2,8,16,128]{3,2,1,0:T(8,128)S(1)}, u32[]{:S(2)}, u32[]{:S(2)}) %collective-permute-start.1) | collective-permute-done | bytes 131104 | tf_op jit(solution)/shard_map/ppermute | solution.py:191
  44.0 8.2 %collective-permute-start.2 = (f32[8,16,128]{2,1,0:T(8,128)S(1)}, f32[8,16,128]{2,1,0:T(8,128)S(1)}, u32[]{:S(2)}, u32[]{:S(2)}) collective-permute-start(f32[8,16,128]{2,1,0:T(8,128)S(1)} %get-tuple-element.14), channel_id=1, source_target_pairs={{0,8},{8,0},{1,9},{9,1},{2,10},{10,2},{3,11},{11,3},{4,12},{12,4},... | collective-permute-start | bytes 196616 | tf_op jit(solution)/shard_map/ppermute | solution.py:193
  52.3 0.0 copy-done.3
  52.3 0.0 copy-done.5
  52.3 0.7 shard_map.69.denominator
  53.0 7.1 %collective-permute-done.2.far = f32[8,16,128]{2,1,0:T(8,128)S(1)} collective-permute-done((f32[8,16,128]{2,1,0:T(8,128)S(1)}, f32[8,16,128]{2,1,0:T(8,128)S(1)}, u32[]{:S(2)}, u32[]{:S(2)}) %collective-permute-start.2) | collective-permute-done | bytes 65568 | tf_op jit(solution)/shard_map/ppermute | solution.py:193
  60.0 4.1 %all-to-all-done.2.cycle = f32[16,104,128]{2,1,0:T(8,128)S(1)} async-done(((f32[16,104,128]{2,1,0:T(8,128)}), f32[16,104,128]{2,1,0:T(8,128)S(1)}, u32[]{:S(2)}, u32[]{:S(2)}) %all-to-all-start.2) | async-done | bytes 852000 | tf_op jit(solution)/shard_map/all_to_all | solution.py:182
  64.2 15.0 %all_to_all.26.window = f32[8,32,128]{2,1,0:T(8,128)S(1)} all-to-all(f32[8,32,128]{2,1,0:T(8,128)S(1)} %shard_map.68), channel_id=1, replica_groups=mesh['zl'=4,'x'=4,'core'=2,'zh'=2,'y'=8] {'y'}, dimensions={0} | all-to-all | bytes 262144 | tf_op jit(solution)/shard_map/all_to_all | solution.py:199
  79.1 0.0 copy-done
  79.1 0.6 shard_map.70
  79.7 33.1 %all_to_all.27.parts = f32[16,104,128]{2,1,0:T(8,128)S(1)} all-to-all(f32[16,104,128]{2,1,0:T(8,128)S(1)} %shard_map.70), channel_id=1, replica_groups=mesh['zl'=4,'x'=4,'core'=2,'zh'=2,'y'=8] {'zh','y'}, dimensions={0} | all-to-all | bytes 1703936 | tf_op jit(solution)/shard_map/all_to_all | solution.py:203
  112.8 0.7 shard_map.71
  (3 shorter events, 0.0 us)
Async XLA Ops:
  0.0 21.0 %copy-start.1 = (f32[512,256]{1,0:T(8,128)S(1)}, f32[512,256]{1,0:T(8,128)}, u32[]{:S(2)}) copy-start(f32[512,256]{1,0:T(8,128)} %own.1) | copy-start | bytes 1572868
  0.0 0.9 copy-start.2
  16.7 14.9 %all-to-all-start.1 = ((f32[4,416,128]{2,1,0:T(8,128)}), f32[4,416,128]{2,1,0:T(8,128)S(1)}, u32[]{:S(2)}, u32[]{:S(2)}) async-start(f32[4,416,128]{2,1,0:T(8,128)} %broadcast_in_dim.8), calls=%async_computation.1 | async-start | bytes 1703936 | tf_op jit(solution)/shard_map/all_to_all | solution.py:178
  21.0 3.8 %collective-permute-start = (f32[512,256]{1,0:T(8,128)S(1)}, f32[512,256]{1,0:T(8,128)S(1)}, u32[]{:S(2)}, u32[]{:S(2)}) collective-permute-start(f32[512,256]{1,0:T(8,128)S(1)} %copy-done.1), channel_id=1, source_target_pairs={{0,16},{16,0},{1,17},{17,1},{2,18},{18,2},{3,19},{19,3},{4,20},{20... | collective-permute-start | bytes 1572872 | tf_op jit(solution)/shard_map/ppermute | solution.py:174
  31.7 7.7 %copy-start.4 = (s32[2]{0:T(128)S(1)}, s32[2]{0:T(128)}, u32[]{:S(2)}) copy-start(s32[2]{0:T(128)} %tiles.3) | copy-start | bytes 28
  33.7 18.5 %copy-start.3 = (f32[832]{0:T(1024)S(1)}, f32[832]{0:T(1024)}, u32[]{:S(2)}) copy-start(f32[832]{0:T(1024)} %virtual.1) | copy-start | bytes 9988
  33.7 18.6 %copy-start.5 = (f32[128]{0:T(128)S(1)}, f32[128]{0:T(128)}, u32[]{:S(2)}) copy-start(f32[128]{0:T(128)} %occupied.1) | copy-start | bytes 1540
  33.7 45.4 %copy-start = (f32[4,64,1664]{2,1,0:T(8,128)S(1)}, f32[4,64,1664]{2,1,0:T(8,128)}, u32[]{:S(2)}) copy-start(f32[4,64,1664]{2,1,0:T(8,128)} %param.8) | copy-start | bytes 5111812
  33.7 30.4 %all-to-all-start.2 = ((f32[16,104,128]{2,1,0:T(8,128)}), f32[16,104,128]{2,1,0:T(8,128)S(1)}, u32[]{:S(2)}, u32[]{:S(2)}) async-start(f32[16,104,128]{2,1,0:T(8,128)} %bitcast.3), calls=%async_computation.2 | async-start | bytes 1703936 | tf_op jit(solution)/shard_map/all_to_all | solution.py:182
  40.8 3.2 %collective-permute-start.1 = (f32[2,8,16,128]{3,2,1,0:T(8,128)S(1)}, f32[2,8,16,128]{3,2,1,0:T(8,128)S(1)}, u32[]{:S(2)}, u32[]{:S(2)}) collective-permute-start(f32[2,8,16,128]{3,2,1,0:T(8,128)S(1)} %bitcast.8), channel_id=1, source_target_pairs={{0,16},{16,0},{1,17},{17,1},{2,18},{18,2},{3,19},{19,3},{4,20},{20... | collective-permute-start | bytes 393224 | tf_op jit(solution)/shard_map/ppermute | solution.py:191
  44.0 16.0 %collective-permute-start.2 = (f32[8,16,128]{2,1,0:T(8,128)S(1)}, f32[8,16,128]{2,1,0:T(8,128)S(1)}, u32[]{:S(2)}, u32[]{:S(2)}) collective-permute-start(f32[8,16,128]{2,1,0:T(8,128)S(1)} %get-tuple-element.14), channel_id=1, source_target_pairs={{0,8},{8,0},{1,9},{9,1},{2,10},{10,2},{3,11},{11,3},{4,12},{12,4},... | collective-permute-start | bytes 196616 | tf_op jit(solution)/shard_map/ppermute | solution.py:193

commit v16 on v15

--- a/solution.py
+++ b/solution.py
@@ -8,14 +8,15 @@
 from jax.sharding import Mesh
 from jax.sharding import PartitionSpec as P
 
-ZL, X, CORE, ZH, Y = 4, 4, 2, 2, 8
+ZL, X, CORE, ZH, YH, YL = 4, 4, 2, 2, 4, 2
+Y = YH * YL
 CHIPS = ZL * X
 ROWS = 8
 TILE = 64
 PAIRS = 13
 LANES = 2 * TILE
 BLOCK = PAIRS * ROWS
-EVERY = ("zl", "x", "core", "zh", "y")
+EVERY = ("zl", "x", "core", "zh", "yh", "yl")
 VMEM = pl.BlockSpec(memory_space=pltpu.VMEM)
 SMEM = pl.BlockSpec(memory_space=pltpu.SMEM)
 PARAMS = pltpu.CompilerParams(vmem_limit_bytes=32 * 1024 * 1024)
@@ -45,6 +46,10 @@
 
 def block_of(chip):
     return chip % X * ZL + chip // X
+
+
+def peer_of(place):
+    return place // Y * Y + place % YL * YH + place % Y // YL
 
 
 def pack_kernel(amplitudes, out):
@@ -128,12 +133,12 @@
             rows = pl.ds(column // LANES * ROWS, ROWS)
             for chip in range(CHIPS):
                 part = value[chip * ROWS : (chip + 1) * ROWS]
-                out[chip, rows, :] = part + cycle[block_of(chip), rows, :]
+                out[peer_of(chip), rows, :] = part + cycle[block_of(chip), rows, :]
 
 
 def denominator_kernel(tiles, occupied, virtual, out):
     column = lax.axis_index("zl") * (X * CORE) + lax.axis_index("x") * CORE + lax.axis_index("core")
-    row = lax.axis_index("zh") * Y + lax.axis_index("y")
+    row = lax.axis_index("zh") * Y + lax.axis_index("yh") * YL + lax.axis_index("yl")
     shape = (ROWS, LANES)
     lane = lax.broadcasted_iota(jnp.int32, shape, 1)
     line = lax.broadcasted_iota(jnp.int32, shape, 0)
@@ -174,6 +179,7 @@
     other = lax.ppermute(cycle_block, "core", swap)
     (copies,) = call(pack_kernel, [(ZL, BLOCK, LANES)], [VMEM])(amplitudes)
     column = lax.all_to_all(copies, "zl", 0, 0, tiled=True)
+    column, other = lax.optimization_barrier((column, other))
     copies = jnp.broadcast_to(column.reshape(1, ZL * BLOCK, LANES), (X, ZL * BLOCK, LANES))
     gathered = lax.all_to_all(copies, "x", 0, 0, tiled=True)
     gathered = gathered.reshape(CHIPS * BLOCK, LANES)
@@ -196,18 +202,18 @@
         tiles, occupied, virtual
     )
     window, denominator, cycle = lax.optimization_barrier((window, denominator, cycle))
-    window = lax.all_to_all(window, "y", 0, 0, tiled=True)
+    window = lax.all_to_all(window, ("yh", "yl"), 0, 0, tiled=True)
 
     integrals = ladder_block.reshape(-1, ladder_block.shape[2])
     (parts,) = call(ladder_kernel, [(CHIPS, BLOCK, LANES)], [VMEM] * 3)(window, integrals, cycle)
-    parts = lax.all_to_all(parts, ("zh", "y"), 0, 0, tiled=True)
+    parts = lax.all_to_all(parts, ("zh", "yl", "yh"), 0, 0, tiled=True)
     (result,) = call(last_kernel, [amplitudes.shape], [VMEM] * 2)(denominator, parts)
     return result
 
 
 def solution(mesh):
-    parts = Mesh(mesh.devices.reshape(ZL, X, CORE, ZH, Y), EVERY)
-    amp, intg = ("zl", "x", "core"), ("zh", "y")
+    parts = Mesh(mesh.devices.reshape(ZL, X, CORE, ZH, YH, YL), EVERY)
+    amp, intg = ("zl", "x", "core"), ("zh", "yh", "yl")
     return jax.shard_map(
         per_device,
         mesh=parts,

time: 114 us -> 115 us (level)
  blocking collectives: 62.9 us -> 78.4 us
  waiting for transfers between devices: 21.2 us -> 12.5 us
  starting transfers between devices: 21.9 us -> 17 us
    all_to_all x2 -> x3, blocking collectives: 48 us -> 62.9 us  [the longest x1 32.3 us: per_device(): parts = lax.all_to_all(parts, ('zh', 'yl', 'yh'), 0, 0, tiled=True)]
    all_to_all x1 -> x0, waiting for transfers between devices: 6.84 us -> none  [per_device(): gathered = lax.all_to_all(copies, 'x', 0, 0, tiled=True)]
    all_to_all x1 -> x0, starting transfers between devices: 4.29 us -> none  [per_device(): gathered = lax.all_to_all(copies, 'x', 0, 0, tiled=True)]
    ppermute x1, waiting for transfers between devices: 1.88 us -> 0.01 us  [per_device(): other = lax.ppermute(cycle_block, 'core', swap)]
  transfers between devices with their start and end apart: 5 -> 4, of which waited for: 5 -> 3; matrix products, arithmetic and copies ran while one was open for 0% -> 0% of each run, Pallas kernels for 2% -> 2%
where the time goes in v16:
time: 115 us; the launch traced here: 114 us
  blocking collectives  78.4 us (68%)
  starting transfers between devices  17 us (15%)
  waiting for transfers between devices  12.5 us (11%)
  Pallas kernels  5.5 us (5%)
    all_to_all x1, blocking collectives, per_device(): parts = lax.all_to_all(parts, ('zh', 'yl', 'yh'), 0, 0, tiled=True)  32.3 us
    all_to_all x1, blocking collectives, per_device(): gathered = lax.all_to_all(copies, 'x', 0, 0, tiled=True)  15.6 us
    all_to_all x1, blocking collectives, per_device(): column = lax.all_to_all(copies, 'zl', 0, 0, tiled=True)  15.5 us
    all_to_all x1, blocking collectives, per_device(): window = lax.all_to_all(window, ('yh', 'yl'), 0, 0, tiled=True)  15 us
    ppermute x1, starting transfers between devices, per_device(): far = lax.ppermute(far, 'zh', swap)  8.22 us
    ppermute x1, waiting for transfers between devices, per_device(): far = lax.ppermute(far, 'zh', swap)  7.07 us
    all_to_all x1, starting transfers between devices, per_device(): lax.all_to_all(cycle.reshape(CHIPS, BLOCK, LANES), ('x', 'zl'), 0, 0, til...  4.78 us
    all_to_all x1, waiting for transfers between devices, per_device(): lax.all_to_all(cycle.reshape(CHIPS, BLOCK, LANES), ('x', 'zl'), 0, 0, til...  4.14 us
  transfers between devices with their start and end apart: 4, of which 3 were waited for; matrix products, arithmetic and copies ran while one was open for 0% of the time, Pallas kernels for 2%

profile of v16, /device:TPU:8, one launch (start us, length us, event | category | flops | bytes accessed | tf_op | source)
XLA Modules:
  0.0 114.4 jit_solution(13674094946025748694)
XLA Ops:
  0.0 0.0 copy-start.1
  0.0 2.0 %collective-permute-start = (f32[512,256]{1,0:T(8,128)}, f32[512,256]{1,0:T(8,128)S(1)}, u32[]{:S(2)}, u32[]{:S(2)}) collective-permute-start(f32[512,256]{1,0:T(8,128)} %own.1), channel_id=1, source_target_pairs={{0,16},{16,0},{1,17},{17,1},{2,18},{18,2},{3,19},{19,3},{4,20},{20... | collective-permute-start | bytes 1572872 | tf_op jit(solution)/shard_map/ppermute | solution.py:179
  2.0 0.0 copy-start.2
  2.1 0.8 copy-done.2
  2.9 15.5 %all_to_all.25 = f32[4,104,128]{2,1,0:T(8,128)S(1)} all-to-all(f32[4,104,128]{2,1,0:T(8,128)S(1)} %shard_map.64), channel_id=1, replica_groups=mesh['zl'=4,'x'=4,'core'=2,'zh'=2,'yh'=4,'yl'=2] {'zl'}, dimensions={0} | all-to-all | bytes 425984 | tf_op jit(solution)/shard_map/all_to_all | solution.py:181
  18.4 0.0 collective-permute-done.other
  18.4 0.1 broadcast_in_dim.8
  18.5 15.6 %all_to_all.26 = f32[4,416,128]{2,1,0:T(8,128)S(1)} all-to-all(f32[4,416,128]{2,1,0:T(8,128)S(1)} %broadcast_in_dim.8), channel_id=1, replica_groups=mesh['zl'=4,'x'=4,'core'=2,'zh'=2,'yh'=4,'yl'=2] {'x'}, dimensions={0} | all-to-all | bytes 1703936 | tf_op jit(solution)/shard_map/all_to_all | solution.py:184
  34.1 0.0 copy-done.1
  34.1 0.0 copy-start.4
  34.1 2.1 %shard_map.65 = f32[1664,128]{1,0:T(8,128)} custom-call(f32[1664,128]{1,0:T(8,128)S(1)} %bitcast.5, f32[512,256]{1,0:T(8,128)S(1)} %copy-done.1, f32[512,256]{1,0:T(8,128)S(1)} %collective-permute-done.other), custom_call_target="tpu_custom_call" | custom-call | tf_op jit(solution)/shard_map/pallas_call | solution.py:186
  36.2 0.0 copy-start.3
  36.2 0.0 copy-start.5
  36.2 0.0 copy-start
  36.2 4.8 %all-to-all-start.2 = ((f32[16,104,128]{2,1,0:T(8,128)}), f32[16,104,128]{2,1,0:T(8,128)S(1)}, u32[]{:S(2)}, u32[]{:S(2)}) async-start(f32[16,104,128]{2,1,0:T(8,128)} %bitcast.3), calls=%async_computation.2 | async-start | bytes 1703936 | tf_op jit(solution)/shard_map/all_to_all | solution.py:188
  41.0 0.0 copy-done.4
  41.0 1.4 %shard_map.66 = f32[2,128,128]{2,1,0:T(8,128)S(1)} custom-call(s32[2]{0:T(128)S(1)} %copy-done.4, f32[1664,128]{1,0:T(8,128)S(1)} %bitcast.6), custom_call_target="tpu_custom_call" | custom-call | tf_op jit(solution)/shard_map/pallas_call | solution.py:190
  42.4 1.9 %collective-permute-start.1 = (f32[2,8,16,128]{3,2,1,0:T(8,128)S(1)}, f32[2,8,16,128]{3,2,1,0:T(8,128)S(1)}, u32[]{:S(2)}, u32[]{:S(2)}) collective-permute-start(f32[2,8,16,128]{3,2,1,0:T(8,128)S(1)} %bitcast.8), channel_id=1, source_target_pairs={{0,16},{16,0},{1,17},{17,1},{2,18},{18,2},{3,19},{19,3},{4,20},{20... | collective-permute-start | bytes 393224 | tf_op jit(solution)/shard_map/ppermute | solution.py:197
  44.3 1.3 %collective-permute-done.1.other = f32[2,8,16,128]{3,2,1,0:T(8,128)S(1)} collective-permute-done((f32[2,8,16,128]{3,2,1,0:T(8,128)S(1)}, f32[2,8,16,128]{3,2,1,0:T(8,128)S(1)}, u32[]{:S(2)}, u32[]{:S(2)}) %collective-permute-start.1) | collective-permute-done | bytes 131104 | tf_op jit(solution)/shard_map/ppermute | solution.py:197
  45.7 8.2 %collective-permute-start.2 = (f32[8,16,128]{2,1,0:T(8,128)S(1)}, f32[8,16,128]{2,1,0:T(8,128)S(1)}, u32[]{:S(2)}, u32[]{:S(2)}) collective-permute-start(f32[8,16,128]{2,1,0:T(8,128)S(1)} %get-tuple-element.18), channel_id=1, source_target_pairs={{0,8},{8,0},{1,9},{9,1},{2,10},{10,2},{3,11},{11,3},{4,12},{12,4},... | collective-permute-start | bytes 196616 | tf_op jit(solution)/shard_map/ppermute | solution.py:199
  53.9 0.0 copy-done.3
  53.9 0.0 copy-done.5
  53.9 0.7 shard_map.69.denominator
  54.6 7.1 %collective-permute-done.2.far = f32[8,16,128]{2,1,0:T(8,128)S(1)} collective-permute-done((f32[8,16,128]{2,1,0:T(8,128)S(1)}, f32[8,16,128]{2,1,0:T(8,128)S(1)}, u32[]{:S(2)}, u32[]{:S(2)}) %collective-permute-start.2) | collective-permute-done | bytes 65568 | tf_op jit(solution)/shard_map/ppermute | solution.py:199
  61.7 4.1 %all-to-all-done.2.cycle = f32[16,104,128]{2,1,0:T(8,128)S(1)} async-done(((f32[16,104,128]{2,1,0:T(8,128)}), f32[16,104,128]{2,1,0:T(8,128)S(1)}, u32[]{:S(2)}, u32[]{:S(2)}) %all-to-all-start.2) | async-done | bytes 852000 | tf_op jit(solution)/shard_map/all_to_all | solution.py:188
  65.8 15.0 %all_to_all.27.window = f32[8,32,128]{2,1,0:T(8,128)S(1)} all-to-all(f32[8,32,128]{2,1,0:T(8,128)S(1)} %shard_map.68), channel_id=1, replica_groups=mesh['zl'=4,'x'=4,'core'=2,'zh'=2,'yh'=4,'yl'=2] {'yh','yl'}, dimensions={0} | all-to-all | bytes 262144 | tf_op jit(solution)/shard_map/all_to_all | solution.py:205
  80.8 0.0 copy-done
  80.8 0.6 shard_map.70
  81.4 32.3 %all_to_all.28.parts = f32[16,104,128]{2,1,0:T(8,128)S(1)} all-to-all(f32[16,104,128]{2,1,0:T(8,128)S(1)} %shard_map.70), channel_id=1, replica_groups=mesh['zl'=4,'x'=4,'core'=2,'zh'=2,'yh'=4,'yl'=2] {'zh','yl','yh'}, dimensions={0} | all-to-all | bytes 1703936 | tf_op jit(solution)/shard_map/all_to_all | solution.py:209
  113.7 0.7 shard_map.71
  (3 shorter events, 0.0 us)
Async XLA Ops:
  0.0 34.1 %copy-start.1 = (f32[512,256]{1,0:T(8,128)S(1)}, f32[512,256]{1,0:T(8,128)}, u32[]{:S(2)}) copy-start(f32[512,256]{1,0:T(8,128)} %own.1) | copy-start | bytes 1572868
  0.0 18.4 %collective-permute-start = (f32[512,256]{1,0:T(8,128)}, f32[512,256]{1,0:T(8,128)S(1)}, u32[]{:S(2)}, u32[]{:S(2)}) collective-permute-start(f32[512,256]{1,0:T(8,128)} %own.1), channel_id=1, source_target_pairs={{0,16},{16,0},{1,17},{17,1},{2,18},{18,2},{3,19},{19,3},{4,20},{20... | collective-permute-start | bytes 1572872 | tf_op jit(solution)/shard_map/ppermute | solution.py:179
  2.0 0.8 copy-start.2
  34.1 6.9 %copy-start.4 = (s32[2]{0:T(128)S(1)}, s32[2]{0:T(128)}, u32[]{:S(2)}) copy-start(s32[2]{0:T(128)} %tiles.3) | copy-start | bytes 28
  36.2 17.7 %copy-start.3 = (f32[832]{0:T(1024)S(1)}, f32[832]{0:T(1024)}, u32[]{:S(2)}) copy-start(f32[832]{0:T(1024)} %virtual.1) | copy-start | bytes 9988
  36.2 17.7 %copy-start.5 = (f32[128]{0:T(128)S(1)}, f32[128]{0:T(128)}, u32[]{:S(2)}) copy-start(f32[128]{0:T(128)} %occupied.1) | copy-start | bytes 1540
  36.2 44.6 %copy-start = (f32[4,64,1664]{2,1,0:T(8,128)S(1)}, f32[4,64,1664]{2,1,0:T(8,128)}, u32[]{:S(2)}) copy-start(f32[4,64,1664]{2,1,0:T(8,128)} %param.8) | copy-start | bytes 5111812
  36.2 29.7 %all-to-all-start.2 = ((f32[16,104,128]{2,1,0:T(8,128)}), f32[16,104,128]{2,1,0:T(8,128)S(1)}, u32[]{:S(2)}, u32[]{:S(2)}) async-start(f32[16,104,128]{2,1,0:T(8,128)} %bitcast.3), calls=%async_computation.2 | async-start | bytes 1703936 | tf_op jit(solution)/shard_map/all_to_all | solution.py:188
  42.4 3.2 %collective-permute-start.1 = (f32[2,8,16,128]{3,2,1,0:T(8,128)S(1)}, f32[2,8,16,128]{3,2,1,0:T(8,128)S(1)}, u32[]{:S(2)}, u32[]{:S(2)}) collective-permute-start(f32[2,8,16,128]{3,2,1,0:T(8,128)S(1)} %bitcast.8), channel_id=1, source_target_pairs={{0,16},{16,0},{1,17},{17,1},{2,18},{18,2},{3,19},{19,3},{4,20},{20... | collective-permute-start | bytes 393224 | tf_op jit(solution)/shard_map/ppermute | solution.py:197
  45.7 16.0 %collective-permute-start.2 = (f32[8,16,128]{2,1,0:T(8,128)S(1)}, f32[8,16,128]{2,1,0:T(8,128)S(1)}, u32[]{:S(2)}, u32[]{:S(2)}) collective-permute-start(f32[8,16,128]{2,1,0:T(8,128)S(1)} %get-tuple-element.18), channel_id=1, source_target_pairs={{0,8},{8,0},{1,9},{9,1},{2,10},{10,2},{3,11},{11,3},{4,12},{12,4},... | collective-permute-start | bytes 196616 | tf_op jit(solution)/shard_map/ppermute | solution.py:199

commit v17 on v15

--- a/solution.py
+++ b/solution.py
@@ -49,9 +49,17 @@
 
 def pack_kernel(amplitudes, out):
     for pair in range(PAIRS):
-        tile = amplitudes[0, :, pair * LANES : (pair + 1) * LANES]
-        for chip in range(ZL):
-            out[chip, pair * ROWS : (pair + 1) * ROWS, :] = tile
+        out[pair * ROWS : (pair + 1) * ROWS, :] = amplitudes[0, :, pair * LANES : (pair + 1) * LANES]
+
+
+def spread_kernel(*blocks):
+    out = blocks[-1]
+    zl = lax.axis_index("zl")
+    for back, block in enumerate(blocks[:-1]):
+        start = pl.multiple_of((zl + ZL - back) % ZL * BLOCK, ROWS)
+        value = block[...]
+        for x in range(X):
+            out[x, pl.ds(start, BLOCK), :] = value
 
 
 def window_kernel(tiles, gathered, out, window, columns, turned):
@@ -172,9 +180,11 @@
 def per_device(amplitudes, cycle_block, ladder_block, occupied, virtual, tiles):
     swap = [(0, 1), (1, 0)]
     other = lax.ppermute(cycle_block, "core", swap)
-    (copies,) = call(pack_kernel, [(ZL, BLOCK, LANES)], [VMEM])(amplitudes)
-    column = lax.all_to_all(copies, "zl", 0, 0, tiled=True)
-    copies = jnp.broadcast_to(column.reshape(1, ZL * BLOCK, LANES), (X, ZL * BLOCK, LANES))
+    (packed,) = call(pack_kernel, [(BLOCK, LANES)], [VMEM])(amplitudes)
+    blocks = [packed]
+    for step in range(1, ZL):
+        blocks.append(lax.ppermute(packed, "zl", [(i, (i + step) % ZL) for i in range(ZL)]))
+    (copies,) = call(spread_kernel, [(X, ZL * BLOCK, LANES)], [VMEM] * ZL)(*blocks)
     gathered = lax.all_to_all(copies, "x", 0, 0, tiled=True)
     gathered = gathered.reshape(CHIPS * BLOCK, LANES)
     (cycle,) = call(cycle_kernel, [(CHIPS * BLOCK, LANES)], [VMEM] * 3)(gathered, cycle_block, other)

time: 114 us -> 113 us (level)
  blocking collectives: 62.9 us -> 48.4 us
  starting transfers between devices: 21.9 us -> 34.5 us
  waiting for transfers between devices: 21.2 us -> 22.5 us
    all_to_all x1 -> x0, blocking collectives: 14.9 us -> none  [per_device(): column = lax.all_to_all(copies, 'zl', 0, 0, tiled=True)]
    ppermute x0 -> x3, starting transfers between devices: none -> 12.8 us  [per_device(): lax.ppermute(packed, 'zl', [(i, (i + step) % ZL) for i in range(ZL)])]
    ppermute x0 -> x3, waiting for transfers between devices: none -> 3.54 us  [per_device(): lax.ppermute(packed, 'zl', [(i, (i + step) % ZL) for i in range(ZL)])]
    ppermute x1, waiting for transfers between devices: 7.05 us -> 5.32 us  [per_device(): far = lax.ppermute(far, 'zh', swap)]
    all_to_all x1, waiting for transfers between devices: 4.13 us -> 2.96 us  [per_device(): lax.all_to_all(cycle.reshape(CHIPS, BLOCK, LANES), ('x', 'zl'), 0, 0, til...]
  transfers between devices with their start and end apart: 5 -> 8, of which waited for: 5 -> 6; matrix products, arithmetic and copies ran while one was open for 0% -> 0% of each run, Pallas kernels for 2% -> 2%
where the time goes in v17:
time: 113 us
  blocking collectives  48.4 us (43%)
  starting transfers between devices  34.5 us (31%)
  waiting for transfers between devices  22.5 us (20%)
  Pallas kernels  6.42 us (6%)
    all_to_all x1, blocking collectives, per_device(): parts = lax.all_to_all(parts, ('zh', 'y'), 0, 0, tiled=True)  33.5 us
    all_to_all x1, blocking collectives, per_device(): window = lax.all_to_all(window, 'y', 0, 0, tiled=True)  15 us
    ppermute x3, starting transfers between devices, per_device(): lax.ppermute(packed, 'zl', [(i, (i + step) % ZL) for i in range(ZL)])  12.8 us
    ppermute x1, starting transfers between devices, per_device(): far = lax.ppermute(far, 'zh', swap)  9.12 us
    all_to_all x1, waiting for transfers between devices, per_device(): gathered = lax.all_to_all(copies, 'x', 0, 0, tiled=True)  7.48 us
    ppermute x1, waiting for transfers between devices, per_device(): far = lax.ppermute(far, 'zh', swap)  5.32 us
    all_to_all x1, starting transfers between devices, per_device(): lax.all_to_all(cycle.reshape(CHIPS, BLOCK, LANES), ('x', 'zl'), 0, 0, til...  4.47 us
    all_to_all x1, starting transfers between devices, per_device(): gathered = lax.all_to_all(copies, 'x', 0, 0, tiled=True)  4.29 us
  transfers between devices with their start and end apart: 8, of which 6 were waited for; matrix products, arithmetic and copies ran while one was open for 0% of the time, Pallas kernels for 2%

profile of v17, /device:TPU:8, one launch (start us, length us, event | category | flops | bytes accessed | tf_op | source)
XLA Modules:
  0.0 112.9 jit_solution(16883539141316660612)
XLA Ops:
  0.0 0.0 copy-start.1
  0.0 0.0 copy-start.2
  0.0 0.9 copy-done.2
  0.9 4.3 %collective-permute-start = (f32[104,128]{1,0:T(8,128)S(1)}, f32[104,128]{1,0:T(8,128)S(1)}, u32[]{:S(2)}, u32[]{:S(2)}) collective-permute-start(f32[104,128]{1,0:T(8,128)S(1)} %shard_map.64.blocks_0_), channel_id=1, source_target_pairs={{0,128},{128,256},{256,384},{384,0},{1,129},{129,257},{257,385},{3... | collective-permute-start | bytes 159752 | tf_op jit(solution)/shard_map/ppermute | solution.py:186
  5.2 6.1 %collective-permute-start.1 = (f32[104,128]{1,0:T(8,128)S(1)}, f32[104,128]{1,0:T(8,128)S(1)}, u32[]{:S(2)}, u32[]{:S(2)}) collective-permute-start(f32[104,128]{1,0:T(8,128)S(1)} %shard_map.64.blocks_0_), channel_id=1, source_target_pairs={{0,256},{128,384},{256,0},{384,128},{1,257},{129,385},{257,1},{385... | collective-permute-start | bytes 159752 | tf_op jit(solution)/shard_map/ppermute | solution.py:186
  11.2 2.5 %collective-permute-start.2 = (f32[104,128]{1,0:T(8,128)S(1)}, f32[104,128]{1,0:T(8,128)S(1)}, u32[]{:S(2)}, u32[]{:S(2)}) collective-permute-start(f32[104,128]{1,0:T(8,128)S(1)} %shard_map.64.blocks_0_), channel_id=1, source_target_pairs={{0,384},{128,0},{256,128},{384,256},{1,385},{129,1},{257,129},{385... | collective-permute-start | bytes 159752 | tf_op jit(solution)/shard_map/ppermute | solution.py:186
  13.7 0.0 collective-permute-done.blocks_1_
  13.7 0.0 collective-permute-done.1.blocks_2_
  13.7 3.5 %collective-permute-done.2.blocks_3_ = f32[104,128]{1,0:T(8,128)S(1)} collective-permute-done((f32[104,128]{1,0:T(8,128)S(1)}, f32[104,128]{1,0:T(8,128)S(1)}, u32[]{:S(2)}, u32[]{:S(2)}) %collective-permute-start.2) | collective-permute-done | bytes 53280 | tf_op jit(solution)/shard_map/ppermute | solution.py:186
  17.3 1.0 shard_map.65
  18.2 4.3 %all-to-all-start = ((f32[4,416,128]{2,1,0:T(8,128)}), f32[4,416,128]{2,1,0:T(8,128)S(1)}, u32[]{:S(2)}, u32[]{:S(2)}) async-start(f32[4,416,128]{2,1,0:T(8,128)} %shard_map.65), calls=%async_computation | async-start | bytes 1703936 | tf_op jit(solution)/shard_map/all_to_all | solution.py:188
  22.5 0.0 copy-done.1
  22.5 1.9 %collective-permute-start.3 = (f32[512,256]{1,0:T(8,128)S(1)}, f32[512,256]{1,0:T(8,128)S(1)}, u32[]{:S(2)}, u32[]{:S(2)}) collective-permute-start(f32[512,256]{1,0:T(8,128)S(1)} %copy-done.1), channel_id=1, source_target_pairs={{0,16},{16,0},{1,17},{17,1},{2,18},{18,2},{3,19},{19,3},{4,20},{20... | collective-permute-start | bytes 1572872 | tf_op jit(solution)/shard_map/ppermute | solution.py:182
  24.5 1.9 %collective-permute-done.3.other = f32[512,256]{1,0:T(8,128)S(1)} collective-permute-done((f32[512,256]{1,0:T(8,128)S(1)}, f32[512,256]{1,0:T(8,128)S(1)}, u32[]{:S(2)}, u32[]{:S(2)}) %collective-permute-start.3) | collective-permute-done | bytes 524320 | tf_op jit(solution)/shard_map/ppermute | solution.py:182
  26.3 7.5 %all-to-all-done = f32[4,416,128]{2,1,0:T(8,128)S(1)} async-done(((f32[4,416,128]{2,1,0:T(8,128)}), f32[4,416,128]{2,1,0:T(8,128)S(1)}, u32[]{:S(2)}, u32[]{:S(2)}) %all-to-all-start) | async-done | bytes 852000 | tf_op jit(solution)/shard_map/all_to_all | solution.py:188
  33.8 0.0 copy-start.4
  33.8 2.0 %shard_map.66 = f32[1664,128]{1,0:T(8,128)} custom-call(f32[1664,128]{1,0:T(8,128)S(1)} %bitcast.4, f32[512,256]{1,0:T(8,128)S(1)} %copy-done.1, f32[512,256]{1,0:T(8,128)S(1)} %collective-permute-done.3.other), custom_call_target="tpu_custom_call" | custom-call | tf_op jit(solution)/shard_map/pallas_call | solution.py:190
  35.8 0.0 copy-start.3
  35.8 0.0 copy-start.5
  35.8 0.0 copy-start
  35.9 4.5 %all-to-all-start.1 = ((f32[16,104,128]{2,1,0:T(8,128)}), f32[16,104,128]{2,1,0:T(8,128)S(1)}, u32[]{:S(2)}, u32[]{:S(2)}) async-start(f32[16,104,128]{2,1,0:T(8,128)} %bitcast.2), calls=%async_computation.1 | async-start | bytes 1703936 | tf_op jit(solution)/shard_map/all_to_all | solution.py:192
  40.3 0.0 copy-done.4
  40.3 1.4 %shard_map.67 = f32[2,128,128]{2,1,0:T(8,128)S(1)} custom-call(s32[2]{0:T(128)S(1)} %copy-done.4, f32[1664,128]{1,0:T(8,128)S(1)} %bitcast.5), custom_call_target="tpu_custom_call" | custom-call | tf_op jit(solution)/shard_map/pallas_call | solution.py:194
  41.8 1.9 %collective-permute-start.4 = (f32[2,8,16,128]{3,2,1,0:T(8,128)S(1)}, f32[2,8,16,128]{3,2,1,0:T(8,128)S(1)}, u32[]{:S(2)}, u32[]{:S(2)}) collective-permute-start(f32[2,8,16,128]{3,2,1,0:T(8,128)S(1)} %bitcast.7), channel_id=1, source_target_pairs={{0,16},{16,0},{1,17},{17,1},{2,18},{18,2},{3,19},{19,3},{4,20},{20... | collective-permute-start | bytes 393224 | tf_op jit(solution)/shard_map/ppermute | solution.py:201
  43.7 1.3 %collective-permute-done.4.other = f32[2,8,16,128]{3,2,1,0:T(8,128)S(1)} collective-permute-done((f32[2,8,16,128]{3,2,1,0:T(8,128)S(1)}, f32[2,8,16,128]{3,2,1,0:T(8,128)S(1)}, u32[]{:S(2)}, u32[]{:S(2)}) %collective-permute-start.4) | collective-permute-done | bytes 131104 | tf_op jit(solution)/shard_map/ppermute | solution.py:201
  45.0 9.1 %collective-permute-start.5 = (f32[8,16,128]{2,1,0:T(8,128)S(1)}, f32[8,16,128]{2,1,0:T(8,128)S(1)}, u32[]{:S(2)}, u32[]{:S(2)}) collective-permute-start(f32[8,16,128]{2,1,0:T(8,128)S(1)} %get-tuple-element.14), channel_id=1, source_target_pairs={{0,8},{8,0},{1,9},{9,1},{2,10},{10,2},{3,11},{11,3},{4,12},{12,4},... | collective-permute-start | bytes 196616 | tf_op jit(solution)/shard_map/ppermute | solution.py:203
  54.2 0.0 copy-done.3
  54.2 0.0 copy-done.5
  54.2 0.7 shard_map.70.denominator
  54.9 5.3 %collective-permute-done.5.far = f32[8,16,128]{2,1,0:T(8,128)S(1)} collective-permute-done((f32[8,16,128]{2,1,0:T(8,128)S(1)}, f32[8,16,128]{2,1,0:T(8,128)S(1)}, u32[]{:S(2)}, u32[]{:S(2)}) %collective-permute-start.5) | collective-permute-done | bytes 65568 | tf_op jit(solution)/shard_map/ppermute | solution.py:203
  60.2 3.0 %all-to-all-done.1.cycle = f32[16,104,128]{2,1,0:T(8,128)S(1)} async-done(((f32[16,104,128]{2,1,0:T(8,128)}), f32[16,104,128]{2,1,0:T(8,128)S(1)}, u32[]{:S(2)}, u32[]{:S(2)}) %all-to-all-start.1) | async-done | bytes 852000 | tf_op jit(solution)/shard_map/all_to_all | solution.py:192
  63.2 15.0 %all_to_all.20.window = f32[8,32,128]{2,1,0:T(8,128)S(1)} all-to-all(f32[8,32,128]{2,1,0:T(8,128)S(1)} %shard_map.69), channel_id=1, replica_groups=mesh['zl'=4,'x'=4,'core'=2,'zh'=2,'y'=8] {'y'}, dimensions={0} | all-to-all | bytes 262144 | tf_op jit(solution)/shard_map/all_to_all | solution.py:209
  78.1 0.0 copy-done
  78.1 0.6 shard_map.71
  78.7 33.5 %all_to_all.21.parts = f32[16,104,128]{2,1,0:T(8,128)S(1)} all-to-all(f32[16,104,128]{2,1,0:T(8,128)S(1)} %shard_map.71), channel_id=1, replica_groups=mesh['zl'=4,'x'=4,'core'=2,'zh'=2,'y'=8] {'zh','y'}, dimensions={0} | all-to-all | bytes 1703936 | tf_op jit(solution)/shard_map/all_to_all | solution.py:213
  112.2 0.7 shard_map.72
  (3 shorter events, 0.0 us)
Async XLA Ops:
  0.0 22.5 %copy-start.1 = (f32[512,256]{1,0:T(8,128)S(1)}, f32[512,256]{1,0:T(8,128)}, u32[]{:S(2)}) copy-start(f32[512,256]{1,0:T(8,128)} %own.1) | copy-start | bytes 1572868
  0.0 0.9 copy-start.2
  0.9 12.8 %collective-permute-start = (f32[104,128]{1,0:T(8,128)S(1)}, f32[104,128]{1,0:T(8,128)S(1)}, u32[]{:S(2)}, u32[]{:S(2)}) collective-permute-start(f32[104,128]{1,0:T(8,128)S(1)} %shard_map.64.blocks_0_), channel_id=1, source_target_pairs={{0,128},{128,256},{256,384},{384,0},{1,129},{129,257},{257,385},{3... | collective-permute-start | bytes 159752 | tf_op jit(solution)/shard_map/ppermute | solution.py:186
  5.2 8.6 %collective-permute-start.1 = (f32[104,128]{1,0:T(8,128)S(1)}, f32[104,128]{1,0:T(8,128)S(1)}, u32[]{:S(2)}, u32[]{:S(2)}) collective-permute-start(f32[104,128]{1,0:T(8,128)S(1)} %shard_map.64.blocks_0_), channel_id=1, source_target_pairs={{0,256},{128,384},{256,0},{384,128},{1,257},{129,385},{257,1},{385... | collective-permute-start | bytes 159752 | tf_op jit(solution)/shard_map/ppermute | solution.py:186
  11.2 6.0 %collective-permute-start.2 = (f32[104,128]{1,0:T(8,128)S(1)}, f32[104,128]{1,0:T(8,128)S(1)}, u32[]{:S(2)}, u32[]{:S(2)}) collective-permute-start(f32[104,128]{1,0:T(8,128)S(1)} %shard_map.64.blocks_0_), channel_id=1, source_target_pairs={{0,384},{128,0},{256,128},{384,256},{1,385},{129,1},{257,129},{385... | collective-permute-start | bytes 159752 | tf_op jit(solution)/shard_map/ppermute | solution.py:186
  18.2 15.6 %all-to-all-start = ((f32[4,416,128]{2,1,0:T(8,128)}), f32[4,416,128]{2,1,0:T(8,128)S(1)}, u32[]{:S(2)}, u32[]{:S(2)}) async-start(f32[4,416,128]{2,1,0:T(8,128)} %shard_map.65), calls=%async_computation | async-start | bytes 1703936 | tf_op jit(solution)/shard_map/all_to_all | solution.py:188
  22.5 3.8 %collective-permute-start.3 = (f32[512,256]{1,0:T(8,128)S(1)}, f32[512,256]{1,0:T(8,128)S(1)}, u32[]{:S(2)}, u32[]{:S(2)}) collective-permute-start(f32[512,256]{1,0:T(8,128)S(1)} %copy-done.1), channel_id=1, source_target_pairs={{0,16},{16,0},{1,17},{17,1},{2,18},{18,2},{3,19},{19,3},{4,20},{20... | collective-permute-start | bytes 1572872 | tf_op jit(solution)/shard_map/ppermute | solution.py:182
  33.8 6.5 %copy-start.4 = (s32[2]{0:T(128)S(1)}, s32[2]{0:T(128)}, u32[]{:S(2)}) copy-start(s32[2]{0:T(128)} %tiles.3) | copy-start | bytes 28
  35.8 18.3 %copy-start.3 = (f32[832]{0:T(1024)S(1)}, f32[832]{0:T(1024)}, u32[]{:S(2)}) copy-start(f32[832]{0:T(1024)} %virtual.1) | copy-start | bytes 9988
  35.8 18.3 %copy-start.5 = (f32[128]{0:T(128)S(1)}, f32[128]{0:T(128)}, u32[]{:S(2)}) copy-start(f32[128]{0:T(128)} %occupied.1) | copy-start | bytes 1540
  35.8 42.3 %copy-start = (f32[4,64,1664]{2,1,0:T(8,128)S(1)}, f32[4,64,1664]{2,1,0:T(8,128)}, u32[]{:S(2)}) copy-start(f32[4,64,1664]{2,1,0:T(8,128)} %param.8) | copy-start | bytes 5111812
  35.9 27.3 %all-to-all-start.1 = ((f32[16,104,128]{2,1,0:T(8,128)}), f32[16,104,128]{2,1,0:T(8,128)S(1)}, u32[]{:S(2)}, u32[]{:S(2)}) async-start(f32[16,104,128]{2,1,0:T(8,128)} %bitcast.2), calls=%async_computation.1 | async-start | bytes 1703936 | tf_op jit(solution)/shard_map/all_to_all | solution.py:192
  41.8 3.2 %collective-permute-start.4 = (f32[2,8,16,128]{3,2,1,0:T(8,128)S(1)}, f32[2,8,16,128]{3,2,1,0:T(8,128)S(1)}, u32[]{:S(2)}, u32[]{:S(2)}) collective-permute-start(f32[2,8,16,128]{3,2,1,0:T(8,128)S(1)} %bitcast.7), channel_id=1, source_target_pairs={{0,16},{16,0},{1,17},{17,1},{2,18},{18,2},{3,19},{19,3},{4,20},{20... | collective-permute-start | bytes 393224 | tf_op jit(solution)/shard_map/ppermute | solution.py:201
  45.0 15.2 %collective-permute-start.5 = (f32[8,16,128]{2,1,0:T(8,128)S(1)}, f32[8,16,128]{2,1,0:T(8,128)S(1)}, u32[]{:S(2)}, u32[]{:S(2)}) collective-permute-start(f32[8,16,128]{2,1,0:T(8,128)S(1)} %get-tuple-element.14), channel_id=1, source_target_pairs={{0,8},{8,0},{1,9},{9,1},{2,10},{10,2},{3,11},{11,3},{4,12},{12,4},... | collective-permute-start | bytes 196616 | tf_op jit(solution)/shard_map/ppermute | solution.py:203

commit v18 on v15

--- a/solution.py
+++ b/solution.py
@@ -79,13 +79,17 @@
 
 
 def add_kernel(own, other, near, far):
+    core = lax.axis_index("core")
     near[...] = own[0] + other[0]
-    far[...] = own[1] + other[1]
-
-
-def join_kernel(near, far, out):
+    total = own[1] + other[1]
+    far[...] = jnp.where(core == 0, total[:, :ROWS], total[:, ROWS:])
+
+
+def join_kernel(near, mine, theirs, out):
+    core = lax.axis_index("core")
     out[:, : 2 * ROWS, :] = near[...]
-    out[:, 2 * ROWS :, :] = far[...]
+    out[:, 2 * ROWS : 3 * ROWS, :] = jnp.where(core == 0, mine[...], theirs[...])
+    out[:, 3 * ROWS :, :] = jnp.where(core == 0, theirs[...], mine[...])
 
 
 def cycle_kernel(gathered, own, other, out):
@@ -189,9 +193,12 @@
     )(tiles, gathered)
     window = window.reshape(2, Y, 2 * ROWS, LANES)
     other_window = lax.ppermute(window, "core", swap)
-    near, far = call(add_kernel, [(Y, 2 * ROWS, LANES)] * 2, [VMEM] * 2)(window, other_window)
-    far = lax.ppermute(far, "zh", swap)
-    (window,) = call(join_kernel, [(Y, 4 * ROWS, LANES)], [VMEM] * 2)(near, far)
+    near, far = call(
+        add_kernel, [(Y, 2 * ROWS, LANES), (Y, ROWS, LANES)], [VMEM] * 2
+    )(window, other_window)
+    mine = lax.ppermute(far, "zh", swap)
+    theirs = lax.ppermute(mine, "core", swap)
+    (window,) = call(join_kernel, [(Y, 4 * ROWS, LANES)], [VMEM] * 3)(near, mine, theirs)
     (denominator,) = call(denominator_kernel, [(BLOCK, LANES)], [SMEM] * 3)(
         tiles, occupied, virtual
     )

time: 114 us -> 113 us (level)
  waiting for transfers between devices: 21.2 us -> 17.9 us
  starting transfers between devices: 21.9 us -> 23.8 us
    all_to_all x1, waiting for transfers between devices: 4.13 us -> 0.19 us  [per_device(): lax.all_to_all(cycle.reshape(CHIPS, BLOCK, LANES), ('x', 'zl'), 0, 0, til...]
    ppermute x1 -> x2, starting transfers between devices: 8.22 us -> 10.1 us  [the longest x1 8.22 us: per_device(): mine = lax.ppermute(far, 'zh', swap)]
    ppermute x1 -> x2, waiting for transfers between devices: 7.05 us -> 7.67 us  [the longest x1 7.2 us: per_device(): mine = lax.ppermute(far, 'zh', swap)]
  transfers between devices with their start and end apart: 5 -> 6, of which waited for: 5 -> 6; matrix products, arithmetic and copies ran while one was open for 0% -> 0% of each run, Pallas kernels for 2% -> 2%
where the time goes in v18:
time: 113 us; the launch traced here: 112 us
  blocking collectives  62.9 us (56%)
  starting transfers between devices  23.8 us (21%)
  waiting for transfers between devices  17.9 us (16%)
  Pallas kernels  5.48 us (5%)
  local copies, waits for them, and re-layouts  1.85 us (2%)
    all_to_all x1, blocking collectives, per_device(): parts = lax.all_to_all(parts, ('zh', 'y'), 0, 0, tiled=True)  33 us
    all_to_all x1, blocking collectives, per_device(): window = lax.all_to_all(window, 'y', 0, 0, tiled=True)  15.1 us
    all_to_all x1, blocking collectives, per_device(): column = lax.all_to_all(copies, 'zl', 0, 0, tiled=True)  14.9 us
    ppermute x1, starting transfers between devices, per_device(): mine = lax.ppermute(far, 'zh', swap)  8.22 us
    ppermute x1, waiting for transfers between devices, per_device(): mine = lax.ppermute(far, 'zh', swap)  7.2 us
    all_to_all x1, waiting for transfers between devices, per_device(): gathered = lax.all_to_all(copies, 'x', 0, 0, tiled=True)  6.84 us
    all_to_all x1, starting transfers between devices, per_device(): lax.all_to_all(cycle.reshape(CHIPS, BLOCK, LANES), ('x', 'zl'), 0, 0, til...  5.59 us
    all_to_all x1, starting transfers between devices, per_device(): gathered = lax.all_to_all(copies, 'x', 0, 0, tiled=True)  4.29 us
  transfers between devices with their start and end apart: 6, of which 6 were waited for; matrix products, arithmetic and copies ran while one was open for 0% of the time, Pallas kernels for 2%

profile of v18, /device:TPU:8, one launch (start us, length us, event | category | flops | bytes accessed | tf_op | source)
XLA Modules:
  0.0 112.1 jit_solution(5524297906048144176)
XLA Ops:
  0.0 0.0 copy-start.1
  0.0 0.0 copy-start.2
  0.0 0.9 copy-done.2
  0.9 14.9 %all_to_all.25 = f32[4,104,128]{2,1,0:T(8,128)S(1)} all-to-all(f32[4,104,128]{2,1,0:T(8,128)S(1)} %shard_map.64), channel_id=1, replica_groups=mesh['zl'=4,'x'=4,'core'=2,'zh'=2,'y'=8] {'zl'}, dimensions={0} | all-to-all | bytes 425984 | tf_op jit(solution)/shard_map/all_to_all | solution.py:180
  15.8 1.0 broadcast_in_dim.8
  16.7 4.3 %all-to-all-start.1 = ((f32[4,416,128]{2,1,0:T(8,128)}), f32[4,416,128]{2,1,0:T(8,128)S(1)}, u32[]{:S(2)}, u32[]{:S(2)}) async-start(f32[4,416,128]{2,1,0:T(8,128)} %broadcast_in_dim.8), calls=%async_computation.1 | async-start | bytes 1703936 | tf_op jit(solution)/shard_map/all_to_all | solution.py:182
  21.0 0.0 copy-done.1
  21.0 1.9 %collective-permute-start = (f32[512,256]{1,0:T(8,128)S(1)}, f32[512,256]{1,0:T(8,128)S(1)}, u32[]{:S(2)}, u32[]{:S(2)}) collective-permute-start(f32[512,256]{1,0:T(8,128)S(1)} %copy-done.1), channel_id=1, source_target_pairs={{0,16},{16,0},{1,17},{17,1},{2,18},{18,2},{3,19},{19,3},{4,20},{20... | collective-permute-start | bytes 1572872 | tf_op jit(solution)/shard_map/ppermute | solution.py:178
  22.9 1.9 %collective-permute-done.other = f32[512,256]{1,0:T(8,128)S(1)} collective-permute-done((f32[512,256]{1,0:T(8,128)S(1)}, f32[512,256]{1,0:T(8,128)S(1)}, u32[]{:S(2)}, u32[]{:S(2)}) %collective-permute-start) | collective-permute-done | bytes 524320 | tf_op jit(solution)/shard_map/ppermute | solution.py:178
  24.8 6.8 %all-to-all-done.1 = f32[4,416,128]{2,1,0:T(8,128)S(1)} async-done(((f32[4,416,128]{2,1,0:T(8,128)}), f32[4,416,128]{2,1,0:T(8,128)S(1)}, u32[]{:S(2)}, u32[]{:S(2)}) %all-to-all-start.1) | async-done | bytes 852000 | tf_op jit(solution)/shard_map/all_to_all | solution.py:182
  31.7 0.0 copy-start.4
  31.7 2.0 %shard_map.65 = f32[1664,128]{1,0:T(8,128)} custom-call(f32[1664,128]{1,0:T(8,128)S(1)} %bitcast.5, f32[512,256]{1,0:T(8,128)S(1)} %copy-done.1, f32[512,256]{1,0:T(8,128)S(1)} %collective-permute-done.other), custom_call_target="tpu_custom_call" | custom-call | tf_op jit(solution)/shard_map/pallas_call | solution.py:184
  33.7 0.0 copy-start.3
  33.7 0.0 copy-start.5
  33.7 0.0 copy-start
  33.7 5.6 %all-to-all-start.2 = ((f32[16,104,128]{2,1,0:T(8,128)}), f32[16,104,128]{2,1,0:T(8,128)S(1)}, u32[]{:S(2)}, u32[]{:S(2)}) async-start(f32[16,104,128]{2,1,0:T(8,128)} %bitcast.3), calls=%async_computation.2 | async-start | bytes 1703936 | tf_op jit(solution)/shard_map/all_to_all | solution.py:186
  39.3 0.0 copy-done.4
  39.3 1.4 %shard_map.66 = f32[2,128,128]{2,1,0:T(8,128)S(1)} custom-call(s32[2]{0:T(128)S(1)} %copy-done.4, f32[1664,128]{1,0:T(8,128)S(1)} %bitcast.6), custom_call_target="tpu_custom_call" | custom-call | tf_op jit(solution)/shard_map/pallas_call | solution.py:188
  40.8 1.9 %collective-permute-start.1 = (f32[2,8,16,128]{3,2,1,0:T(8,128)S(1)}, f32[2,8,16,128]{3,2,1,0:T(8,128)S(1)}, u32[]{:S(2)}, u32[]{:S(2)}) collective-permute-start(f32[2,8,16,128]{3,2,1,0:T(8,128)S(1)} %bitcast.8), channel_id=1, source_target_pairs={{0,16},{16,0},{1,17},{17,1},{2,18},{18,2},{3,19},{19,3},{4,20},{20... | collective-permute-start | bytes 393224 | tf_op jit(solution)/shard_map/ppermute | solution.py:195
  42.7 1.3 %collective-permute-done.1.other = f32[2,8,16,128]{3,2,1,0:T(8,128)S(1)} collective-permute-done((f32[2,8,16,128]{3,2,1,0:T(8,128)S(1)}, f32[2,8,16,128]{3,2,1,0:T(8,128)S(1)}, u32[]{:S(2)}, u32[]{:S(2)}) %collective-permute-start.1) | collective-permute-done | bytes 131104 | tf_op jit(solution)/shard_map/ppermute | solution.py:195
  44.0 8.2 %collective-permute-start.2 = (f32[8,8,128]{2,1,0:T(8,128)S(1)}, f32[8,8,128]{2,1,0:T(8,128)S(1)}, u32[]{:S(2)}, u32[]{:S(2)}) collective-permute-start(f32[8,8,128]{2,1,0:T(8,128)S(1)} %get-tuple-element.14), channel_id=1, source_target_pairs={{0,8},{8,0},{1,9},{9,1},{2,10},{10,2},{3,11},{11,3},{4,12},{12,4},... | collective-permute-start | bytes 98312 | tf_op jit(solution)/shard_map/ppermute | solution.py:199
  52.2 7.2 %collective-permute-done.2.mine = f32[8,8,128]{2,1,0:T(8,128)S(1)} collective-permute-done((f32[8,8,128]{2,1,0:T(8,128)S(1)}, f32[8,8,128]{2,1,0:T(8,128)S(1)}, u32[]{:S(2)}, u32[]{:S(2)}) %collective-permute-start.2) | collective-permute-done | bytes 32800 | tf_op jit(solution)/shard_map/ppermute | solution.py:199
  59.4 1.9 %collective-permute-start.3 = (f32[8,8,128]{2,1,0:T(8,128)S(1)}, f32[8,8,128]{2,1,0:T(8,128)S(1)}, u32[]{:S(2)}, u32[]{:S(2)}) collective-permute-start(f32[8,8,128]{2,1,0:T(8,128)S(1)} %collective-permute-done.2.mine), channel_id=1, source_target_pairs={{0,16},{16,0},{1,17},{17,1},{2,18},{18,2},{3,19},{19,3},{4,20},{20... | collective-permute-start | bytes 98312 | tf_op jit(solution)/shard_map/ppermute | solution.py:200
  61.4 0.0 copy-done.3
  61.4 0.0 copy-done.5
  61.4 0.7 shard_map.69.denominator
  62.1 0.5 collective-permute-done.3.theirs
  62.6 0.2 all-to-all-done.2.cycle
  62.7 15.1 %all_to_all.26.window = f32[8,32,128]{2,1,0:T(8,128)S(1)} all-to-all(f32[8,32,128]{2,1,0:T(8,128)S(1)} %shard_map.68), channel_id=1, replica_groups=mesh['zl'=4,'x'=4,'core'=2,'zh'=2,'y'=8] {'y'}, dimensions={0} | all-to-all | bytes 262144 | tf_op jit(solution)/shard_map/all_to_all | solution.py:206
  77.8 0.0 copy-done
  77.8 0.6 shard_map.70
  78.5 33.0 %all_to_all.27.parts = f32[16,104,128]{2,1,0:T(8,128)S(1)} all-to-all(f32[16,104,128]{2,1,0:T(8,128)S(1)} %shard_map.70), channel_id=1, replica_groups=mesh['zl'=4,'x'=4,'core'=2,'zh'=2,'y'=8] {'zh','y'}, dimensions={0} | all-to-all | bytes 1703936 | tf_op jit(solution)/shard_map/all_to_all | solution.py:210
  111.4 0.7 shard_map.71
  (3 shorter events, 0.0 us)
Async XLA Ops:
  0.0 21.0 %copy-start.1 = (f32[512,256]{1,0:T(8,128)S(1)}, f32[512,256]{1,0:T(8,128)}, u32[]{:S(2)}) copy-start(f32[512,256]{1,0:T(8,128)} %own.1) | copy-start | bytes 1572868
  0.0 0.9 copy-start.2
  16.7 14.9 %all-to-all-start.1 = ((f32[4,416,128]{2,1,0:T(8,128)}), f32[4,416,128]{2,1,0:T(8,128)S(1)}, u32[]{:S(2)}, u32[]{:S(2)}) async-start(f32[4,416,128]{2,1,0:T(8,128)} %broadcast_in_dim.8), calls=%async_computation.1 | async-start | bytes 1703936 | tf_op jit(solution)/shard_map/all_to_all | solution.py:182
  21.0 3.8 %collective-permute-start = (f32[512,256]{1,0:T(8,128)S(1)}, f32[512,256]{1,0:T(8,128)S(1)}, u32[]{:S(2)}, u32[]{:S(2)}) collective-permute-start(f32[512,256]{1,0:T(8,128)S(1)} %copy-done.1), channel_id=1, source_target_pairs={{0,16},{16,0},{1,17},{17,1},{2,18},{18,2},{3,19},{19,3},{4,20},{20... | collective-permute-start | bytes 1572872 | tf_op jit(solution)/shard_map/ppermute | solution.py:178
  31.7 7.6 %copy-start.4 = (s32[2]{0:T(128)S(1)}, s32[2]{0:T(128)}, u32[]{:S(2)}) copy-start(s32[2]{0:T(128)} %tiles.3) | copy-start | bytes 28
  33.7 27.7 %copy-start.3 = (f32[832]{0:T(1024)S(1)}, f32[832]{0:T(1024)}, u32[]{:S(2)}) copy-start(f32[832]{0:T(1024)} %virtual.1) | copy-start | bytes 9988
  33.7 27.7 %copy-start.5 = (f32[128]{0:T(128)S(1)}, f32[128]{0:T(128)}, u32[]{:S(2)}) copy-start(f32[128]{0:T(128)} %occupied.1) | copy-start | bytes 1540
  33.7 44.1 %copy-start = (f32[4,64,1664]{2,1,0:T(8,128)S(1)}, f32[4,64,1664]{2,1,0:T(8,128)}, u32[]{:S(2)}) copy-start(f32[4,64,1664]{2,1,0:T(8,128)} %param.8) | copy-start | bytes 5111812
  33.7 29.0 %all-to-all-start.2 = ((f32[16,104,128]{2,1,0:T(8,128)}), f32[16,104,128]{2,1,0:T(8,128)S(1)}, u32[]{:S(2)}, u32[]{:S(2)}) async-start(f32[16,104,128]{2,1,0:T(8,128)} %bitcast.3), calls=%async_computation.2 | async-start | bytes 1703936 | tf_op jit(solution)/shard_map/all_to_all | solution.py:186
  40.8 3.2 %collective-permute-start.1 = (f32[2,8,16,128]{3,2,1,0:T(8,128)S(1)}, f32[2,8,16,128]{3,2,1,0:T(8,128)S(1)}, u32[]{:S(2)}, u32[]{:S(2)}) collective-permute-start(f32[2,8,16,128]{3,2,1,0:T(8,128)S(1)} %bitcast.8), channel_id=1, source_target_pairs={{0,16},{16,0},{1,17},{17,1},{2,18},{18,2},{3,19},{19,3},{4,20},{20... | collective-permute-start | bytes 393224 | tf_op jit(solution)/shard_map/ppermute | solution.py:195
  44.0 15.4 %collective-permute-start.2 = (f32[8,8,128]{2,1,0:T(8,128)S(1)}, f32[8,8,128]{2,1,0:T(8,128)S(1)}, u32[]{:S(2)}, u32[]{:S(2)}) collective-permute-start(f32[8,8,128]{2,1,0:T(8,128)S(1)} %get-tuple-element.14), channel_id=1, source_target_pairs={{0,8},{8,0},{1,9},{9,1},{2,10},{10,2},{3,11},{11,3},{4,12},{12,4},... | collective-permute-start | bytes 98312 | tf_op jit(solution)/shard_map/ppermute | solution.py:199
  59.4 3.1 %collective-permute-start.3 = (f32[8,8,128]{2,1,0:T(8,128)S(1)}, f32[8,8,128]{2,1,0:T(8,128)S(1)}, u32[]{:S(2)}, u32[]{:S(2)}) collective-permute-start(f32[8,8,128]{2,1,0:T(8,128)S(1)} %collective-permute-done.2.mine), channel_id=1, source_target_pairs={{0,16},{16,0},{1,17},{17,1},{2,18},{18,2},{3,19},{19,3},{4,20},{20... | collective-permute-start | bytes 98312 | tf_op jit(solution)/shard_map/ppermute | solution.py:200

commit v19 on v18

--- a/solution.py
+++ b/solution.py
@@ -92,24 +92,38 @@
     out[:, 3 * ROWS :, :] = jnp.where(core == 0, theirs[...], mine[...])
 
 
-def cycle_kernel(gathered, own, other, out):
+def prepare_kernel(own, other, high, low):
     core = lax.axis_index("core")
-    chunks = ([], [])
-    for k in range(0, ROWS, 2):
-        first = gathered[pl.ds(k, CHIPS * PAIRS, stride=ROWS), :]
-        second = gathered[pl.ds(k + 1, CHIPS * PAIRS, stride=ROWS), :]
-        for chunk, value in zip(chunks, pair_up(first, second)):
-            chunk.append(value)
-    left = split(jnp.concatenate([jnp.concatenate(chunk, 1) for chunk in chunks], 0))
     for side in range(2):
-        right = split(jnp.where(core == side, own[...], other[...]))
-        result = product(left, right)
-        for quarter in range(2):
-            both = result[:, quarter * LANES : (quarter + 1) * LANES]
-            rows = pair_up(both[: CHIPS * PAIRS], both[CHIPS * PAIRS :])
-            for inner, value in enumerate(rows):
-                j = side * 4 + quarter * 2 + inner
-                out[pl.ds(j, CHIPS * PAIRS, stride=ROWS), :] = value
+        columns = slice(side * own.shape[1], (side + 1) * own.shape[1])
+        high[:, columns], low[:, columns] = split(jnp.where(core == side, own[...], other[...]))
+
+
+def cycle_kernel(gathered, high, low, out, staged, done):
+    span = CHIPS // 2 * BLOCK
+    rows = CHIPS // 2 * PAIRS
+    copies = []
+    for half in range(2):
+        chunks = ([], [])
+        for k in range(0, ROWS, 2):
+            first = gathered[pl.ds(half * span + k, rows, stride=ROWS), :]
+            second = gathered[pl.ds(half * span + k + 1, rows, stride=ROWS), :]
+            for chunk, value in zip(chunks, pair_up(first, second)):
+                chunk.append(value)
+        left = split(jnp.concatenate([jnp.concatenate(chunk, 1) for chunk in chunks], 0))
+        for pair in range(0, ROWS // 2, 2):
+            columns = slice(pair * LANES, (pair + 2) * LANES)
+            result = product(left, (high[:, columns], low[:, columns]))
+            for quarter in range(2):
+                both = result[:, quarter * LANES : (quarter + 1) * LANES]
+                for inner, value in enumerate(pair_up(both[:rows], both[rows:])):
+                    j = (pair + quarter) * 2 + inner
+                    staged[pl.ds(half * span + j, rows, stride=ROWS), :] = value
+        piece = pl.ds(half * span, span)
+        copies.append(pltpu.make_async_copy(staged.at[piece], out.at[piece], done.at[half]))
+        copies[-1].start()
+    for copy in copies:
+        copy.wait()
 
 
 def ladder_kernel(window, integrals, cycle, out):
@@ -181,7 +195,25 @@
     copies = jnp.broadcast_to(column.reshape(1, ZL * BLOCK, LANES), (X, ZL * BLOCK, LANES))
     gathered = lax.all_to_all(copies, "x", 0, 0, tiled=True)
     gathered = gathered.reshape(CHIPS * BLOCK, LANES)
-    (cycle,) = call(cycle_kernel, [(CHIPS * BLOCK, LANES)], [VMEM] * 3)(gathered, cycle_block, other)
+    halves = jax.ShapeDtypeStruct((cycle_block.shape[0], 2 * cycle_block.shape[1]), jnp.bfloat16)
+    high, low = pl.pallas_call(
+        prepare_kernel,
+        out_shape=[halves] * 2,
+        in_specs=[VMEM] * 2,
+        out_specs=[VMEM] * 2,
+        compiler_params=PARAMS,
+    )(cycle_block, other)
+    cycle = pl.pallas_call(
+        cycle_kernel,
+        out_shape=jax.ShapeDtypeStruct((CHIPS * BLOCK, LANES), jnp.float32),
+        in_specs=[VMEM] * 3,
+        out_specs=pl.BlockSpec(memory_space=pl.ANY),
+        scratch_shapes=[
+            pltpu.VMEM((CHIPS * BLOCK, LANES), jnp.float32),
+            pltpu.SemaphoreType.DMA((2,)),
+        ],
+        compiler_params=PARAMS,
+    )(gathered, high, low)
     cycle, gathered = lax.optimization_barrier((cycle, gathered))
     cycle = lax.all_to_all(cycle.reshape(CHIPS, BLOCK, LANES), ("x", "zl"), 0, 0, tiled=True)
 

time: 113 us -> 112 us (level)
  no operation moved by 1% of the time
where the time goes in v19:
time: 112 us
  blocking collectives  62.9 us (56%)
  starting transfers between devices  23.9 us (21%)
  waiting for transfers between devices  17.7 us (16%)
  Pallas kernels  5.41 us (5%)
  local copies, waits for them, and re-layouts  1.86 us (2%)
    all_to_all x1, blocking collectives, per_device(): parts = lax.all_to_all(parts, ('zh', 'y'), 0, 0, tiled=True)  32.9 us
    all_to_all x1, blocking collectives, per_device(): window = lax.all_to_all(window, 'y', 0, 0, tiled=True)  15.1 us
    all_to_all x1, blocking collectives, per_device(): column = lax.all_to_all(copies, 'zl', 0, 0, tiled=True)  14.9 us
    ppermute x1, starting transfers between devices, per_device(): mine = lax.ppermute(far, 'zh', swap)  8.22 us
    ppermute x1, waiting for transfers between devices, per_device(): mine = lax.ppermute(far, 'zh', swap)  7.2 us
    all_to_all x1, waiting for transfers between devices, per_device(): gathered = lax.all_to_all(copies, 'x', 0, 0, tiled=True)  6.62 us
    all_to_all x1, starting transfers between devices, per_device(): lax.all_to_all(cycle.reshape(CHIPS, BLOCK, LANES), ('x', 'zl'), 0, 0, til...  5.6 us
    all_to_all x1, starting transfers between devices, per_device(): gathered = lax.all_to_all(copies, 'x', 0, 0, tiled=True)  4.29 us
  transfers between devices with their start and end apart: 6, of which 6 were waited for; matrix products, arithmetic and copies ran while one was open for 0% of the time, Pallas kernels for 2%

profile of v19, /device:TPU:8, one launch (start us, length us, event | category | flops | bytes accessed | tf_op | source)
XLA Modules:
  0.0 111.9 jit_solution(7450978361081333797)
XLA Ops:
  0.0 0.0 copy-start.1
  0.0 0.0 copy-start.2
  0.0 0.9 copy-done.2
  0.9 14.9 %all_to_all.25 = f32[4,104,128]{2,1,0:T(8,128)S(1)} all-to-all(f32[4,104,128]{2,1,0:T(8,128)S(1)} %shard_map.64), channel_id=1, replica_groups=mesh['zl'=4,'x'=4,'core'=2,'zh'=2,'y'=8] {'zl'}, dimensions={0} | all-to-all | bytes 425984 | tf_op jit(solution)/shard_map/all_to_all | solution.py:194
  15.8 1.0 broadcast_in_dim.8
  16.7 4.3 %all-to-all-start.1 = ((f32[4,416,128]{2,1,0:T(8,128)}), f32[4,416,128]{2,1,0:T(8,128)S(1)}, u32[]{:S(2)}, u32[]{:S(2)}) async-start(f32[4,416,128]{2,1,0:T(8,128)} %broadcast_in_dim.8), calls=%async_computation.1 | async-start | bytes 1703936 | tf_op jit(solution)/shard_map/all_to_all | solution.py:196
  21.0 0.0 copy-done.1
  21.0 1.9 %collective-permute-start = (f32[512,256]{1,0:T(8,128)S(1)}, f32[512,256]{1,0:T(8,128)S(1)}, u32[]{:S(2)}, u32[]{:S(2)}) collective-permute-start(f32[512,256]{1,0:T(8,128)S(1)} %copy-done.1), channel_id=1, source_target_pairs={{0,16},{16,0},{1,17},{17,1},{2,18},{18,2},{3,19},{19,3},{4,20},{20... | collective-permute-start | bytes 1572872 | tf_op jit(solution)/shard_map/ppermute | solution.py:192
  22.9 1.9 %collective-permute-done.other = f32[512,256]{1,0:T(8,128)S(1)} collective-permute-done((f32[512,256]{1,0:T(8,128)S(1)}, f32[512,256]{1,0:T(8,128)S(1)}, u32[]{:S(2)}, u32[]{:S(2)}) %collective-permute-start) | collective-permute-done | bytes 524320 | tf_op jit(solution)/shard_map/ppermute | solution.py:192
  24.8 0.2 shard_map.65
  25.0 6.6 %all-to-all-done.1 = f32[4,416,128]{2,1,0:T(8,128)S(1)} async-done(((f32[4,416,128]{2,1,0:T(8,128)}), f32[4,416,128]{2,1,0:T(8,128)S(1)}, u32[]{:S(2)}, u32[]{:S(2)}) %all-to-all-start.1) | async-done | bytes 852000 | tf_op jit(solution)/shard_map/all_to_all | solution.py:196
  31.7 0.0 copy-start.4
  31.7 1.8 %shard_map.66 = f32[1664,128]{1,0:T(8,128)} custom-call(f32[1664,128]{1,0:T(8,128)S(1)} %bitcast.5, bf16[512,512]{1,0:T(8,128)(2,1)S(1)} %get-tuple-element.14.high, bf16[512,512]{1,0:T(8,128)(2,1)S(1)} %get-tuple-element.15.low), custom_call_target="tpu_custom_call" | custom-call | tf_op jit(solution)/shard_map/pallas_call | solution.py:206
  33.4 0.0 copy-start.3
  33.4 0.0 copy-start.5
  33.5 0.0 copy-start
  33.5 5.6 %all-to-all-start.2 = ((f32[16,104,128]{2,1,0:T(8,128)}), f32[16,104,128]{2,1,0:T(8,128)S(1)}, u32[]{:S(2)}, u32[]{:S(2)}) async-start(f32[16,104,128]{2,1,0:T(8,128)} %bitcast.3), calls=%async_computation.2 | async-start | bytes 1703936 | tf_op jit(solution)/shard_map/all_to_all | solution.py:218
  39.1 0.0 copy-done.4
  39.1 1.4 %shard_map.67 = f32[2,128,128]{2,1,0:T(8,128)S(1)} custom-call(s32[2]{0:T(128)S(1)} %copy-done.4, f32[1664,128]{1,0:T(8,128)S(1)} %bitcast.6), custom_call_target="tpu_custom_call" | custom-call | tf_op jit(solution)/shard_map/pallas_call | solution.py:220
  40.5 1.9 %collective-permute-start.1 = (f32[2,8,16,128]{3,2,1,0:T(8,128)S(1)}, f32[2,8,16,128]{3,2,1,0:T(8,128)S(1)}, u32[]{:S(2)}, u32[]{:S(2)}) collective-permute-start(f32[2,8,16,128]{3,2,1,0:T(8,128)S(1)} %bitcast.8), channel_id=1, source_target_pairs={{0,16},{16,0},{1,17},{17,1},{2,18},{18,2},{3,19},{19,3},{4,20},{20... | collective-permute-start | bytes 393224 | tf_op jit(solution)/shard_map/ppermute | solution.py:227
  42.5 1.3 %collective-permute-done.1.other = f32[2,8,16,128]{3,2,1,0:T(8,128)S(1)} collective-permute-done((f32[2,8,16,128]{3,2,1,0:T(8,128)S(1)}, f32[2,8,16,128]{3,2,1,0:T(8,128)S(1)}, u32[]{:S(2)}, u32[]{:S(2)}) %collective-permute-start.1) | collective-permute-done | bytes 131104 | tf_op jit(solution)/shard_map/ppermute | solution.py:227
  43.8 8.2 %collective-permute-start.2 = (f32[8,8,128]{2,1,0:T(8,128)S(1)}, f32[8,8,128]{2,1,0:T(8,128)S(1)}, u32[]{:S(2)}, u32[]{:S(2)}) collective-permute-start(f32[8,8,128]{2,1,0:T(8,128)S(1)} %get-tuple-element.18), channel_id=1, source_target_pairs={{0,8},{8,0},{1,9},{9,1},{2,10},{10,2},{3,11},{11,3},{4,12},{12,4},... | collective-permute-start | bytes 98312 | tf_op jit(solution)/shard_map/ppermute | solution.py:231
  52.0 7.2 %collective-permute-done.2.mine = f32[8,8,128]{2,1,0:T(8,128)S(1)} collective-permute-done((f32[8,8,128]{2,1,0:T(8,128)S(1)}, f32[8,8,128]{2,1,0:T(8,128)S(1)}, u32[]{:S(2)}, u32[]{:S(2)}) %collective-permute-start.2) | collective-permute-done | bytes 32800 | tf_op jit(solution)/shard_map/ppermute | solution.py:231
  59.2 1.9 %collective-permute-start.3 = (f32[8,8,128]{2,1,0:T(8,128)S(1)}, f32[8,8,128]{2,1,0:T(8,128)S(1)}, u32[]{:S(2)}, u32[]{:S(2)}) collective-permute-start(f32[8,8,128]{2,1,0:T(8,128)S(1)} %collective-permute-done.2.mine), channel_id=1, source_target_pairs={{0,16},{16,0},{1,17},{17,1},{2,18},{18,2},{3,19},{19,3},{4,20},{20... | collective-permute-start | bytes 98312 | tf_op jit(solution)/shard_map/ppermute | solution.py:232
  61.1 0.0 copy-done.3
  61.1 0.0 copy-done.5
  61.1 0.7 shard_map.70.denominator
  61.8 0.5 collective-permute-done.3.theirs
  62.3 0.2 all-to-all-done.2.cycle
  62.5 15.1 %all_to_all.26.window = f32[8,32,128]{2,1,0:T(8,128)S(1)} all-to-all(f32[8,32,128]{2,1,0:T(8,128)S(1)} %shard_map.69), channel_id=1, replica_groups=mesh['zl'=4,'x'=4,'core'=2,'zh'=2,'y'=8] {'y'}, dimensions={0} | all-to-all | bytes 262144 | tf_op jit(solution)/shard_map/all_to_all | solution.py:238
  77.6 0.0 copy-done
  77.6 0.6 shard_map.71
  78.2 32.9 %all_to_all.27.parts = f32[16,104,128]{2,1,0:T(8,128)S(1)} all-to-all(f32[16,104,128]{2,1,0:T(8,128)S(1)} %shard_map.71), channel_id=1, replica_groups=mesh['zl'=4,'x'=4,'core'=2,'zh'=2,'y'=8] {'zh','y'}, dimensions={0} | all-to-all | bytes 1703936 | tf_op jit(solution)/shard_map/all_to_all | solution.py:242
  111.2 0.7 shard_map.72
  (3 shorter events, 0.0 us)
Async XLA Ops:
  0.0 21.0 %copy-start.1 = (f32[512,256]{1,0:T(8,128)S(1)}, f32[512,256]{1,0:T(8,128)}, u32[]{:S(2)}) copy-start(f32[512,256]{1,0:T(8,128)} %own.1) | copy-start | bytes 1572868
  0.0 0.9 copy-start.2
  16.7 14.9 %all-to-all-start.1 = ((f32[4,416,128]{2,1,0:T(8,128)}), f32[4,416,128]{2,1,0:T(8,128)S(1)}, u32[]{:S(2)}, u32[]{:S(2)}) async-start(f32[4,416,128]{2,1,0:T(8,128)} %broadcast_in_dim.8), calls=%async_computation.1 | async-start | bytes 1703936 | tf_op jit(solution)/shard_map/all_to_all | solution.py:196
  21.0 3.8 %collective-permute-start = (f32[512,256]{1,0:T(8,128)S(1)}, f32[512,256]{1,0:T(8,128)S(1)}, u32[]{:S(2)}, u32[]{:S(2)}) collective-permute-start(f32[512,256]{1,0:T(8,128)S(1)} %copy-done.1), channel_id=1, source_target_pairs={{0,16},{16,0},{1,17},{17,1},{2,18},{18,2},{3,19},{19,3},{4,20},{20... | collective-permute-start | bytes 1572872 | tf_op jit(solution)/shard_map/ppermute | solution.py:192
  31.7 7.4 %copy-start.4 = (s32[2]{0:T(128)S(1)}, s32[2]{0:T(128)}, u32[]{:S(2)}) copy-start(s32[2]{0:T(128)} %tiles.3) | copy-start | bytes 28
  33.4 27.7 %copy-start.3 = (f32[832]{0:T(1024)S(1)}, f32[832]{0:T(1024)}, u32[]{:S(2)}) copy-start(f32[832]{0:T(1024)} %virtual.1) | copy-start | bytes 9988
  33.4 27.7 %copy-start.5 = (f32[128]{0:T(128)S(1)}, f32[128]{0:T(128)}, u32[]{:S(2)}) copy-start(f32[128]{0:T(128)} %occupied.1) | copy-start | bytes 1540
  33.5 44.2 %copy-start = (f32[4,64,1664]{2,1,0:T(8,128)S(1)}, f32[4,64,1664]{2,1,0:T(8,128)}, u32[]{:S(2)}) copy-start(f32[4,64,1664]{2,1,0:T(8,128)} %param.8) | copy-start | bytes 5111812
  33.5 29.0 %all-to-all-start.2 = ((f32[16,104,128]{2,1,0:T(8,128)}), f32[16,104,128]{2,1,0:T(8,128)S(1)}, u32[]{:S(2)}, u32[]{:S(2)}) async-start(f32[16,104,128]{2,1,0:T(8,128)} %bitcast.3), calls=%async_computation.2 | async-start | bytes 1703936 | tf_op jit(solution)/shard_map/all_to_all | solution.py:218
  40.5 3.2 %collective-permute-start.1 = (f32[2,8,16,128]{3,2,1,0:T(8,128)S(1)}, f32[2,8,16,128]{3,2,1,0:T(8,128)S(1)}, u32[]{:S(2)}, u32[]{:S(2)}) collective-permute-start(f32[2,8,16,128]{3,2,1,0:T(8,128)S(1)} %bitcast.8), channel_id=1, source_target_pairs={{0,16},{16,0},{1,17},{17,1},{2,18},{18,2},{3,19},{19,3},{4,20},{20... | collective-permute-start | bytes 393224 | tf_op jit(solution)/shard_map/ppermute | solution.py:227
  43.8 15.4 %collective-permute-start.2 = (f32[8,8,128]{2,1,0:T(8,128)S(1)}, f32[8,8,128]{2,1,0:T(8,128)S(1)}, u32[]{:S(2)}, u32[]{:S(2)}) collective-permute-start(f32[8,8,128]{2,1,0:T(8,128)S(1)} %get-tuple-element.18), channel_id=1, source_target_pairs={{0,8},{8,0},{1,9},{9,1},{2,10},{10,2},{3,11},{11,3},{4,12},{12,4},... | collective-permute-start | bytes 98312 | tf_op jit(solution)/shard_map/ppermute | solution.py:231
  59.2 3.1 %collective-permute-start.3 = (f32[8,8,128]{2,1,0:T(8,128)S(1)}, f32[8,8,128]{2,1,0:T(8,128)S(1)}, u32[]{:S(2)}, u32[]{:S(2)}) collective-permute-start(f32[8,8,128]{2,1,0:T(8,128)S(1)} %collective-permute-done.2.mine), channel_id=1, source_target_pairs={{0,16},{16,0},{1,17},{17,1},{2,18},{18,2},{3,19},{19,3},{4,20},{20... | collective-permute-start | bytes 98312 | tf_op jit(solution)/shard_map/ppermute | solution.py:232

commit v20 on v19

--- a/solution.py
+++ b/solution.py
@@ -47,11 +47,13 @@
     return chip % X * ZL + chip // X
 
 
-def pack_kernel(amplitudes, out):
-    for pair in range(PAIRS):
-        tile = amplitudes[0, :, pair * LANES : (pair + 1) * LANES]
-        for chip in range(ZL):
-            out[chip, pair * ROWS : (pair + 1) * ROWS, :] = tile
+def spread_kernel(column, out):
+    for zl in range(ZL):
+        for pair in range(PAIRS):
+            tile = column[zl, :, pair * LANES : (pair + 1) * LANES]
+            start = zl * BLOCK + pair * ROWS
+            for x in range(X):
+                out[x, start : start + ROWS, :] = tile
 
 
 def window_kernel(tiles, gathered, out, window, columns, turned):
@@ -190,9 +192,9 @@
 def per_device(amplitudes, cycle_block, ladder_block, occupied, virtual, tiles):
     swap = [(0, 1), (1, 0)]
     other = lax.ppermute(cycle_block, "core", swap)
-    (copies,) = call(pack_kernel, [(ZL, BLOCK, LANES)], [VMEM])(amplitudes)
+    copies = jnp.broadcast_to(amplitudes, (ZL,) + amplitudes.shape[1:])
     column = lax.all_to_all(copies, "zl", 0, 0, tiled=True)
-    copies = jnp.broadcast_to(column.reshape(1, ZL * BLOCK, LANES), (X, ZL * BLOCK, LANES))
+    (copies,) = call(spread_kernel, [(X, ZL * BLOCK, LANES)], [VMEM])(column)
     gathered = lax.all_to_all(copies, "x", 0, 0, tiled=True)
     gathered = gathered.reshape(CHIPS * BLOCK, LANES)
     halves = jax.ShapeDtypeStruct((cycle_block.shape[0], 2 * cycle_block.shape[1]), jnp.bfloat16)

time: 112 us -> 112 us (level)
  no operation moved by 1% of the time
where the time goes in v20:
time: 112 us
  blocking collectives  62.9 us (56%)
  starting transfers between devices  23.9 us (21%)
  waiting for transfers between devices  17.7 us (16%)
  Pallas kernels  6.39 us (6%)
    all_to_all x1, blocking collectives, per_device(): parts = lax.all_to_all(parts, ('zh', 'y'), 0, 0, tiled=True)  32.9 us
    all_to_all x1, blocking collectives, per_device(): window = lax.all_to_all(window, 'y', 0, 0, tiled=True)  15.1 us
    all_to_all x1, blocking collectives, per_device(): column = lax.all_to_all(copies, 'zl', 0, 0, tiled=True)  14.9 us
    ppermute x1, starting transfers between devices, per_device(): mine = lax.ppermute(far, 'zh', swap)  8.22 us
    ppermute x1, waiting for transfers between devices, per_device(): mine = lax.ppermute(far, 'zh', swap)  7.2 us
    all_to_all x1, waiting for transfers between devices, per_device(): gathered = lax.all_to_all(copies, 'x', 0, 0, tiled=True)  6.62 us
    all_to_all x1, starting transfers between devices, per_device(): lax.all_to_all(cycle.reshape(CHIPS, BLOCK, LANES), ('x', 'zl'), 0, 0, til...  5.6 us
    all_to_all x1, starting transfers between devices, per_device(): gathered = lax.all_to_all(copies, 'x', 0, 0, tiled=True)  4.29 us
  transfers between devices with their start and end apart: 6, of which 6 were waited for; matrix products, arithmetic and copies ran while one was open for 0% of the time, Pallas kernels for 2%

profile of v20, /device:TPU:8, one launch (start us, length us, event | category | flops | bytes accessed | tf_op | source)
XLA Modules:
  0.0 111.9 jit_solution(16187829537016245346)
XLA Ops:
  0.0 0.0 copy-start.1
  0.0 0.9 broadcast_in_dim.8
  0.9 14.9 %all_to_all.25.column = f32[4,8,1664]{2,1,0:T(8,128)S(1)} all-to-all(f32[4,8,1664]{2,1,0:T(8,128)S(1)} %broadcast_in_dim.8), channel_id=1, replica_groups=mesh['zl'=4,'x'=4,'core'=2,'zh'=2,'y'=8] {'zl'}, dimensions={0} | all-to-all | bytes 425984 | tf_op jit(solution)/shard_map/all_to_all | solution.py:196
  15.8 1.0 shard_map.64
  16.7 4.3 %all-to-all-start.1 = ((f32[4,416,128]{2,1,0:T(8,128)}), f32[4,416,128]{2,1,0:T(8,128)S(1)}, u32[]{:S(2)}, u32[]{:S(2)}) async-start(f32[4,416,128]{2,1,0:T(8,128)} %shard_map.64), calls=%async_computation.1 | async-start | bytes 1703936 | tf_op jit(solution)/shard_map/all_to_all | solution.py:198
  21.0 0.0 copy-done.1
  21.0 1.9 %collective-permute-start = (f32[512,256]{1,0:T(8,128)S(1)}, f32[512,256]{1,0:T(8,128)S(1)}, u32[]{:S(2)}, u32[]{:S(2)}) collective-permute-start(f32[512,256]{1,0:T(8,128)S(1)} %copy-done.1), channel_id=1, source_target_pairs={{0,16},{16,0},{1,17},{17,1},{2,18},{18,2},{3,19},{19,3},{4,20},{20... | collective-permute-start | bytes 1572872 | tf_op jit(solution)/shard_map/ppermute | solution.py:194
  22.9 1.9 %collective-permute-done.other = f32[512,256]{1,0:T(8,128)S(1)} collective-permute-done((f32[512,256]{1,0:T(8,128)S(1)}, f32[512,256]{1,0:T(8,128)S(1)}, u32[]{:S(2)}, u32[]{:S(2)}) %collective-permute-start) | collective-permute-done | bytes 524320 | tf_op jit(solution)/shard_map/ppermute | solution.py:194
  24.8 0.2 shard_map.65
  25.0 6.6 %all-to-all-done.1 = f32[4,416,128]{2,1,0:T(8,128)S(1)} async-done(((f32[4,416,128]{2,1,0:T(8,128)}), f32[4,416,128]{2,1,0:T(8,128)S(1)}, u32[]{:S(2)}, u32[]{:S(2)}) %all-to-all-start.1) | async-done | bytes 852000 | tf_op jit(solution)/shard_map/all_to_all | solution.py:198
  31.7 0.0 copy-start.3
  31.7 1.8 %shard_map.66 = f32[1664,128]{1,0:T(8,128)} custom-call(f32[1664,128]{1,0:T(8,128)S(1)} %bitcast.5, bf16[512,512]{1,0:T(8,128)(2,1)S(1)} %get-tuple-element.14.high, bf16[512,512]{1,0:T(8,128)(2,1)S(1)} %get-tuple-element.15.low), custom_call_target="tpu_custom_call" | custom-call | tf_op jit(solution)/shard_map/pallas_call | solution.py:208
  33.5 0.0 copy-start.2
  33.5 0.0 copy-start.4
  33.5 0.0 copy-start
  33.5 5.6 %all-to-all-start.2 = ((f32[16,104,128]{2,1,0:T(8,128)}), f32[16,104,128]{2,1,0:T(8,128)S(1)}, u32[]{:S(2)}, u32[]{:S(2)}) async-start(f32[16,104,128]{2,1,0:T(8,128)} %bitcast.3), calls=%async_computation.2 | async-start | bytes 1703936 | tf_op jit(solution)/shard_map/all_to_all | solution.py:220
  39.1 0.0 copy-done.3
  39.1 1.4 %shard_map.67 = f32[2,128,128]{2,1,0:T(8,128)S(1)} custom-call(s32[2]{0:T(128)S(1)} %copy-done.3, f32[1664,128]{1,0:T(8,128)S(1)} %bitcast.6), custom_call_target="tpu_custom_call" | custom-call | tf_op jit(solution)/shard_map/pallas_call | solution.py:222
  40.5 1.9 %collective-permute-start.1 = (f32[2,8,16,128]{3,2,1,0:T(8,128)S(1)}, f32[2,8,16,128]{3,2,1,0:T(8,128)S(1)}, u32[]{:S(2)}, u32[]{:S(2)}) collective-permute-start(f32[2,8,16,128]{3,2,1,0:T(8,128)S(1)} %bitcast.8), channel_id=1, source_target_pairs={{0,16},{16,0},{1,17},{17,1},{2,18},{18,2},{3,19},{19,3},{4,20},{20... | collective-permute-start | bytes 393224 | tf_op jit(solution)/shard_map/ppermute | solution.py:229
  42.5 1.3 %collective-permute-done.1.other = f32[2,8,16,128]{3,2,1,0:T(8,128)S(1)} collective-permute-done((f32[2,8,16,128]{3,2,1,0:T(8,128)S(1)}, f32[2,8,16,128]{3,2,1,0:T(8,128)S(1)}, u32[]{:S(2)}, u32[]{:S(2)}) %collective-permute-start.1) | collective-permute-done | bytes 131104 | tf_op jit(solution)/shard_map/ppermute | solution.py:229
  43.8 8.2 %collective-permute-start.2 = (f32[8,8,128]{2,1,0:T(8,128)S(1)}, f32[8,8,128]{2,1,0:T(8,128)S(1)}, u32[]{:S(2)}, u32[]{:S(2)}) collective-permute-start(f32[8,8,128]{2,1,0:T(8,128)S(1)} %get-tuple-element.18), channel_id=1, source_target_pairs={{0,8},{8,0},{1,9},{9,1},{2,10},{10,2},{3,11},{11,3},{4,12},{12,4},... | collective-permute-start | bytes 98312 | tf_op jit(solution)/shard_map/ppermute | solution.py:233
  52.0 7.2 %collective-permute-done.2.mine = f32[8,8,128]{2,1,0:T(8,128)S(1)} collective-permute-done((f32[8,8,128]{2,1,0:T(8,128)S(1)}, f32[8,8,128]{2,1,0:T(8,128)S(1)}, u32[]{:S(2)}, u32[]{:S(2)}) %collective-permute-start.2) | collective-permute-done | bytes 32800 | tf_op jit(solution)/shard_map/ppermute | solution.py:233
  59.2 1.9 %collective-permute-start.3 = (f32[8,8,128]{2,1,0:T(8,128)S(1)}, f32[8,8,128]{2,1,0:T(8,128)S(1)}, u32[]{:S(2)}, u32[]{:S(2)}) collective-permute-start(f32[8,8,128]{2,1,0:T(8,128)S(1)} %collective-permute-done.2.mine), channel_id=1, source_target_pairs={{0,16},{16,0},{1,17},{17,1},{2,18},{18,2},{3,19},{19,3},{4,20},{20... | collective-permute-start | bytes 98312 | tf_op jit(solution)/shard_map/ppermute | solution.py:234
  61.1 0.0 copy-done.2
  61.2 0.0 copy-done.4
  61.2 0.7 shard_map.70.denominator
  61.9 0.5 collective-permute-done.3.theirs
  62.3 0.2 all-to-all-done.2.cycle
  62.5 15.1 %all_to_all.26.window = f32[8,32,128]{2,1,0:T(8,128)S(1)} all-to-all(f32[8,32,128]{2,1,0:T(8,128)S(1)} %shard_map.69), channel_id=1, replica_groups=mesh['zl'=4,'x'=4,'core'=2,'zh'=2,'y'=8] {'y'}, dimensions={0} | all-to-all | bytes 262144 | tf_op jit(solution)/shard_map/all_to_all | solution.py:240
  77.6 0.0 copy-done
  77.6 0.6 shard_map.71
  78.3 32.9 %all_to_all.27.parts = f32[16,104,128]{2,1,0:T(8,128)S(1)} all-to-all(f32[16,104,128]{2,1,0:T(8,128)S(1)} %shard_map.71), channel_id=1, replica_groups=mesh['zl'=4,'x'=4,'core'=2,'zh'=2,'y'=8] {'zh','y'}, dimensions={0} | all-to-all | bytes 1703936 | tf_op jit(solution)/shard_map/all_to_all | solution.py:244
  111.2 0.7 shard_map.72
  (2 shorter events, 0.0 us)
Async XLA Ops:
  0.0 21.0 %copy-start.1 = (f32[512,256]{1,0:T(8,128)S(1)}, f32[512,256]{1,0:T(8,128)}, u32[]{:S(2)}) copy-start(f32[512,256]{1,0:T(8,128)} %own.1) | copy-start | bytes 1572868
  16.7 14.9 %all-to-all-start.1 = ((f32[4,416,128]{2,1,0:T(8,128)}), f32[4,416,128]{2,1,0:T(8,128)S(1)}, u32[]{:S(2)}, u32[]{:S(2)}) async-start(f32[4,416,128]{2,1,0:T(8,128)} %shard_map.64), calls=%async_computation.1 | async-start | bytes 1703936 | tf_op jit(solution)/shard_map/all_to_all | solution.py:198
  21.0 3.8 %collective-permute-start = (f32[512,256]{1,0:T(8,128)S(1)}, f32[512,256]{1,0:T(8,128)S(1)}, u32[]{:S(2)}, u32[]{:S(2)}) collective-permute-start(f32[512,256]{1,0:T(8,128)S(1)} %copy-done.1), channel_id=1, source_target_pairs={{0,16},{16,0},{1,17},{17,1},{2,18},{18,2},{3,19},{19,3},{4,20},{20... | collective-permute-start | bytes 1572872 | tf_op jit(solution)/shard_map/ppermute | solution.py:194
  31.7 7.4 %copy-start.3 = (s32[2]{0:T(128)S(1)}, s32[2]{0:T(128)}, u32[]{:S(2)}) copy-start(s32[2]{0:T(128)} %tiles.3) | copy-start | bytes 28
  33.5 27.7 %copy-start.2 = (f32[832]{0:T(1024)S(1)}, f32[832]{0:T(1024)}, u32[]{:S(2)}) copy-start(f32[832]{0:T(1024)} %virtual.1) | copy-start | bytes 9988
  33.5 27.7 %copy-start.4 = (f32[128]{0:T(128)S(1)}, f32[128]{0:T(128)}, u32[]{:S(2)}) copy-start(f32[128]{0:T(128)} %occupied.1) | copy-start | bytes 1540
  33.5 44.2 %copy-start = (f32[4,64,1664]{2,1,0:T(8,128)S(1)}, f32[4,64,1664]{2,1,0:T(8,128)}, u32[]{:S(2)}) copy-start(f32[4,64,1664]{2,1,0:T(8,128)} %param.8) | copy-start | bytes 5111812
  33.5 29.0 %all-to-all-start.2 = ((f32[16,104,128]{2,1,0:T(8,128)}), f32[16,104,128]{2,1,0:T(8,128)S(1)}, u32[]{:S(2)}, u32[]{:S(2)}) async-start(f32[16,104,128]{2,1,0:T(8,128)} %bitcast.3), calls=%async_computation.2 | async-start | bytes 1703936 | tf_op jit(solution)/shard_map/all_to_all | solution.py:220
  40.5 3.2 %collective-permute-start.1 = (f32[2,8,16,128]{3,2,1,0:T(8,128)S(1)}, f32[2,8,16,128]{3,2,1,0:T(8,128)S(1)}, u32[]{:S(2)}, u32[]{:S(2)}) collective-permute-start(f32[2,8,16,128]{3,2,1,0:T(8,128)S(1)} %bitcast.8), channel_id=1, source_target_pairs={{0,16},{16,0},{1,17},{17,1},{2,18},{18,2},{3,19},{19,3},{4,20},{20... | collective-permute-start | bytes 393224 | tf_op jit(solution)/shard_map/ppermute | solution.py:229
  43.8 15.4 %collective-permute-start.2 = (f32[8,8,128]{2,1,0:T(8,128)S(1)}, f32[8,8,128]{2,1,0:T(8,128)S(1)}, u32[]{:S(2)}, u32[]{:S(2)}) collective-permute-start(f32[8,8,128]{2,1,0:T(8,128)S(1)} %get-tuple-element.18), channel_id=1, source_target_pairs={{0,8},{8,0},{1,9},{9,1},{2,10},{10,2},{3,11},{11,3},{4,12},{12,4},... | collective-permute-start | bytes 98312 | tf_op jit(solution)/shard_map/ppermute | solution.py:233
  59.2 3.1 %collective-permute-start.3 = (f32[8,8,128]{2,1,0:T(8,128)S(1)}, f32[8,8,128]{2,1,0:T(8,128)S(1)}, u32[]{:S(2)}, u32[]{:S(2)}) collective-permute-start(f32[8,8,128]{2,1,0:T(8,128)S(1)} %collective-permute-done.2.mine), channel_id=1, source_target_pairs={{0,16},{16,0},{1,17},{17,1},{2,18},{18,2},{3,19},{19,3},{4,20},{20... | collective-permute-start | bytes 98312 | tf_op jit(solution)/shard_map/ppermute | solution.py:234

commit v21 on v19

--- a/solution.py
+++ b/solution.py
@@ -8,14 +8,15 @@
 from jax.sharding import Mesh
 from jax.sharding import PartitionSpec as P
 
-ZL, X, CORE, ZH, Y = 4, 4, 2, 2, 8
+ZL, X, CORE, ZH, YH, YL = 4, 4, 2, 2, 4, 2
+Y = YH * YL
 CHIPS = ZL * X
 ROWS = 8
 TILE = 64
 PAIRS = 13
 LANES = 2 * TILE
 BLOCK = PAIRS * ROWS
-EVERY = ("zl", "x", "core", "zh", "y")
+EVERY = ("zl", "x", "core", "zh", "yh", "yl")
 VMEM = pl.BlockSpec(memory_space=pltpu.VMEM)
 SMEM = pl.BlockSpec(memory_space=pltpu.SMEM)
 PARAMS = pltpu.CompilerParams(vmem_limit_bytes=32 * 1024 * 1024)
@@ -45,6 +46,10 @@
 
 def block_of(chip):
     return chip % X * ZL + chip // X
+
+
+def peer_of(place):
+    return place // Y * Y + place % YL * YH + place % Y // YL
 
 
 def pack_kernel(amplitudes, out):
@@ -146,12 +151,12 @@
             rows = pl.ds(column // LANES * ROWS, ROWS)
             for chip in range(CHIPS):
                 part = value[chip * ROWS : (chip + 1) * ROWS]
-                out[chip, rows, :] = part + cycle[block_of(chip), rows, :]
+                out[peer_of(chip), rows, :] = part + cycle[block_of(chip), rows, :]
 
 
 def denominator_kernel(tiles, occupied, virtual, out):
     column = lax.axis_index("zl") * (X * CORE) + lax.axis_index("x") * CORE + lax.axis_index("core")
-    row = lax.axis_index("zh") * Y + lax.axis_index("y")
+    row = lax.axis_index("zh") * Y + lax.axis_index("yh") * YL + lax.axis_index("yl")
     shape = (ROWS, LANES)
     lane = lax.broadcasted_iota(jnp.int32, shape, 1)
     line = lax.broadcasted_iota(jnp.int32, shape, 0)
@@ -235,18 +240,18 @@
         tiles, occupied, virtual
     )
     window, denominator, cycle = lax.optimization_barrier((window, denominator, cycle))
-    window = lax.all_to_all(window, "y", 0, 0, tiled=True)
+    window = lax.all_to_all(window, ("yh", "yl"), 0, 0, tiled=True)
 
     integrals = ladder_block.reshape(-1, ladder_block.shape[2])
     (parts,) = call(ladder_kernel, [(CHIPS, BLOCK, LANES)], [VMEM] * 3)(window, integrals, cycle)
-    parts = lax.all_to_all(parts, ("zh", "y"), 0, 0, tiled=True)
+    parts = lax.all_to_all(parts, ("zh", "yl", "yh"), 0, 0, tiled=True)
     (result,) = call(last_kernel, [amplitudes.shape], [VMEM] * 2)(denominator, parts)
     return result
 
 
 def solution(mesh):
-    parts = Mesh(mesh.devices.reshape(ZL, X, CORE, ZH, Y), EVERY)
-    amp, intg = ("zl", "x", "core"), ("zh", "y")
+    parts = Mesh(mesh.devices.reshape(ZL, X, CORE, ZH, YH, YL), EVERY)
+    amp, intg = ("zl", "x", "core"), ("zh", "yh", "yl")
     return jax.shard_map(
         per_device,
         mesh=parts,

time: 112 us -> 112 us (level)
  no operation moved by 1% of the time
where the time goes in v21:
time: 112 us; the launch traced here: 111 us
  blocking collectives  62.1 us (55%)
  starting transfers between devices  23.9 us (21%)
  waiting for transfers between devices  17.7 us (16%)
  Pallas kernels  5.42 us (5%)
  local copies, waits for them, and re-layouts  1.86 us (2%)
    all_to_all x1, blocking collectives, per_device(): parts = lax.all_to_all(parts, ('zh', 'yl', 'yh'), 0, 0, tiled=True)  32.1 us
    all_to_all x1, blocking collectives, per_device(): window = lax.all_to_all(window, ('yh', 'yl'), 0, 0, tiled=True)  15.1 us
    all_to_all x1, blocking collectives, per_device(): column = lax.all_to_all(copies, 'zl', 0, 0, tiled=True)  14.9 us
    ppermute x1, starting transfers between devices, per_device(): mine = lax.ppermute(far, 'zh', swap)  8.22 us
    ppermute x1, waiting for transfers between devices, per_device(): mine = lax.ppermute(far, 'zh', swap)  7.2 us
    all_to_all x1, waiting for transfers between devices, per_device(): gathered = lax.all_to_all(copies, 'x', 0, 0, tiled=True)  6.62 us
    all_to_all x1, starting transfers between devices, per_device(): lax.all_to_all(cycle.reshape(CHIPS, BLOCK, LANES), ('x', 'zl'), 0, 0, til...  5.6 us
    all_to_all x1, starting transfers between devices, per_device(): gathered = lax.all_to_all(copies, 'x', 0, 0, tiled=True)  4.29 us
  transfers between devices with their start and end apart: 6, of which 6 were waited for; matrix products, arithmetic and copies ran while one was open for 0% of the time, Pallas kernels for 2%

profile of v21, /device:TPU:8, one launch (start us, length us, event | category | flops | bytes accessed | tf_op | source)
XLA Modules:
  0.0 111.0 jit_solution(15202202182203564928)
XLA Ops:
  0.0 0.0 copy-start.1
  0.0 0.0 copy-start.2
  0.0 0.9 copy-done.2
  0.9 14.9 %all_to_all.25 = f32[4,104,128]{2,1,0:T(8,128)S(1)} all-to-all(f32[4,104,128]{2,1,0:T(8,128)S(1)} %shard_map.64), channel_id=1, replica_groups=mesh['zl'=4,'x'=4,'core'=2,'zh'=2,'yh'=4,'yl'=2] {'zl'}, dimensions={0} | all-to-all | bytes 425984 | tf_op jit(solution)/shard_map/all_to_all | solution.py:199
  15.8 1.0 broadcast_in_dim.8
  16.7 4.3 %all-to-all-start.1 = ((f32[4,416,128]{2,1,0:T(8,128)}), f32[4,416,128]{2,1,0:T(8,128)S(1)}, u32[]{:S(2)}, u32[]{:S(2)}) async-start(f32[4,416,128]{2,1,0:T(8,128)} %broadcast_in_dim.8), calls=%async_computation.1 | async-start | bytes 1703936 | tf_op jit(solution)/shard_map/all_to_all | solution.py:201
  21.0 0.0 copy-done.1
  21.0 1.9 %collective-permute-start = (f32[512,256]{1,0:T(8,128)S(1)}, f32[512,256]{1,0:T(8,128)S(1)}, u32[]{:S(2)}, u32[]{:S(2)}) collective-permute-start(f32[512,256]{1,0:T(8,128)S(1)} %copy-done.1), channel_id=1, source_target_pairs={{0,16},{16,0},{1,17},{17,1},{2,18},{18,2},{3,19},{19,3},{4,20},{20... | collective-permute-start | bytes 1572872 | tf_op jit(solution)/shard_map/ppermute | solution.py:197
  22.9 1.9 %collective-permute-done.other = f32[512,256]{1,0:T(8,128)S(1)} collective-permute-done((f32[512,256]{1,0:T(8,128)S(1)}, f32[512,256]{1,0:T(8,128)S(1)}, u32[]{:S(2)}, u32[]{:S(2)}) %collective-permute-start) | collective-permute-done | bytes 524320 | tf_op jit(solution)/shard_map/ppermute | solution.py:197
  24.8 0.2 shard_map.65
  25.0 6.6 %all-to-all-done.1 = f32[4,416,128]{2,1,0:T(8,128)S(1)} async-done(((f32[4,416,128]{2,1,0:T(8,128)}), f32[4,416,128]{2,1,0:T(8,128)S(1)}, u32[]{:S(2)}, u32[]{:S(2)}) %all-to-all-start.1) | async-done | bytes 852000 | tf_op jit(solution)/shard_map/all_to_all | solution.py:201
  31.7 0.0 copy-start.4
  31.7 1.8 %shard_map.66 = f32[1664,128]{1,0:T(8,128)} custom-call(f32[1664,128]{1,0:T(8,128)S(1)} %bitcast.5, bf16[512,512]{1,0:T(8,128)(2,1)S(1)} %get-tuple-element.14.high, bf16[512,512]{1,0:T(8,128)(2,1)S(1)} %get-tuple-element.15.low), custom_call_target="tpu_custom_call" | custom-call | tf_op jit(solution)/shard_map/pallas_call | solution.py:211
  33.4 0.0 copy-start.3
  33.4 0.0 copy-start.5
  33.5 0.0 copy-start
  33.5 5.6 %all-to-all-start.2 = ((f32[16,104,128]{2,1,0:T(8,128)}), f32[16,104,128]{2,1,0:T(8,128)S(1)}, u32[]{:S(2)}, u32[]{:S(2)}) async-start(f32[16,104,128]{2,1,0:T(8,128)} %bitcast.3), calls=%async_computation.2 | async-start | bytes 1703936 | tf_op jit(solution)/shard_map/all_to_all | solution.py:223
  39.1 0.0 copy-done.4
  39.1 1.4 %shard_map.67 = f32[2,128,128]{2,1,0:T(8,128)S(1)} custom-call(s32[2]{0:T(128)S(1)} %copy-done.4, f32[1664,128]{1,0:T(8,128)S(1)} %bitcast.6), custom_call_target="tpu_custom_call" | custom-call | tf_op jit(solution)/shard_map/pallas_call | solution.py:225
  40.5 1.9 %collective-permute-start.1 = (f32[2,8,16,128]{3,2,1,0:T(8,128)S(1)}, f32[2,8,16,128]{3,2,1,0:T(8,128)S(1)}, u32[]{:S(2)}, u32[]{:S(2)}) collective-permute-start(f32[2,8,16,128]{3,2,1,0:T(8,128)S(1)} %bitcast.8), channel_id=1, source_target_pairs={{0,16},{16,0},{1,17},{17,1},{2,18},{18,2},{3,19},{19,3},{4,20},{20... | collective-permute-start | bytes 393224 | tf_op jit(solution)/shard_map/ppermute | solution.py:232
  42.5 1.3 %collective-permute-done.1.other = f32[2,8,16,128]{3,2,1,0:T(8,128)S(1)} collective-permute-done((f32[2,8,16,128]{3,2,1,0:T(8,128)S(1)}, f32[2,8,16,128]{3,2,1,0:T(8,128)S(1)}, u32[]{:S(2)}, u32[]{:S(2)}) %collective-permute-start.1) | collective-permute-done | bytes 131104 | tf_op jit(solution)/shard_map/ppermute | solution.py:232
  43.8 8.2 %collective-permute-start.2 = (f32[8,8,128]{2,1,0:T(8,128)S(1)}, f32[8,8,128]{2,1,0:T(8,128)S(1)}, u32[]{:S(2)}, u32[]{:S(2)}) collective-permute-start(f32[8,8,128]{2,1,0:T(8,128)S(1)} %get-tuple-element.18), channel_id=1, source_target_pairs={{0,8},{8,0},{1,9},{9,1},{2,10},{10,2},{3,11},{11,3},{4,12},{12,4},... | collective-permute-start | bytes 98312 | tf_op jit(solution)/shard_map/ppermute | solution.py:236
  52.0 7.2 %collective-permute-done.2.mine = f32[8,8,128]{2,1,0:T(8,128)S(1)} collective-permute-done((f32[8,8,128]{2,1,0:T(8,128)S(1)}, f32[8,8,128]{2,1,0:T(8,128)S(1)}, u32[]{:S(2)}, u32[]{:S(2)}) %collective-permute-start.2) | collective-permute-done | bytes 32800 | tf_op jit(solution)/shard_map/ppermute | solution.py:236
  59.2 1.9 %collective-permute-start.3 = (f32[8,8,128]{2,1,0:T(8,128)S(1)}, f32[8,8,128]{2,1,0:T(8,128)S(1)}, u32[]{:S(2)}, u32[]{:S(2)}) collective-permute-start(f32[8,8,128]{2,1,0:T(8,128)S(1)} %collective-permute-done.2.mine), channel_id=1, source_target_pairs={{0,16},{16,0},{1,17},{17,1},{2,18},{18,2},{3,19},{19,3},{4,20},{20... | collective-permute-start | bytes 98312 | tf_op jit(solution)/shard_map/ppermute | solution.py:237
  61.1 0.0 copy-done.3
  61.1 0.0 copy-done.5
  61.1 0.7 shard_map.70.denominator
  61.8 0.5 collective-permute-done.3.theirs
  62.3 0.2 all-to-all-done.2.cycle
  62.5 15.1 %all_to_all.26.window = f32[8,32,128]{2,1,0:T(8,128)S(1)} all-to-all(f32[8,32,128]{2,1,0:T(8,128)S(1)} %shard_map.69), channel_id=1, replica_groups=mesh['zl'=4,'x'=4,'core'=2,'zh'=2,'yh'=4,'yl'=2] {'yh','yl'}, dimensions={0} | all-to-all | bytes 262144 | tf_op jit(solution)/shard_map/all_to_all | solution.py:243
  77.6 0.0 copy-done
  77.6 0.6 shard_map.71
  78.2 32.1 %all_to_all.27.parts = f32[16,104,128]{2,1,0:T(8,128)S(1)} all-to-all(f32[16,104,128]{2,1,0:T(8,128)S(1)} %shard_map.71), channel_id=1, replica_groups=mesh['zl'=4,'x'=4,'core'=2,'zh'=2,'yh'=4,'yl'=2] {'zh','yl','yh'}, dimensions={0} | all-to-all | bytes 1703936 | tf_op jit(solution)/shard_map/all_to_all | solution.py:247
  110.4 0.7 shard_map.72
  (3 shorter events, 0.0 us)
Async XLA Ops:
  0.0 21.0 %copy-start.1 = (f32[512,256]{1,0:T(8,128)S(1)}, f32[512,256]{1,0:T(8,128)}, u32[]{:S(2)}) copy-start(f32[512,256]{1,0:T(8,128)} %own.1) | copy-start | bytes 1572868
  0.0 0.9 copy-start.2
  16.7 14.9 %all-to-all-start.1 = ((f32[4,416,128]{2,1,0:T(8,128)}), f32[4,416,128]{2,1,0:T(8,128)S(1)}, u32[]{:S(2)}, u32[]{:S(2)}) async-start(f32[4,416,128]{2,1,0:T(8,128)} %broadcast_in_dim.8), calls=%async_computation.1 | async-start | bytes 1703936 | tf_op jit(solution)/shard_map/all_to_all | solution.py:201
  21.0 3.8 %collective-permute-start = (f32[512,256]{1,0:T(8,128)S(1)}, f32[512,256]{1,0:T(8,128)S(1)}, u32[]{:S(2)}, u32[]{:S(2)}) collective-permute-start(f32[512,256]{1,0:T(8,128)S(1)} %copy-done.1), channel_id=1, source_target_pairs={{0,16},{16,0},{1,17},{17,1},{2,18},{18,2},{3,19},{19,3},{4,20},{20... | collective-permute-start | bytes 1572872 | tf_op jit(solution)/shard_map/ppermute | solution.py:197
  31.7 7.4 %copy-start.4 = (s32[2]{0:T(128)S(1)}, s32[2]{0:T(128)}, u32[]{:S(2)}) copy-start(s32[2]{0:T(128)} %tiles.3) | copy-start | bytes 28
  33.4 27.7 %copy-start.3 = (f32[832]{0:T(1024)S(1)}, f32[832]{0:T(1024)}, u32[]{:S(2)}) copy-start(f32[832]{0:T(1024)} %virtual.1) | copy-start | bytes 9988
  33.4 27.7 %copy-start.5 = (f32[128]{0:T(128)S(1)}, f32[128]{0:T(128)}, u32[]{:S(2)}) copy-start(f32[128]{0:T(128)} %occupied.1) | copy-start | bytes 1540
  33.5 44.2 %copy-start = (f32[4,64,1664]{2,1,0:T(8,128)S(1)}, f32[4,64,1664]{2,1,0:T(8,128)}, u32[]{:S(2)}) copy-start(f32[4,64,1664]{2,1,0:T(8,128)} %param.8) | copy-start | bytes 5111812
  33.5 29.0 %all-to-all-start.2 = ((f32[16,104,128]{2,1,0:T(8,128)}), f32[16,104,128]{2,1,0:T(8,128)S(1)}, u32[]{:S(2)}, u32[]{:S(2)}) async-start(f32[16,104,128]{2,1,0:T(8,128)} %bitcast.3), calls=%async_computation.2 | async-start | bytes 1703936 | tf_op jit(solution)/shard_map/all_to_all | solution.py:223
  40.5 3.2 %collective-permute-start.1 = (f32[2,8,16,128]{3,2,1,0:T(8,128)S(1)}, f32[2,8,16,128]{3,2,1,0:T(8,128)S(1)}, u32[]{:S(2)}, u32[]{:S(2)}) collective-permute-start(f32[2,8,16,128]{3,2,1,0:T(8,128)S(1)} %bitcast.8), channel_id=1, source_target_pairs={{0,16},{16,0},{1,17},{17,1},{2,18},{18,2},{3,19},{19,3},{4,20},{20... | collective-permute-start | bytes 393224 | tf_op jit(solution)/shard_map/ppermute | solution.py:232
  43.8 15.4 %collective-permute-start.2 = (f32[8,8,128]{2,1,0:T(8,128)S(1)}, f32[8,8,128]{2,1,0:T(8,128)S(1)}, u32[]{:S(2)}, u32[]{:S(2)}) collective-permute-start(f32[8,8,128]{2,1,0:T(8,128)S(1)} %get-tuple-element.18), channel_id=1, source_target_pairs={{0,8},{8,0},{1,9},{9,1},{2,10},{10,2},{3,11},{11,3},{4,12},{12,4},... | collective-permute-start | bytes 98312 | tf_op jit(solution)/shard_map/ppermute | solution.py:236
  59.2 3.1 %collective-permute-start.3 = (f32[8,8,128]{2,1,0:T(8,128)S(1)}, f32[8,8,128]{2,1,0:T(8,128)S(1)}, u32[]{:S(2)}, u32[]{:S(2)}) collective-permute-start(f32[8,8,128]{2,1,0:T(8,128)S(1)} %collective-permute-done.2.mine), channel_id=1, source_target_pairs={{0,16},{16,0},{1,17},{17,1},{2,18},{18,2},{3,19},{19,3},{4,20},{20... | collective-permute-start | bytes 98312 | tf_op jit(solution)/shard_map/ppermute | solution.py:237

commit v22 on v21

--- a/solution.py
+++ b/solution.py
@@ -49,7 +49,7 @@
 
 
 def peer_of(place):
-    return place // Y * Y + place % YL * YH + place % Y // YL
+    return (place % YL * YH + place % Y // YL) * ZH + place // Y
 
 
 def pack_kernel(amplitudes, out):
@@ -244,7 +244,7 @@
 
     integrals = ladder_block.reshape(-1, ladder_block.shape[2])
     (parts,) = call(ladder_kernel, [(CHIPS, BLOCK, LANES)], [VMEM] * 3)(window, integrals, cycle)
-    parts = lax.all_to_all(parts, ("zh", "yl", "yh"), 0, 0, tiled=True)
+    parts = lax.all_to_all(parts, ("yl", "yh", "zh"), 0, 0, tiled=True)
     (result,) = call(last_kernel, [amplitudes.shape], [VMEM] * 2)(denominator, parts)
     return result
 

time: 112 us -> 113 us (level)
  blocking collectives: 62.1 us -> 63.7 us
    all_to_all x1, blocking collectives: 32.1 us -> 33.7 us  [per_device(): parts = lax.all_to_all(parts, ('yl', 'yh', 'zh'), 0, 0, tiled=True)]
where the time goes in v22:
time: 113 us
  blocking collectives  63.7 us (56%)
  starting transfers between devices  23.9 us (21%)
  waiting for transfers between devices  17.7 us (16%)
  Pallas kernels  5.42 us (5%)
  local copies, waits for them, and re-layouts  1.86 us (2%)
    all_to_all x1, blocking collectives, per_device(): parts = lax.all_to_all(parts, ('yl', 'yh', 'zh'), 0, 0, tiled=True)  33.7 us
    all_to_all x1, blocking collectives, per_device(): window = lax.all_to_all(window, ('yh', 'yl'), 0, 0, tiled=True)  15.1 us
    all_to_all x1, blocking collectives, per_device(): column = lax.all_to_all(copies, 'zl', 0, 0, tiled=True)  14.9 us
    ppermute x1, starting transfers between devices, per_device(): mine = lax.ppermute(far, 'zh', swap)  8.22 us
    ppermute x1, waiting for transfers between devices, per_device(): mine = lax.ppermute(far, 'zh', swap)  7.2 us
    all_to_all x1, waiting for transfers between devices, per_device(): gathered = lax.all_to_all(copies, 'x', 0, 0, tiled=True)  6.62 us
    all_to_all x1, starting transfers between devices, per_device(): lax.all_to_all(cycle.reshape(CHIPS, BLOCK, LANES), ('x', 'zl'), 0, 0, til...  5.6 us
    all_to_all x1, starting transfers between devices, per_device(): gathered = lax.all_to_all(copies, 'x', 0, 0, tiled=True)  4.29 us
  transfers between devices with their start and end apart: 6, of which 6 were waited for; matrix products, arithmetic and copies ran while one was open for 0% of the time, Pallas kernels for 2%

profile of v22, /device:TPU:8, one launch (start us, length us, event | category | flops | bytes accessed | tf_op | source)
XLA Modules:
  0.0 112.6 jit_solution(14596587793134082068)
XLA Ops:
  0.0 0.0 copy-start.1
  0.0 0.0 copy-start.2
  0.0 0.9 copy-done.2
  0.9 14.9 %all_to_all.25 = f32[4,104,128]{2,1,0:T(8,128)S(1)} all-to-all(f32[4,104,128]{2,1,0:T(8,128)S(1)} %shard_map.64), channel_id=1, replica_groups=mesh['zl'=4,'x'=4,'core'=2,'zh'=2,'yh'=4,'yl'=2] {'zl'}, dimensions={0} | all-to-all | bytes 425984 | tf_op jit(solution)/shard_map/all_to_all | solution.py:199
  15.8 1.0 broadcast_in_dim.8
  16.7 4.3 %all-to-all-start.1 = ((f32[4,416,128]{2,1,0:T(8,128)}), f32[4,416,128]{2,1,0:T(8,128)S(1)}, u32[]{:S(2)}, u32[]{:S(2)}) async-start(f32[4,416,128]{2,1,0:T(8,128)} %broadcast_in_dim.8), calls=%async_computation.1 | async-start | bytes 1703936 | tf_op jit(solution)/shard_map/all_to_all | solution.py:201
  21.0 0.0 copy-done.1
  21.0 1.9 %collective-permute-start = (f32[512,256]{1,0:T(8,128)S(1)}, f32[512,256]{1,0:T(8,128)S(1)}, u32[]{:S(2)}, u32[]{:S(2)}) collective-permute-start(f32[512,256]{1,0:T(8,128)S(1)} %copy-done.1), channel_id=1, source_target_pairs={{0,16},{16,0},{1,17},{17,1},{2,18},{18,2},{3,19},{19,3},{4,20},{20... | collective-permute-start | bytes 1572872 | tf_op jit(solution)/shard_map/ppermute | solution.py:197
  22.9 1.9 %collective-permute-done.other = f32[512,256]{1,0:T(8,128)S(1)} collective-permute-done((f32[512,256]{1,0:T(8,128)S(1)}, f32[512,256]{1,0:T(8,128)S(1)}, u32[]{:S(2)}, u32[]{:S(2)}) %collective-permute-start) | collective-permute-done | bytes 524320 | tf_op jit(solution)/shard_map/ppermute | solution.py:197
  24.8 0.2 shard_map.65
  25.0 6.6 %all-to-all-done.1 = f32[4,416,128]{2,1,0:T(8,128)S(1)} async-done(((f32[4,416,128]{2,1,0:T(8,128)}), f32[4,416,128]{2,1,0:T(8,128)S(1)}, u32[]{:S(2)}, u32[]{:S(2)}) %all-to-all-start.1) | async-done | bytes 852000 | tf_op jit(solution)/shard_map/all_to_all | solution.py:201
  31.7 0.0 copy-start.4
  31.7 1.8 %shard_map.66 = f32[1664,128]{1,0:T(8,128)} custom-call(f32[1664,128]{1,0:T(8,128)S(1)} %bitcast.5, bf16[512,512]{1,0:T(8,128)(2,1)S(1)} %get-tuple-element.14.high, bf16[512,512]{1,0:T(8,128)(2,1)S(1)} %get-tuple-element.15.low), custom_call_target="tpu_custom_call" | custom-call | tf_op jit(solution)/shard_map/pallas_call | solution.py:211
  33.4 0.0 copy-start.3
  33.4 0.0 copy-start.5
  33.5 0.0 copy-start
  33.5 5.6 %all-to-all-start.2 = ((f32[16,104,128]{2,1,0:T(8,128)}), f32[16,104,128]{2,1,0:T(8,128)S(1)}, u32[]{:S(2)}, u32[]{:S(2)}) async-start(f32[16,104,128]{2,1,0:T(8,128)} %bitcast.3), calls=%async_computation.2 | async-start | bytes 1703936 | tf_op jit(solution)/shard_map/all_to_all | solution.py:223
  39.1 0.0 copy-done.4
  39.1 1.4 %shard_map.67 = f32[2,128,128]{2,1,0:T(8,128)S(1)} custom-call(s32[2]{0:T(128)S(1)} %copy-done.4, f32[1664,128]{1,0:T(8,128)S(1)} %bitcast.6), custom_call_target="tpu_custom_call" | custom-call | tf_op jit(solution)/shard_map/pallas_call | solution.py:225
  40.5 1.9 %collective-permute-start.1 = (f32[2,8,16,128]{3,2,1,0:T(8,128)S(1)}, f32[2,8,16,128]{3,2,1,0:T(8,128)S(1)}, u32[]{:S(2)}, u32[]{:S(2)}) collective-permute-start(f32[2,8,16,128]{3,2,1,0:T(8,128)S(1)} %bitcast.8), channel_id=1, source_target_pairs={{0,16},{16,0},{1,17},{17,1},{2,18},{18,2},{3,19},{19,3},{4,20},{20... | collective-permute-start | bytes 393224 | tf_op jit(solution)/shard_map/ppermute | solution.py:232
  42.5 1.3 %collective-permute-done.1.other = f32[2,8,16,128]{3,2,1,0:T(8,128)S(1)} collective-permute-done((f32[2,8,16,128]{3,2,1,0:T(8,128)S(1)}, f32[2,8,16,128]{3,2,1,0:T(8,128)S(1)}, u32[]{:S(2)}, u32[]{:S(2)}) %collective-permute-start.1) | collective-permute-done | bytes 131104 | tf_op jit(solution)/shard_map/ppermute | solution.py:232
  43.8 8.2 %collective-permute-start.2 = (f32[8,8,128]{2,1,0:T(8,128)S(1)}, f32[8,8,128]{2,1,0:T(8,128)S(1)}, u32[]{:S(2)}, u32[]{:S(2)}) collective-permute-start(f32[8,8,128]{2,1,0:T(8,128)S(1)} %get-tuple-element.18), channel_id=1, source_target_pairs={{0,8},{8,0},{1,9},{9,1},{2,10},{10,2},{3,11},{11,3},{4,12},{12,4},... | collective-permute-start | bytes 98312 | tf_op jit(solution)/shard_map/ppermute | solution.py:236
  52.0 7.2 %collective-permute-done.2.mine = f32[8,8,128]{2,1,0:T(8,128)S(1)} collective-permute-done((f32[8,8,128]{2,1,0:T(8,128)S(1)}, f32[8,8,128]{2,1,0:T(8,128)S(1)}, u32[]{:S(2)}, u32[]{:S(2)}) %collective-permute-start.2) | collective-permute-done | bytes 32800 | tf_op jit(solution)/shard_map/ppermute | solution.py:236
  59.2 1.9 %collective-permute-start.3 = (f32[8,8,128]{2,1,0:T(8,128)S(1)}, f32[8,8,128]{2,1,0:T(8,128)S(1)}, u32[]{:S(2)}, u32[]{:S(2)}) collective-permute-start(f32[8,8,128]{2,1,0:T(8,128)S(1)} %collective-permute-done.2.mine), channel_id=1, source_target_pairs={{0,16},{16,0},{1,17},{17,1},{2,18},{18,2},{3,19},{19,3},{4,20},{20... | collective-permute-start | bytes 98312 | tf_op jit(solution)/shard_map/ppermute | solution.py:237
  61.1 0.0 copy-done.3
  61.1 0.0 copy-done.5
  61.1 0.7 shard_map.70.denominator
  61.8 0.5 collective-permute-done.3.theirs
  62.3 0.2 all-to-all-done.2.cycle
  62.5 15.1 %all_to_all.26.window = f32[8,32,128]{2,1,0:T(8,128)S(1)} all-to-all(f32[8,32,128]{2,1,0:T(8,128)S(1)} %shard_map.69), channel_id=1, replica_groups=mesh['zl'=4,'x'=4,'core'=2,'zh'=2,'yh'=4,'yl'=2] {'yh','yl'}, dimensions={0} | all-to-all | bytes 262144 | tf_op jit(solution)/shard_map/all_to_all | solution.py:243
  77.6 0.0 copy-done
  77.6 0.6 shard_map.71
  78.2 33.7 %all_to_all.27.parts = f32[16,104,128]{2,1,0:T(8,128)S(1)} all-to-all(f32[16,104,128]{2,1,0:T(8,128)S(1)} %shard_map.71), channel_id=1, replica_groups=mesh['zl'=4,'x'=4,'core'=2,'zh'=2,'yh'=4,'yl'=2] {'yl','yh','zh'}, dimensions={0} | all-to-all | bytes 1703936 | tf_op jit(solution)/shard_map/all_to_all | solution.py:247
  111.9 0.7 shard_map.72
  (3 shorter events, 0.0 us)
Async XLA Ops:
  0.0 21.0 %copy-start.1 = (f32[512,256]{1,0:T(8,128)S(1)}, f32[512,256]{1,0:T(8,128)}, u32[]{:S(2)}) copy-start(f32[512,256]{1,0:T(8,128)} %own.1) | copy-start | bytes 1572868
  0.0 0.9 copy-start.2
  16.7 14.9 %all-to-all-start.1 = ((f32[4,416,128]{2,1,0:T(8,128)}), f32[4,416,128]{2,1,0:T(8,128)S(1)}, u32[]{:S(2)}, u32[]{:S(2)}) async-start(f32[4,416,128]{2,1,0:T(8,128)} %broadcast_in_dim.8), calls=%async_computation.1 | async-start | bytes 1703936 | tf_op jit(solution)/shard_map/all_to_all | solution.py:201
  21.0 3.8 %collective-permute-start = (f32[512,256]{1,0:T(8,128)S(1)}, f32[512,256]{1,0:T(8,128)S(1)}, u32[]{:S(2)}, u32[]{:S(2)}) collective-permute-start(f32[512,256]{1,0:T(8,128)S(1)} %copy-done.1), channel_id=1, source_target_pairs={{0,16},{16,0},{1,17},{17,1},{2,18},{18,2},{3,19},{19,3},{4,20},{20... | collective-permute-start | bytes 1572872 | tf_op jit(solution)/shard_map/ppermute | solution.py:197
  31.7 7.4 %copy-start.4 = (s32[2]{0:T(128)S(1)}, s32[2]{0:T(128)}, u32[]{:S(2)}) copy-start(s32[2]{0:T(128)} %tiles.3) | copy-start | bytes 28
  33.4 27.7 %copy-start.3 = (f32[832]{0:T(1024)S(1)}, f32[832]{0:T(1024)}, u32[]{:S(2)}) copy-start(f32[832]{0:T(1024)} %virtual.1) | copy-start | bytes 9988
  33.4 27.7 %copy-start.5 = (f32[128]{0:T(128)S(1)}, f32[128]{0:T(128)}, u32[]{:S(2)}) copy-start(f32[128]{0:T(128)} %occupied.1) | copy-start | bytes 1540
  33.5 44.2 %copy-start = (f32[4,64,1664]{2,1,0:T(8,128)S(1)}, f32[4,64,1664]{2,1,0:T(8,128)}, u32[]{:S(2)}) copy-start(f32[4,64,1664]{2,1,0:T(8,128)} %param.8) | copy-start | bytes 5111812
  33.5 29.0 %all-to-all-start.2 = ((f32[16,104,128]{2,1,0:T(8,128)}), f32[16,104,128]{2,1,0:T(8,128)S(1)}, u32[]{:S(2)}, u32[]{:S(2)}) async-start(f32[16,104,128]{2,1,0:T(8,128)} %bitcast.3), calls=%async_computation.2 | async-start | bytes 1703936 | tf_op jit(solution)/shard_map/all_to_all | solution.py:223
  40.5 3.2 %collective-permute-start.1 = (f32[2,8,16,128]{3,2,1,0:T(8,128)S(1)}, f32[2,8,16,128]{3,2,1,0:T(8,128)S(1)}, u32[]{:S(2)}, u32[]{:S(2)}) collective-permute-start(f32[2,8,16,128]{3,2,1,0:T(8,128)S(1)} %bitcast.8), channel_id=1, source_target_pairs={{0,16},{16,0},{1,17},{17,1},{2,18},{18,2},{3,19},{19,3},{4,20},{20... | collective-permute-start | bytes 393224 | tf_op jit(solution)/shard_map/ppermute | solution.py:232
  43.8 15.4 %collective-permute-start.2 = (f32[8,8,128]{2,1,0:T(8,128)S(1)}, f32[8,8,128]{2,1,0:T(8,128)S(1)}, u32[]{:S(2)}, u32[]{:S(2)}) collective-permute-start(f32[8,8,128]{2,1,0:T(8,128)S(1)} %get-tuple-element.18), channel_id=1, source_target_pairs={{0,8},{8,0},{1,9},{9,1},{2,10},{10,2},{3,11},{11,3},{4,12},{12,4},... | collective-permute-start | bytes 98312 | tf_op jit(solution)/shard_map/ppermute | solution.py:236
  59.2 3.1 %collective-permute-start.3 = (f32[8,8,128]{2,1,0:T(8,128)S(1)}, f32[8,8,128]{2,1,0:T(8,128)S(1)}, u32[]{:S(2)}, u32[]{:S(2)}) collective-permute-start(f32[8,8,128]{2,1,0:T(8,128)S(1)} %collective-permute-done.2.mine), channel_id=1, source_target_pairs={{0,16},{16,0},{1,17},{17,1},{2,18},{18,2},{3,19},{19,3},{4,20},{20... | collective-permute-start | bytes 98312 | tf_op jit(solution)/shard_map/ppermute | solution.py:237

commit v23 on v21

--- a/solution.py
+++ b/solution.py
@@ -92,9 +92,10 @@
 
 def join_kernel(near, mine, theirs, out):
     core = lax.axis_index("core")
-    out[:, : 2 * ROWS, :] = near[...]
-    out[:, 2 * ROWS : 3 * ROWS, :] = jnp.where(core == 0, mine[...], theirs[...])
-    out[:, 3 * ROWS :, :] = jnp.where(core == 0, theirs[...], mine[...])
+    for y in range(Y):
+        out[peer_of(y), : 2 * ROWS, :] = near[y]
+        out[peer_of(y), 2 * ROWS : 3 * ROWS, :] = jnp.where(core == 0, mine[y], theirs[y])
+        out[peer_of(y), 3 * ROWS :, :] = jnp.where(core == 0, theirs[y], mine[y])
 
 
 def prepare_kernel(own, other, high, low):
@@ -136,7 +137,7 @@
     lefts = []
     for part in range(2):
         near, far = [
-            window[:, start : start + ROWS, :].reshape(Y * ROWS, LANES)
+            jnp.concatenate([window[peer_of(y), start : start + ROWS, :] for y in range(Y)], 0)
             for start in (part * ROWS, (2 + part) * ROWS)
         ]
         halves = [jnp.where(first, near, far), jnp.where(first, far, near)]
@@ -240,7 +241,7 @@
         tiles, occupied, virtual
     )
     window, denominator, cycle = lax.optimization_barrier((window, denominator, cycle))
-    window = lax.all_to_all(window, ("yh", "yl"), 0, 0, tiled=True)
+    window = lax.all_to_all(window, ("yl", "yh"), 0, 0, tiled=True)
 
     integrals = ladder_block.reshape(-1, ladder_block.shape[2])
     (parts,) = call(ladder_kernel, [(CHIPS, BLOCK, LANES)], [VMEM] * 3)(window, integrals, cycle)

time: 112 us -> 112 us (level)
  no operation moved by 1% of the time
where the time goes in v23:
time: 112 us; the launch traced here: 111 us
  blocking collectives  62.3 us (56%)
  starting transfers between devices  23.9 us (21%)
  waiting for transfers between devices  17.7 us (16%)
  Pallas kernels  5.42 us (5%)
  local copies, waits for them, and re-layouts  1.86 us (2%)
    all_to_all x1, blocking collectives, per_device(): parts = lax.all_to_all(parts, ('zh', 'yl', 'yh'), 0, 0, tiled=True)  32.3 us
    all_to_all x1, blocking collectives, per_device(): window = lax.all_to_all(window, ('yl', 'yh'), 0, 0, tiled=True)  15.1 us
    all_to_all x1, blocking collectives, per_device(): column = lax.all_to_all(copies, 'zl', 0, 0, tiled=True)  14.9 us
    ppermute x1, starting transfers between devices, per_device(): mine = lax.ppermute(far, 'zh', swap)  8.22 us
    ppermute x1, waiting for transfers between devices, per_device(): mine = lax.ppermute(far, 'zh', swap)  7.2 us
    all_to_all x1, waiting for transfers between devices, per_device(): gathered = lax.all_to_all(copies, 'x', 0, 0, tiled=True)  6.62 us
    all_to_all x1, starting transfers between devices, per_device(): lax.all_to_all(cycle.reshape(CHIPS, BLOCK, LANES), ('x', 'zl'), 0, 0, til...  5.6 us
    all_to_all x1, starting transfers between devices, per_device(): gathered = lax.all_to_all(copies, 'x', 0, 0, tiled=True)  4.29 us
  transfers between devices with their start and end apart: 6, of which 6 were waited for; matrix products, arithmetic and copies ran while one was open for 0% of the time, Pallas kernels for 2%

profile of v23, /device:TPU:8, one launch (start us, length us, event | category | flops | bytes accessed | tf_op | source)
XLA Modules:
  0.0 111.2 jit_solution(16554598989534374387)
XLA Ops:
  0.0 0.0 copy-start.1
  0.0 0.0 copy-start.2
  0.0 0.9 copy-done.2
  0.9 14.9 %all_to_all.25 = f32[4,104,128]{2,1,0:T(8,128)S(1)} all-to-all(f32[4,104,128]{2,1,0:T(8,128)S(1)} %shard_map.64), channel_id=1, replica_groups=mesh['zl'=4,'x'=4,'core'=2,'zh'=2,'yh'=4,'yl'=2] {'zl'}, dimensions={0} | all-to-all | bytes 425984 | tf_op jit(solution)/shard_map/all_to_all | solution.py:200
  15.8 1.0 broadcast_in_dim.8
  16.7 4.3 %all-to-all-start.1 = ((f32[4,416,128]{2,1,0:T(8,128)}), f32[4,416,128]{2,1,0:T(8,128)S(1)}, u32[]{:S(2)}, u32[]{:S(2)}) async-start(f32[4,416,128]{2,1,0:T(8,128)} %broadcast_in_dim.8), calls=%async_computation.1 | async-start | bytes 1703936 | tf_op jit(solution)/shard_map/all_to_all | solution.py:202
  21.0 0.0 copy-done.1
  21.0 1.9 %collective-permute-start = (f32[512,256]{1,0:T(8,128)S(1)}, f32[512,256]{1,0:T(8,128)S(1)}, u32[]{:S(2)}, u32[]{:S(2)}) collective-permute-start(f32[512,256]{1,0:T(8,128)S(1)} %copy-done.1), channel_id=1, source_target_pairs={{0,16},{16,0},{1,17},{17,1},{2,18},{18,2},{3,19},{19,3},{4,20},{20... | collective-permute-start | bytes 1572872 | tf_op jit(solution)/shard_map/ppermute | solution.py:198
  22.9 1.9 %collective-permute-done.other = f32[512,256]{1,0:T(8,128)S(1)} collective-permute-done((f32[512,256]{1,0:T(8,128)S(1)}, f32[512,256]{1,0:T(8,128)S(1)}, u32[]{:S(2)}, u32[]{:S(2)}) %collective-permute-start) | collective-permute-done | bytes 524320 | tf_op jit(solution)/shard_map/ppermute | solution.py:198
  24.8 0.2 shard_map.65
  25.0 6.6 %all-to-all-done.1 = f32[4,416,128]{2,1,0:T(8,128)S(1)} async-done(((f32[4,416,128]{2,1,0:T(8,128)}), f32[4,416,128]{2,1,0:T(8,128)S(1)}, u32[]{:S(2)}, u32[]{:S(2)}) %all-to-all-start.1) | async-done | bytes 852000 | tf_op jit(solution)/shard_map/all_to_all | solution.py:202
  31.7 0.0 copy-start.4
  31.7 1.8 %shard_map.66 = f32[1664,128]{1,0:T(8,128)} custom-call(f32[1664,128]{1,0:T(8,128)S(1)} %bitcast.5, bf16[512,512]{1,0:T(8,128)(2,1)S(1)} %get-tuple-element.14.high, bf16[512,512]{1,0:T(8,128)(2,1)S(1)} %get-tuple-element.15.low), custom_call_target="tpu_custom_call" | custom-call | tf_op jit(solution)/shard_map/pallas_call | solution.py:212
  33.4 0.0 copy-start.3
  33.4 0.0 copy-start.5
  33.5 0.0 copy-start
  33.5 5.6 %all-to-all-start.2 = ((f32[16,104,128]{2,1,0:T(8,128)}), f32[16,104,128]{2,1,0:T(8,128)S(1)}, u32[]{:S(2)}, u32[]{:S(2)}) async-start(f32[16,104,128]{2,1,0:T(8,128)} %bitcast.3), calls=%async_computation.2 | async-start | bytes 1703936 | tf_op jit(solution)/shard_map/all_to_all | solution.py:224
  39.1 0.0 copy-done.4
  39.1 1.4 %shard_map.67 = f32[2,128,128]{2,1,0:T(8,128)S(1)} custom-call(s32[2]{0:T(128)S(1)} %copy-done.4, f32[1664,128]{1,0:T(8,128)S(1)} %bitcast.6), custom_call_target="tpu_custom_call" | custom-call | tf_op jit(solution)/shard_map/pallas_call | solution.py:226
  40.5 1.9 %collective-permute-start.1 = (f32[2,8,16,128]{3,2,1,0:T(8,128)S(1)}, f32[2,8,16,128]{3,2,1,0:T(8,128)S(1)}, u32[]{:S(2)}, u32[]{:S(2)}) collective-permute-start(f32[2,8,16,128]{3,2,1,0:T(8,128)S(1)} %bitcast.8), channel_id=1, source_target_pairs={{0,16},{16,0},{1,17},{17,1},{2,18},{18,2},{3,19},{19,3},{4,20},{20... | collective-permute-start | bytes 393224 | tf_op jit(solution)/shard_map/ppermute | solution.py:233
  42.5 1.3 %collective-permute-done.1.other = f32[2,8,16,128]{3,2,1,0:T(8,128)S(1)} collective-permute-done((f32[2,8,16,128]{3,2,1,0:T(8,128)S(1)}, f32[2,8,16,128]{3,2,1,0:T(8,128)S(1)}, u32[]{:S(2)}, u32[]{:S(2)}) %collective-permute-start.1) | collective-permute-done | bytes 131104 | tf_op jit(solution)/shard_map/ppermute | solution.py:233
  43.8 8.2 %collective-permute-start.2 = (f32[8,8,128]{2,1,0:T(8,128)S(1)}, f32[8,8,128]{2,1,0:T(8,128)S(1)}, u32[]{:S(2)}, u32[]{:S(2)}) collective-permute-start(f32[8,8,128]{2,1,0:T(8,128)S(1)} %get-tuple-element.18), channel_id=1, source_target_pairs={{0,8},{8,0},{1,9},{9,1},{2,10},{10,2},{3,11},{11,3},{4,12},{12,4},... | collective-permute-start | bytes 98312 | tf_op jit(solution)/shard_map/ppermute | solution.py:237
  52.0 7.2 %collective-permute-done.2.mine = f32[8,8,128]{2,1,0:T(8,128)S(1)} collective-permute-done((f32[8,8,128]{2,1,0:T(8,128)S(1)}, f32[8,8,128]{2,1,0:T(8,128)S(1)}, u32[]{:S(2)}, u32[]{:S(2)}) %collective-permute-start.2) | collective-permute-done | bytes 32800 | tf_op jit(solution)/shard_map/ppermute | solution.py:237
  59.2 1.9 %collective-permute-start.3 = (f32[8,8,128]{2,1,0:T(8,128)S(1)}, f32[8,8,128]{2,1,0:T(8,128)S(1)}, u32[]{:S(2)}, u32[]{:S(2)}) collective-permute-start(f32[8,8,128]{2,1,0:T(8,128)S(1)} %collective-permute-done.2.mine), channel_id=1, source_target_pairs={{0,16},{16,0},{1,17},{17,1},{2,18},{18,2},{3,19},{19,3},{4,20},{20... | collective-permute-start | bytes 98312 | tf_op jit(solution)/shard_map/ppermute | solution.py:238
  61.1 0.0 copy-done.3
  61.1 0.0 copy-done.5
  61.1 0.7 shard_map.70.denominator
  61.8 0.5 collective-permute-done.3.theirs
  62.3 0.2 all-to-all-done.2.cycle
  62.5 15.1 %all_to_all.26.window = f32[8,32,128]{2,1,0:T(8,128)S(1)} all-to-all(f32[8,32,128]{2,1,0:T(8,128)S(1)} %shard_map.69), channel_id=1, replica_groups=mesh['zl'=4,'x'=4,'core'=2,'zh'=2,'yh'=4,'yl'=2] {'yl','yh'}, dimensions={0} | all-to-all | bytes 262144 | tf_op jit(solution)/shard_map/all_to_all | solution.py:244
  77.6 0.0 copy-done
  77.6 0.6 shard_map.71
  78.2 32.3 %all_to_all.27.parts = f32[16,104,128]{2,1,0:T(8,128)S(1)} all-to-all(f32[16,104,128]{2,1,0:T(8,128)S(1)} %shard_map.71), channel_id=1, replica_groups=mesh['zl'=4,'x'=4,'core'=2,'zh'=2,'yh'=4,'yl'=2] {'zh','yl','yh'}, dimensions={0} | all-to-all | bytes 1703936 | tf_op jit(solution)/shard_map/all_to_all | solution.py:248
  110.5 0.7 shard_map.72
  (3 shorter events, 0.0 us)
Async XLA Ops:
  0.0 21.0 %copy-start.1 = (f32[512,256]{1,0:T(8,128)S(1)}, f32[512,256]{1,0:T(8,128)}, u32[]{:S(2)}) copy-start(f32[512,256]{1,0:T(8,128)} %own.1) | copy-start | bytes 1572868
  0.0 0.9 copy-start.2
  16.7 14.9 %all-to-all-start.1 = ((f32[4,416,128]{2,1,0:T(8,128)}), f32[4,416,128]{2,1,0:T(8,128)S(1)}, u32[]{:S(2)}, u32[]{:S(2)}) async-start(f32[4,416,128]{2,1,0:T(8,128)} %broadcast_in_dim.8), calls=%async_computation.1 | async-start | bytes 1703936 | tf_op jit(solution)/shard_map/all_to_all | solution.py:202
  21.0 3.8 %collective-permute-start = (f32[512,256]{1,0:T(8,128)S(1)}, f32[512,256]{1,0:T(8,128)S(1)}, u32[]{:S(2)}, u32[]{:S(2)}) collective-permute-start(f32[512,256]{1,0:T(8,128)S(1)} %copy-done.1), channel_id=1, source_target_pairs={{0,16},{16,0},{1,17},{17,1},{2,18},{18,2},{3,19},{19,3},{4,20},{20... | collective-permute-start | bytes 1572872 | tf_op jit(solution)/shard_map/ppermute | solution.py:198
  31.7 7.4 %copy-start.4 = (s32[2]{0:T(128)S(1)}, s32[2]{0:T(128)}, u32[]{:S(2)}) copy-start(s32[2]{0:T(128)} %tiles.3) | copy-start | bytes 28
  33.4 27.7 %copy-start.3 = (f32[832]{0:T(1024)S(1)}, f32[832]{0:T(1024)}, u32[]{:S(2)}) copy-start(f32[832]{0:T(1024)} %virtual.1) | copy-start | bytes 9988
  33.4 27.7 %copy-start.5 = (f32[128]{0:T(128)S(1)}, f32[128]{0:T(128)}, u32[]{:S(2)}) copy-start(f32[128]{0:T(128)} %occupied.1) | copy-start | bytes 1540
  33.5 44.2 %copy-start = (f32[4,64,1664]{2,1,0:T(8,128)S(1)}, f32[4,64,1664]{2,1,0:T(8,128)}, u32[]{:S(2)}) copy-start(f32[4,64,1664]{2,1,0:T(8,128)} %param.8) | copy-start | bytes 5111812
  33.5 29.0 %all-to-all-start.2 = ((f32[16,104,128]{2,1,0:T(8,128)}), f32[16,104,128]{2,1,0:T(8,128)S(1)}, u32[]{:S(2)}, u32[]{:S(2)}) async-start(f32[16,104,128]{2,1,0:T(8,128)} %bitcast.3), calls=%async_computation.2 | async-start | bytes 1703936 | tf_op jit(solution)/shard_map/all_to_all | solution.py:224
  40.5 3.2 %collective-permute-start.1 = (f32[2,8,16,128]{3,2,1,0:T(8,128)S(1)}, f32[2,8,16,128]{3,2,1,0:T(8,128)S(1)}, u32[]{:S(2)}, u32[]{:S(2)}) collective-permute-start(f32[2,8,16,128]{3,2,1,0:T(8,128)S(1)} %bitcast.8), channel_id=1, source_target_pairs={{0,16},{16,0},{1,17},{17,1},{2,18},{18,2},{3,19},{19,3},{4,20},{20... | collective-permute-start | bytes 393224 | tf_op jit(solution)/shard_map/ppermute | solution.py:233
  43.8 15.4 %collective-permute-start.2 = (f32[8,8,128]{2,1,0:T(8,128)S(1)}, f32[8,8,128]{2,1,0:T(8,128)S(1)}, u32[]{:S(2)}, u32[]{:S(2)}) collective-permute-start(f32[8,8,128]{2,1,0:T(8,128)S(1)} %get-tuple-element.18), channel_id=1, source_target_pairs={{0,8},{8,0},{1,9},{9,1},{2,10},{10,2},{3,11},{11,3},{4,12},{12,4},... | collective-permute-start | bytes 98312 | tf_op jit(solution)/shard_map/ppermute | solution.py:237
  59.2 3.1 %collective-permute-start.3 = (f32[8,8,128]{2,1,0:T(8,128)S(1)}, f32[8,8,128]{2,1,0:T(8,128)S(1)}, u32[]{:S(2)}, u32[]{:S(2)}) collective-permute-start(f32[8,8,128]{2,1,0:T(8,128)S(1)} %collective-permute-done.2.mine), channel_id=1, source_target_pairs={{0,16},{16,0},{1,17},{17,1},{2,18},{18,2},{3,19},{19,3},{4,20},{20... | collective-permute-start | bytes 98312 | tf_op jit(solution)/shard_map/ppermute | solution.py:238

commit v24 on v21

--- a/solution.py
+++ b/solution.py
@@ -19,7 +19,7 @@
 EVERY = ("zl", "x", "core", "zh", "yh", "yl")
 VMEM = pl.BlockSpec(memory_space=pltpu.VMEM)
 SMEM = pl.BlockSpec(memory_space=pltpu.SMEM)
-PARAMS = pltpu.CompilerParams(vmem_limit_bytes=32 * 1024 * 1024)
+PARAMS = pltpu.CompilerParams(vmem_limit_bytes=16 * 1024 * 1024)
 
 
 def split(value):

time: 112 us -> 112 us (level)
  no operation moved by 1% of the time
where the time goes in v24:
time: 112 us; the launch traced here: 111 us
  blocking collectives  62.1 us (55%)
  starting transfers between devices  23.9 us (21%)
  waiting for transfers between devices  17.7 us (16%)
  Pallas kernels  5.42 us (5%)
  local copies, waits for them, and re-layouts  1.86 us (2%)
    all_to_all x1, blocking collectives, per_device(): parts = lax.all_to_all(parts, ('zh', 'yl', 'yh'), 0, 0, tiled=True)  32.1 us
    all_to_all x1, blocking collectives, per_device(): window = lax.all_to_all(window, ('yh', 'yl'), 0, 0, tiled=True)  15.1 us
    all_to_all x1, blocking collectives, per_device(): column = lax.all_to_all(copies, 'zl', 0, 0, tiled=True)  14.9 us
    ppermute x1, starting transfers between devices, per_device(): mine = lax.ppermute(far, 'zh', swap)  8.22 us
    ppermute x1, waiting for transfers between devices, per_device(): mine = lax.ppermute(far, 'zh', swap)  7.2 us
    all_to_all x1, waiting for transfers between devices, per_device(): gathered = lax.all_to_all(copies, 'x', 0, 0, tiled=True)  6.62 us
    all_to_all x1, starting transfers between devices, per_device(): lax.all_to_all(cycle.reshape(CHIPS, BLOCK, LANES), ('x', 'zl'), 0, 0, til...  5.6 us
    all_to_all x1, starting transfers between devices, per_device(): gathered = lax.all_to_all(copies, 'x', 0, 0, tiled=True)  4.29 us
  transfers between devices with their start and end apart: 6, of which 6 were waited for; matrix products, arithmetic and copies ran while one was open for 0% of the time, Pallas kernels for 2%

profile of v24, /device:TPU:8, one launch (start us, length us, event | category | flops | bytes accessed | tf_op | source)
XLA Modules:
  0.0 111.0 jit_solution(15226457082991452737)
XLA Ops:
  0.0 0.0 copy-start.1
  0.0 0.0 copy-start.2
  0.0 0.9 copy-done.2
  0.9 14.9 %all_to_all.25 = f32[4,104,128]{2,1,0:T(8,128)S(1)} all-to-all(f32[4,104,128]{2,1,0:T(8,128)S(1)} %shard_map.64), channel_id=1, replica_groups=mesh['zl'=4,'x'=4,'core'=2,'zh'=2,'yh'=4,'yl'=2] {'zl'}, dimensions={0} | all-to-all | bytes 425984 | tf_op jit(solution)/shard_map/all_to_all | solution.py:199
  15.8 1.0 broadcast_in_dim.8
  16.7 4.3 %all-to-all-start.1 = ((f32[4,416,128]{2,1,0:T(8,128)}), f32[4,416,128]{2,1,0:T(8,128)S(1)}, u32[]{:S(2)}, u32[]{:S(2)}) async-start(f32[4,416,128]{2,1,0:T(8,128)} %broadcast_in_dim.8), calls=%async_computation.1 | async-start | bytes 1703936 | tf_op jit(solution)/shard_map/all_to_all | solution.py:201
  21.0 0.0 copy-done.1
  21.0 1.9 %collective-permute-start = (f32[512,256]{1,0:T(8,128)S(1)}, f32[512,256]{1,0:T(8,128)S(1)}, u32[]{:S(2)}, u32[]{:S(2)}) collective-permute-start(f32[512,256]{1,0:T(8,128)S(1)} %copy-done.1), channel_id=1, source_target_pairs={{0,16},{16,0},{1,17},{17,1},{2,18},{18,2},{3,19},{19,3},{4,20},{20... | collective-permute-start | bytes 1572872 | tf_op jit(solution)/shard_map/ppermute | solution.py:197
  22.9 1.9 %collective-permute-done.other = f32[512,256]{1,0:T(8,128)S(1)} collective-permute-done((f32[512,256]{1,0:T(8,128)S(1)}, f32[512,256]{1,0:T(8,128)S(1)}, u32[]{:S(2)}, u32[]{:S(2)}) %collective-permute-start) | collective-permute-done | bytes 524320 | tf_op jit(solution)/shard_map/ppermute | solution.py:197
  24.8 0.2 shard_map.65
  25.0 6.6 %all-to-all-done.1 = f32[4,416,128]{2,1,0:T(8,128)S(1)} async-done(((f32[4,416,128]{2,1,0:T(8,128)}), f32[4,416,128]{2,1,0:T(8,128)S(1)}, u32[]{:S(2)}, u32[]{:S(2)}) %all-to-all-start.1) | async-done | bytes 852000 | tf_op jit(solution)/shard_map/all_to_all | solution.py:201
  31.7 0.0 copy-start.4
  31.7 1.8 %shard_map.66 = f32[1664,128]{1,0:T(8,128)} custom-call(f32[1664,128]{1,0:T(8,128)S(1)} %bitcast.5, bf16[512,512]{1,0:T(8,128)(2,1)S(1)} %get-tuple-element.14.high, bf16[512,512]{1,0:T(8,128)(2,1)S(1)} %get-tuple-element.15.low), custom_call_target="tpu_custom_call" | custom-call | tf_op jit(solution)/shard_map/pallas_call | solution.py:211
  33.4 0.0 copy-start.3
  33.4 0.0 copy-start.5
  33.5 0.0 copy-start
  33.5 5.6 %all-to-all-start.2 = ((f32[16,104,128]{2,1,0:T(8,128)}), f32[16,104,128]{2,1,0:T(8,128)S(1)}, u32[]{:S(2)}, u32[]{:S(2)}) async-start(f32[16,104,128]{2,1,0:T(8,128)} %bitcast.3), calls=%async_computation.2 | async-start | bytes 1703936 | tf_op jit(solution)/shard_map/all_to_all | solution.py:223
  39.1 0.0 copy-done.4
  39.1 1.4 %shard_map.67 = f32[2,128,128]{2,1,0:T(8,128)S(1)} custom-call(s32[2]{0:T(128)S(1)} %copy-done.4, f32[1664,128]{1,0:T(8,128)S(1)} %bitcast.6), custom_call_target="tpu_custom_call" | custom-call | tf_op jit(solution)/shard_map/pallas_call | solution.py:225
  40.5 1.9 %collective-permute-start.1 = (f32[2,8,16,128]{3,2,1,0:T(8,128)S(1)}, f32[2,8,16,128]{3,2,1,0:T(8,128)S(1)}, u32[]{:S(2)}, u32[]{:S(2)}) collective-permute-start(f32[2,8,16,128]{3,2,1,0:T(8,128)S(1)} %bitcast.8), channel_id=1, source_target_pairs={{0,16},{16,0},{1,17},{17,1},{2,18},{18,2},{3,19},{19,3},{4,20},{20... | collective-permute-start | bytes 393224 | tf_op jit(solution)/shard_map/ppermute | solution.py:232
  42.5 1.3 %collective-permute-done.1.other = f32[2,8,16,128]{3,2,1,0:T(8,128)S(1)} collective-permute-done((f32[2,8,16,128]{3,2,1,0:T(8,128)S(1)}, f32[2,8,16,128]{3,2,1,0:T(8,128)S(1)}, u32[]{:S(2)}, u32[]{:S(2)}) %collective-permute-start.1) | collective-permute-done | bytes 131104 | tf_op jit(solution)/shard_map/ppermute | solution.py:232
  43.8 8.2 %collective-permute-start.2 = (f32[8,8,128]{2,1,0:T(8,128)S(1)}, f32[8,8,128]{2,1,0:T(8,128)S(1)}, u32[]{:S(2)}, u32[]{:S(2)}) collective-permute-start(f32[8,8,128]{2,1,0:T(8,128)S(1)} %get-tuple-element.18), channel_id=1, source_target_pairs={{0,8},{8,0},{1,9},{9,1},{2,10},{10,2},{3,11},{11,3},{4,12},{12,4},... | collective-permute-start | bytes 98312 | tf_op jit(solution)/shard_map/ppermute | solution.py:236
  52.0 7.2 %collective-permute-done.2.mine = f32[8,8,128]{2,1,0:T(8,128)S(1)} collective-permute-done((f32[8,8,128]{2,1,0:T(8,128)S(1)}, f32[8,8,128]{2,1,0:T(8,128)S(1)}, u32[]{:S(2)}, u32[]{:S(2)}) %collective-permute-start.2) | collective-permute-done | bytes 32800 | tf_op jit(solution)/shard_map/ppermute | solution.py:236
  59.2 1.9 %collective-permute-start.3 = (f32[8,8,128]{2,1,0:T(8,128)S(1)}, f32[8,8,128]{2,1,0:T(8,128)S(1)}, u32[]{:S(2)}, u32[]{:S(2)}) collective-permute-start(f32[8,8,128]{2,1,0:T(8,128)S(1)} %collective-permute-done.2.mine), channel_id=1, source_target_pairs={{0,16},{16,0},{1,17},{17,1},{2,18},{18,2},{3,19},{19,3},{4,20},{20... | collective-permute-start | bytes 98312 | tf_op jit(solution)/shard_map/ppermute | solution.py:237
  61.1 0.0 copy-done.3
  61.1 0.0 copy-done.5
  61.1 0.7 shard_map.70.denominator
  61.8 0.5 collective-permute-done.3.theirs
  62.3 0.2 all-to-all-done.2.cycle
  62.5 15.1 %all_to_all.26.window = f32[8,32,128]{2,1,0:T(8,128)S(1)} all-to-all(f32[8,32,128]{2,1,0:T(8,128)S(1)} %shard_map.69), channel_id=1, replica_groups=mesh['zl'=4,'x'=4,'core'=2,'zh'=2,'yh'=4,'yl'=2] {'yh','yl'}, dimensions={0} | all-to-all | bytes 262144 | tf_op jit(solution)/shard_map/all_to_all | solution.py:243
  77.6 0.0 copy-done
  77.6 0.6 shard_map.71
  78.2 32.1 %all_to_all.27.parts = f32[16,104,128]{2,1,0:T(8,128)S(1)} all-to-all(f32[16,104,128]{2,1,0:T(8,128)S(1)} %shard_map.71), channel_id=1, replica_groups=mesh['zl'=4,'x'=4,'core'=2,'zh'=2,'yh'=4,'yl'=2] {'zh','yl','yh'}, dimensions={0} | all-to-all | bytes 1703936 | tf_op jit(solution)/shard_map/all_to_all | solution.py:247
  110.4 0.7 shard_map.72
  (3 shorter events, 0.0 us)
Async XLA Ops:
  0.0 21.0 %copy-start.1 = (f32[512,256]{1,0:T(8,128)S(1)}, f32[512,256]{1,0:T(8,128)}, u32[]{:S(2)}) copy-start(f32[512,256]{1,0:T(8,128)} %own.1) | copy-start | bytes 1572868
  0.0 0.9 copy-start.2
  16.7 14.9 %all-to-all-start.1 = ((f32[4,416,128]{2,1,0:T(8,128)}), f32[4,416,128]{2,1,0:T(8,128)S(1)}, u32[]{:S(2)}, u32[]{:S(2)}) async-start(f32[4,416,128]{2,1,0:T(8,128)} %broadcast_in_dim.8), calls=%async_computation.1 | async-start | bytes 1703936 | tf_op jit(solution)/shard_map/all_to_all | solution.py:201
  21.0 3.8 %collective-permute-start = (f32[512,256]{1,0:T(8,128)S(1)}, f32[512,256]{1,0:T(8,128)S(1)}, u32[]{:S(2)}, u32[]{:S(2)}) collective-permute-start(f32[512,256]{1,0:T(8,128)S(1)} %copy-done.1), channel_id=1, source_target_pairs={{0,16},{16,0},{1,17},{17,1},{2,18},{18,2},{3,19},{19,3},{4,20},{20... | collective-permute-start | bytes 1572872 | tf_op jit(solution)/shard_map/ppermute | solution.py:197
  31.7 7.4 %copy-start.4 = (s32[2]{0:T(128)S(1)}, s32[2]{0:T(128)}, u32[]{:S(2)}) copy-start(s32[2]{0:T(128)} %tiles.3) | copy-start | bytes 28
  33.4 27.7 %copy-start.3 = (f32[832]{0:T(1024)S(1)}, f32[832]{0:T(1024)}, u32[]{:S(2)}) copy-start(f32[832]{0:T(1024)} %virtual.1) | copy-start | bytes 9988
  33.4 27.7 %copy-start.5 = (f32[128]{0:T(128)S(1)}, f32[128]{0:T(128)}, u32[]{:S(2)}) copy-start(f32[128]{0:T(128)} %occupied.1) | copy-start | bytes 1540
  33.5 44.2 %copy-start = (f32[4,64,1664]{2,1,0:T(8,128)S(1)}, f32[4,64,1664]{2,1,0:T(8,128)}, u32[]{:S(2)}) copy-start(f32[4,64,1664]{2,1,0:T(8,128)} %param.8) | copy-start | bytes 5111812
  33.5 29.0 %all-to-all-start.2 = ((f32[16,104,128]{2,1,0:T(8,128)}), f32[16,104,128]{2,1,0:T(8,128)S(1)}, u32[]{:S(2)}, u32[]{:S(2)}) async-start(f32[16,104,128]{2,1,0:T(8,128)} %bitcast.3), calls=%async_computation.2 | async-start | bytes 1703936 | tf_op jit(solution)/shard_map/all_to_all | solution.py:223
  40.5 3.2 %collective-permute-start.1 = (f32[2,8,16,128]{3,2,1,0:T(8,128)S(1)}, f32[2,8,16,128]{3,2,1,0:T(8,128)S(1)}, u32[]{:S(2)}, u32[]{:S(2)}) collective-permute-start(f32[2,8,16,128]{3,2,1,0:T(8,128)S(1)} %bitcast.8), channel_id=1, source_target_pairs={{0,16},{16,0},{1,17},{17,1},{2,18},{18,2},{3,19},{19,3},{4,20},{20... | collective-permute-start | bytes 393224 | tf_op jit(solution)/shard_map/ppermute | solution.py:232
  43.8 15.4 %collective-permute-start.2 = (f32[8,8,128]{2,1,0:T(8,128)S(1)}, f32[8,8,128]{2,1,0:T(8,128)S(1)}, u32[]{:S(2)}, u32[]{:S(2)}) collective-permute-start(f32[8,8,128]{2,1,0:T(8,128)S(1)} %get-tuple-element.18), channel_id=1, source_target_pairs={{0,8},{8,0},{1,9},{9,1},{2,10},{10,2},{3,11},{11,3},{4,12},{12,4},... | collective-permute-start | bytes 98312 | tf_op jit(solution)/shard_map/ppermute | solution.py:236
  59.2 3.1 %collective-permute-start.3 = (f32[8,8,128]{2,1,0:T(8,128)S(1)}, f32[8,8,128]{2,1,0:T(8,128)S(1)}, u32[]{:S(2)}, u32[]{:S(2)}) collective-permute-start(f32[8,8,128]{2,1,0:T(8,128)S(1)} %collective-permute-done.2.mine), channel_id=1, source_target_pairs={{0,16},{16,0},{1,17},{17,1},{2,18},{18,2},{3,19},{19,3},{4,20},{20... | collective-permute-start | bytes 98312 | tf_op jit(solution)/shard_map/ppermute | solution.py:237
